TPU v7x, 32 devices: a whole 2x2x4 slice. The times are simulated.
32 devices in a mesh: dp: 4 (over y, core), expert: 8 (over z, x).
Axes of the slice: x: 2, y: 2, z: 4, core: 2. Of those that a mesh axis runs over, the one named last changes fastest.
Arguments:
- tokens: bfloat16 [4096, 3584], P(('dp', 'expert')), may hold values from -6 to 6
- route_weight: float32 [4096], P(('dp', 'expert')), may hold values from 0.1 to 1
- cotangent: bfloat16 [4096, 1024], P(('dp', 'expert')), may hold values from -6 to 6
- slot_ids: int32 [4096], P(('dp', 'expert')), may hold values from 0 to 7, as said below
- placement: int32 [8], replicated, may hold values from 0 to 4, as said below
- weight: bfloat16 [8, 3584, 1024], P('expert'), as said below
- momentum: bfloat16 [8, 3584, 1024], P('expert', 'dp'), as said below
Outputs:
- expert_out: bfloat16 [4096, 1024], P(('dp', 'expert'))
- token_grad: bfloat16 [4096, 3584], P(('dp', 'expert'))
- new_weight: bfloat16 [8, 3584, 1024], P('expert', 'dp')
- new_momentum: bfloat16 [8, 3584, 1024], P('expert', 'dp')
Inputs may be any that keep to these rules, and one draw needn't show every extreme that they name: `slot_ids`: one device's 128 tokens (an aligned block) send at most 18 tokens to one slot; in each group of 8 consecutive blocks some slot gets exactly 18 from every block. `placement`: slots j and j + 4 carry the same number for exactly 3 values of j below 4; all other slots carry distinct numbers, and every number is used. `weight`: slots with equal placement numbers hold equal matrices. `momentum`: slots with equal placement numbers hold equal matrices.
All inputs are finite; a program needn't handle non-finite values.
Results may differ from a plain program's by a relative error of at most 0.018.
Values may be sent and summed in bfloat16 or wider, within the bound.
No kernel may reach another device: no remote copies, remote signals or barrier semaphores. Data moves between devices by JAX's collectives and lax.ppermute only.
A program may use at most 64 MiB of HBM per device.

v0:
```python
import jax
import jax.numpy as jnp
from jax import lax
from jax.sharding import PartitionSpec as P

D = 3584
F = 1024


learning_rate = 0.004
decay_rate = 0.9


def shifted(shard, axis, by):
    devices = lax.axis_size(axis)
    return lax.ppermute(shard, axis, [(i, (i + by) % devices) for i in range(devices)])


def shards(tokens, route_weight, cotangent, slot_ids, placement, weight, momentum):
    n_slots = lax.axis_size("expert")
    n_groups = lax.axis_size("dp")
    tok_count = tokens.shape[0]
    capacity = tok_count * 9 // 8 // n_slots
    onehot = (slot_ids[:, None] == jnp.arange(n_slots, dtype=jnp.int32)[None, :]).astype(jnp.int32)
    ranks = jnp.sum((jnp.cumsum(onehot, axis=0) - 1) * onehot, axis=1)
    position = slot_ids * capacity + ranks
    send_rows = jnp.zeros((n_slots * capacity, D), jnp.bfloat16).at[position].set(tokens)
    scaled = (route_weight[:, None] * cotangent.astype(jnp.float32)).astype(jnp.bfloat16)
    send_grads = jnp.zeros((n_slots * capacity, F), jnp.bfloat16).at[position].set(scaled)
    matrix = weight[0]
    rows_x = lax.all_to_all(
        send_rows.reshape(n_slots, capacity, D), "expert", split_axis=0, concat_axis=0, tiled=True
    )
    rows_g = lax.all_to_all(
        send_grads.reshape(n_slots, capacity, F), "expert", split_axis=0, concat_axis=0, tiled=True
    )
    width = rows_x.shape[1]
    flat_x = rows_x.reshape(-1, D)
    preact = jnp.dot(flat_x, matrix, preferred_element_type=jnp.float32)
    sigma = jax.nn.sigmoid(preact)
    act = (preact * sigma).astype(jnp.bfloat16)
    grad_pre = (
        rows_g.reshape(-1, F).astype(jnp.float32) * sigma * (1.0 + preact * (1.0 - sigma))
    ).astype(jnp.bfloat16)
    back = lax.dot_general(
        grad_pre, matrix, (((1,), (1,)), ((), ())), preferred_element_type=jnp.float32
    ).astype(jnp.bfloat16)
    back_act = lax.all_to_all(
        act.reshape(n_slots, width, F), "expert", split_axis=0, concat_axis=0, tiled=True
    )
    back_grad = lax.all_to_all(
        back.reshape(n_slots, width, D), "expert", split_axis=0, concat_axis=0, tiled=True
    )
    back_act, back_grad, recv_x, recv_grad = (
        back_act,
        back_grad,
        rows_x,
        grad_pre.reshape(n_slots, width, F),
    )
    act_rows = back_act.reshape(-1, F)[position]
    expert_out = (route_weight[:, None] * act_rows.astype(jnp.float32)).astype(jnp.bfloat16)
    token_grad = back_grad.reshape(-1, D)[position]
    flat_x = recv_x.reshape(-1, D)
    flat_grad = recv_grad.reshape(-1, F)
    row_count = flat_x.shape[0]
    share = D // n_groups
    columns = lax.all_to_all(
        flat_x.reshape(1, row_count, n_groups, share), "dp", split_axis=2, concat_axis=0, tiled=True
    )
    columns = columns.reshape(n_groups, row_count, share)
    terms = jnp.einsum(
        "krd,krf->kdf",
        columns,
        lax.all_gather(flat_grad[None], "dp", axis=0, tiled=True),
        preferred_element_type=jnp.float32,
    )
    terms = lax.optimization_barrier(terms.astype(jnp.bfloat16)).astype(jnp.float32)
    summed = jnp.sum(terms, axis=0)
    reduced = summed.astype(jnp.bfloat16)
    half = n_slots // 2
    partner_grad = shifted(reduced, "expert", half).astype(jnp.float32)
    my_slot = lax.axis_index("expert")
    partner_slot = (my_slot + half) % n_slots
    slot_range = jnp.arange(n_slots, dtype=jnp.int32)
    own_label = jnp.sum(jnp.where(slot_range == my_slot, placement, 0))
    partner_label = jnp.sum(jnp.where(slot_range == partner_slot, placement, 0))
    total = reduced.astype(jnp.float32) + jnp.where(
        own_label == partner_label, partner_grad, jnp.float32(0.0)
    )
    new_momentum = (decay_rate * momentum[0].astype(jnp.float32) + total).astype(jnp.bfloat16)
    old = lax.dynamic_slice_in_dim(matrix, lax.axis_index("dp") * share, share, 0).astype(
        jnp.float32
    )
    new_weight = (old - learning_rate * new_momentum.astype(jnp.float32)).astype(jnp.bfloat16)
    return (expert_out, token_grad, new_weight[None], new_momentum[None])


def solution(mesh):
    return jax.shard_map(
        shards,
        mesh=mesh,
        in_specs=(
            P(("dp", "expert"), None),
            P(("dp", "expert")),
            P(("dp", "expert"), None),
            P(("dp", "expert")),
            P(),
            P("expert", None, None),
            P("expert", "dp", None),
        ),
        out_specs=(
            P(("dp", "expert"), None),
            P(("dp", "expert"), None),
            P("expert", "dp", None),
            P("expert", "dp", None),
        ),
        check_vma=False,
    )
```

profile of v0, /device:TPU:0, one launch (start us, length us, event | category | flops | bytes accessed | tf_op | source)
XLA Modules:
  0.0 242.6 jit_solution(6013581003829654186)
XLA Ops:
  7.2 0.7 fusion.16
  7.9 0.2 reduce_window_sum.11
  8.1 0.8 select_reduce_fusion
  8.9 0.7 compare_select_fusion
  9.6 1.7 scatter_custom_fusion.1
  11.3 0.8 reshape.48
  12.1 7.3 %all-to-all-start.2 = ((bf16[8,18,1024]{2,1,0:T(8,128)(2,1)}), bf16[8,18,1024]{2,1,0:T(8,128)(2,1)S(1)}, u32[]{:S(2)}, u32[]{:S(2)}) async-start(bf16[8,18,1024]{2,1,0:T(8,128)(2,1)} %reshape.48), calls=%async_computation.2 | async-start | bytes 786432 | tf_op jit(solution)/shard_map/all_to_all | solution.py:34
  19.4 2.8 %scatter_custom_fusion = bf16[144,3584]{1,0:T(8,128)(2,1)S(1)} fusion(s32[128]{0:T(128)S(1)} %compare_select_fusion, bf16[128,3584]{1,0:T(8,128)(2,1)} %param.7, bf16[]{:T(256)} %constant.16.clone.1), kind=kCustom, calls=%fused_computation.21 | custom fusion | bytes 1032704 | tf_op jit(solution)/shard_map/scatter | solution.py:27
  22.2 1.3 reshape.44
  23.4 7.7 %all-to-all-done.2 = bf16[8,18,1024]{2,1,0:T(8,128)(2,1)S(1)} async-done(((bf16[8,18,1024]{2,1,0:T(8,128)(2,1)}), bf16[8,18,1024]{2,1,0:T(8,128)(2,1)S(1)}, u32[]{:S(2)}, u32[]{:S(2)}) %all-to-all-start.2) | async-done | bytes 294944 | tf_op jit(solution)/shard_map/all_to_all | solution.py:34
  31.1 0.0 copy-done.3
  31.1 3.6 %all-to-all-start = ((bf16[8,18,3584]{2,1,0:T(8,128)(2,1)}), bf16[8,18,3584]{2,1,0:T(8,128)(2,1)S(1)}, u32[]{:S(2)}, u32[]{:S(2)}) async-start(bf16[8,18,3584]{2,1,0:T(8,128)(2,1)} %reshape.44), calls=%async_computation | async-start | bytes 2752512 | tf_op jit(solution)/shard_map/all_to_all | solution.py:31
  34.7 0.0 all-gather.3.cloned.1.call-start
  34.7 0.1 reshape.52
  34.8 32.5 %all-to-all-done = bf16[8,18,3584]{2,1,0:T(8,128)(2,1)S(1)} async-done(((bf16[8,18,3584]{2,1,0:T(8,128)(2,1)}), bf16[8,18,3584]{2,1,0:T(8,128)(2,1)S(1)}, u32[]{:S(2)}, u32[]{:S(2)}) %all-to-all-start) | async-done | bytes 1032224 | tf_op jit(solution)/shard_map/all_to_all | solution.py:31
  67.3 0.4 reshape.45
  67.7 5.2 %multiply_convert_fusion = (bf16[144,1024]{1,0:T(8,128)(2,1)}, bf16[144,1024]{1,0:T(8,128)(2,1)S(1)}) fusion(f32[144,1024]{1,0:T(8,128)S(1)} %reshape.52, bf16[144,3584]{1,0:T(8,128)(2,1)S(1)} %reshape.45, bf16[1,3584,1024]{2,1,0:T(8,128)(2,1)} %param.12), kind=kOutput, calls=%fused_computation.16 | convolution fusion | flops 1058586624 | bytes 9551872 | tf_op jit(solution)/shard_map/dot_general | solution.py:39
  72.9 0.0 all-gather.3.cloned.1.call-update
  73.0 0.5 reshape_reshape.3
  73.5 1.1 copy.12
  74.6 3.5 %all-to-all-start.4 = ((bf16[1,144,4,896]{3,1,0,2:T(8,128)(2,1)}), bf16[1,144,4,896]{3,1,0,2:T(8,128)(2,1)S(1)}, u32[]{:S(2)}, u32[]{:S(2)}) async-start(bf16[1,144,4,896]{3,1,0,2:T(8,128)(2,1)} %copy.12), calls=%async_computation.4 | async-start | bytes 2064384 | tf_op jit(solution)/shard_map/all_to_all | solution.py:67
  78.1 0.8 reshape.46
  78.9 19.7 %all-to-all-done.4 = bf16[1,144,4,896]{3,1,0,2:T(8,128)(2,1)S(1)} async-done(((bf16[1,144,4,896]{3,1,0,2:T(8,128)(2,1)}), bf16[1,144,4,896]{3,1,0,2:T(8,128)(2,1)S(1)}, u32[]{:S(2)}, u32[]{:S(2)}) %all-to-all-start.4) | async-done | bytes 1032224 | tf_op jit(solution)/shard_map/all_to_all | solution.py:67
  98.7 3.6 %all-to-all-start.1 = ((bf16[8,18,1024]{2,1,0:T(8,128)(2,1)}), bf16[8,18,1024]{2,1,0:T(8,128)(2,1)S(1)}, u32[]{:S(2)}, u32[]{:S(2)}) async-start(bf16[8,18,1024]{2,1,0:T(8,128)(2,1)} %reshape.46), calls=%async_computation.1 | async-start | bytes 786432 | tf_op jit(solution)/shard_map/all_to_all | solution.py:48
  102.3 0.0 all-gather.3.cloned.1.call-done
  102.3 6.4 %convolution_convert_fusion = bf16[4,896,1024]{2,1,0:T(8,128)(2,1)} fusion(bf16[4,144,1024]{2,1,0:T(8,128)(2,1)} %bitcast.32, bf16[1,144,4,896]{3,1,0,2:T(8,128)(2,1)S(1)} %all-to-all-done.4), kind=kOutput, calls=%fused_computation.8 | convolution fusion | flops 1060634624 | bytes 9551872 | tf_op jit(solution)/shard_map/krd,krf->kdf/dot_general | solution.py:71
  108.7 5.7 %reduce_sum.40 = bf16[896,1024]{1,0:T(8,128)(2,1)S(1)} reduce(bf16[4,896,1024]{2,1,0:T(8,128)(2,1)} %convolution_convert_fusion, bf16[]{:T(256)} %constant.16.clone.1), dimensions={0}, to_apply=%region_4.5 | reduce | flops 2752512 | bytes 9175042 | tf_op jit(solution)/shard_map/reduce_sum | solution.py:78
  114.5 3.0 %collective-permute-start = (bf16[896,1024]{1,0:T(8,128)(2,1)S(1)}, bf16[896,1024]{1,0:T(8,128)(2,1)}, u32[]{:S(2)}, u32[]{:S(2)}) collective-permute-start(bf16[896,1024]{1,0:T(8,128)(2,1)S(1)} %reduce_sum.40), channel_id=1, source_target_pairs={{0,4},{1,5},{2,6},{3,7},{4,0},{5,1},{6,2},{7,3},{8,12},{9,13},{10,... | collective-permute-start | bytes 5505032 | tf_op jit(solution)/shard_map/ppermute | solution.py:16
  117.5 0.0 copy-done
  117.5 5.6 %fusion.4 = bf16[144,3584]{1,0:T(8,128)(2,1)S(1)} fusion(bf16[144,1024]{1,0:T(8,128)(2,1)S(1)} %copy-done, bf16[1,3584,1024]{2,1,0:T(8,128)(2,1)} %param.12), kind=kOutput, calls=%fused_computation.9 | convolution fusion | flops 1057480704 | bytes 8667136 | tf_op jit(solution)/shard_map/dot_general | solution.py:45
  123.1 0.0 copy-start.2
  123.1 0.0 copy-start.4
  123.1 0.0 copy-start.1
  123.1 1.3 reshape.49
  124.4 0.0 all-to-all-done.1
  124.4 4.3 %all-to-all-start.3 = ((bf16[8,18,3584]{2,1,0:T(8,128)(2,1)}), bf16[8,18,3584]{2,1,0:T(8,128)(2,1)}, u32[]{:S(2)}, u32[]{:S(2)}) async-start(bf16[8,18,3584]{2,1,0:T(8,128)(2,1)} %reshape.49), calls=%async_computation.3 | async-start | bytes 2752512 | tf_op jit(solution)/shard_map/all_to_all | solution.py:51
  128.7 0.0 copy-done.2
  128.7 0.6 fusion.18
  130.7 0.0 copy-done.4
  130.7 0.1 reshape.47
  130.8 0.9 gather_fusion
  131.6 0.0 copy-done.1
  131.6 0.8 multiply_convert_fusion.3
  132.5 93.5 %all-to-all-done.3 = bf16[8,18,3584]{2,1,0:T(8,128)(2,1)} async-done(((bf16[8,18,3584]{2,1,0:T(8,128)(2,1)}), bf16[8,18,3584]{2,1,0:T(8,128)(2,1)}, u32[]{:S(2)}, u32[]{:S(2)}) %all-to-all-start.3) | async-done | bytes 1032224 | tf_op jit(solution)/shard_map/all_to_all | solution.py:51
  225.9 1.5 reshape.50
  227.4 2.0 gather_fusion.1
  229.5 0.0 collective-permute-done
  229.5 6.3 %fusion.9 = (bf16[1,896,1024]{2,1,0:T(8,128)(2,1)}, bf16[896,1024]{1,0:T(8,128)(2,1)}) fusion(bf16[1,3584,1024]{2,1,0:T(8,128)(2,1)} %param.12, s32[]{:T(128)S(6)} %select_n.32, bf16[896,1024]{1,0:T(8,128)(2,1)} %collective-permute-done, pred[]{:T(512)S(6)} %eq.37, bf16[896,1024]{1,0:T(8,128)(2,1)S(1)} %reduce_sum.40, bf16[1,896,1024]{2,1,0:T(8,128)(2,1)} %param.13), kind=kLoop, calls=%fused_computation.14 | loop fusion | flops 11927552 | bytes 11010053 | tf_op jit(solution)/shard_map/broadcast_in_dim | solution.py:95
  (3 shorter events, 0.0 us)
Async XLA Ops:
  9.6 21.5 %copy-start.3 = (s32[128]{0:T(128)}, s32[128]{0:T(128)S(1)}, u32[]{:S(2)}) copy-start(s32[128]{0:T(128)S(1)} %compare_select_fusion) | copy-start | bytes 1540
  12.1 18.9 %all-to-all-start.2 = ((bf16[8,18,1024]{2,1,0:T(8,128)(2,1)}), bf16[8,18,1024]{2,1,0:T(8,128)(2,1)S(1)}, u32[]{:S(2)}, u32[]{:S(2)}) async-start(bf16[8,18,1024]{2,1,0:T(8,128)(2,1)} %reshape.48), calls=%async_computation.2 | async-start | bytes 786432 | tf_op jit(solution)/shard_map/all_to_all | solution.py:34
  31.1 36.3 %all-to-all-start = ((bf16[8,18,3584]{2,1,0:T(8,128)(2,1)}), bf16[8,18,3584]{2,1,0:T(8,128)(2,1)S(1)}, u32[]{:S(2)}, u32[]{:S(2)}) async-start(bf16[8,18,3584]{2,1,0:T(8,128)(2,1)} %reshape.44), calls=%async_computation | async-start | bytes 2752512 | tf_op jit(solution)/shard_map/all_to_all | solution.py:31
  34.7 67.6 %all-gather.3.cloned.1.call-start = ((), (), s32[]{:S(2)}) async-start(), calls=%async_computation.5 | async-start | bytes 1474560 | tf_op jit(solution)/shard_map/all_gather | solution.py:74
  74.6 24.1 %all-to-all-start.4 = ((bf16[1,144,4,896]{3,1,0,2:T(8,128)(2,1)}), bf16[1,144,4,896]{3,1,0,2:T(8,128)(2,1)S(1)}, u32[]{:S(2)}, u32[]{:S(2)}) async-start(bf16[1,144,4,896]{3,1,0,2:T(8,128)(2,1)} %copy.12), calls=%async_computation.4 | async-start | bytes 2064384 | tf_op jit(solution)/shard_map/all_to_all | solution.py:67
  98.7 25.7 %all-to-all-start.1 = ((bf16[8,18,1024]{2,1,0:T(8,128)(2,1)}), bf16[8,18,1024]{2,1,0:T(8,128)(2,1)S(1)}, u32[]{:S(2)}, u32[]{:S(2)}) async-start(bf16[8,18,1024]{2,1,0:T(8,128)(2,1)} %reshape.46), calls=%async_computation.1 | async-start | bytes 786432 | tf_op jit(solution)/shard_map/all_to_all | solution.py:48
  108.7 8.7 %copy-start = (bf16[144,1024]{1,0:T(8,128)(2,1)S(1)}, bf16[144,1024]{1,0:T(8,128)(2,1)}, u32[]{:S(2)}) copy-start(bf16[144,1024]{1,0:T(8,128)(2,1)} %get-tuple-element.8) | copy-start | bytes 884740
  114.5 115.0 %collective-permute-start = (bf16[896,1024]{1,0:T(8,128)(2,1)S(1)}, bf16[896,1024]{1,0:T(8,128)(2,1)}, u32[]{:S(2)}, u32[]{:S(2)}) collective-permute-start(bf16[896,1024]{1,0:T(8,128)(2,1)S(1)} %reduce_sum.40), channel_id=1, source_target_pairs={{0,4},{1,5},{2,6},{3,7},{4,0},{5,1},{6,2},{7,3},{8,12},{9,13},{10,... | collective-permute-start | bytes 5505032 | tf_op jit(solution)/shard_map/ppermute | solution.py:16
  123.1 5.6 %copy-start.2 = (s32[8]{0:T(128)S(1)}, s32[8]{0:T(128)}, u32[]{:S(2)}) copy-start(s32[8]{0:T(128)} %param.11) | copy-start | bytes 100
  123.1 7.5 %copy-start.4 = (s32[128]{0:T(128)S(1)}, s32[128]{0:T(128)}, u32[]{:S(2)}) copy-start(s32[128]{0:T(128)} %copy-done.3) | copy-start | bytes 1540
  123.1 8.5 %copy-start.1 = (f32[128]{0:T(128)S(1)}, f32[128]{0:T(128)}, u32[]{:S(2)}) copy-start(f32[128]{0:T(128)} %param.8) | copy-start | bytes 1540
  124.4 101.5 %all-to-all-start.3 = ((bf16[8,18,3584]{2,1,0:T(8,128)(2,1)}), bf16[8,18,3584]{2,1,0:T(8,128)(2,1)}, u32[]{:S(2)}, u32[]{:S(2)}) async-start(bf16[8,18,3584]{2,1,0:T(8,128)(2,1)} %reshape.49), calls=%async_computation.3 | async-start | bytes 2752512 | tf_op jit(solution)/shard_map/all_to_all | solution.py:51
Sparse Core Ops, SparseCore 0:
  73.1 22.7 all-gather.2
where the time goes:
time: 243 us
  waiting for transfers between devices  153 us (63%)
  starting transfers between devices  25.3 us (10%)
  other arithmetic  17.6 us (7%)
  matrix products  17.3 us (7%)
  between operations  15.5 us (6%)
  local copies, waits for them, and re-layouts  13.5 us (6%)
    all_to_all x1, waiting for transfers between devices, shards(): lax.all_to_all(back.reshape(n_slots, width, D), 'expert', split_axis=0, c...  93.5 us
    all_to_all x1, waiting for transfers between devices, shards(): lax.all_to_all(send_rows.reshape(n_slots, capacity, D), 'expert', split_a...  32.5 us
    all_to_all x1, waiting for transfers between devices, shards(): lax.all_to_all(flat_x.reshape(1, row_count, n_groups, share), 'dp', split...  19.7 us
    all_to_all x1, waiting for transfers between devices, shards(): lax.all_to_all(send_grads.reshape(n_slots, capacity, F), 'expert', split_...  7.66 us
    all_to_all x1, starting transfers between devices, shards(): lax.all_to_all(send_grads.reshape(n_slots, capacity, F), 'expert', split_...  7.25 us
    dot_general x1, matrix products, shards(): jnp.einsum('krd,krf->kdf', columns, lax.all_gather(flat_grad[None], 'dp',...  6.41 us
    broadcast_in_dim x1, other arithmetic, shards(): return (expert_out, token_grad, new_weight[None], new_momentum[None])  6.32 us
    reduce_sum x1, other arithmetic, shards(): summed = jnp.sum(terms, axis=0)  5.75 us
  transfers between devices with their start and end apart: 7, of which 4 were waited for; matrix products, arithmetic and copies ran while one was open for 13% of the time, Pallas kernels for 0%

commit v1 on v0

v1 whole, which is shorter than its diff:
```python
import functools

import jax
import jax.numpy as jnp
from jax import lax
from jax.experimental import pallas as pl
from jax.experimental.pallas import tpu as pltpu
from jax.sharding import PartitionSpec as P

learning_rate = 0.004
decay_rate = 0.9

BF16 = jnp.bfloat16
F32 = jnp.float32
SUB = 8
LANES = 128


class Plan:
    def __init__(self, slots, groups, tokens, features, hidden):
        self.slots, self.groups, self.tokens = slots, groups, tokens
        self.D, self.F = features, hidden
        self.half = slots // 2
        self.cap = tokens * 9 // 8 // slots
        self.full, self.rest = divmod(self.cap, SUB)
        self.cuts = SUB // self.rest if self.rest else 1
        self.rows = self.half * self.cap
        self.share = features // groups
        self.DX = features * self.cap // SUB
        self.FG = hidden * self.cap // SUB
        self.C = self.DX + self.FG
        self.pieces = self.cap * groups // SUB

    def fits(self):
        return (
            self.slots % 2 == 0
            and (self.rest == 0 or SUB % self.rest == 0)
            and self.D % (self.cuts * LANES) == 0
            and self.F % (self.cuts * LANES) == 0
            and self.D % (self.groups * LANES) == 0
            and (self.cap * self.groups) % SUB == 0
            and self.rows % SUB == 0
            and (self.half * self.rest) % SUB == 0
            and self.tokens % LANES == 0
        )


def away(place, step, count):
    if count & (count - 1) == 0:
        return place ^ step
    return (place + step) % count


def away_traced(place, step, count):
    if count & (count - 1) == 0:
        return jnp.bitwise_xor(place, step)
    return lax.rem(place + step, count)


def steps_between(first, second, count):
    if count & (count - 1) == 0:
        return jnp.bitwise_xor(first, second)
    return lax.rem(first - second + count, count)


def iota(shape, dim):
    return lax.broadcasted_iota(jnp.int32, shape, dim)


def dot(a, b):
    return jnp.dot(a, b, preferred_element_type=F32)


def dot_nt(a, b):
    return lax.dot_general(a, b, (((1,), (1,)), ((), ())), preferred_element_type=F32)


def dot_tn(a, b):
    return lax.dot_general(a, b, (((0,), (0,)), ((), ())), preferred_element_type=F32)


def picker(plan, cut):
    shape = (plan.half * plan.rest, plan.half * SUB)
    row, col = iota(shape, 0), iota(shape, 1)
    wanted = (row // plan.rest) * SUB + cut * plan.rest + row % plan.rest
    return (wanted == col).astype(BF16)


def unfold(plan, blocks, width):
    parts = [
        jnp.concatenate([b[:, i * width : (i + 1) * width] for b in blocks], axis=0)
        for i in range(plan.full)
    ]
    if plan.rest:
        piece = width // plan.cuts
        tail = jnp.concatenate([b[:, plan.full * width :] for b in blocks], axis=0).astype(BF16)
        parts.append(
            jnp.concatenate([dot(picker(plan, q), tail) for q in range(plan.cuts)], axis=1)
        )
    return jnp.concatenate(parts, axis=0).astype(BF16)


def fold(plan, rows):
    width = rows.shape[1]
    block = plan.half * SUB
    parts = [rows[i * block : (i + 1) * block] for i in range(plan.full)]
    if plan.rest:
        piece = width // plan.cuts
        tail = rows[plan.full * block :].astype(BF16)
        total = None
        for q in range(plan.cuts):
            term = dot_tn(picker(plan, q), tail[:, q * piece : (q + 1) * piece])
            total = term if total is None else total + term
        parts.append(total)
    return jnp.concatenate(parts, axis=1)


def is_hot(plan, placement_ref):
    me = lax.axis_index("expert")
    partner = lax.rem(me + plan.half, plan.slots)
    return placement_ref[me] == placement_ref[partner]


def token_places(plan, slot):
    me = lax.axis_index("expert")
    my_half = me // plan.half
    my_place = lax.rem(me, plan.half)
    upper = (slot >= plan.half).astype(jnp.int32)
    place = slot - plan.half * upper
    far = jnp.where(upper == my_half, 0, 1)
    step = steps_between(place, jnp.zeros_like(place) + my_place, plan.half)
    block = 2 * step + far
    count = plan.tokens
    onehot = (iota((2 * plan.half, count), 0) == block).astype(F32)
    upto = (iota((count, count), 0) <= iota((count, count), 1)).astype(BF16)
    seen = dot(onehot.astype(BF16), upto)
    rank = jnp.sum(onehot * (seen - 1.0), axis=0, keepdims=True).astype(jnp.int32)
    return block, rank


def row_targets(plan, block, rank):
    targets = []
    for i in range(plan.full):
        inside = (rank >= i * SUB) & (rank < (i + 1) * SUB)
        targets.append(jnp.where(inside, block * SUB + rank - i * SUB, -1))
    for q in range(plan.cuts if plan.rest else 0):
        inside = rank >= plan.full * SUB
        targets.append(
            jnp.where(inside, block * SUB + q * plan.rest + rank - plan.full * SUB, -1)
        )
    return targets


def to_column(row):
    n = row.shape[1]
    eye = (iota((n, n), 0) == iota((n, n), 1)).astype(F32)
    return jnp.sum(eye * row.astype(F32), axis=1, keepdims=True)


def pack_kernel(plan, slot_ref, gate_ref, tok_ref, cot_ref, *outs):
    near, far = outs[: plan.half], outs[plan.half :]
    block, rank = token_places(plan, slot_ref[...])
    targets = row_targets(plan, block, rank)
    height = 2 * plan.half * SUB
    onehots = [(iota((height, plan.tokens), 0) == t).astype(BF16) for t in targets]
    tok = tok_ref[...]
    scaled = (to_column(gate_ref[...]) * cot_ref[...].astype(F32)).astype(BF16)

    def store(values, start):
        stop = start + values.shape[1]
        for m in range(plan.half):
            low = 2 * m * SUB
            near[m][:, start:stop] = values[low : low + 2 * SUB].astype(BF16)
            far[m][:, start:stop] = values[low + SUB : low + 2 * SUB].astype(BF16)

    for data, base in ((tok, 0), (scaled, plan.DX)):
        width = data.shape[1]
        for i in range(plan.full):
            store(dot(onehots[i], data), base + i * width)
        if plan.rest:
            piece = width // plan.cuts
            total = None
            for q in range(plan.cuts):
                term = dot(onehots[plan.full + q], data[:, q * piece : (q + 1) * piece])
                total = term if total is None else total + term
            store(total, base + plan.full * width)


def near_blocks(plan, refs, far, start, stop):
    low = SUB if far else 0
    return [r[:, start:stop].astype(F32)[low : low + SUB] for r in refs]


def columns_kernel(plan, *refs):
    near, outs, rows = refs[: plan.half], refs[plan.half : -1], refs[-1]
    rows[...] = unfold(plan, near_blocks(plan, near, False, 0, plan.DX), plan.D)
    group = lax.axis_index("dp")
    for m in range(plan.groups):
        start = pl.multiple_of(away_traced(group, m, plan.groups) * plan.share, LANES)
        outs[m][...] = rows[:, pl.ds(start, plan.share)]


def load_weight(plan, weight_ref, held, sems):
    count = sems.shape[0]
    height = plan.D // count
    copies = []
    for c in range(count):
        span = pl.ds(c * height, height)
        copy = pltpu.make_async_copy(weight_ref.at[0, span, :], held.at[span, :], sems.at[c])
        copy.start()
        copies.append(copy)
    return copies, height


def project(x, held, copies, height):
    preact = None
    for c, copy in enumerate(copies):
        copy.wait()
        span = slice(c * height, (c + 1) * height)
        term = dot(x[:, span], held[span, :])
        preact = term if preact is None else preact + term
    return preact


def activate(preact, scaled):
    sigma = jax.nn.sigmoid(preact)
    act = (preact * sigma).astype(BF16)
    grad_pre = (scaled.astype(F32) * sigma * (1.0 + preact * (1.0 - sigma))).astype(BF16)
    return act, grad_pre


def pull_back(grad_pre, held, copies, height):
    return jnp.concatenate(
        [
            dot_nt(grad_pre, held[c * height : (c + 1) * height, :])
            for c in range(len(copies))
        ],
        axis=1,
    )


def near_kernel(plan, placement_ref, weight_ref, *refs):
    half, groups = plan.half, plan.groups
    near, refs = refs[:half], refs[half:]
    back_near, refs = refs[:half], refs[half:]
    local_far, folded_grad, refs = refs[0], refs[1], refs[2:]
    share, refs = refs[:groups], refs[groups:]
    held, far_rows, sems = refs
    copies, height = load_weight(plan, weight_ref, held, sems)
    x_near = unfold(plan, near_blocks(plan, near, False, 0, plan.DX), plan.D)
    x_far = unfold(plan, near_blocks(plan, near, True, 0, plan.DX), plan.D)
    g_near = unfold(plan, near_blocks(plan, near, False, plan.DX, plan.C), plan.F)
    g_far = unfold(plan, near_blocks(plan, near, True, plan.DX, plan.C), plan.F)
    far_rows[...] = x_far
    x = jnp.concatenate([x_near.astype(F32), x_far.astype(F32)], axis=0).astype(BF16)
    g = jnp.concatenate([g_near.astype(F32), g_far.astype(F32)], axis=0).astype(BF16)
    act, grad_pre = activate(project(x, held, copies, height), g)
    back = pull_back(grad_pre, held, copies, height)
    act, grad32 = act.astype(F32), grad_pre.astype(F32)
    near_back = fold(plan, back[: plan.rows])
    near_act = fold(plan, act[: plan.rows])
    for m in range(half):
        back_near[m][:, : plan.DX] = near_back[m * SUB : (m + 1) * SUB].astype(BF16)
        back_near[m][:, plan.DX :] = near_act[m * SUB : (m + 1) * SUB].astype(BF16)
    local_far[:, : plan.DX] = fold(plan, back[plan.rows :]).astype(BF16)
    local_far[:, plan.DX :] = fold(plan, act[plan.rows :]).astype(BF16)
    grad_near = grad32[: plan.rows]
    grad_far = jnp.where(is_hot(plan, placement_ref), grad32[plan.rows :], 0.0).astype(BF16)
    folded_grad[...] = fold(plan, grad_near).astype(BF16)
    group = lax.axis_index("dp")
    for m in range(groups):
        start = pl.multiple_of(away_traced(group, m, groups) * plan.share, LANES)
        share[m][:, : plan.share] = far_rows[:, pl.ds(start, plan.share)]
        share[m][:, plan.share : plan.share + plan.F] = grad_near.astype(BF16)
        share[m][:, plan.share + plan.F :] = grad_far


def far_kernel(plan, placement_ref, weight_ref, folded_grad, *refs):
    half, groups = plan.half, plan.groups
    far, refs = refs[:half], refs[half:]
    columns, refs = refs[:groups], refs[groups:]
    payload, refs = refs[0], refs[1:]
    share, refs = refs[:groups], refs[groups:]
    held, rows, sems = refs
    copies, height = load_weight(plan, weight_ref, held, sems)
    x = unfold(plan, [r[:, : plan.DX].astype(F32) for r in far], plan.D)
    g = unfold(plan, [r[:, plan.DX :].astype(F32) for r in far], plan.F)
    rows[...] = x
    act, grad_pre = activate(project(x, held, copies, height), g)
    hot = is_hot(plan, placement_ref)

    @pl.when(jnp.logical_not(hot))
    def _():
        back = pull_back(grad_pre, held, copies, height)
        payload[:, : plan.DX] = fold(plan, back).astype(BF16)
        payload[:, plan.DX :] = fold(plan, act.astype(F32)).astype(BF16)

    @pl.when(hot)
    def _():
        together = jnp.concatenate([c[...].astype(F32) for c in columns], axis=0)
        block = half * SUB
        for i in range(plan.pieces):
            payload[:, i * plan.share : (i + 1) * plan.share] = together[
                i * block : (i + 1) * block
            ].astype(BF16)
        payload[:, plan.DX :] = folded_grad[...]

    group = lax.axis_index("dp")
    for m in range(groups):
        start = pl.multiple_of(away_traced(group, m, groups) * plan.share, LANES)
        share[m][:, : plan.share] = rows[:, pl.ds(start, plan.share)]
        share[m][:, plan.share :] = grad_pre


def after_kernel(plan, placement_ref, payload, local_far, *outs):
    hot = is_hot(plan, placement_ref)
    chosen = jnp.where(hot, local_far[...].astype(F32), payload[...].astype(F32))
    for m in range(plan.half):
        outs[m][...] = chosen[m * SUB : (m + 1) * SUB].astype(BF16)
    g = payload[:, plan.DX :].astype(F32)
    blocks = [g[m * SUB : (m + 1) * SUB] for m in range(plan.half)]
    outs[plan.half][...] = jnp.where(hot, unfold(plan, blocks, plan.F).astype(F32), 0.0).astype(BF16)


def unpack_kernel(plan, slot_ref, gate_ref, *refs):
    near, refs = refs[: plan.half], refs[plan.half :]
    far, refs = refs[: plan.half], refs[plan.half :]
    out_ref, grad_ref = refs
    block, rank = token_places(plan, slot_ref[...])
    width = 2 * plan.half * SUB
    picks = []
    for target in row_targets(plan, block, rank):
        column = to_column(target).astype(jnp.int32)
        picks.append((iota((plan.tokens, width), 1) == column).astype(BF16))
    stacked = []
    for m in range(plan.half):
        stacked += [near[m][...].astype(F32), far[m][...].astype(F32)]
    stacked = jnp.concatenate(stacked, axis=0).astype(BF16)

    def gather(base, size):
        total = None
        for i in range(plan.full):
            term = dot(picks[i], stacked[:, base + i * size : base + (i + 1) * size])
            total = term if total is None else total + term
        if plan.rest:
            piece = size // plan.cuts
            tail = stacked[:, base + plan.full * size : base + plan.full * size + piece]
            term = jnp.concatenate(
                [dot(picks[plan.full + q], tail) for q in range(plan.cuts)], axis=1
            )
            total = term if total is None else total + term
        return total

    grad_ref[...] = gather(0, plan.D).astype(BF16)
    out_ref[...] = (to_column(gate_ref[...]) * gather(plan.DX, plan.F)).astype(BF16)


def update_kernel(plan, placement_ref, payload, *refs):
    groups, share, width = plan.groups, plan.share, plan.F
    near_x, refs = refs[:groups], refs[groups:]
    near_rest, refs = refs[:groups], refs[groups:]
    far_all, refs = refs[:groups], refs[groups:]
    other_g, refs = refs[:groups], refs[groups:]
    weight_ref, momentum_ref, new_weight, new_momentum, x_all, g_all = refs
    step = pl.program_id(0)
    tile = new_weight.shape[1]

    @pl.when(step == 0)
    def _():
        hot = is_hot(plan, placement_ref)
        x_parts, g_parts = [], []
        for m in range(groups):
            x_parts += [near_x[m][...], near_rest[m][:, :share], far_all[m][:, :share]]
            g_parts += [
                near_rest[m][:, share : share + width],
                near_rest[m][:, share + width :],
                far_all[m][:, share:],
            ]
        for i in range(plan.pieces):
            piece = payload[:, i * share : (i + 1) * share].astype(F32)
            x_parts.append(jnp.where(hot, piece, 0.0))
        g_parts += [g[...] for g in other_g]
        x_all[...] = jnp.concatenate([p.astype(F32) for p in x_parts], axis=0).astype(BF16)
        g_all[...] = jnp.concatenate([p.astype(F32) for p in g_parts], axis=0).astype(BF16)

    start = pl.multiple_of(step * tile, LANES)
    total = dot_tn(x_all[:, pl.ds(start, tile)], g_all[...])
    momentum = (decay_rate * momentum_ref[0].astype(F32) + total).astype(BF16)
    new_momentum[0] = momentum
    new_weight[0] = (
        weight_ref[0].astype(F32) - learning_rate * momentum.astype(F32)
    ).astype(BF16)


VMEM_LIMIT = 48 * 1024 * 1024
SMEM_SPEC = pl.BlockSpec(memory_space=pltpu.SMEM)
ANY_SPEC = pl.BlockSpec(memory_space=pl.ANY)
VMEM_SPEC = pl.BlockSpec(memory_space=pltpu.VMEM)


def call(kernel, plan, ins, specs, outs, scratch, flops, name):
    moved = sum(a.size * a.dtype.itemsize for a in ins) + sum(2 * r * c for r, c in outs)
    return pl.pallas_call(
        functools.partial(kernel, plan),
        out_shape=[jax.ShapeDtypeStruct(s, BF16) for s in outs],
        in_specs=specs,
        out_specs=[VMEM_SPEC] * len(outs),
        scratch_shapes=scratch,
        compiler_params=pltpu.CompilerParams(vmem_limit_bytes=VMEM_LIMIT),
        cost_estimate=pl.CostEstimate(flops=flops, bytes_accessed=moved, transcendentals=0),
        name=name,
    )(*ins)


def routed(plan, tokens, route_weight, cotangent, slot_ids, placement, weight, momentum):
    half, groups = plan.half, plan.groups
    D, F, C, rows, share = plan.D, plan.F, plan.C, plan.rows, plan.share
    slot = slot_ids.reshape(1, -1)
    gate = route_weight.reshape(1, -1)
    chunks = 7 if D % (7 * LANES) == 0 else 1

    def to_slot(data, m, flip):
        pairs = []
        for e in range(plan.slots):
            h, k = divmod(e, half)
            pairs.append((e, (h ^ flip) * half + away(k, m, half)))
        return lax.ppermute(data, "expert", pairs)

    def to_source(data, m):
        pairs = []
        for e in range(plan.slots):
            h, k = divmod(e, half)
            pairs.append((h * half + away(k, m, half), e))
        return lax.ppermute(data, "expert", pairs)

    def to_group(data, m):
        return lax.ppermute(data, "dp", [(d, away(d, m, groups)) for d in range(groups)])

    def spread(per_step):
        back = [m if groups & (groups - 1) == 0 else groups - m for m in range(groups)]
        return [per_step[0]] + [to_group(per_step[m], m) for m in back[1:]]

    packed = call(
        pack_kernel,
        plan,
        [slot, gate, tokens, cotangent],
        [VMEM_SPEC] * 4,
        [(2 * SUB, C)] * half + [(SUB, C)] * half,
        [],
        2 * 4 * half * SUB * plan.tokens * (D + F),
        "pack",
    )
    near = [packed[0]] + [to_slot(packed[m], m, 0) for m in range(1, half)]
    far = [to_slot(packed[half + m], m, 1) for m in range(half)]

    columns = call(
        columns_kernel,
        plan,
        near,
        [VMEM_SPEC] * half,
        [(rows, share)] * groups,
        [pltpu.VMEM((rows, D), BF16)],
        2 * rows * SUB * D,
        "near_columns",
    )
    near_x = spread(columns)
    held = [
        pltpu.VMEM((D, F), BF16),
        pltpu.VMEM((rows, D), BF16),
        pltpu.SemaphoreType.DMA((chunks,)),
    ]
    outs = call(
        near_kernel,
        plan,
        [placement, weight] + near,
        [SMEM_SPEC, ANY_SPEC] + [VMEM_SPEC] * half,
        [(SUB, C)] * half
        + [(half * SUB, C), (half * SUB, plan.FG)]
        + [(rows, share + 2 * F)] * groups,
        held,
        8 * rows * D * F,
        "near_rows",
    )
    back_near = [outs[0]] + [to_source(outs[m], m) for m in range(1, half)]
    local_far, folded_grad = outs[half], outs[half + 1]
    near_rest = spread(outs[half + 2 :])

    outs = call(
        far_kernel,
        plan,
        [placement, weight, folded_grad] + far + near_x,
        [SMEM_SPEC, ANY_SPEC] + [VMEM_SPEC] * (1 + half + groups),
        [(half * SUB, C)] + [(rows, share + F)] * groups,
        held,
        4 * rows * D * F,
        "far_rows",
    )
    payload = lax.ppermute(
        outs[0], "expert", [(e, (e + half) % plan.slots) for e in range(plan.slots)]
    )
    far_all = spread(outs[1:])

    outs = call(
        after_kernel,
        plan,
        [placement, payload, local_far],
        [SMEM_SPEC] + [VMEM_SPEC] * 2,
        [(SUB, C)] * half + [(rows, F)],
        [],
        1000000,
        "after_swap",
    )
    back_far = [outs[0]] + [to_source(outs[m], m) for m in range(1, half)]
    other_g = spread([outs[half]] * groups)

    tile = LANES
    steps = share // tile
    offset = share // tile
    total_rows = plan.groups * plan.rows * 4
    group = lax.axis_index("dp").reshape(1)

    def whole(*shape):
        return pl.BlockSpec(shape, lambda i, g: (0,) * len(shape))

    new_weight, new_momentum = pl.pallas_call(
        lambda g_ref, *refs: update_kernel(plan, *refs),
        grid_spec=pltpu.PrefetchScalarGridSpec(
            num_scalar_prefetch=1,
            grid=(steps,),
            in_specs=[SMEM_SPEC, whole(half * SUB, C)]
            + [whole(rows, share)] * groups
            + [whole(rows, share + 2 * F)] * groups
            + [whole(rows, share + F)] * groups
            + [whole(rows, F)] * groups
            + [
                pl.BlockSpec((1, tile, F), lambda i, g: (0, g[0] * offset + i, 0)),
                pl.BlockSpec((1, tile, F), lambda i, g: (0, i, 0)),
            ],
            out_specs=[pl.BlockSpec((1, tile, F), lambda i, g: (0, i, 0))] * 2,
            scratch_shapes=[
                pltpu.VMEM((total_rows, share), BF16),
                pltpu.VMEM((total_rows, F), BF16),
            ],
        ),
        out_shape=[jax.ShapeDtypeStruct((1, share, F), BF16)] * 2,
        compiler_params=pltpu.CompilerParams(vmem_limit_bytes=VMEM_LIMIT),
        cost_estimate=pl.CostEstimate(
            flops=2 * total_rows * share * F, bytes_accessed=16 * share * F, transcendentals=0
        ),
        name="update",
    )(group, placement, payload, *near_x, *near_rest, *far_all, *other_g, weight, momentum)

    expert_out, token_grad = call(
        unpack_kernel,
        plan,
        [slot, gate] + back_near + back_far,
        [VMEM_SPEC] * (2 + 2 * half),
        [(plan.tokens, F), (plan.tokens, D)],
        [],
        2 * 4 * half * SUB * plan.tokens * (D + F),
        "unpack",
    )
    return expert_out, token_grad, new_weight, new_momentum


def general(tokens, route_weight, cotangent, slot_ids, placement, weight, momentum):
    n_slots = lax.axis_size("expert")
    n_groups = lax.axis_size("dp")
    tok_count, D = tokens.shape
    F = cotangent.shape[1]
    capacity = tok_count * 9 // 8 // n_slots
    onehot = (slot_ids[:, None] == jnp.arange(n_slots, dtype=jnp.int32)[None, :]).astype(jnp.int32)
    ranks = jnp.sum((jnp.cumsum(onehot, axis=0) - 1) * onehot, axis=1)
    position = slot_ids * capacity + ranks
    send_rows = jnp.zeros((n_slots * capacity, D), BF16).at[position].set(tokens)
    scaled = (route_weight[:, None] * cotangent.astype(F32)).astype(BF16)
    send_grads = jnp.zeros((n_slots * capacity, F), BF16).at[position].set(scaled)
    matrix = weight[0]

    def exchange(rows):
        width = rows.shape[-1]
        return lax.all_to_all(
            rows.reshape(n_slots, capacity, width), "expert", split_axis=0, concat_axis=0, tiled=True
        ).reshape(-1, width)

    flat_x = exchange(send_rows)
    act, flat_grad = activate(dot(flat_x, matrix), exchange(send_grads))
    back = dot_nt(flat_grad, matrix).astype(BF16)
    act_rows = exchange(act)[position]
    expert_out = (route_weight[:, None] * act_rows.astype(F32)).astype(BF16)
    token_grad = exchange(back)[position]
    row_count = flat_x.shape[0]
    share = D // n_groups
    columns = lax.all_to_all(
        flat_x.reshape(1, row_count, n_groups, share), "dp", split_axis=2, concat_axis=0, tiled=True
    )
    columns = columns.reshape(n_groups, row_count, share)
    terms = jnp.einsum(
        "krd,krf->kdf",
        columns,
        lax.all_gather(flat_grad[None], "dp", axis=0, tiled=True),
        preferred_element_type=F32,
    )
    terms = lax.optimization_barrier(terms.astype(BF16)).astype(F32)
    reduced = jnp.sum(terms, axis=0).astype(BF16)
    half = n_slots // 2
    partner_grad = lax.ppermute(
        reduced, "expert", [(i, (i + half) % n_slots) for i in range(n_slots)]
    ).astype(F32)
    my_slot = lax.axis_index("expert")
    partner_slot = (my_slot + half) % n_slots
    same = placement[my_slot] == placement[partner_slot]
    total = reduced.astype(F32) + jnp.where(same, partner_grad, 0.0)
    new_momentum = (decay_rate * momentum[0].astype(F32) + total).astype(BF16)
    old = lax.dynamic_slice_in_dim(matrix, lax.axis_index("dp") * share, share, 0).astype(F32)
    new_weight = (old - learning_rate * new_momentum.astype(F32)).astype(BF16)
    return expert_out, token_grad, new_weight[None], new_momentum[None]


def solution(mesh):
    def shards(tokens, route_weight, cotangent, slot_ids, placement, weight, momentum):
        plan = Plan(
            mesh.shape["expert"],
            mesh.shape["dp"],
            tokens.shape[0],
            tokens.shape[1],
            cotangent.shape[1],
        )
        body = functools.partial(routed, plan) if plan.fits() else general
        return body(tokens, route_weight, cotangent, slot_ids, placement, weight, momentum)

    return jax.shard_map(
        shards,
        mesh=mesh,
        in_specs=(
            P(("dp", "expert"), None),
            P(("dp", "expert")),
            P(("dp", "expert"), None),
            P(("dp", "expert")),
            P(),
            P("expert", None, None),
            P("expert", "dp", None),
        ),
        out_specs=(
            P(("dp", "expert"), None),
            P(("dp", "expert"), None),
            P("expert", "dp", None),
            P("expert", "dp", None),
        ),
        check_vma=False,
    )
```

time: 243 us -> 116 us (0.48)
  waiting for transfers between devices: 153 us -> 34.6 us
  Pallas kernels: 0 us -> 25.1 us
  other arithmetic: 17.6 us -> 0 us
  starting transfers between devices: 25.3 us -> 42.9 us
  matrix products: 17.3 us -> 0 us
  between operations: 15.5 us -> 0.87 us
  local copies, waits for them, and re-layouts: 13.5 us -> 10.8 us
    all_to_all x5 -> x0, waiting for transfers between devices: 153 us -> none  [the longest x1 93.5 us: shards(): lax.all_to_all(back.reshape(n_slots, width, D), 'expert', split_axis=0, c...]
    ppermute x1 -> x26, starting transfers between devices: 2.97 us -> 42.9 us  [the longest x7 17.2 us: to_slot(): return lax.ppermute(data, 'expert', pairs)]
    ppermute x1 -> x26, waiting for transfers between devices: 0.01 us -> 34.6 us  [the longest x1 19.4 us: routed(): lax.ppermute(outs[0], 'expert', [(e, (e + half) % plan.slots) for e in ra...]
    pallas_call x0 -> x7, Pallas kernels: none -> 25.1 us  [the longest x6 16.5 us: call(): pl.pallas_call(functools.partial(kernel, plan), out_shape=[jax.ShapeDtype...]
    all_to_all x5 -> x0, starting transfers between devices: 22.3 us -> none  [the longest x1 7.25 us: shards(): lax.all_to_all(send_grads.reshape(n_slots, capacity, F), 'expert', split_...]
    dot_general x3 -> x0, matrix products: 17.3 us -> none  [the longest x1 6.41 us: shards(): jnp.einsum('krd,krf->kdf', columns, lax.all_gather(flat_grad[None], 'dp',...]
    unnamed x10 -> x44, local copies, waits for them, and re-layouts: 0.03 us -> 10.8 us
    reduce_sum x3 -> x0, other arithmetic: 7.21 us -> none  [the longest x1 5.75 us: shards(): summed = jnp.sum(terms, axis=0)]
  transfers between devices with their start and end apart: 7 -> 26, of which waited for: 4 -> 6; matrix products, arithmetic and copies ran while one was open for 13% -> 0% of each run, Pallas kernels for 0% -> 16%
where the time goes in v1:
time: 116 us; the launch traced here: 114 us
  starting transfers between devices  42.9 us (37%)
  waiting for transfers between devices  34.6 us (30%)
  Pallas kernels  25.1 us (22%)
  local copies, waits for them, and re-layouts  10.8 us (9%)
    ppermute x1, waiting for transfers between devices, routed(): lax.ppermute(outs[0], 'expert', [(e, (e + half) % plan.slots) for e in ra...  19.4 us
    ppermute x7, starting transfers between devices, to_slot(): return lax.ppermute(data, 'expert', pairs)  17.2 us
    pallas_call x6, Pallas kernels, call(): pl.pallas_call(functools.partial(kernel, plan), out_shape=[jax.ShapeDtype...  16.5 us
    ppermute x6, starting transfers between devices, to_source(): return lax.ppermute(data, 'expert', pairs)  15.4 us
    unnamed x44, local copies, waits for them, and re-layouts  10.8 us
    ppermute x7, waiting for transfers between devices, to_slot(): return lax.ppermute(data, 'expert', pairs)  9.09 us
    pallas_call x1, Pallas kernels, routed(): pl.pallas_call(lambda g_ref, *refs: update_kernel(plan, *refs), grid_spec...  8.57 us
    ppermute x12, starting transfers between devices, to_group(): lax.ppermute(data, 'dp', [(d, away(d, m, groups)) for d in range(groups)])  6.96 us
  transfers between devices with their start and end apart: 26, of which 6 were waited for; matrix products, arithmetic and copies ran while one was open for 0% of the time, Pallas kernels for 16%

profile of v1, /device:TPU:0, one launch (start us, length us, event | category | flops | bytes accessed | tf_op | source)
XLA Modules:
  0.0 114.3 jit_solution(14176457589428648143)
XLA Ops:
  0.7 1.2 %copy-done = bf16[128,3584]{1,0:T(8,128)(2,1)S(1)} copy-done((bf16[128,3584]{1,0:T(8,128)(2,1)S(1)}, bf16[128,3584]{1,0:T(8,128)(2,1)}, u32[]{:S(2)}) %copy-start) | copy-done | bytes 917528
  1.8 0.9 copy-done.5
  2.8 0.7 copy-done.13
  3.4 0.7 copy-done.15
  4.1 0.8 pack.1
  4.9 3.0 %collective-permute-start = (bf16[16,10368]{1,0:T(8,128)(2,1)S(1)}, bf16[16,10368]{1,0:T(8,128)(2,1)S(1)}, u32[]{:S(2)}, u32[]{:S(2)}) collective-permute-start(bf16[16,10368]{1,0:T(8,128)(2,1)S(1)} %get-tuple-element.41), channel_id=1, source_target_pairs={{0,1},{1,0},{2,3},{3,2},{4,5},{5,4},{6,7},{7,6},{8,9},{9,8},{10,11... | collective-permute-start | bytes 995336 | tf_op jit(solution)/shard_map/ppermute | solution.py:427
  7.9 1.6 %collective-permute-start.1 = (bf16[16,10368]{1,0:T(8,128)(2,1)S(1)}, bf16[16,10368]{1,0:T(8,128)(2,1)S(1)}, u32[]{:S(2)}, u32[]{:S(2)}) collective-permute-start(bf16[16,10368]{1,0:T(8,128)(2,1)S(1)} %get-tuple-element.42), channel_id=1, source_target_pairs={{0,2},{1,3},{2,0},{3,1},{4,6},{5,7},{6,4},{7,5},{8,10},{9,11},{10,... | collective-permute-start | bytes 995336 | tf_op jit(solution)/shard_map/ppermute | solution.py:427
  9.5 3.0 %collective-permute-start.6 = (bf16[8,10368]{1,0:T(8,128)(2,1)S(1)}, bf16[8,10368]{1,0:T(8,128)(2,1)S(1)}, u32[]{:S(2)}, u32[]{:S(2)}) collective-permute-start(bf16[8,10368]{1,0:T(8,128)(2,1)S(1)} %get-tuple-element.49), channel_id=1, source_target_pairs={{0,4},{1,5},{2,6},{3,7},{4,0},{5,1},{6,2},{7,3},{8,12},{9,13},{10,... | collective-permute-start | bytes 497672 | tf_op jit(solution)/shard_map/ppermute | solution.py:427
  12.5 1.3 %collective-permute-start.7 = (bf16[8,10368]{1,0:T(8,128)(2,1)S(1)}, bf16[8,10368]{1,0:T(8,128)(2,1)S(1)}, u32[]{:S(2)}, u32[]{:S(2)}) collective-permute-start(bf16[8,10368]{1,0:T(8,128)(2,1)S(1)} %get-tuple-element.50), channel_id=1, source_target_pairs={{0,5},{1,4},{2,7},{3,6},{4,1},{5,0},{6,3},{7,2},{8,13},{9,12},{10,... | collective-permute-start | bytes 497672 | tf_op jit(solution)/shard_map/ppermute | solution.py:427
  13.7 2.0 %collective-permute-done.refs_1_ = bf16[16,10368]{1,0:T(8,128)(2,1)S(1)} collective-permute-done((bf16[16,10368]{1,0:T(8,128)(2,1)S(1)}, bf16[16,10368]{1,0:T(8,128)(2,1)S(1)}, u32[]{:S(2)}, u32[]{:S(2)}) %collective-permute-start) | collective-permute-done | bytes 331808 | tf_op jit(solution)/shard_map/ppermute | solution.py:427
  15.7 4.8 %collective-permute-start.8 = (bf16[8,10368]{1,0:T(8,128)(2,1)S(1)}, bf16[8,10368]{1,0:T(8,128)(2,1)S(1)}, u32[]{:S(2)}, u32[]{:S(2)}) collective-permute-start(bf16[8,10368]{1,0:T(8,128)(2,1)S(1)} %get-tuple-element.51), channel_id=1, source_target_pairs={{0,6},{1,7},{2,4},{3,5},{4,2},{5,3},{6,0},{7,1},{8,14},{9,15},{10,... | collective-permute-start | bytes 497672 | tf_op jit(solution)/shard_map/ppermute | solution.py:427
  20.5 5.2 %collective-permute-done.1.refs_2_ = bf16[16,10368]{1,0:T(8,128)(2,1)S(1)} collective-permute-done((bf16[16,10368]{1,0:T(8,128)(2,1)S(1)}, bf16[16,10368]{1,0:T(8,128)(2,1)S(1)}, u32[]{:S(2)}, u32[]{:S(2)}) %collective-permute-start.1) | collective-permute-done | bytes 331808 | tf_op jit(solution)/shard_map/ppermute | solution.py:427
  25.7 3.6 %collective-permute-start.9 = (bf16[8,10368]{1,0:T(8,128)(2,1)S(1)}, bf16[8,10368]{1,0:T(8,128)(2,1)S(1)}, u32[]{:S(2)}, u32[]{:S(2)}) collective-permute-start(bf16[8,10368]{1,0:T(8,128)(2,1)S(1)} %get-tuple-element.52), channel_id=1, source_target_pairs={{0,7},{1,6},{2,5},{3,4},{4,3},{5,2},{6,1},{7,0},{8,15},{9,14},{10,... | collective-permute-start | bytes 497672 | tf_op jit(solution)/shard_map/ppermute | solution.py:427
  29.3 1.9 %collective-permute-done.2.refs_3_ = bf16[16,10368]{1,0:T(8,128)(2,1)S(1)} collective-permute-done((bf16[16,10368]{1,0:T(8,128)(2,1)S(1)}, bf16[16,10368]{1,0:T(8,128)(2,1)S(1)}, u32[]{:S(2)}, u32[]{:S(2)}) %collective-permute-start.2) | collective-permute-done | bytes 331808 | tf_op jit(solution)/shard_map/ppermute | solution.py:427
  31.2 0.2 near_columns.1
  31.4 1.8 %collective-permute-start.11 = (bf16[72,896]{1,0:T(8,128)(2,1)S(1)}, bf16[72,896]{1,0:T(8,128)(2,1)S(1)}, u32[]{:S(2)}, u32[]{:S(2)}) collective-permute-start(bf16[72,896]{1,0:T(8,128)(2,1)S(1)} %get-tuple-element.55), channel_id=1, source_target_pairs={{0,16},{8,24},{16,0},{24,8},{1,17},{9,25},{17,1},{25,9},{2,18},{10... | collective-permute-start | bytes 387080 | tf_op jit(solution)/shard_map/ppermute | solution.py:437
  33.2 0.1 collective-permute-start.12
  33.3 7.7 %near_rows.1 = (bf16[8,10368]{1,0:T(8,128)(2,1)S(1)}, bf16[8,10368]{1,0:T(8,128)(2,1)S(1)}, bf16[8,10368]{1,0:T(8,128)(2,1)S(1)}, bf16[8,10368]{1,0:T(8,128)(2,1...) custom-call(s32[8]{0:T(128)S(1)} %copy-done.12, ...), custom_call_target="tpu_custom_call" | custom-call | flops 2113929216 | bytes 11837472 | tf_op jit(solution)/shard_map/near_rows/pallas_call | solution.py:403
  41.0 0.7 copy-done.6
  41.7 4.2 %far_rows.1 = (bf16[32,10368]{1,0:T(8,128)(2,1)S(1)}, bf16[72,1920]{1,0:T(8,128)(2,1)S(1)}, bf16[72,1920]{1,0:T(8,128)(2,1)S(1)}, bf16[72,1920]{1,0:T(8,128)(2,1)S(1)}, bf16[72,1920]{1,0:T(8,128)(2,1)S(1)}) custom-call(s32[8]{0:T(128)S(1)} %copy-done.12, bf16[1,3584,1024]{2,1,0:T(8,128)(2,1)} %refs_18_.1, ...), custom_call_target="tpu_custom_call" | custom-call | flops 1056964608 | bytes 10436640 | tf_op jit(solution)/shard_map/far_rows/pallas_call | solution.py:403
  46.0 3.4 %collective-permute-start.13 = (bf16[32,10368]{1,0:T(8,128)(2,1)S(1)}, bf16[32,10368]{1,0:T(8,128)(2,1)S(1)}, u32[]{:S(2)}, u32[]{:S(2)}) collective-permute-start(bf16[32,10368]{1,0:T(8,128)(2,1)S(1)} %get-tuple-element.57), channel_id=1, source_target_pairs={{0,4},{1,5},{2,6},{3,7},{4,0},{5,1},{6,2},{7,3},{8,12},{9,13},{10,... | collective-permute-start | bytes 1990664 | tf_op jit(solution)/shard_map/ppermute | solution.py:498
  49.4 3.9 %collective-permute-start.3 = (bf16[8,10368]{1,0:T(8,128)(2,1)S(1)}, bf16[8,10368]{1,0:T(8,128)(2,1)S(1)}, u32[]{:S(2)}, u32[]{:S(2)}) collective-permute-start(bf16[8,10368]{1,0:T(8,128)(2,1)S(1)} %get-tuple-element.45), channel_id=1, source_target_pairs={{1,0},{0,1},{3,2},{2,3},{5,4},{4,5},{7,6},{6,7},{9,8},{8,9},{11,10... | collective-permute-start | bytes 497672 | tf_op jit(solution)/shard_map/ppermute | solution.py:434
  53.4 0.7 collective-permute-start.18
  54.1 3.7 %collective-permute-done.3.refs_1_ = bf16[8,10368]{1,0:T(8,128)(2,1)S(1)} collective-permute-done((bf16[8,10368]{1,0:T(8,128)(2,1)S(1)}, bf16[8,10368]{1,0:T(8,128)(2,1)S(1)}, u32[]{:S(2)}, u32[]{:S(2)}) %collective-permute-start.3) | collective-permute-done | bytes 165920 | tf_op jit(solution)/shard_map/ppermute | solution.py:434
  57.8 0.7 copy-done.8
  58.5 0.5 collective-permute-start.19
  58.9 0.6 collective-permute-start.21
  59.6 19.4 %collective-permute-done.13.payload.refs_1_ = bf16[32,10368]{1,0:T(8,128)(2,1)S(1)} collective-permute-done((bf16[32,10368]{1,0:T(8,128)(2,1)S(1)}, bf16[32,10368]{1,0:T(8,128)(2,1)S(1)}, u32[]{:S(2)}, u32[]{:S(2)}) %collective-permute-start.13) | collective-permute-done | bytes 663584 | tf_op jit(solution)/shard_map/ppermute | solution.py:498
  79.0 0.9 collective-permute-start.22
  79.9 1.5 %after_swap.1 = (bf16[8,10368]{1,0:T(8,128)(2,1)S(1)}, bf16[8,10368]{1,0:T(8,128)(2,1)S(1)}, bf16[8,10368]{1,0:T(8,128)(2,1)S(1)}, bf16[8,10368]{1,0:T(8,128)(2,1)S(1)}, bf16[72,1024]{1,0:T(8,128)(2,1)}) custom-call(s32[8]{0:T(128)S(1)} %copy-done.12, bf16[32,10368]{1,0:T(8,128)(2,1)S(1)} %collective-permute-done.13.payload.refs_1_, ...), custom_call_target="tpu_custom_call" | custom-call | flops 1000000 | bytes 2138144 | tf_op jit(solution)/shard_map/after_swap/pallas_call | solution.py:403
  81.4 0.7 copy-done.10
  82.1 0.7 copy-done.19
  82.8 0.7 copy-done.20
  83.5 0.7 copy-done.21
  84.1 0.7 copy-done.1
  84.9 0.7 collective-permute-start.23
  85.6 2.3 %collective-permute-done.22.refs_13_ = bf16[72,1920]{1,0:T(8,128)(2,1)S(1)} collective-permute-done((bf16[72,1920]{1,0:T(8,128)(2,1)S(1)}, bf16[72,1920]{1,0:T(8,128)(2,1)S(1)}, u32[]{:S(2)}, u32[]{:S(2)}) %collective-permute-start.22) | collective-permute-done | bytes 276512 | tf_op jit(solution)/shard_map/ppermute | solution.py:437
  87.9 0.7 copy-done.3
  88.6 1.5 %collective-permute-start.24 = (bf16[72,1024]{1,0:T(8,128)(2,1)}, bf16[72,1024]{1,0:T(8,128)(2,1)}, u32[]{:S(2)}, u32[]{:S(2)}) collective-permute-start(bf16[72,1024]{1,0:T(8,128)(2,1)} %get-tuple-element.73.refs_14_), channel_id=1, source_target_pairs={{0,16},{8,24},{16,0},{24,8},{1,17},{9,25},{17,1},{25,9},{2,18},{10... | collective-permute-start | bytes 442376 | tf_op jit(solution)/shard_map/ppermute | solution.py:437
  90.1 4.1 %collective-permute-start.4 = (bf16[8,10368]{1,0:T(8,128)(2,1)}, bf16[8,10368]{1,0:T(8,128)(2,1)S(1)}, u32[]{:S(2)}, u32[]{:S(2)}) collective-permute-start(bf16[8,10368]{1,0:T(8,128)(2,1)} %copy-done.18), channel_id=1, source_target_pairs={{2,0},{3,1},{0,2},{1,3},{6,4},{7,5},{4,6},{5,7},{10,8},{11,9},{8,1... | collective-permute-start | bytes 497672 | tf_op jit(solution)/shard_map/ppermute | solution.py:434
  94.3 1.1 collective-permute-start.5
  95.3 0.5 collective-permute-start.14
  95.8 3.7 %collective-permute-start.15 = (bf16[8,10368]{1,0:T(8,128)(2,1)}, bf16[8,10368]{1,0:T(8,128)(2,1)S(1)}, u32[]{:S(2)}, u32[]{:S(2)}) collective-permute-start(bf16[8,10368]{1,0:T(8,128)(2,1)} %copy-done.20), channel_id=1, source_target_pairs={{2,0},{3,1},{0,2},{1,3},{6,4},{7,5},{4,6},{5,7},{10,8},{11,9},{8,1... | collective-permute-start | bytes 497672 | tf_op jit(solution)/shard_map/ppermute | solution.py:434
  99.5 2.0 %collective-permute-start.16 = (bf16[8,10368]{1,0:T(8,128)(2,1)}, bf16[8,10368]{1,0:T(8,128)(2,1)S(1)}, u32[]{:S(2)}, u32[]{:S(2)}) collective-permute-start(bf16[8,10368]{1,0:T(8,128)(2,1)} %copy-done.19), channel_id=1, source_target_pairs={{3,0},{2,1},{1,2},{0,3},{7,4},{6,5},{5,6},{4,7},{11,8},{10,9},{9,1... | collective-permute-start | bytes 497672 | tf_op jit(solution)/shard_map/ppermute | solution.py:434
  101.6 1.0 copy-done.2
  102.5 1.0 copy-done.4
  103.5 8.6 %update.1 = (bf16[1,896,1024]{2,1,0:T(8,128)(2,1)}, bf16[1,896,1024]{2,1,0:T(8,128)(2,1)}) custom-call(s32[1]{0:T(128)} %bitcast.2.g_ref, s32[8]{0:T(128)S(1)} %copy-done.12, bf16[32,10368]{1,0:T(8,128)(2,1)S(1)} %collective-permute-done.13.payload.refs_1_, bf16[72,896]{1,0:T(8,128)(2,1)S(1)} %get-tuple-element.53.refs_4_.refs_2_, ...), custom_call_target="tpu_custom_call" | custom-call | flops 2113929216 | bytes 14680064 | tf_op jit(solution)/shard_map/update/pallas_call | solution.py:525
  112.2 2.1 %unpack.1 = (bf16[128,1024]{1,0:T(8,128)(2,1)}, bf16[128,3584]{1,0:T(8,128)(2,1)}) custom-call(s32[1,128]{1,0:T(1,128)S(1)} %bitcast.4, f32[1,128]{1,0:T(1,128)S(1)} %bitcast.6, bf16[8,10368]{1,0:T(8,128)(2,1)S(1)} %copy-done.7, bf16[8,10368]{1,0:T(8,128)(2,1)S(1)} %copy-done.9, bf16[8,10368]{1,0:T(8,128)(2,1)S(1)} %collective-permute-done.4.refs_2_, ...), custom_call_target="tpu_custom_call" | custom-call | flops 150994944 | bytes 2507776 | tf_op jit(solution)/shard_map/unpack/pallas_call | solution.py:403
  (55 shorter events, 0.3 us)
Async XLA Ops:
  0.6 32.7 %copy-start.12 = (s32[8]{0:T(128)S(1)}, s32[8]{0:T(128)}, u32[]{:S(2)}) copy-start(s32[8]{0:T(128)} %refs_0_.1) | copy-start | bytes 100
  0.6 1.2 %copy-start = (bf16[128,3584]{1,0:T(8,128)(2,1)S(1)}, bf16[128,3584]{1,0:T(8,128)(2,1)}, u32[]{:S(2)}) copy-start(bf16[128,3584]{1,0:T(8,128)(2,1)} %tok_ref.1) | copy-start | bytes 2752516
  1.8 0.9 copy-start.5
  2.8 0.7 copy-start.13
  3.4 0.7 copy-start.15
  4.9 10.9 %collective-permute-start = (bf16[16,10368]{1,0:T(8,128)(2,1)S(1)}, bf16[16,10368]{1,0:T(8,128)(2,1)S(1)}, u32[]{:S(2)}, u32[]{:S(2)}) collective-permute-start(bf16[16,10368]{1,0:T(8,128)(2,1)S(1)} %get-tuple-element.41), channel_id=1, source_target_pairs={{0,1},{1,0},{2,3},{3,2},{4,5},{5,4},{6,7},{7,6},{8,9},{9,8},{10,11... | collective-permute-start | bytes 995336 | tf_op jit(solution)/shard_map/ppermute | solution.py:427
  7.9 17.8 %collective-permute-start.1 = (bf16[16,10368]{1,0:T(8,128)(2,1)S(1)}, bf16[16,10368]{1,0:T(8,128)(2,1)S(1)}, u32[]{:S(2)}, u32[]{:S(2)}) collective-permute-start(bf16[16,10368]{1,0:T(8,128)(2,1)S(1)} %get-tuple-element.42), channel_id=1, source_target_pairs={{0,2},{1,3},{2,0},{3,1},{4,6},{5,7},{6,4},{7,5},{8,10},{9,11},{10,... | collective-permute-start | bytes 995336 | tf_op jit(solution)/shard_map/ppermute | solution.py:427
  9.5 21.7 %collective-permute-start.2 = (bf16[16,10368]{1,0:T(8,128)(2,1)S(1)}, bf16[16,10368]{1,0:T(8,128)(2,1)S(1)}, u32[]{:S(2)}, u32[]{:S(2)}) collective-permute-start(bf16[16,10368]{1,0:T(8,128)(2,1)S(1)} %get-tuple-element.43), channel_id=1, source_target_pairs={{0,3},{1,2},{2,1},{3,0},{4,7},{5,6},{6,5},{7,4},{8,11},{9,10},{10,... | collective-permute-start | bytes 995336 | tf_op jit(solution)/shard_map/ppermute | solution.py:427
  9.5 22.0 %collective-permute-start.6 = (bf16[8,10368]{1,0:T(8,128)(2,1)S(1)}, bf16[8,10368]{1,0:T(8,128)(2,1)S(1)}, u32[]{:S(2)}, u32[]{:S(2)}) collective-permute-start(bf16[8,10368]{1,0:T(8,128)(2,1)S(1)} %get-tuple-element.49), channel_id=1, source_target_pairs={{0,4},{1,5},{2,6},{3,7},{4,0},{5,1},{6,2},{7,3},{8,12},{9,13},{10,... | collective-permute-start | bytes 497672 | tf_op jit(solution)/shard_map/ppermute | solution.py:427
  12.5 20.7 %collective-permute-start.7 = (bf16[8,10368]{1,0:T(8,128)(2,1)S(1)}, bf16[8,10368]{1,0:T(8,128)(2,1)S(1)}, u32[]{:S(2)}, u32[]{:S(2)}) collective-permute-start(bf16[8,10368]{1,0:T(8,128)(2,1)S(1)} %get-tuple-element.50), channel_id=1, source_target_pairs={{0,5},{1,4},{2,7},{3,6},{4,1},{5,0},{6,3},{7,2},{8,13},{9,12},{10,... | collective-permute-start | bytes 497672 | tf_op jit(solution)/shard_map/ppermute | solution.py:427
  15.7 25.9 %collective-permute-start.8 = (bf16[8,10368]{1,0:T(8,128)(2,1)S(1)}, bf16[8,10368]{1,0:T(8,128)(2,1)S(1)}, u32[]{:S(2)}, u32[]{:S(2)}) collective-permute-start(bf16[8,10368]{1,0:T(8,128)(2,1)S(1)} %get-tuple-element.51), channel_id=1, source_target_pairs={{0,6},{1,7},{2,4},{3,5},{4,2},{5,3},{6,0},{7,1},{8,14},{9,15},{10,... | collective-permute-start | bytes 497672 | tf_op jit(solution)/shard_map/ppermute | solution.py:427
  25.7 16.0 %collective-permute-start.9 = (bf16[8,10368]{1,0:T(8,128)(2,1)S(1)}, bf16[8,10368]{1,0:T(8,128)(2,1)S(1)}, u32[]{:S(2)}, u32[]{:S(2)}) collective-permute-start(bf16[8,10368]{1,0:T(8,128)(2,1)S(1)} %get-tuple-element.52), channel_id=1, source_target_pairs={{0,7},{1,6},{2,5},{3,4},{4,3},{5,2},{6,1},{7,0},{8,15},{9,14},{10,... | collective-permute-start | bytes 497672 | tf_op jit(solution)/shard_map/ppermute | solution.py:427
  31.4 10.3 %collective-permute-start.10 = (bf16[72,896]{1,0:T(8,128)(2,1)S(1)}, bf16[72,896]{1,0:T(8,128)(2,1)S(1)}, u32[]{:S(2)}, u32[]{:S(2)}) collective-permute-start(bf16[72,896]{1,0:T(8,128)(2,1)S(1)} %get-tuple-element.54), channel_id=1, source_target_pairs={{0,8},{8,0},{16,24},{24,16},{1,9},{9,1},{17,25},{25,17},{2,10},{10... | collective-permute-start | bytes 387080 | tf_op jit(solution)/shard_map/ppermute | solution.py:437
  31.4 10.3 %collective-permute-start.11 = (bf16[72,896]{1,0:T(8,128)(2,1)S(1)}, bf16[72,896]{1,0:T(8,128)(2,1)S(1)}, u32[]{:S(2)}, u32[]{:S(2)}) collective-permute-start(bf16[72,896]{1,0:T(8,128)(2,1)S(1)} %get-tuple-element.55), channel_id=1, source_target_pairs={{0,16},{8,24},{16,0},{24,8},{1,17},{9,25},{17,1},{25,9},{2,18},{10... | collective-permute-start | bytes 387080 | tf_op jit(solution)/shard_map/ppermute | solution.py:437
  33.2 8.5 %collective-permute-start.12 = (bf16[72,896]{1,0:T(8,128)(2,1)S(1)}, bf16[72,896]{1,0:T(8,128)(2,1)S(1)}, u32[]{:S(2)}, u32[]{:S(2)}) collective-permute-start(bf16[72,896]{1,0:T(8,128)(2,1)S(1)} %get-tuple-element.56), channel_id=1, source_target_pairs={{0,24},{8,16},{16,8},{24,0},{1,25},{9,17},{17,9},{25,1},{2,26},{10... | collective-permute-start | bytes 387080 | tf_op jit(solution)/shard_map/ppermute | solution.py:437
  41.0 0.7 copy-start.6
  41.7 4.3 %copy-start.17 = (bf16[8,10368]{1,0:T(8,128)(2,1)}, bf16[8,10368]{1,0:T(8,128)(2,1)S(1)}, u32[]{:S(2)}) copy-start(bf16[8,10368]{1,0:T(8,128)(2,1)S(1)} %get-tuple-element.47) | copy-start | bytes 497668
  41.7 4.3 %copy-start.18 = (bf16[8,10368]{1,0:T(8,128)(2,1)}, bf16[8,10368]{1,0:T(8,128)(2,1)S(1)}, u32[]{:S(2)}) copy-start(bf16[8,10368]{1,0:T(8,128)(2,1)S(1)} %get-tuple-element.46) | copy-start | bytes 497668
  46.0 33.0 %collective-permute-start.13 = (bf16[32,10368]{1,0:T(8,128)(2,1)S(1)}, bf16[32,10368]{1,0:T(8,128)(2,1)S(1)}, u32[]{:S(2)}, u32[]{:S(2)}) collective-permute-start(bf16[32,10368]{1,0:T(8,128)(2,1)S(1)} %get-tuple-element.57), channel_id=1, source_target_pairs={{0,4},{1,5},{2,6},{3,7},{4,0},{5,1},{6,2},{7,3},{8,12},{9,13},{10,... | collective-permute-start | bytes 1990664 | tf_op jit(solution)/shard_map/ppermute | solution.py:498
  49.4 9.6 %collective-permute-start.20 = (bf16[72,1920]{1,0:T(8,128)(2,1)S(1)}, bf16[72,1920]{1,0:T(8,128)(2,1)S(1)}, u32[]{:S(2)}, u32[]{:S(2)}) collective-permute-start(bf16[72,1920]{1,0:T(8,128)(2,1)S(1)} %get-tuple-element.70), channel_id=1, source_target_pairs={{0,8},{8,0},{16,24},{24,16},{1,9},{9,1},{17,25},{25,17},{2,10},{10... | collective-permute-start | bytes 829448 | tf_op jit(solution)/shard_map/ppermute | solution.py:437
  49.4 8.4 %collective-permute-start.3 = (bf16[8,10368]{1,0:T(8,128)(2,1)S(1)}, bf16[8,10368]{1,0:T(8,128)(2,1)S(1)}, u32[]{:S(2)}, u32[]{:S(2)}) collective-permute-start(bf16[8,10368]{1,0:T(8,128)(2,1)S(1)} %get-tuple-element.45), channel_id=1, source_target_pairs={{1,0},{0,1},{3,2},{2,3},{5,4},{4,5},{7,6},{6,7},{9,8},{8,9},{11,10... | collective-permute-start | bytes 497672 | tf_op jit(solution)/shard_map/ppermute | solution.py:434
  53.4 36.7 %collective-permute-start.17 = (bf16[72,2944]{1,0:T(8,128)(2,1)S(1)}, bf16[72,2944]{1,0:T(8,128)(2,1)S(1)}, u32[]{:S(2)}, u32[]{:S(2)}) collective-permute-start(bf16[72,2944]{1,0:T(8,128)(2,1)S(1)} %get-tuple-element.66), channel_id=1, source_target_pairs={{0,8},{8,0},{16,24},{24,16},{1,9},{9,1},{17,25},{25,17},{2,10},{10... | collective-permute-start | bytes 1271816 | tf_op jit(solution)/shard_map/ppermute | solution.py:437
  53.4 36.7 %collective-permute-start.18 = (bf16[72,2944]{1,0:T(8,128)(2,1)}, bf16[72,2944]{1,0:T(8,128)(2,1)S(1)}, u32[]{:S(2)}, u32[]{:S(2)}) collective-permute-start(bf16[72,2944]{1,0:T(8,128)(2,1)} %get-tuple-element.67), channel_id=1, source_target_pairs={{0,16},{8,24},{16,0},{24,8},{1,17},{9,25},{17,1},{25,9},{2,18},{10... | collective-permute-start | bytes 1271816 | tf_op jit(solution)/shard_map/ppermute | solution.py:437
  57.8 0.7 copy-start.8
  58.5 35.8 %collective-permute-start.19 = (bf16[72,2944]{1,0:T(8,128)(2,1)}, bf16[72,2944]{1,0:T(8,128)(2,1)S(1)}, u32[]{:S(2)}, u32[]{:S(2)}) collective-permute-start(bf16[72,2944]{1,0:T(8,128)(2,1)} %get-tuple-element.68), channel_id=1, source_target_pairs={{0,24},{8,16},{16,8},{24,0},{1,25},{9,17},{17,9},{25,1},{2,26},{10... | collective-permute-start | bytes 1271816 | tf_op jit(solution)/shard_map/ppermute | solution.py:437
  58.9 25.2 %collective-permute-start.21 = (bf16[72,1920]{1,0:T(8,128)(2,1)S(1)}, bf16[72,1920]{1,0:T(8,128)(2,1)S(1)}, u32[]{:S(2)}, u32[]{:S(2)}) collective-permute-start(bf16[72,1920]{1,0:T(8,128)(2,1)S(1)} %get-tuple-element.71), channel_id=1, source_target_pairs={{0,16},{8,24},{16,0},{24,8},{1,17},{9,25},{17,1},{25,9},{2,18},{10... | collective-permute-start | bytes 829448 | tf_op jit(solution)/shard_map/ppermute | solution.py:437
  79.0 8.9 %collective-permute-start.22 = (bf16[72,1920]{1,0:T(8,128)(2,1)S(1)}, bf16[72,1920]{1,0:T(8,128)(2,1)S(1)}, u32[]{:S(2)}, u32[]{:S(2)}) collective-permute-start(bf16[72,1920]{1,0:T(8,128)(2,1)S(1)} %get-tuple-element.72), channel_id=1, source_target_pairs={{0,24},{8,16},{16,8},{24,0},{1,25},{9,17},{17,9},{25,1},{2,26},{10... | collective-permute-start | bytes 829448 | tf_op jit(solution)/shard_map/ppermute | solution.py:437
  81.4 0.7 copy-start.10
  82.1 0.7 copy-start.19
  82.8 0.7 copy-start.20
  83.5 0.7 copy-start.21
  84.1 0.7 copy-start.1
  84.9 10.5 %collective-permute-start.23 = (bf16[72,1024]{1,0:T(8,128)(2,1)}, bf16[72,1024]{1,0:T(8,128)(2,1)}, u32[]{:S(2)}, u32[]{:S(2)}) collective-permute-start(bf16[72,1024]{1,0:T(8,128)(2,1)} %get-tuple-element.73.refs_14_), channel_id=1, source_target_pairs={{0,8},{8,0},{16,24},{24,16},{1,9},{9,1},{17,25},{25,17},{2,10},{10... | collective-permute-start | bytes 442376 | tf_op jit(solution)/shard_map/ppermute | solution.py:437
  87.9 0.7 copy-start.3
  88.6 7.2 %collective-permute-start.24 = (bf16[72,1024]{1,0:T(8,128)(2,1)}, bf16[72,1024]{1,0:T(8,128)(2,1)}, u32[]{:S(2)}, u32[]{:S(2)}) collective-permute-start(bf16[72,1024]{1,0:T(8,128)(2,1)} %get-tuple-element.73.refs_14_), channel_id=1, source_target_pairs={{0,16},{8,24},{16,0},{24,8},{1,17},{9,25},{17,1},{25,9},{2,18},{10... | collective-permute-start | bytes 442376 | tf_op jit(solution)/shard_map/ppermute | solution.py:437
  90.1 9.4 %collective-permute-start.25 = (bf16[72,1024]{1,0:T(8,128)(2,1)}, bf16[72,1024]{1,0:T(8,128)(2,1)}, u32[]{:S(2)}, u32[]{:S(2)}) collective-permute-start(bf16[72,1024]{1,0:T(8,128)(2,1)} %get-tuple-element.73.refs_14_), channel_id=1, source_target_pairs={{0,24},{8,16},{16,8},{24,0},{1,25},{9,17},{17,9},{25,1},{2,26},{10... | collective-permute-start | bytes 442376 | tf_op jit(solution)/shard_map/ppermute | solution.py:437
  90.1 21.9 %collective-permute-start.4 = (bf16[8,10368]{1,0:T(8,128)(2,1)}, bf16[8,10368]{1,0:T(8,128)(2,1)S(1)}, u32[]{:S(2)}, u32[]{:S(2)}) collective-permute-start(bf16[8,10368]{1,0:T(8,128)(2,1)} %copy-done.18), channel_id=1, source_target_pairs={{2,0},{3,1},{0,2},{1,3},{6,4},{7,5},{4,6},{5,7},{10,8},{11,9},{8,1... | collective-permute-start | bytes 497672 | tf_op jit(solution)/shard_map/ppermute | solution.py:434
  94.3 17.8 %collective-permute-start.5 = (bf16[8,10368]{1,0:T(8,128)(2,1)}, bf16[8,10368]{1,0:T(8,128)(2,1)S(1)}, u32[]{:S(2)}, u32[]{:S(2)}) collective-permute-start(bf16[8,10368]{1,0:T(8,128)(2,1)} %copy-done.17), channel_id=1, source_target_pairs={{3,0},{2,1},{1,2},{0,3},{7,4},{6,5},{5,6},{4,7},{11,8},{10,9},{9,1... | collective-permute-start | bytes 497672 | tf_op jit(solution)/shard_map/ppermute | solution.py:434
  95.3 16.8 %collective-permute-start.14 = (bf16[8,10368]{1,0:T(8,128)(2,1)}, bf16[8,10368]{1,0:T(8,128)(2,1)S(1)}, u32[]{:S(2)}, u32[]{:S(2)}) collective-permute-start(bf16[8,10368]{1,0:T(8,128)(2,1)} %copy-done.21), channel_id=1, source_target_pairs={{1,0},{0,1},{3,2},{2,3},{5,4},{4,5},{7,6},{6,7},{9,8},{8,9},{11,10... | collective-permute-start | bytes 497672 | tf_op jit(solution)/shard_map/ppermute | solution.py:434
  95.8 16.3 %collective-permute-start.15 = (bf16[8,10368]{1,0:T(8,128)(2,1)}, bf16[8,10368]{1,0:T(8,128)(2,1)S(1)}, u32[]{:S(2)}, u32[]{:S(2)}) collective-permute-start(bf16[8,10368]{1,0:T(8,128)(2,1)} %copy-done.20), channel_id=1, source_target_pairs={{2,0},{3,1},{0,2},{1,3},{6,4},{7,5},{4,6},{5,7},{10,8},{11,9},{8,1... | collective-permute-start | bytes 497672 | tf_op jit(solution)/shard_map/ppermute | solution.py:434
  99.5 12.6 %collective-permute-start.16 = (bf16[8,10368]{1,0:T(8,128)(2,1)}, bf16[8,10368]{1,0:T(8,128)(2,1)S(1)}, u32[]{:S(2)}, u32[]{:S(2)}) collective-permute-start(bf16[8,10368]{1,0:T(8,128)(2,1)} %copy-done.19), channel_id=1, source_target_pairs={{3,0},{2,1},{1,2},{0,3},{7,4},{6,5},{5,6},{4,7},{11,8},{10,9},{9,1... | collective-permute-start | bytes 497672 | tf_op jit(solution)/shard_map/ppermute | solution.py:434
  101.6 1.0 copy-start.2
  102.5 1.0 copy-start.4
  103.5 8.6 %copy-start.7 = (bf16[8,10368]{1,0:T(8,128)(2,1)S(1)}, bf16[8,10368]{1,0:T(8,128)(2,1)}, u32[]{:S(2)}) copy-start(bf16[8,10368]{1,0:T(8,128)(2,1)} %copy-done.6) | copy-start | bytes 497668
  103.5 8.7 %copy-start.9 = (bf16[8,10368]{1,0:T(8,128)(2,1)S(1)}, bf16[8,10368]{1,0:T(8,128)(2,1)}, u32[]{:S(2)}) copy-start(bf16[8,10368]{1,0:T(8,128)(2,1)} %copy-done.8) | copy-start | bytes 497668
  103.5 8.7 %copy-start.11 = (bf16[8,10368]{1,0:T(8,128)(2,1)S(1)}, bf16[8,10368]{1,0:T(8,128)(2,1)}, u32[]{:S(2)}) copy-start(bf16[8,10368]{1,0:T(8,128)(2,1)} %copy-done.10) | copy-start | bytes 497668
  103.5 8.7 %copy-start.14 = (s32[128]{0:T(128)S(1)}, s32[128]{0:T(128)}, u32[]{:S(2)}) copy-start(s32[128]{0:T(128)} %param.10) | copy-start | bytes 1540
  103.5 8.7 %copy-start.16 = (f32[128]{0:T(128)S(1)}, f32[128]{0:T(128)}, u32[]{:S(2)}) copy-start(f32[128]{0:T(128)} %param.8) | copy-start | bytes 1540

commit v2 on v1

v2 whole, which is shorter than its diff:
```python
import functools
import math

import jax
import jax.numpy as jnp
from jax import lax
from jax.experimental import pallas as pl
from jax.experimental.pallas import tpu as pltpu
from jax.sharding import PartitionSpec as P

learning_rate = 0.004
decay_rate = 0.9

BF16 = jnp.bfloat16
F32 = jnp.float32
SUB = 8
LANES = 128
INNER = 2


class Plan:
    def __init__(self, slots, groups, tokens, features, hidden):
        self.slots, self.groups, self.tokens = slots, groups, tokens
        self.D, self.F = features, hidden
        self.half = slots // 2
        self.cap = tokens * 9 // 8 // slots
        self.full, self.rest = divmod(self.cap, SUB)
        self.cuts = SUB // self.rest if self.rest else 1
        self.rows = self.half * self.cap
        self.share = features // groups
        self.DX = features * self.cap // SUB
        self.FG = hidden * self.cap // SUB
        self.C = self.DX + self.FG
        self.pieces = self.cap * groups // SUB
        self.outer = groups // INNER

    def group_at(self, group, step):
        chip, core = group // INNER, group % INNER
        if isinstance(group, int):
            return away(chip, step // INNER, self.outer) * INNER + (core ^ (step % INNER))
        return away_traced(chip, step // INNER, self.outer) * INNER + jnp.bitwise_xor(
            core, step % INNER
        )

    def group_from(self, step):
        chips = step // INNER
        if self.outer & (self.outer - 1):
            chips = (self.outer - chips) % self.outer
        return chips * INNER + step % INNER

    def fits(self):
        return (
            self.slots % 2 == 0
            and (self.rest == 0 or SUB % self.rest == 0)
            and self.D % (self.cuts * LANES) == 0
            and self.F % (self.cuts * LANES) == 0
            and self.D % (self.groups * LANES) == 0
            and self.groups % INNER == 0
            and (self.cap * self.groups) % SUB == 0
            and self.rows % SUB == 0
            and (self.half * self.rest) % SUB == 0
            and self.tokens % LANES == 0
        )


def away(place, step, count):
    if count & (count - 1) == 0:
        return place ^ step
    return (place + step) % count


def away_traced(place, step, count):
    if count & (count - 1) == 0:
        return jnp.bitwise_xor(place, step)
    return lax.rem(place + step, count)


def steps_between(first, second, count):
    if count & (count - 1) == 0:
        return jnp.bitwise_xor(first, second)
    return lax.rem(first - second + count, count)


def iota(shape, dim):
    return lax.broadcasted_iota(jnp.int32, shape, dim)


def dot(a, b):
    return jnp.dot(a, b, preferred_element_type=F32)


def dot_nt(a, b):
    return lax.dot_general(a, b, (((1,), (1,)), ((), ())), preferred_element_type=F32)


def dot_tn(a, b):
    return lax.dot_general(a, b, (((0,), (0,)), ((), ())), preferred_element_type=F32)


def picker(plan, cut):
    shape = (plan.half * plan.rest, plan.half * SUB)
    row, col = iota(shape, 0), iota(shape, 1)
    wanted = (row // plan.rest) * SUB + cut * plan.rest + row % plan.rest
    return (wanted == col).astype(BF16)


def unfold(plan, blocks, width):
    parts = [
        jnp.concatenate([b[:, i * width : (i + 1) * width] for b in blocks], axis=0)
        for i in range(plan.full)
    ]
    if plan.rest:
        piece = width // plan.cuts
        tail = jnp.concatenate([b[:, plan.full * width :] for b in blocks], axis=0).astype(BF16)
        parts.append(
            jnp.concatenate([dot(picker(plan, q), tail) for q in range(plan.cuts)], axis=1)
        )
    return jnp.concatenate(parts, axis=0).astype(BF16)


def fold(plan, rows):
    width = rows.shape[1]
    block = plan.half * SUB
    parts = [rows[i * block : (i + 1) * block] for i in range(plan.full)]
    if plan.rest:
        piece = width // plan.cuts
        tail = rows[plan.full * block :].astype(BF16)
        total = None
        for q in range(plan.cuts):
            term = dot_tn(picker(plan, q), tail[:, q * piece : (q + 1) * piece])
            total = term if total is None else total + term
        parts.append(total)
    return jnp.concatenate(parts, axis=1)


def is_hot(plan, placement_ref):
    me = lax.axis_index("expert")
    partner = lax.rem(me + plan.half, plan.slots)
    return placement_ref[me] == placement_ref[partner]


def token_places(plan, slot):
    me = lax.axis_index("expert")
    my_half = me // plan.half
    my_place = lax.rem(me, plan.half)
    upper = (slot >= plan.half).astype(jnp.int32)
    place = slot - plan.half * upper
    far = jnp.where(upper == my_half, 0, 1)
    step = steps_between(place, jnp.zeros_like(place) + my_place, plan.half)
    block = 2 * step + far
    count = plan.tokens
    onehot = (iota((2 * plan.half, count), 0) == block).astype(F32)
    upto = (iota((count, count), 0) <= iota((count, count), 1)).astype(BF16)
    seen = dot(onehot.astype(BF16), upto)
    rank = jnp.sum(onehot * (seen - 1.0), axis=0, keepdims=True).astype(jnp.int32)
    return block, rank


def row_targets(plan, block, rank):
    targets = []
    for i in range(plan.full):
        inside = (rank >= i * SUB) & (rank < (i + 1) * SUB)
        targets.append(jnp.where(inside, block * SUB + rank - i * SUB, -1))
    for q in range(plan.cuts if plan.rest else 0):
        inside = rank >= plan.full * SUB
        targets.append(
            jnp.where(inside, block * SUB + q * plan.rest + rank - plan.full * SUB, -1)
        )
    return targets


def to_column(row):
    n = row.shape[1]
    eye = (iota((n, n), 0) == iota((n, n), 1)).astype(F32)
    return jnp.sum(eye * row.astype(F32), axis=1, keepdims=True)


def pack_kernel(far, plan, slot_hbm, gate_hbm, tok_hbm, cot_hbm, *refs):
    half = plan.half
    outs, refs = refs[-half - 5 : -5], refs[-5:]
    slot_ref, gate_ref, tok_ref, cot_ref, sems = refs
    copies = [
        pltpu.make_async_copy(source, held, sems.at[i])
        for i, (source, held) in enumerate(
            ((slot_hbm, slot_ref), (tok_hbm, tok_ref), (gate_hbm, gate_ref), (cot_hbm, cot_ref))
        )
    ]
    for copy in copies:
        copy.start()
    copies[0].wait()
    block, rank = token_places(plan, slot_ref[...])
    wanted = lax.rem(block, 2) == far
    block = jnp.where(wanted, block // 2, -2)
    targets = row_targets(plan, block, rank)
    height = half * SUB
    onehots = [(iota((height, plan.tokens), 0) == t).astype(BF16) for t in targets]

    def store(values, start):
        stop = start + values.shape[1]
        for m in range(half):
            outs[m][:, start:stop] = values[m * SUB : (m + 1) * SUB].astype(BF16)

    def place(data, base):
        width = data.shape[1]
        for i in range(plan.full):
            store(dot(onehots[i], data), base + i * width)
        if plan.rest:
            piece = width // plan.cuts
            total = None
            for q in range(plan.cuts):
                term = dot(onehots[plan.full + q], data[:, q * piece : (q + 1) * piece])
                total = term if total is None else total + term
            store(total, base + plan.full * width)

    copies[1].wait()
    place(tok_ref[...], 0)
    copies[2].wait()
    copies[3].wait()
    scaled = (to_column(gate_ref[...]) * cot_ref[...].astype(F32)).astype(BF16)
    place(scaled, plan.DX)


def blocks_of(refs, start, stop):
    return [r[:, start:stop].astype(F32) for r in refs]


def columns_kernel(plan, *refs):
    half = plan.half
    near, far = refs[:half], refs[half : 2 * half]
    outs, held = refs[-plan.groups - 1 : -1], refs[-1]
    for i, blocks in enumerate((near, far)):
        held[i] = unfold(plan, blocks_of(blocks, 0, plan.DX), plan.D)
    for m in range(plan.groups):
        start = pl.multiple_of(plan.group_at(lax.axis_index("dp"), m) * plan.share, LANES)
        for i in range(2):
            outs[m][i] = held[i, :, pl.ds(start, plan.share)]


def activate(preact, scaled):
    sigma = jax.nn.sigmoid(preact)
    act = (preact * sigma).astype(BF16)
    grad_pre = (scaled.astype(F32) * sigma * (1.0 + preact * (1.0 - sigma))).astype(BF16)
    return act, grad_pre


def chip_columns(plan, rows, outs):
    width = INNER * plan.share
    chip = lax.axis_index("dp") // INNER
    for o in range(plan.outer):
        start = pl.multiple_of(away_traced(chip, o, plan.outer) * width, LANES)
        outs[o][:, :width] = rows[:, pl.ds(start, width)]


def near_kernel(plan, placement_ref, weight_ref, *refs):
    half = plan.half
    near, refs = refs[:half], refs[half:]
    far, refs = refs[:half], refs[half:]
    back_near, local_back, local_act, folded_grad, grads = refs[-5:]
    x_near = unfold(plan, blocks_of(near, 0, plan.DX), plan.D)
    x_far = unfold(plan, blocks_of(far, 0, plan.DX), plan.D)
    g_near = unfold(plan, blocks_of(near, plan.DX, plan.C), plan.F)
    g_far = unfold(plan, blocks_of(far, plan.DX, plan.C), plan.F)
    x = jnp.concatenate([x_near.astype(F32), x_far.astype(F32)], axis=0).astype(BF16)
    g = jnp.concatenate([g_near.astype(F32), g_far.astype(F32)], axis=0).astype(BF16)
    act, grad_pre = activate(dot(x, weight_ref[0]), g)
    back = dot_nt(grad_pre, weight_ref[0])
    act, grad32 = act.astype(F32), grad_pre.astype(F32)
    back_near[:, : plan.DX] = fold(plan, back[: plan.rows]).astype(BF16)
    back_near[:, plan.DX :] = fold(plan, act[: plan.rows]).astype(BF16)
    local_back[...] = fold(plan, back[plan.rows :]).astype(BF16)
    local_act[...] = fold(plan, act[plan.rows :]).astype(BF16)
    grad_near = grad32[: plan.rows]
    grad_far = jnp.where(is_hot(plan, placement_ref), grad32[plan.rows :], 0.0)
    folded_grad[...] = fold(plan, grad_near).astype(BF16)
    grads[:, : plan.F] = grad_near.astype(BF16)
    grads[:, plan.F :] = grad_far.astype(BF16)


def payload_kernel(
    plan, placement_ref, weight_ref, folded_grad, near_grads, *refs
):
    half, groups = plan.half, plan.groups
    far, refs = refs[:half], refs[half:]
    columns, refs = refs[:groups], refs[groups:]
    small, large, refs = refs[0], refs[1], refs[2:]
    share, refs = refs[:groups], refs[groups:]
    (rows,) = refs
    hot = is_hot(plan, placement_ref)
    width = plan.share
    x = unfold(plan, blocks_of(far, 0, plan.DX), plan.D)
    g = unfold(plan, blocks_of(far, plan.DX, plan.C), plan.F)
    rows[...] = x
    act, grad_pre = activate(dot(x, weight_ref[0]), g)

    @pl.when(jnp.logical_not(hot))
    def _():
        back = dot_nt(grad_pre, weight_ref[0])
        large[...] = fold(plan, back).astype(BF16)
        small[...] = fold(plan, act.astype(F32)).astype(BF16)

    @pl.when(hot)
    def _():
        together = jnp.concatenate([c[0].astype(F32) for c in columns], axis=0)
        block = half * SUB
        for i in range(plan.pieces):
            large[:, i * plan.share : (i + 1) * plan.share] = together[
                i * block : (i + 1) * block
            ].astype(BF16)
        small[...] = folded_grad[...]

    group = lax.axis_index("dp")
    for o in range(groups):
        start = pl.multiple_of(plan.group_at(group, o) * width, LANES)
        share[o][:, :width] = rows[:, pl.ds(start, width)]
        share[o][:, width : width + 2 * plan.F] = near_grads[...]
        share[o][:, width + 2 * plan.F :] = grad_pre


def after_small_kernel(plan, placement_ref, small, local_act, near_back, *outs):
    hot = is_hot(plan, placement_ref)
    payload = small[...].astype(F32)
    chosen = jnp.where(hot, local_act[...].astype(F32), payload)
    back = near_back[...].astype(F32)
    for m in range(plan.half):
        span = slice(m * SUB, (m + 1) * SUB)
        outs[m][:, : plan.C] = back[span].astype(BF16)
        outs[m][:, plan.C :] = chosen[span].astype(BF16)
    blocks = [payload[m * SUB : (m + 1) * SUB] for m in range(plan.half)]
    outs[plan.half][...] = jnp.where(hot, unfold(plan, blocks, plan.F).astype(F32), 0.0).astype(BF16)


def after_large_kernel(plan, placement_ref, large, local_back, *refs):
    outs = refs[-plan.half :]
    hot = is_hot(plan, placement_ref)
    chosen = jnp.where(hot, local_back[...].astype(F32), large[...].astype(F32))
    for m in range(plan.half):
        outs[m][...] = chosen[m * SUB : (m + 1) * SUB].astype(BF16)


def unpack_kernel(plan, slot_ref, gate_ref, *refs):
    early, refs = refs[: plan.half], refs[plan.half :]
    late, refs = refs[: plan.half], refs[plan.half :]
    out_ref, grad_ref = refs
    block, rank = token_places(plan, slot_ref[...])
    width = 2 * plan.half * SUB
    picks = []
    for target in row_targets(plan, block, rank):
        column = to_column(target).astype(jnp.int32)
        picks.append((iota((plan.tokens, width), 1) == column).astype(BF16))

    def gather(near, far, size):
        stacked = []
        for m in range(plan.half):
            stacked += [near[m], far[m]]
        stacked = jnp.concatenate(stacked, axis=0).astype(BF16)
        total = None
        for i in range(plan.full):
            term = dot(picks[i], stacked[:, i * size : (i + 1) * size])
            total = term if total is None else total + term
        if plan.rest:
            tail = stacked[:, plan.full * size :]
            term = jnp.concatenate(
                [dot(picks[plan.full + q], tail) for q in range(plan.cuts)], axis=1
            )
            total = term if total is None else total + term
        return total

    near = blocks_of(early, 0, plan.DX)
    grad_ref[...] = gather(near, blocks_of(late, 0, plan.DX), plan.D).astype(BF16)
    near = blocks_of(early, plan.DX, plan.C)
    far = blocks_of(early, plan.C, plan.C + plan.FG)
    out_ref[...] = (to_column(gate_ref[...]) * gather(near, far, plan.F)).astype(BF16)


def rows_of(parts):
    return jnp.concatenate([p.astype(F32) for p in parts], axis=0).astype(BF16)


def gather_kernel(plan, *refs):
    groups, share, width = plan.groups, plan.share, plan.F
    columns, refs = refs[:groups], refs[groups:]
    shared, refs = refs[:groups], refs[groups:]
    total, x_all = refs
    base = share
    x_parts, g_parts = [], []
    for m in range(groups):
        x_parts += [columns[m][0], columns[m][1], shared[m][:, :share]]
        g_parts += [shared[m][:, base + i * width : base + (i + 1) * width] for i in range(3)]
    x_all[...] = rows_of(x_parts)
    g_all = rows_of(g_parts)
    for i in range(share // LANES):
        span = slice(i * LANES, (i + 1) * LANES)
        total[span, :] = dot_tn(x_all[:, span], g_all)


def update_kernel(plan, placement_ref, large, *refs):
    other_g, refs = refs[: plan.groups], refs[plan.groups :]
    total_ref, weight_ref, momentum_ref, new_weight, new_momentum, x_all, g_all = refs
    step = pl.program_id(0)
    share = plan.share
    tile = new_weight.shape[1]

    @pl.when(step == 0)
    def _():
        hot = is_hot(plan, placement_ref)
        pieces = [
            large[:, i * share : (i + 1) * share].astype(F32) for i in range(plan.pieces)
        ]
        x_all[...] = jnp.where(hot, jnp.concatenate(pieces, axis=0), 0.0).astype(BF16)
        g_all[...] = rows_of([g[...] for g in other_g])

    start = pl.multiple_of(step * tile, LANES)
    total = total_ref[...] + dot_tn(x_all[:, pl.ds(start, tile)], g_all[...])
    momentum = (decay_rate * momentum_ref[0].astype(F32) + total).astype(BF16)
    new_momentum[0] = momentum
    new_weight[0] = (
        weight_ref[0].astype(F32) - learning_rate * momentum.astype(F32)
    ).astype(BF16)


MIB = 1024 * 1024
SMEM_SPEC = pl.BlockSpec(memory_space=pltpu.SMEM)
ANY_SPEC = pl.BlockSpec(memory_space=pl.ANY)
VMEM_SPEC = pl.BlockSpec(memory_space=pltpu.VMEM)


def call(kernel, plan, ins, specs, outs, scratch, flops, name, limit=16, dtype=BF16):
    moved = sum(a.size * a.dtype.itemsize for a in ins) + sum(2 * math.prod(o) for o in outs)
    return pl.pallas_call(
        functools.partial(kernel, plan),
        out_shape=[jax.ShapeDtypeStruct(s, dtype) for s in outs],
        in_specs=specs,
        out_specs=[VMEM_SPEC] * len(outs),
        scratch_shapes=scratch,
        compiler_params=pltpu.CompilerParams(vmem_limit_bytes=limit * MIB),
        cost_estimate=pl.CostEstimate(
            flops=flops, bytes_accessed=moved if flops else 0, transcendentals=0
        ),
        name=name,
    )(*ins)


def routed(plan, tokens, route_weight, cotangent, slot_ids, placement, weight, momentum):
    half, groups, outer = plan.half, plan.groups, plan.outer
    D, F, C, rows, share = plan.D, plan.F, plan.C, plan.rows, plan.share
    slot = slot_ids.reshape(1, -1)
    gate = route_weight.reshape(1, -1)

    def to_slot(data, m):
        pairs = []
        for e in range(plan.slots):
            h, k = divmod(e, half)
            pairs.append((e, h * half + away(k, m, half)))
        return lax.ppermute(data, "expert", pairs)

    def to_source(data, m):
        pairs = []
        for e in range(plan.slots):
            h, k = divmod(e, half)
            pairs.append((h * half + away(k, m, half), e))
        return lax.ppermute(data, "expert", pairs)

    def to_partner(data):
        pairs = [(e, (e + half) % plan.slots) for e in range(plan.slots)]
        return lax.ppermute(data, "expert", pairs)

    def from_group(data, m):
        pairs = []
        for d in range(groups):
            pairs.append((plan.group_at(d, m), d))
        return lax.ppermute(data, "dp", pairs)

    def from_chips(per_chip):
        got = [per_chip[0]]
        for o in range(1, outer):
            sent = o if outer & (outer - 1) == 0 else outer - o
            got.append(from_group(per_chip[sent], INNER * o))
        return got

    def with_sisters(got):
        return [data for own in got for data in (own, from_group(own, 1))]

    def pack(far, name, after, limit):
        return call(
            functools.partial(pack_kernel, far),
            plan,
            [slot, gate, tokens, cotangent] + after,
            [ANY_SPEC] * (4 + len(after)),
            [(SUB, C)] * half,
            [
                pltpu.VMEM(slot.shape, slot.dtype),
                pltpu.VMEM(gate.shape, gate.dtype),
                pltpu.VMEM(tokens.shape, tokens.dtype),
                pltpu.VMEM(cotangent.shape, cotangent.dtype),
                pltpu.SemaphoreType.DMA((4,)),
            ],
            2 * 4 * half * SUB * plan.tokens * (D + F),
            name,
            limit=limit,
        )

    packed = pack(1, "pack_far", [], 60)
    relay = [packed[0]] + [to_slot(packed[m], m) for m in range(1, half)]
    far = [to_partner(block) for block in relay]
    packed = pack(0, "pack_near", relay[1:] + far[:1], 8)
    near = [packed[0]] + [to_slot(packed[m], m) for m in range(1, half)]

    columns = call(
        columns_kernel,
        plan,
        near + relay + far[1:2],
        [VMEM_SPEC] * (2 * half) + [ANY_SPEC],
        [(2, rows, share)] * groups,
        [pltpu.VMEM((2, rows, D), BF16)],
        0,
        "near_columns",
    )
    columns_here = [columns[0]] + [
        from_group(columns[plan.group_from(m)], m) for m in range(1, groups)
    ]
    back_near, local_back, local_act, folded_grad, grads = call(
        near_kernel,
        plan,
        [placement, weight] + near + relay + [columns[0], far[2]],
        [SMEM_SPEC, VMEM_SPEC] + [VMEM_SPEC] * (2 * half) + [ANY_SPEC] * 2,
        [
            (half * SUB, C),
            (half * SUB, plan.DX),
            (half * SUB, plan.FG),
            (half * SUB, plan.FG),
            (rows, 2 * F),
        ],
        [],
        8 * rows * D * F,
        "near_rows",
    )
    outs = call(
        payload_kernel,
        plan,
        [placement, weight, folded_grad, grads] + far + columns_here,
        [SMEM_SPEC] + [VMEM_SPEC] * (3 + half + groups),
        [(half * SUB, plan.FG), (half * SUB, plan.DX)]
        + [(rows, share + 3 * F)] * groups,
        [pltpu.VMEM((rows, D), BF16)],
        4 * rows * D * F,
        "payload",
    )
    small = to_partner(outs[0])
    large = to_partner(outs[1])
    shared = outs[2 : 2 + groups]
    shared = [shared[0]] + [from_group(shared[plan.group_from(m)], m) for m in range(1, groups)]
    outs = call(
        after_small_kernel,
        plan,
        [placement, small, local_act, back_near],
        [SMEM_SPEC] + [VMEM_SPEC] * 3,
        [(SUB, C + plan.FG)] * half + [(rows, F)],
        [],
        0,
        "after_small",
    )
    early = [outs[0]] + [to_source(outs[m], m) for m in range(1, half)]
    other_g = with_sisters(from_chips([outs[half]] * outer))
    (total,) = call(
        gather_kernel,
        plan,
        columns_here + shared,
        [VMEM_SPEC] * (2 * groups),
        [(share, F)],
        [pltpu.VMEM((3 * groups * rows, share), BF16)],
        0,
        "own_terms",
        dtype=F32,
    )
    first = [total] + other_g[1:]
    outs = call(
        after_large_kernel,
        plan,
        [placement, large, local_back] + first,
        [SMEM_SPEC] + [VMEM_SPEC] * 2 + [ANY_SPEC] * len(first),
        [(SUB, plan.DX)] * half,
        [],
        1000000,
        "after_large",
    )
    far_back = [outs[0]] + [to_source(outs[m], m) for m in range(1, half)]

    tile = LANES
    steps = share // tile
    group = lax.axis_index("dp").reshape(1)

    def whole(*shape):
        return pl.BlockSpec(shape, lambda i, g: (0,) * len(shape))

    new_weight, new_momentum = pl.pallas_call(
        lambda g_ref, *refs: update_kernel(plan, *refs),
        grid_spec=pltpu.PrefetchScalarGridSpec(
            num_scalar_prefetch=1,
            grid=(steps,),
            in_specs=[SMEM_SPEC, whole(half * SUB, plan.DX)]
            + [whole(rows, F)] * groups
            + [
                pl.BlockSpec((tile, F), lambda i, g: (i, 0)),
                pl.BlockSpec((1, tile, F), lambda i, g: (0, g[0] * steps + i, 0)),
                pl.BlockSpec((1, tile, F), lambda i, g: (0, i, 0)),
            ],
            out_specs=[pl.BlockSpec((1, tile, F), lambda i, g: (0, i, 0))] * 2,
            scratch_shapes=[
                pltpu.VMEM((groups * rows, share), BF16),
                pltpu.VMEM((groups * rows, F), BF16),
            ],
        ),
        out_shape=[jax.ShapeDtypeStruct((1, share, F), BF16)] * 2,
        compiler_params=pltpu.CompilerParams(vmem_limit_bytes=16 * MIB),
        cost_estimate=pl.CostEstimate(
            flops=2 * groups * rows * share * F, bytes_accessed=12 * share * F, transcendentals=0
        ),
        name="update",
    )(group, placement, large, *other_g, total, weight, momentum)

    expert_out, token_grad = call(
        unpack_kernel,
        plan,
        [slot, gate] + early + far_back,
        [VMEM_SPEC] * (2 + 2 * half),
        [(plan.tokens, F), (plan.tokens, D)],
        [],
        2 * 4 * half * SUB * plan.tokens * (D + F),
        "unpack",
    )
    return expert_out, token_grad, new_weight, new_momentum


def general(tokens, route_weight, cotangent, slot_ids, placement, weight, momentum):
    n_slots = lax.axis_size("expert")
    n_groups = lax.axis_size("dp")
    tok_count, D = tokens.shape
    F = cotangent.shape[1]
    capacity = tok_count * 9 // 8 // n_slots
    onehot = (slot_ids[:, None] == jnp.arange(n_slots, dtype=jnp.int32)[None, :]).astype(jnp.int32)
    ranks = jnp.sum((jnp.cumsum(onehot, axis=0) - 1) * onehot, axis=1)
    position = slot_ids * capacity + ranks
    send_rows = jnp.zeros((n_slots * capacity, D), BF16).at[position].set(tokens)
    scaled = (route_weight[:, None] * cotangent.astype(F32)).astype(BF16)
    send_grads = jnp.zeros((n_slots * capacity, F), BF16).at[position].set(scaled)
    matrix = weight[0]

    def exchange(rows):
        width = rows.shape[-1]
        return lax.all_to_all(
            rows.reshape(n_slots, capacity, width), "expert", split_axis=0, concat_axis=0, tiled=True
        ).reshape(-1, width)

    flat_x = exchange(send_rows)
    act, flat_grad = activate(dot(flat_x, matrix), exchange(send_grads))
    back = dot_nt(flat_grad, matrix).astype(BF16)
    act_rows = exchange(act)[position]
    expert_out = (route_weight[:, None] * act_rows.astype(F32)).astype(BF16)
    token_grad = exchange(back)[position]
    row_count = flat_x.shape[0]
    share = D // n_groups
    columns = lax.all_to_all(
        flat_x.reshape(1, row_count, n_groups, share), "dp", split_axis=2, concat_axis=0, tiled=True
    )
    columns = columns.reshape(n_groups, row_count, share)
    terms = jnp.einsum(
        "krd,krf->kdf",
        columns,
        lax.all_gather(flat_grad[None], "dp", axis=0, tiled=True),
        preferred_element_type=F32,
    )
    terms = lax.optimization_barrier(terms.astype(BF16)).astype(F32)
    reduced = jnp.sum(terms, axis=0).astype(BF16)
    half = n_slots // 2
    partner_grad = lax.ppermute(
        reduced, "expert", [(i, (i + half) % n_slots) for i in range(n_slots)]
    ).astype(F32)
    my_slot = lax.axis_index("expert")
    partner_slot = (my_slot + half) % n_slots
    same = placement[my_slot] == placement[partner_slot]
    total = reduced.astype(F32) + jnp.where(same, partner_grad, 0.0)
    new_momentum = (decay_rate * momentum[0].astype(F32) + total).astype(BF16)
    old = lax.dynamic_slice_in_dim(matrix, lax.axis_index("dp") * share, share, 0).astype(F32)
    new_weight = (old - learning_rate * new_momentum.astype(F32)).astype(BF16)
    return expert_out, token_grad, new_weight[None], new_momentum[None]


def solution(mesh):
    def shards(tokens, route_weight, cotangent, slot_ids, placement, weight, momentum):
        plan = Plan(
            mesh.shape["expert"],
            mesh.shape["dp"],
            tokens.shape[0],
            tokens.shape[1],
            cotangent.shape[1],
        )
        body = functools.partial(routed, plan) if plan.fits() else general
        return body(tokens, route_weight, cotangent, slot_ids, placement, weight, momentum)

    return jax.shard_map(
        shards,
        mesh=mesh,
        in_specs=(
            P(("dp", "expert"), None),
            P(("dp", "expert")),
            P(("dp", "expert"), None),
            P(("dp", "expert")),
            P(),
            P("expert", None, None),
            P("expert", "dp", None),
        ),
        out_specs=(
            P(("dp", "expert"), None),
            P(("dp", "expert"), None),
            P("expert", "dp", None),
            P("expert", "dp", None),
        ),
        check_vma=False,
    )
```

time: 116 us -> 119 us (1.026)
  waiting for transfers between devices: 34.6 us -> 44.7 us
  starting transfers between devices: 42.9 us -> 33.1 us
  local copies, waits for them, and re-layouts: 10.8 us -> 13.7 us
    ppermute x7 -> x6, waiting for transfers between devices: 9.09 us -> 17.7 us  [to_slot(): return lax.ppermute(data, 'expert', pairs)]
    ppermute x7 -> x6, starting transfers between devices: 17.2 us -> 8.89 us  [to_slot(): return lax.ppermute(data, 'expert', pairs)]
    ppermute x6, starting transfers between devices: 15.4 us -> 8.83 us  [to_source(): return lax.ppermute(data, 'expert', pairs)]
    ppermute x13 -> x15, waiting for transfers between devices: 21.8 us -> 27 us  [the longest x6 19.3 us: to_partner(): return lax.ppermute(data, 'expert', pairs)]
    ppermute x13 -> x15, starting transfers between devices: 10.4 us -> 15.4 us  [the longest x6 10.1 us: to_partner(): return lax.ppermute(data, 'expert', pairs)]
    ppermute x6, waiting for transfers between devices: 3.71 us -> 0.02 us  [to_source(): return lax.ppermute(data, 'expert', pairs)]
    pallas_call x6 -> x9, Pallas kernels: 16.5 us -> 19.8 us  [call(): pl.pallas_call(functools.partial(kernel, plan), out_shape=[jax.ShapeDtype...]
    pallas_call x1, Pallas kernels: 8.57 us -> 5.42 us  [routed(): pl.pallas_call(lambda g_ref, *refs: update_kernel(plan, *refs), grid_spec...]
  transfers between devices with their start and end apart: 26 -> 27, of which waited for: 6 -> 9; matrix products, arithmetic and copies ran while one was open for 0% -> 0% of each run, Pallas kernels for 16% -> 13%
where the time goes in v2:
time: 119 us; the launch traced here: 118 us
  waiting for transfers between devices  44.7 us (38%)
  starting transfers between devices  33.1 us (28%)
  Pallas kernels  25.2 us (21%)
  local copies, waits for them, and re-layouts  13.7 us (12%)
    pallas_call x9, Pallas kernels, call(): pl.pallas_call(functools.partial(kernel, plan), out_shape=[jax.ShapeDtype...  19.8 us
    ppermute x6, waiting for transfers between devices, to_partner(): return lax.ppermute(data, 'expert', pairs)  19.3 us
    ppermute x6, waiting for transfers between devices, to_slot(): return lax.ppermute(data, 'expert', pairs)  17.7 us
    unnamed x34, local copies, waits for them, and re-layouts  13.7 us
    ppermute x6, starting transfers between devices, to_partner(): return lax.ppermute(data, 'expert', pairs)  10.1 us
    ppermute x6, starting transfers between devices, to_slot(): return lax.ppermute(data, 'expert', pairs)  8.89 us
    ppermute x6, starting transfers between devices, to_source(): return lax.ppermute(data, 'expert', pairs)  8.83 us
    ppermute x9, waiting for transfers between devices, from_group(): return lax.ppermute(data, 'dp', pairs)  7.66 us
  transfers between devices with their start and end apart: 27, of which 9 were waited for; matrix products, arithmetic and copies ran while one was open for 0% of the time, Pallas kernels for 13%

profile of v2, /device:TPU:0, one launch (start us, length us, event | category | flops | bytes accessed | tf_op | source)
XLA Modules:
  0.0 117.5 jit_solution(16511268988055328453)
XLA Ops:
  0.6 2.9 %pack_far.1 = (bf16[8,10368]{1,0:T(8,128)(2,1)}, bf16[8,10368]{1,0:T(8,128)(2,1)}, bf16[8,10368]{1,0:T(8,128)(2,1)}, bf16[8,10368]{1,0:T(8,128)(2,1)}) custom-call(s32[1,128]{1,0:T(1,128)} %bitcast.3, f32[1,128]{1,0:T(1,128)} %bitcast.6, bf16[128,3584]{1,0:T(8,128)(2,1)} %tok_hbm.3, bf16[128,1024]{1,0:T(8,128)(2,1)} %cot_hbm.3), custom_call_target="tpu_custom_call" | custom-call | flops 150994944 | bytes 1844224 | tf_op jit(solution)/shard_map/pack_far/pallas_call | solution.py:429
  3.6 3.0 %collective-permute-start = (bf16[8,10368]{1,0:T(8,128)(2,1)}, bf16[8,10368]{1,0:T(8,128)(2,1)S(1)}, u32[]{:S(2)}, u32[]{:S(2)}) collective-permute-start(bf16[8,10368]{1,0:T(8,128)(2,1)} %get-tuple-element.40), channel_id=1, source_target_pairs={{0,1},{1,0},{2,3},{3,2},{4,5},{5,4},{6,7},{7,6},{8,9},{9,8},{10,11... | collective-permute-start | bytes 497672 | tf_op jit(solution)/shard_map/ppermute | solution.py:454
  6.6 1.6 %collective-permute-start.1 = (bf16[8,10368]{1,0:T(8,128)(2,1)}, bf16[8,10368]{1,0:T(8,128)(2,1)S(1)}, u32[]{:S(2)}, u32[]{:S(2)}) collective-permute-start(bf16[8,10368]{1,0:T(8,128)(2,1)} %get-tuple-element.41), channel_id=1, source_target_pairs={{0,2},{1,3},{2,0},{3,1},{4,6},{5,7},{6,4},{7,5},{8,10},{9,11},{10,... | collective-permute-start | bytes 497672 | tf_op jit(solution)/shard_map/ppermute | solution.py:454
  8.2 3.0 %collective-permute-start.3 = (bf16[8,10368]{1,0:T(8,128)(2,1)}, bf16[8,10368]{1,0:T(8,128)(2,1)S(1)}, u32[]{:S(2)}, u32[]{:S(2)}) collective-permute-start(bf16[8,10368]{1,0:T(8,128)(2,1)} %get-tuple-element.43.refs_4_), channel_id=1, source_target_pairs={{0,4},{1,5},{2,6},{3,7},{4,0},{5,1},{6,2},{7,3},{8,12},{9,13},{10,... | collective-permute-start | bytes 497672 | tf_op jit(solution)/shard_map/ppermute | solution.py:465
  11.2 6.3 %collective-permute-done.1.refs_1_.refs_6_ = bf16[8,10368]{1,0:T(8,128)(2,1)S(1)} collective-permute-done((bf16[8,10368]{1,0:T(8,128)(2,1)}, bf16[8,10368]{1,0:T(8,128)(2,1)S(1)}, u32[]{:S(2)}, u32[]{:S(2)}) %collective-permute-start.1) | collective-permute-done | bytes 165920 | tf_op jit(solution)/shard_map/ppermute | solution.py:454
  17.5 1.9 %collective-permute-done.2.refs_2_.refs_7_ = bf16[8,10368]{1,0:T(8,128)(2,1)S(1)} collective-permute-done((bf16[8,10368]{1,0:T(8,128)(2,1)}, bf16[8,10368]{1,0:T(8,128)(2,1)S(1)}, u32[]{:S(2)}, u32[]{:S(2)}) %collective-permute-start.2) | collective-permute-done | bytes 165920 | tf_op jit(solution)/shard_map/ppermute | solution.py:454
  19.4 1.2 %copy-done.5 = bf16[128,3584]{1,0:T(8,128)(2,1)S(1)} copy-done((bf16[128,3584]{1,0:T(8,128)(2,1)S(1)}, bf16[128,3584]{1,0:T(8,128)(2,1)}, u32[]{:S(2)}) %copy-start.5) | copy-done | bytes 917528
  20.6 0.9 copy-done.7
  21.5 0.7 copy-done.13
  22.2 0.7 copy-done.15
  22.9 1.3 %pack_near.1 = (bf16[8,10368]{1,0:T(8,128)(2,1)S(1)}, bf16[8,10368]{1,0:T(8,128)(2,1)S(1)}, bf16[8,10368]{1,0:T(8,128)(2,1)S(1)}, bf16[8,10368]{1,0:T(8,128)(2,1)S(1)}) custom-call(s32[1,128]{1,0:T(1,128)S(1)} %bitcast.4, f32[1,128]{1,0:T(1,128)S(1)} %bitcast.7, bf16[128,3584]{1,0:T(8,128)(2,1)S(1)} %copy-done.5, bf16[128,1024]{1,0:T(8,128)(2,1)S(1)} %copy-done.7, ...), custom_call_target="tpu_custom_call" | custom-call | flops 150994944 | bytes 2507776 | tf_op jit(solution)/shard_map/pack_near/pallas_call | solution.py:429
  24.2 1.7 %collective-permute-start.4 = (bf16[8,10368]{1,0:T(8,128)(2,1)S(1)}, bf16[8,10368]{1,0:T(8,128)(2,1)S(1)}, u32[]{:S(2)}, u32[]{:S(2)}) collective-permute-start(bf16[8,10368]{1,0:T(8,128)(2,1)S(1)} %get-tuple-element.45), channel_id=1, source_target_pairs={{0,1},{1,0},{2,3},{3,2},{4,5},{5,4},{6,7},{7,6},{8,9},{9,8},{10,11... | collective-permute-start | bytes 497672 | tf_op jit(solution)/shard_map/ppermute | solution.py:454
  25.9 1.7 %collective-permute-start.5 = (bf16[8,10368]{1,0:T(8,128)(2,1)S(1)}, bf16[8,10368]{1,0:T(8,128)(2,1)S(1)}, u32[]{:S(2)}, u32[]{:S(2)}) collective-permute-start(bf16[8,10368]{1,0:T(8,128)(2,1)S(1)} %get-tuple-element.46), channel_id=1, source_target_pairs={{0,2},{1,3},{2,0},{3,1},{4,6},{5,7},{6,4},{7,5},{8,10},{9,11},{10,... | collective-permute-start | bytes 497672 | tf_op jit(solution)/shard_map/ppermute | solution.py:454
  27.6 0.9 collective-permute-start.6
  28.5 1.9 %collective-permute-start.7 = (bf16[8,10368]{1,0:T(8,128)(2,1)S(1)}, bf16[8,10368]{1,0:T(8,128)(2,1)S(1)}, u32[]{:S(2)}, u32[]{:S(2)}) collective-permute-start(bf16[8,10368]{1,0:T(8,128)(2,1)S(1)} %collective-permute-done.refs_0_.refs_5_), channel_id=1, source_target_pairs={{0,4},{1,5},{2,6},{3,7},{4,0},{5,1},{6,2},{7,3},{8,12},{9,13},{10,... | collective-permute-start | bytes 497672 | tf_op jit(solution)/shard_map/ppermute | solution.py:465
  30.4 1.0 collective-permute-start.8
  31.4 7.1 %collective-permute-done.5.refs_2_ = bf16[8,10368]{1,0:T(8,128)(2,1)S(1)} collective-permute-done((bf16[8,10368]{1,0:T(8,128)(2,1)S(1)}, bf16[8,10368]{1,0:T(8,128)(2,1)S(1)}, u32[]{:S(2)}, u32[]{:S(2)}) %collective-permute-start.5) | collective-permute-done | bytes 165920 | tf_op jit(solution)/shard_map/ppermute | solution.py:454
  38.5 2.3 %collective-permute-done.6.refs_3_ = bf16[8,10368]{1,0:T(8,128)(2,1)S(1)} collective-permute-done((bf16[8,10368]{1,0:T(8,128)(2,1)S(1)}, bf16[8,10368]{1,0:T(8,128)(2,1)S(1)}, u32[]{:S(2)}, u32[]{:S(2)}) %collective-permute-start.6) | collective-permute-done | bytes 165920 | tf_op jit(solution)/shard_map/ppermute | solution.py:454
  40.8 0.3 near_columns.1
  41.2 1.6 %collective-permute-start.11 = (bf16[2,72,896]{2,1,0:T(8,128)(2,1)S(1)}, bf16[2,72,896]{2,1,0:T(8,128)(2,1)S(1)}, u32[]{:S(2)}, u32[]{:S(2)}) collective-permute-start(bf16[2,72,896]{2,1,0:T(8,128)(2,1)S(1)} %get-tuple-element.52), channel_id=1, source_target_pairs={{16,0},{24,8},{0,16},{8,24},{17,1},{25,9},{1,17},{9,25},{18,2},{26... | collective-permute-start | bytes 774152 | tf_op jit(solution)/shard_map/ppermute | solution.py:471
  43.1 1.2 %collective-permute-start.9 = (bf16[8,10368]{1,0:T(8,128)(2,1)S(1)}, bf16[8,10368]{1,0:T(8,128)(2,1)S(1)}, u32[]{:S(2)}, u32[]{:S(2)}) collective-permute-start(bf16[8,10368]{1,0:T(8,128)(2,1)S(1)} %collective-permute-done.2.refs_2_.refs_7_), channel_id=1, source_target_pairs={{0,4},{1,5},{2,6},{3,7},{4,0},{5,1},{6,2},{7,3},{8,12},{9,13},{10,... | collective-permute-start | bytes 497672 | tf_op jit(solution)/shard_map/ppermute | solution.py:465
  44.3 3.1 %copy-done = bf16[1,3584,1024]{2,1,0:T(8,128)(2,1)S(1)} copy-done((bf16[1,3584,1024]{2,1,0:T(8,128)(2,1)S(1)}, bf16[1,3584,1024]{2,1,0:T(8,128)(2,1)}, u32[]{:S(2)}) %copy-start) | copy-done | bytes 7340056
  47.4 4.7 %near_rows.1 = (bf16[32,10368]{1,0:T(8,128)(2,1)S(1)}, bf16[32,8064]{1,0:T(8,128)(2,1)S(1)}, bf16[32,2304]{1,0:T(8,128)(2,1)S(1)}, bf16[32,2304]{1,0:T(8,128)(2,1)S(1)}, bf16[72,2048]{1,0:T(8,128)(2,1)S(1)}) custom-call(s32[8]{0:T(128)S(1)} %copy-done.11, bf16[1,3584,1024]{2,1,0:T(8,128)(2,1)S(1)} %copy-done, ...), custom_call_target="tpu_custom_call" | custom-call | flops 2113929216 | bytes 10860576 | tf_op jit(solution)/shard_map/near_rows/pallas_call | solution.py:429
  52.1 1.9 %collective-permute-done.9.refs_3_ = bf16[8,10368]{1,0:T(8,128)(2,1)S(1)} collective-permute-done((bf16[8,10368]{1,0:T(8,128)(2,1)S(1)}, bf16[8,10368]{1,0:T(8,128)(2,1)S(1)}, u32[]{:S(2)}, u32[]{:S(2)}) %collective-permute-start.9) | collective-permute-done | bytes 165920 | tf_op jit(solution)/shard_map/ppermute | solution.py:465
  54.0 0.9 collective-permute-done.12.refs_7_.refs_3_
  54.9 2.5 %payload.1 = (bf16[32,2304]{1,0:T(8,128)(2,1)S(1)}, bf16[32,8064]{1,0:T(8,128)(2,1)S(1)}, bf16[72,3968]{1,0:T(8,128)(2,1)S(1)}, bf16[72,3968]{1,0:T(8,128)(2,1)S...) custom-call(s32[8]{0:T(128)S(1)} %copy-done.11, bf16[1,3584,1024]{2,1,0:T(8,128)(2,1)S(1)} %copy-done.1, ...), custom_call_target="tpu_custom_call" | custom-call | flops 1056964608 | bytes 12427296 | tf_op jit(solution)/shard_map/payload/pallas_call | solution.py:429
  57.4 0.3 collective-permute-start.18
  57.7 1.2 %collective-permute-start.13 = (bf16[32,2304]{1,0:T(8,128)(2,1)S(1)}, bf16[32,2304]{1,0:T(8,128)(2,1)S(1)}, u32[]{:S(2)}, u32[]{:S(2)}) collective-permute-start(bf16[32,2304]{1,0:T(8,128)(2,1)S(1)} %get-tuple-element.54), channel_id=1, source_target_pairs={{0,4},{1,5},{2,6},{3,7},{4,0},{5,1},{6,2},{7,3},{8,12},{9,13},{10,... | collective-permute-start | bytes 442376 | tf_op jit(solution)/shard_map/ppermute | solution.py:465
  59.0 1.5 %collective-permute-start.19 = (bf16[72,3968]{1,0:T(8,128)(2,1)S(1)}, bf16[72,3968]{1,0:T(8,128)(2,1)S(1)}, u32[]{:S(2)}, u32[]{:S(2)}) collective-permute-start(bf16[72,3968]{1,0:T(8,128)(2,1)S(1)} %get-tuple-element.65), channel_id=1, source_target_pairs={{16,0},{24,8},{0,16},{8,24},{17,1},{25,9},{1,17},{9,25},{18,2},{26... | collective-permute-start | bytes 1714184 | tf_op jit(solution)/shard_map/ppermute | solution.py:471
  60.5 1.7 %collective-permute-start.17 = (bf16[32,8064]{1,0:T(8,128)(2,1)S(1)}, bf16[32,8064]{1,0:T(8,128)(2,1)S(1)}, u32[]{:S(2)}, u32[]{:S(2)}) collective-permute-start(bf16[32,8064]{1,0:T(8,128)(2,1)S(1)} %get-tuple-element.61), channel_id=1, source_target_pairs={{0,4},{1,5},{2,6},{3,7},{4,0},{5,1},{6,2},{7,3},{8,12},{9,13},{10,... | collective-permute-start | bytes 1548296 | tf_op jit(solution)/shard_map/ppermute | solution.py:465
  62.2 17.4 %collective-permute-done.13.small = bf16[32,2304]{1,0:T(8,128)(2,1)S(1)} collective-permute-done((bf16[32,2304]{1,0:T(8,128)(2,1)S(1)}, bf16[32,2304]{1,0:T(8,128)(2,1)S(1)}, u32[]{:S(2)}, u32[]{:S(2)}) %collective-permute-start.13) | collective-permute-done | bytes 147488 | tf_op jit(solution)/shard_map/ppermute | solution.py:465
  79.5 1.4 %after_small.1 = (bf16[8,12672]{1,0:T(8,128)(2,1)S(1)}, bf16[8,12672]{1,0:T(8,128)(2,1)S(1)}, bf16[8,12672]{1,0:T(8,128)(2,1)}, bf16[8,12672]{1,0:T(8,128)(2,1)}, bf16[72,1024]{1,0:T(8,128)(2,1)S(1)}) custom-call(s32[8]{0:T(128)S(1)} %copy-done.11, bf16[32,2304]{1,0:T(8,128)(2,1)S(1)} %collective-permute-done.13.small, ...), custom_call_target="tpu_custom_call" | custom-call | tf_op jit(solution)/shard_map/after_small/pallas_call | solution.py:429
  80.9 1.4 %collective-permute-done.21.refs_1_.refs_3_ = bf16[72,1024]{1,0:T(8,128)(2,1)S(1)} collective-permute-done((bf16[72,1024]{1,0:T(8,128)(2,1)S(1)}, bf16[72,1024]{1,0:T(8,128)(2,1)S(1)}, u32[]{:S(2)}, u32[]{:S(2)}) %collective-permute-start.21) | collective-permute-done | bytes 147488 | tf_op jit(solution)/shard_map/ppermute | solution.py:471
  82.3 1.5 %collective-permute-start.22 = (bf16[72,1024]{1,0:T(8,128)(2,1)S(1)}, bf16[72,1024]{1,0:T(8,128)(2,1)S(1)}, u32[]{:S(2)}, u32[]{:S(2)}) collective-permute-start(bf16[72,1024]{1,0:T(8,128)(2,1)S(1)} %get-tuple-element.67.refs_2_), channel_id=1, source_target_pairs={{16,0},{24,8},{0,16},{8,24},{17,1},{25,9},{1,17},{9,25},{18,2},{26... | collective-permute-start | bytes 442376 | tf_op jit(solution)/shard_map/ppermute | solution.py:471
  83.8 5.4 %collective-permute-done.22.refs_2_.refs_4_ = bf16[72,1024]{1,0:T(8,128)(2,1)S(1)} collective-permute-done((bf16[72,1024]{1,0:T(8,128)(2,1)S(1)}, bf16[72,1024]{1,0:T(8,128)(2,1)S(1)}, u32[]{:S(2)}, u32[]{:S(2)}) %collective-permute-start.22) | collective-permute-done | bytes 147488 | tf_op jit(solution)/shard_map/ppermute | solution.py:471
  89.2 3.8 %collective-permute-start.14 = (bf16[8,12672]{1,0:T(8,128)(2,1)S(1)}, bf16[8,12672]{1,0:T(8,128)(2,1)S(1)}, u32[]{:S(2)}, u32[]{:S(2)}) collective-permute-start(bf16[8,12672]{1,0:T(8,128)(2,1)S(1)} %get-tuple-element.58), channel_id=1, source_target_pairs={{1,0},{0,1},{3,2},{2,3},{5,4},{4,5},{7,6},{6,7},{9,8},{8,9},{11,10... | collective-permute-start | bytes 608264 | tf_op jit(solution)/shard_map/ppermute | solution.py:461
  93.0 1.5 %collective-permute-start.15 = (bf16[8,12672]{1,0:T(8,128)(2,1)}, bf16[8,12672]{1,0:T(8,128)(2,1)S(1)}, u32[]{:S(2)}, u32[]{:S(2)}) collective-permute-start(bf16[8,12672]{1,0:T(8,128)(2,1)} %get-tuple-element.59), channel_id=1, source_target_pairs={{2,0},{3,1},{0,2},{1,3},{6,4},{7,5},{4,6},{5,7},{10,8},{11,9},{8,1... | collective-permute-start | bytes 608264 | tf_op jit(solution)/shard_map/ppermute | solution.py:461
  94.5 2.2 %own_terms.1.refs_0_.refs_6_ = f32[896,1024]{1,0:T(8,128)S(1)} custom-call(bf16[2,72,896]{2,1,0:T(8,128)(2,1)S(1)} %get-tuple-element.48.refs_8_.refs_4_.refs_0_, bf16[2,72,896]{2,1,0:T(8,128)(2,1)S(1)} %collective-permute-done.10.refs_5_.refs_1_, bf16[2,72,896]{2,1,0:T(8,128)(2,1)S(1)} %collective-permute-done.11.refs_6_.refs_2_, ...), custom_call_target="tpu_custom_call" | custom-call | tf_op jit(solution)/shard_map/own_terms/pallas_call | solution.py:429
  96.8 1.3 %after_large.1 = (bf16[8,8064]{1,0:T(8,128)(2,1)S(1)}, bf16[8,8064]{1,0:T(8,128)(2,1)}, bf16[8,8064]{1,0:T(8,128)(2,1)}, bf16[8,8064]{1,0:T(8,128)(2,1)}) custom-call(s32[8]{0:T(128)S(1)} %copy-done.11, bf16[32,8064]{1,0:T(8,128)(2,1)S(1)} %collective-permute-done.17.large.refs_1_, bf16[32,8064]{1,0:T(8,128)(2,1)S(1)} %get-tuple-element.62.local_back, ...), custom_call_target="tpu_custom_call" | custom-call | flops 1000000 | bytes 5660704 | tf_op jit(solution)/shard_map/after_large/pallas_call | solution.py:429
  98.2 0.7 copy-done.3
  98.8 0.7 copy-done.9
  99.5 2.0 %collective-permute-start.24 = (bf16[8,8064]{1,0:T(8,128)(2,1)}, bf16[8,8064]{1,0:T(8,128)(2,1)}, u32[]{:S(2)}, u32[]{:S(2)}) collective-permute-start(bf16[8,8064]{1,0:T(8,128)(2,1)} %get-tuple-element.69), channel_id=1, source_target_pairs={{1,0},{0,1},{3,2},{2,3},{5,4},{4,5},{7,6},{6,7},{9,8},{8,9},{11,10... | collective-permute-start | bytes 387080 | tf_op jit(solution)/shard_map/ppermute | solution.py:461
  101.5 1.5 %collective-permute-start.25 = (bf16[8,8064]{1,0:T(8,128)(2,1)}, bf16[8,8064]{1,0:T(8,128)(2,1)}, u32[]{:S(2)}, u32[]{:S(2)}) collective-permute-start(bf16[8,8064]{1,0:T(8,128)(2,1)} %get-tuple-element.70), channel_id=1, source_target_pairs={{2,0},{3,1},{0,2},{1,3},{6,4},{7,5},{4,6},{5,7},{10,8},{11,9},{8,1... | collective-permute-start | bytes 387080 | tf_op jit(solution)/shard_map/ppermute | solution.py:461
  103.0 3.1 %copy-done.2 = bf16[1,3584,1024]{2,1,0:T(8,128)(2,1)S(1)} copy-done((bf16[1,3584,1024]{2,1,0:T(8,128)(2,1)S(1)}, bf16[1,3584,1024]{2,1,0:T(8,128)(2,1)}, u32[]{:S(2)}) %copy-start.2) | copy-done | bytes 7340056
  106.1 2.0 %copy-done.4 = f32[896,1024]{1,0:T(8,128)S(1)} copy-done((f32[896,1024]{1,0:T(8,128)S(1)}, f32[896,1024]{1,0:T(8,128)}, u32[]{:S(2)}) %copy-start.4) | copy-done | bytes 3670040
  108.1 0.7 copy-done.12
  108.8 5.4 %update.1 = (bf16[1,896,1024]{2,1,0:T(8,128)(2,1)}, bf16[1,896,1024]{2,1,0:T(8,128)(2,1)}) custom-call(s32[1]{0:T(128)} %bitcast.2.g_ref, s32[8]{0:T(128)S(1)} %copy-done.12, bf16[32,8064]{1,0:T(8,128)(2,1)S(1)} %collective-permute-done.17.large.refs_1_, bf16[72,1024]{1,0:T(8,128)(2,1)S(1)} %get-tuple-element.67.refs_2_, ...), custom_call_target="tpu_custom_call" | custom-call | flops 528482304 | bytes 11010048 | tf_op jit(solution)/shard_map/update/pallas_call | solution.py:595
  114.3 3.2 %unpack.1 = (bf16[128,1024]{1,0:T(8,128)(2,1)}, bf16[128,3584]{1,0:T(8,128)(2,1)}) custom-call(s32[1,128]{1,0:T(1,128)S(1)} %bitcast.5, f32[1,128]{1,0:T(1,128)S(1)} %bitcast.8, bf16[8,12672]{1,0:T(8,128)(2,1)S(1)} %get-tuple-element.57.refs_0_, bf16[8,12672]{1,0:T(8,128)(2,1)S(1)} %collective-permute-done.14.refs_1_, ...), custom_call_target="tpu_custom_call" | custom-call | flops 150994944 | bytes 2507776 | tf_op jit(solution)/shard_map/unpack/pallas_call | solution.py:429
  (50 shorter events, 0.5 us)
Async XLA Ops:
  3.6 40.8 %copy-start.11 = (s32[8]{0:T(128)S(1)}, s32[8]{0:T(128)}, u32[]{:S(2)}) copy-start(s32[8]{0:T(128)} %refs_0_.1) | copy-start | bytes 100
  3.6 7.6 %collective-permute-start = (bf16[8,10368]{1,0:T(8,128)(2,1)}, bf16[8,10368]{1,0:T(8,128)(2,1)S(1)}, u32[]{:S(2)}, u32[]{:S(2)}) collective-permute-start(bf16[8,10368]{1,0:T(8,128)(2,1)} %get-tuple-element.40), channel_id=1, source_target_pairs={{0,1},{1,0},{2,3},{3,2},{4,5},{5,4},{6,7},{7,6},{8,9},{9,8},{10,11... | collective-permute-start | bytes 497672 | tf_op jit(solution)/shard_map/ppermute | solution.py:454
  6.6 10.9 %collective-permute-start.1 = (bf16[8,10368]{1,0:T(8,128)(2,1)}, bf16[8,10368]{1,0:T(8,128)(2,1)S(1)}, u32[]{:S(2)}, u32[]{:S(2)}) collective-permute-start(bf16[8,10368]{1,0:T(8,128)(2,1)} %get-tuple-element.41), channel_id=1, source_target_pairs={{0,2},{1,3},{2,0},{3,1},{4,6},{5,7},{6,4},{7,5},{8,10},{9,11},{10,... | collective-permute-start | bytes 497672 | tf_op jit(solution)/shard_map/ppermute | solution.py:454
  8.2 11.3 %collective-permute-start.2 = (bf16[8,10368]{1,0:T(8,128)(2,1)}, bf16[8,10368]{1,0:T(8,128)(2,1)S(1)}, u32[]{:S(2)}, u32[]{:S(2)}) collective-permute-start(bf16[8,10368]{1,0:T(8,128)(2,1)} %get-tuple-element.42), channel_id=1, source_target_pairs={{0,3},{1,2},{2,1},{3,0},{4,7},{5,6},{6,5},{7,4},{8,11},{9,10},{10,... | collective-permute-start | bytes 497672 | tf_op jit(solution)/shard_map/ppermute | solution.py:454
  8.2 11.3 %collective-permute-start.3 = (bf16[8,10368]{1,0:T(8,128)(2,1)}, bf16[8,10368]{1,0:T(8,128)(2,1)S(1)}, u32[]{:S(2)}, u32[]{:S(2)}) collective-permute-start(bf16[8,10368]{1,0:T(8,128)(2,1)} %get-tuple-element.43.refs_4_), channel_id=1, source_target_pairs={{0,4},{1,5},{2,6},{3,7},{4,0},{5,1},{6,2},{7,3},{8,12},{9,13},{10,... | collective-permute-start | bytes 497672 | tf_op jit(solution)/shard_map/ppermute | solution.py:465
  19.4 1.2 %copy-start.5 = (bf16[128,3584]{1,0:T(8,128)(2,1)S(1)}, bf16[128,3584]{1,0:T(8,128)(2,1)}, u32[]{:S(2)}) copy-start(bf16[128,3584]{1,0:T(8,128)(2,1)} %tok_hbm.3) | copy-start | bytes 2752516
  20.6 0.9 copy-start.7
  21.5 0.7 copy-start.13
  22.2 0.7 copy-start.15
  22.9 18.0 %copy-start.8 = (bf16[8,10368]{1,0:T(8,128)(2,1)S(1)}, bf16[8,10368]{1,0:T(8,128)(2,1)}, u32[]{:S(2)}) copy-start(bf16[8,10368]{1,0:T(8,128)(2,1)} %get-tuple-element.43.refs_4_) | copy-start | bytes 497668
  24.2 7.2 %collective-permute-start.4 = (bf16[8,10368]{1,0:T(8,128)(2,1)S(1)}, bf16[8,10368]{1,0:T(8,128)(2,1)S(1)}, u32[]{:S(2)}, u32[]{:S(2)}) collective-permute-start(bf16[8,10368]{1,0:T(8,128)(2,1)S(1)} %get-tuple-element.45), channel_id=1, source_target_pairs={{0,1},{1,0},{2,3},{3,2},{4,5},{5,4},{6,7},{7,6},{8,9},{9,8},{10,11... | collective-permute-start | bytes 497672 | tf_op jit(solution)/shard_map/ppermute | solution.py:454
  25.9 12.6 %collective-permute-start.5 = (bf16[8,10368]{1,0:T(8,128)(2,1)S(1)}, bf16[8,10368]{1,0:T(8,128)(2,1)S(1)}, u32[]{:S(2)}, u32[]{:S(2)}) collective-permute-start(bf16[8,10368]{1,0:T(8,128)(2,1)S(1)} %get-tuple-element.46), channel_id=1, source_target_pairs={{0,2},{1,3},{2,0},{3,1},{4,6},{5,7},{6,4},{7,5},{8,10},{9,11},{10,... | collective-permute-start | bytes 497672 | tf_op jit(solution)/shard_map/ppermute | solution.py:454
  27.6 13.3 %collective-permute-start.6 = (bf16[8,10368]{1,0:T(8,128)(2,1)S(1)}, bf16[8,10368]{1,0:T(8,128)(2,1)S(1)}, u32[]{:S(2)}, u32[]{:S(2)}) collective-permute-start(bf16[8,10368]{1,0:T(8,128)(2,1)S(1)} %get-tuple-element.47), channel_id=1, source_target_pairs={{0,3},{1,2},{2,1},{3,0},{4,7},{5,6},{6,5},{7,4},{8,11},{9,10},{10,... | collective-permute-start | bytes 497672 | tf_op jit(solution)/shard_map/ppermute | solution.py:454
  28.5 12.3 %collective-permute-start.7 = (bf16[8,10368]{1,0:T(8,128)(2,1)S(1)}, bf16[8,10368]{1,0:T(8,128)(2,1)S(1)}, u32[]{:S(2)}, u32[]{:S(2)}) collective-permute-start(bf16[8,10368]{1,0:T(8,128)(2,1)S(1)} %collective-permute-done.refs_0_.refs_5_), channel_id=1, source_target_pairs={{0,4},{1,5},{2,6},{3,7},{4,0},{5,1},{6,2},{7,3},{8,12},{9,13},{10,... | collective-permute-start | bytes 497672 | tf_op jit(solution)/shard_map/ppermute | solution.py:465
  30.4 13.9 %collective-permute-start.8 = (bf16[8,10368]{1,0:T(8,128)(2,1)S(1)}, bf16[8,10368]{1,0:T(8,128)(2,1)S(1)}, u32[]{:S(2)}, u32[]{:S(2)}) collective-permute-start(bf16[8,10368]{1,0:T(8,128)(2,1)S(1)} %collective-permute-done.1.refs_1_.refs_6_), channel_id=1, source_target_pairs={{0,4},{1,5},{2,6},{3,7},{4,0},{5,1},{6,2},{7,3},{8,12},{9,13},{10,... | collective-permute-start | bytes 497672 | tf_op jit(solution)/shard_map/ppermute | solution.py:465
  41.1 12.9 %collective-permute-start.10 = (bf16[2,72,896]{2,1,0:T(8,128)(2,1)S(1)}, bf16[2,72,896]{2,1,0:T(8,128)(2,1)S(1)}, u32[]{:S(2)}, u32[]{:S(2)}) collective-permute-start(bf16[2,72,896]{2,1,0:T(8,128)(2,1)S(1)} %get-tuple-element.51), channel_id=1, source_target_pairs={{8,0},{0,8},{24,16},{16,24},{9,1},{1,9},{25,17},{17,25},{10,2},{2,... | collective-permute-start | bytes 774152 | tf_op jit(solution)/shard_map/ppermute | solution.py:471
  41.2 12.8 %collective-permute-start.11 = (bf16[2,72,896]{2,1,0:T(8,128)(2,1)S(1)}, bf16[2,72,896]{2,1,0:T(8,128)(2,1)S(1)}, u32[]{:S(2)}, u32[]{:S(2)}) collective-permute-start(bf16[2,72,896]{2,1,0:T(8,128)(2,1)S(1)} %get-tuple-element.52), channel_id=1, source_target_pairs={{16,0},{24,8},{0,16},{8,24},{17,1},{25,9},{1,17},{9,25},{18,2},{26... | collective-permute-start | bytes 774152 | tf_op jit(solution)/shard_map/ppermute | solution.py:471
  42.8 12.1 %collective-permute-start.12 = (bf16[2,72,896]{2,1,0:T(8,128)(2,1)S(1)}, bf16[2,72,896]{2,1,0:T(8,128)(2,1)S(1)}, u32[]{:S(2)}, u32[]{:S(2)}) collective-permute-start(bf16[2,72,896]{2,1,0:T(8,128)(2,1)S(1)} %get-tuple-element.53), channel_id=1, source_target_pairs={{24,0},{16,8},{8,16},{0,24},{25,1},{17,9},{9,17},{1,25},{26,2},{18... | collective-permute-start | bytes 774152 | tf_op jit(solution)/shard_map/ppermute | solution.py:471
  43.1 10.9 %collective-permute-start.9 = (bf16[8,10368]{1,0:T(8,128)(2,1)S(1)}, bf16[8,10368]{1,0:T(8,128)(2,1)S(1)}, u32[]{:S(2)}, u32[]{:S(2)}) collective-permute-start(bf16[8,10368]{1,0:T(8,128)(2,1)S(1)} %collective-permute-done.2.refs_2_.refs_7_), channel_id=1, source_target_pairs={{0,4},{1,5},{2,6},{3,7},{4,0},{5,1},{6,2},{7,3},{8,12},{9,13},{10,... | collective-permute-start | bytes 497672 | tf_op jit(solution)/shard_map/ppermute | solution.py:465
  44.3 3.1 %copy-start = (bf16[1,3584,1024]{2,1,0:T(8,128)(2,1)S(1)}, bf16[1,3584,1024]{2,1,0:T(8,128)(2,1)}, u32[]{:S(2)}) copy-start(bf16[1,3584,1024]{2,1,0:T(8,128)(2,1)} %refs_7_.1) | copy-start | bytes 22020100
  47.4 7.5 %copy-start.1 = (bf16[1,3584,1024]{2,1,0:T(8,128)(2,1)S(1)}, bf16[1,3584,1024]{2,1,0:T(8,128)(2,1)}, u32[]{:S(2)}) copy-start(bf16[1,3584,1024]{2,1,0:T(8,128)(2,1)} %refs_7_.1) | copy-start | bytes 22020100
  57.4 35.6 %collective-permute-start.18 = (bf16[72,3968]{1,0:T(8,128)(2,1)S(1)}, bf16[72,3968]{1,0:T(8,128)(2,1)S(1)}, u32[]{:S(2)}, u32[]{:S(2)}) collective-permute-start(bf16[72,3968]{1,0:T(8,128)(2,1)S(1)} %get-tuple-element.64), channel_id=1, source_target_pairs={{8,0},{0,8},{24,16},{16,24},{9,1},{1,9},{25,17},{17,25},{10,2},{2,... | collective-permute-start | bytes 1714184 | tf_op jit(solution)/shard_map/ppermute | solution.py:471
  57.7 21.8 %collective-permute-start.13 = (bf16[32,2304]{1,0:T(8,128)(2,1)S(1)}, bf16[32,2304]{1,0:T(8,128)(2,1)S(1)}, u32[]{:S(2)}, u32[]{:S(2)}) collective-permute-start(bf16[32,2304]{1,0:T(8,128)(2,1)S(1)} %get-tuple-element.54), channel_id=1, source_target_pairs={{0,4},{1,5},{2,6},{3,7},{4,0},{5,1},{6,2},{7,3},{8,12},{9,13},{10,... | collective-permute-start | bytes 442376 | tf_op jit(solution)/shard_map/ppermute | solution.py:465
  59.0 34.0 %collective-permute-start.19 = (bf16[72,3968]{1,0:T(8,128)(2,1)S(1)}, bf16[72,3968]{1,0:T(8,128)(2,1)S(1)}, u32[]{:S(2)}, u32[]{:S(2)}) collective-permute-start(bf16[72,3968]{1,0:T(8,128)(2,1)S(1)} %get-tuple-element.65), channel_id=1, source_target_pairs={{16,0},{24,8},{0,16},{8,24},{17,1},{25,9},{1,17},{9,25},{18,2},{26... | collective-permute-start | bytes 1714184 | tf_op jit(solution)/shard_map/ppermute | solution.py:471
  60.5 34.0 %collective-permute-start.20 = (bf16[72,3968]{1,0:T(8,128)(2,1)S(1)}, bf16[72,3968]{1,0:T(8,128)(2,1)S(1)}, u32[]{:S(2)}, u32[]{:S(2)}) collective-permute-start(bf16[72,3968]{1,0:T(8,128)(2,1)S(1)} %get-tuple-element.66), channel_id=1, source_target_pairs={{24,0},{16,8},{8,16},{0,24},{25,1},{17,9},{9,17},{1,25},{26,2},{18... | collective-permute-start | bytes 1714184 | tf_op jit(solution)/shard_map/ppermute | solution.py:471
  60.5 36.3 %collective-permute-start.17 = (bf16[32,8064]{1,0:T(8,128)(2,1)S(1)}, bf16[32,8064]{1,0:T(8,128)(2,1)S(1)}, u32[]{:S(2)}, u32[]{:S(2)}) collective-permute-start(bf16[32,8064]{1,0:T(8,128)(2,1)S(1)} %get-tuple-element.61), channel_id=1, source_target_pairs={{0,4},{1,5},{2,6},{3,7},{4,0},{5,1},{6,2},{7,3},{8,12},{9,13},{10,... | collective-permute-start | bytes 1548296 | tf_op jit(solution)/shard_map/ppermute | solution.py:465
  80.9 1.4 %collective-permute-start.21 = (bf16[72,1024]{1,0:T(8,128)(2,1)S(1)}, bf16[72,1024]{1,0:T(8,128)(2,1)S(1)}, u32[]{:S(2)}, u32[]{:S(2)}) collective-permute-start(bf16[72,1024]{1,0:T(8,128)(2,1)S(1)} %get-tuple-element.67.refs_2_), channel_id=1, source_target_pairs={{8,0},{0,8},{24,16},{16,24},{9,1},{1,9},{25,17},{17,25},{10,2},{2,... | collective-permute-start | bytes 442376 | tf_op jit(solution)/shard_map/ppermute | solution.py:471
  82.3 6.9 %collective-permute-start.22 = (bf16[72,1024]{1,0:T(8,128)(2,1)S(1)}, bf16[72,1024]{1,0:T(8,128)(2,1)S(1)}, u32[]{:S(2)}, u32[]{:S(2)}) collective-permute-start(bf16[72,1024]{1,0:T(8,128)(2,1)S(1)} %get-tuple-element.67.refs_2_), channel_id=1, source_target_pairs={{16,0},{24,8},{0,16},{8,24},{17,1},{25,9},{1,17},{9,25},{18,2},{26... | collective-permute-start | bytes 442376 | tf_op jit(solution)/shard_map/ppermute | solution.py:471
  89.2 13.8 %collective-permute-start.14 = (bf16[8,12672]{1,0:T(8,128)(2,1)S(1)}, bf16[8,12672]{1,0:T(8,128)(2,1)S(1)}, u32[]{:S(2)}, u32[]{:S(2)}) collective-permute-start(bf16[8,12672]{1,0:T(8,128)(2,1)S(1)} %get-tuple-element.58), channel_id=1, source_target_pairs={{1,0},{0,1},{3,2},{2,3},{5,4},{4,5},{7,6},{6,7},{9,8},{8,9},{11,10... | collective-permute-start | bytes 608264 | tf_op jit(solution)/shard_map/ppermute | solution.py:461
  93.0 3.8 %collective-permute-start.23 = (bf16[72,1024]{1,0:T(8,128)(2,1)S(1)}, bf16[72,1024]{1,0:T(8,128)(2,1)S(1)}, u32[]{:S(2)}, u32[]{:S(2)}) collective-permute-start(bf16[72,1024]{1,0:T(8,128)(2,1)S(1)} %collective-permute-done.22.refs_2_.refs_4_), channel_id=1, source_target_pairs={{8,0},{0,8},{24,16},{16,24},{9,1},{1,9},{25,17},{17,25},{10,2},{2,... | collective-permute-start | bytes 442376 | tf_op jit(solution)/shard_map/ppermute | solution.py:471
  93.0 21.2 %collective-permute-start.15 = (bf16[8,12672]{1,0:T(8,128)(2,1)}, bf16[8,12672]{1,0:T(8,128)(2,1)S(1)}, u32[]{:S(2)}, u32[]{:S(2)}) collective-permute-start(bf16[8,12672]{1,0:T(8,128)(2,1)} %get-tuple-element.59), channel_id=1, source_target_pairs={{2,0},{3,1},{0,2},{1,3},{6,4},{7,5},{4,6},{5,7},{10,8},{11,9},{8,1... | collective-permute-start | bytes 608264 | tf_op jit(solution)/shard_map/ppermute | solution.py:461
  94.5 19.7 %collective-permute-start.16 = (bf16[8,12672]{1,0:T(8,128)(2,1)}, bf16[8,12672]{1,0:T(8,128)(2,1)}, u32[]{:S(2)}, u32[]{:S(2)}) collective-permute-start(bf16[8,12672]{1,0:T(8,128)(2,1)} %get-tuple-element.60), channel_id=1, source_target_pairs={{3,0},{2,1},{1,2},{0,3},{7,4},{6,5},{5,6},{4,7},{11,8},{10,9},{9,1... | collective-permute-start | bytes 608264 | tf_op jit(solution)/shard_map/ppermute | solution.py:461
  96.8 2.0 %copy-start.3 = (f32[896,1024]{1,0:T(8,128)}, f32[896,1024]{1,0:T(8,128)S(1)}, u32[]{:S(2)}) copy-start(f32[896,1024]{1,0:T(8,128)S(1)} %own_terms.1.refs_0_.refs_6_) | copy-start | bytes 11010052
  96.8 6.2 %copy-start.6 = (bf16[1,896,1024]{2,1,0:T(8,128)(2,1)S(1)}, bf16[1,896,1024]{2,1,0:T(8,128)(2,1)}, u32[]{:S(2)}) copy-start(bf16[1,896,1024]{2,1,0:T(8,128)(2,1)} %refs_8_.1) | copy-start | bytes 5505028
  98.8 0.7 copy-start.9
  99.5 14.7 %collective-permute-start.24 = (bf16[8,8064]{1,0:T(8,128)(2,1)}, bf16[8,8064]{1,0:T(8,128)(2,1)}, u32[]{:S(2)}, u32[]{:S(2)}) collective-permute-start(bf16[8,8064]{1,0:T(8,128)(2,1)} %get-tuple-element.69), channel_id=1, source_target_pairs={{1,0},{0,1},{3,2},{2,3},{5,4},{4,5},{7,6},{6,7},{9,8},{8,9},{11,10... | collective-permute-start | bytes 387080 | tf_op jit(solution)/shard_map/ppermute | solution.py:461
  101.5 12.7 %collective-permute-start.25 = (bf16[8,8064]{1,0:T(8,128)(2,1)}, bf16[8,8064]{1,0:T(8,128)(2,1)}, u32[]{:S(2)}, u32[]{:S(2)}) collective-permute-start(bf16[8,8064]{1,0:T(8,128)(2,1)} %get-tuple-element.70), channel_id=1, source_target_pairs={{2,0},{3,1},{0,2},{1,3},{6,4},{7,5},{4,6},{5,7},{10,8},{11,9},{8,1... | collective-permute-start | bytes 387080 | tf_op jit(solution)/shard_map/ppermute | solution.py:461
  103.0 11.3 %collective-permute-start.26 = (bf16[8,8064]{1,0:T(8,128)(2,1)}, bf16[8,8064]{1,0:T(8,128)(2,1)}, u32[]{:S(2)}, u32[]{:S(2)}) collective-permute-start(bf16[8,8064]{1,0:T(8,128)(2,1)} %get-tuple-element.71), channel_id=1, source_target_pairs={{3,0},{2,1},{1,2},{0,3},{7,4},{6,5},{5,6},{4,7},{11,8},{10,9},{9,1... | collective-permute-start | bytes 387080 | tf_op jit(solution)/shard_map/ppermute | solution.py:461
  103.0 3.1 %copy-start.2 = (bf16[1,3584,1024]{2,1,0:T(8,128)(2,1)S(1)}, bf16[1,3584,1024]{2,1,0:T(8,128)(2,1)}, u32[]{:S(2)}) copy-start(bf16[1,3584,1024]{2,1,0:T(8,128)(2,1)} %refs_7_.1) | copy-start | bytes 22020100
  106.1 2.0 %copy-start.4 = (f32[896,1024]{1,0:T(8,128)S(1)}, f32[896,1024]{1,0:T(8,128)}, u32[]{:S(2)}) copy-start(f32[896,1024]{1,0:T(8,128)} %copy-done.3) | copy-start | bytes 11010052
  108.1 0.7 copy-start.12
  108.8 5.5 %copy-start.10 = (bf16[8,8064]{1,0:T(8,128)(2,1)S(1)}, bf16[8,8064]{1,0:T(8,128)(2,1)}, u32[]{:S(2)}) copy-start(bf16[8,8064]{1,0:T(8,128)(2,1)} %copy-done.9) | copy-start | bytes 387076
  108.8 5.5 %copy-start.14 = (s32[128]{0:T(128)S(1)}, s32[128]{0:T(128)}, u32[]{:S(2)}) copy-start(s32[128]{0:T(128)} %param.10) | copy-start | bytes 1540
  108.8 5.5 %copy-start.16 = (f32[128]{0:T(128)S(1)}, f32[128]{0:T(128)}, u32[]{:S(2)}) copy-start(f32[128]{0:T(128)} %param.8) | copy-start | bytes 1540

commit v3 on v2

--- a/solution.py
+++ b/solution.py
@@ -175,10 +175,10 @@
     return jnp.sum(eye * row.astype(F32), axis=1, keepdims=True)
 
 
-def pack_kernel(far, plan, slot_hbm, gate_hbm, tok_hbm, cot_hbm, *refs):
+def pack_kernel(plan, slot_hbm, gate_hbm, tok_hbm, cot_hbm, *refs):
     half = plan.half
-    outs, refs = refs[-half - 5 : -5], refs[-5:]
-    slot_ref, gate_ref, tok_ref, cot_ref, sems = refs
+    near, far = refs[:half], refs[half : 2 * half]
+    slot_ref, gate_ref, tok_ref, cot_ref, sems = refs[2 * half :]
     copies = [
         pltpu.make_async_copy(source, held, sems.at[i])
         for i, (source, held) in enumerate(
@@ -189,16 +189,16 @@
         copy.start()
     copies[0].wait()
     block, rank = token_places(plan, slot_ref[...])
-    wanted = lax.rem(block, 2) == far
-    block = jnp.where(wanted, block // 2, -2)
     targets = row_targets(plan, block, rank)
-    height = half * SUB
+    height = 2 * half * SUB
     onehots = [(iota((height, plan.tokens), 0) == t).astype(BF16) for t in targets]
 
     def store(values, start):
         stop = start + values.shape[1]
         for m in range(half):
-            outs[m][:, start:stop] = values[m * SUB : (m + 1) * SUB].astype(BF16)
+            low = 2 * m * SUB
+            near[m][:, start:stop] = values[low : low + 2 * SUB].astype(BF16)
+            far[m][:, start:stop] = values[low + SUB : low + 2 * SUB].astype(BF16)
 
     def place(data, base):
         width = data.shape[1]
@@ -220,16 +220,26 @@
     place(scaled, plan.DX)
 
 
-def blocks_of(refs, start, stop):
-    return [r[:, start:stop].astype(F32) for r in refs]
+def pass_kernel(plan, *refs):
+    count = plan.half - 2
+    for source, target in zip(refs[:count], refs[-count:]):
+        target[...] = source[...]
+
+
+def hold_kernel(plan, weight_hbm, held, sem):
+    copy = pltpu.make_async_copy(weight_hbm.at[0], held, sem)
+    copy.start()
+    copy.wait()
+
+
+def blocks_of(refs, start, stop, low=0):
+    return [r[:, start:stop].astype(F32)[low : low + SUB] for r in refs]
 
 
 def columns_kernel(plan, *refs):
-    half = plan.half
-    near, far = refs[:half], refs[half : 2 * half]
-    outs, held = refs[-plan.groups - 1 : -1], refs[-1]
-    for i, blocks in enumerate((near, far)):
-        held[i] = unfold(plan, blocks_of(blocks, 0, plan.DX), plan.D)
+    near, outs, held = refs[: plan.half], refs[-plan.groups - 1 : -1], refs[-1]
+    for i in range(2):
+        held[i] = unfold(plan, blocks_of(near, 0, plan.DX, i * SUB), plan.D)
     for m in range(plan.groups):
         start = pl.multiple_of(plan.group_at(lax.axis_index("dp"), m) * plan.share, LANES)
         for i in range(2):
@@ -252,18 +262,16 @@
 
 
 def near_kernel(plan, placement_ref, weight_ref, *refs):
-    half = plan.half
-    near, refs = refs[:half], refs[half:]
-    far, refs = refs[:half], refs[half:]
+    near = refs[: plan.half]
     back_near, local_back, local_act, folded_grad, grads = refs[-5:]
     x_near = unfold(plan, blocks_of(near, 0, plan.DX), plan.D)
-    x_far = unfold(plan, blocks_of(far, 0, plan.DX), plan.D)
+    x_far = unfold(plan, blocks_of(near, 0, plan.DX, SUB), plan.D)
     g_near = unfold(plan, blocks_of(near, plan.DX, plan.C), plan.F)
-    g_far = unfold(plan, blocks_of(far, plan.DX, plan.C), plan.F)
+    g_far = unfold(plan, blocks_of(near, plan.DX, plan.C, SUB), plan.F)
     x = jnp.concatenate([x_near.astype(F32), x_far.astype(F32)], axis=0).astype(BF16)
     g = jnp.concatenate([g_near.astype(F32), g_far.astype(F32)], axis=0).astype(BF16)
-    act, grad_pre = activate(dot(x, weight_ref[0]), g)
-    back = dot_nt(grad_pre, weight_ref[0])
+    act, grad_pre = activate(dot(x, weight_ref[...]), g)
+    back = dot_nt(grad_pre, weight_ref[...])
     act, grad32 = act.astype(F32), grad_pre.astype(F32)
     back_near[:, : plan.DX] = fold(plan, back[: plan.rows]).astype(BF16)
     back_near[:, plan.DX :] = fold(plan, act[: plan.rows]).astype(BF16)
@@ -290,11 +298,11 @@
     x = unfold(plan, blocks_of(far, 0, plan.DX), plan.D)
     g = unfold(plan, blocks_of(far, plan.DX, plan.C), plan.F)
     rows[...] = x
-    act, grad_pre = activate(dot(x, weight_ref[0]), g)
+    act, grad_pre = activate(dot(x, weight_ref[...]), g)
 
     @pl.when(jnp.logical_not(hot))
     def _():
-        back = dot_nt(grad_pre, weight_ref[0])
+        back = dot_nt(grad_pre, weight_ref[...])
         large[...] = fold(plan, back).astype(BF16)
         small[...] = fold(plan, act.astype(F32)).astype(BF16)
 
@@ -376,26 +384,36 @@
     return jnp.concatenate([p.astype(F32) for p in parts], axis=0).astype(BF16)
 
 
-def gather_kernel(plan, *refs):
+def gather_kernel(plan, weight_hbm, momentum_hbm, waiting, *refs):
     groups, share, width = plan.groups, plan.share, plan.F
     columns, refs = refs[:groups], refs[groups:]
     shared, refs = refs[:groups], refs[groups:]
-    total, x_all = refs
-    base = share
+    total, old_weight, passed, x_all, momentum, sems = refs
+    mine = pl.multiple_of(lax.axis_index("dp") * share, LANES)
+    copies = [
+        pltpu.make_async_copy(momentum_hbm.at[0], momentum, sems.at[0]),
+        pltpu.make_async_copy(weight_hbm.at[0, pl.ds(mine, share), :], old_weight, sems.at[1]),
+    ]
+    for copy in copies:
+        copy.start()
+    passed[...] = waiting[...]
     x_parts, g_parts = [], []
     for m in range(groups):
         x_parts += [columns[m][0], columns[m][1], shared[m][:, :share]]
-        g_parts += [shared[m][:, base + i * width : base + (i + 1) * width] for i in range(3)]
+        g_parts += [shared[m][:, share + i * width : share + (i + 1) * width] for i in range(3)]
     x_all[...] = rows_of(x_parts)
     g_all = rows_of(g_parts)
+    for copy in copies:
+        copy.wait()
     for i in range(share // LANES):
         span = slice(i * LANES, (i + 1) * LANES)
-        total[span, :] = dot_tn(x_all[:, span], g_all)
+        before = decay_rate * momentum[span, :].astype(F32)
+        total[span, :] = before + dot_tn(x_all[:, span], g_all)
 
 
 def update_kernel(plan, placement_ref, large, *refs):
     other_g, refs = refs[: plan.groups], refs[plan.groups :]
-    total_ref, weight_ref, momentum_ref, new_weight, new_momentum, x_all, g_all = refs
+    total_ref, weight_ref, new_weight, new_momentum, x_all, g_all = refs
     step = pl.program_id(0)
     share = plan.share
     tile = new_weight.shape[1]
@@ -411,10 +429,10 @@
 
     start = pl.multiple_of(step * tile, LANES)
     total = total_ref[...] + dot_tn(x_all[:, pl.ds(start, tile)], g_all[...])
-    momentum = (decay_rate * momentum_ref[0].astype(F32) + total).astype(BF16)
+    momentum = total.astype(BF16)
     new_momentum[0] = momentum
     new_weight[0] = (
-        weight_ref[0].astype(F32) - learning_rate * momentum.astype(F32)
+        weight_ref[...].astype(F32) - learning_rate * momentum.astype(F32)
     ).astype(BF16)
 
 
@@ -424,11 +442,13 @@
 VMEM_SPEC = pl.BlockSpec(memory_space=pltpu.VMEM)
 
 
-def call(kernel, plan, ins, specs, outs, scratch, flops, name, limit=16, dtype=BF16):
+def call(kernel, plan, ins, specs, outs, scratch, flops, name, limit=16, dtypes=None):
     moved = sum(a.size * a.dtype.itemsize for a in ins) + sum(2 * math.prod(o) for o in outs)
     return pl.pallas_call(
         functools.partial(kernel, plan),
-        out_shape=[jax.ShapeDtypeStruct(s, dtype) for s in outs],
+        out_shape=[
+            jax.ShapeDtypeStruct(s, dtypes[i] if dtypes else BF16) for i, s in enumerate(outs)
+        ],
         in_specs=specs,
         out_specs=[VMEM_SPEC] * len(outs),
         scratch_shapes=scratch,
@@ -446,11 +466,11 @@
     slot = slot_ids.reshape(1, -1)
     gate = route_weight.reshape(1, -1)
 
-    def to_slot(data, m):
+    def to_slot(data, m, flip=0):
         pairs = []
         for e in range(plan.slots):
             h, k = divmod(e, half)
-            pairs.append((e, h * half + away(k, m, half)))
+            pairs.append((e, (h ^ flip) * half + away(k, m, half)))
         return lax.ppermute(data, "expert", pairs)
 
     def to_source(data, m):
@@ -480,36 +500,52 @@
     def with_sisters(got):
         return [data for own in got for data in (own, from_group(own, 1))]
 
-    def pack(far, name, after, limit):
-        return call(
-            functools.partial(pack_kernel, far),
-            plan,
-            [slot, gate, tokens, cotangent] + after,
-            [ANY_SPEC] * (4 + len(after)),
-            [(SUB, C)] * half,
-            [
-                pltpu.VMEM(slot.shape, slot.dtype),
-                pltpu.VMEM(gate.shape, gate.dtype),
-                pltpu.VMEM(tokens.shape, tokens.dtype),
-                pltpu.VMEM(cotangent.shape, cotangent.dtype),
-                pltpu.SemaphoreType.DMA((4,)),
-            ],
-            2 * 4 * half * SUB * plan.tokens * (D + F),
-            name,
-            limit=limit,
-        )
-
-    packed = pack(1, "pack_far", [], 60)
-    relay = [packed[0]] + [to_slot(packed[m], m) for m in range(1, half)]
-    far = [to_partner(block) for block in relay]
-    packed = pack(0, "pack_near", relay[1:] + far[:1], 8)
+    packed = call(
+        pack_kernel,
+        plan,
+        [slot, gate, tokens, cotangent],
+        [ANY_SPEC] * 4,
+        [(2 * SUB, C)] * half + [(SUB, C)] * half,
+        [
+            pltpu.VMEM(slot.shape, slot.dtype),
+            pltpu.VMEM(gate.shape, gate.dtype),
+            pltpu.VMEM(tokens.shape, tokens.dtype),
+            pltpu.VMEM(cotangent.shape, cotangent.dtype),
+            pltpu.SemaphoreType.DMA((4,)),
+        ],
+        2 * 4 * half * SUB * plan.tokens * (D + F),
+        "pack",
+        limit=60,
+    )
     near = [packed[0]] + [to_slot(packed[m], m) for m in range(1, half)]
-
+    far = [to_slot(packed[half + m], m, 1) for m in range(2)]
+    later = call(
+        pass_kernel,
+        plan,
+        list(packed[half + 2 :]) + far[:1],
+        [VMEM_SPEC] * (half - 2) + [ANY_SPEC],
+        [(SUB, C)] * (half - 2),
+        [],
+        0,
+        "pass_on",
+    )
+    far += [to_slot(later[m - 2], m, 1) for m in range(2, half)]
+    (held,) = call(
+        hold_kernel,
+        plan,
+        [weight],
+        [ANY_SPEC],
+        [(D, F)],
+        [pltpu.SemaphoreType.DMA],
+        0,
+        "hold",
+        limit=40,
+    )
     columns = call(
         columns_kernel,
         plan,
-        near + relay + far[1:2],
-        [VMEM_SPEC] * (2 * half) + [ANY_SPEC],
+        near + [held] + [later[0], far[1]],
+        [VMEM_SPEC] * half + [ANY_SPEC] * 3,
         [(2, rows, share)] * groups,
         [pltpu.VMEM((2, rows, D), BF16)],
         0,
@@ -521,8 +557,8 @@
     back_near, local_back, local_act, folded_grad, grads = call(
         near_kernel,
         plan,
-        [placement, weight] + near + relay + [columns[0], far[2]],
-        [SMEM_SPEC, VMEM_SPEC] + [VMEM_SPEC] * (2 * half) + [ANY_SPEC] * 2,
+        [placement, held] + near + [columns[0], far[2]],
+        [SMEM_SPEC] + [VMEM_SPEC] * (1 + half) + [ANY_SPEC] * 2,
         [
             (half * SUB, C),
             (half * SUB, plan.DX),
@@ -537,7 +573,7 @@
     outs = call(
         payload_kernel,
         plan,
-        [placement, weight, folded_grad, grads] + far + columns_here,
+        [placement, held, folded_grad, grads] + far + columns_here,
         [SMEM_SPEC] + [VMEM_SPEC] * (3 + half + groups),
         [(half * SUB, plan.FG), (half * SUB, plan.DX)]
         + [(rows, share + 3 * F)] * groups,
@@ -560,19 +596,24 @@
         "after_small",
     )
     early = [outs[0]] + [to_source(outs[m], m) for m in range(1, half)]
-    other_g = with_sisters(from_chips([outs[half]] * outer))
-    (total,) = call(
+    total, old_weight, passed = call(
         gather_kernel,
         plan,
-        columns_here + shared,
-        [VMEM_SPEC] * (2 * groups),
-        [(share, F)],
-        [pltpu.VMEM((3 * groups * rows, share), BF16)],
+        [weight, momentum, outs[half]] + columns_here + shared,
+        [ANY_SPEC] * 2 + [VMEM_SPEC] * (1 + 2 * groups),
+        [(share, F), (share, F), (rows, F)],
+        [
+            pltpu.VMEM((3 * groups * rows, share), BF16),
+            pltpu.VMEM((share, F), BF16),
+            pltpu.SemaphoreType.DMA((2,)),
+        ],
         0,
         "own_terms",
-        dtype=F32,
-    )
-    first = [total] + other_g[1:]
+        limit=24,
+        dtypes=[F32, BF16, BF16],
+    )
+    other_g = with_sisters(from_chips([passed] * outer))
+    first = [total] + early[1:]
     outs = call(
         after_large_kernel,
         plan,
@@ -601,8 +642,7 @@
             + [whole(rows, F)] * groups
             + [
                 pl.BlockSpec((tile, F), lambda i, g: (i, 0)),
-                pl.BlockSpec((1, tile, F), lambda i, g: (0, g[0] * steps + i, 0)),
-                pl.BlockSpec((1, tile, F), lambda i, g: (0, i, 0)),
+                pl.BlockSpec((tile, F), lambda i, g: (i, 0)),
             ],
             out_specs=[pl.BlockSpec((1, tile, F), lambda i, g: (0, i, 0))] * 2,
             scratch_shapes=[
@@ -616,7 +656,7 @@
             flops=2 * groups * rows * share * F, bytes_accessed=12 * share * F, transcendentals=0
         ),
         name="update",
-    )(group, placement, large, *other_g, total, weight, momentum)
+    )(group, placement, large, *other_g, total, old_weight)
 
     expert_out, token_grad = call(
         unpack_kernel,

time: 119 us -> 123 us (1.034)
  waiting for transfers between devices: 44.7 us -> 60.4 us
  local copies, waits for them, and re-layouts: 13.7 us -> 5.45 us
  starting transfers between devices: 33.1 us -> 28.3 us
  Pallas kernels: 25.2 us -> 27.5 us
    ppermute x6 -> x2, waiting for transfers between devices: 19.3 us -> 29.6 us  [to_partner(): return lax.ppermute(data, 'expert', pairs)]
    unnamed x34 -> x26, local copies, waits for them, and re-layouts: 13.7 us -> 5.45 us
    ppermute x6 -> x2, starting transfers between devices: 10.1 us -> 2.92 us  [to_partner(): return lax.ppermute(data, 'expert', pairs)]
    ppermute x6, waiting for transfers between devices: 0.02 us -> 6.67 us  [to_source(): return lax.ppermute(data, 'expert', pairs)]
    ppermute x6 -> x7, starting transfers between devices: 8.89 us -> 13 us  [to_slot(): return lax.ppermute(data, 'expert', pairs)]
    pallas_call x9 -> x10, Pallas kernels: 19.8 us -> 21.8 us  [call(): pl.pallas_call(functools.partial(kernel, plan), out_shape=[jax.ShapeDtype...]
    ppermute x6, starting transfers between devices: 8.83 us -> 6.98 us  [to_source(): return lax.ppermute(data, 'expert', pairs)]
    ppermute x9, waiting for transfers between devices: 7.66 us -> 6.19 us  [from_group(): return lax.ppermute(data, 'dp', pairs)]
  transfers between devices with their start and end apart: 27 -> 24, of which waited for: 9 -> 9; matrix products, arithmetic and copies ran while one was open for 0% -> 0% of each run, Pallas kernels for 13% -> 13%
where the time goes in v3:
time: 123 us; the launch traced here: 122 us
  waiting for transfers between devices  60.4 us (49%)
  starting transfers between devices  28.3 us (23%)
  Pallas kernels  27.5 us (22%)
  local copies, waits for them, and re-layouts  5.45 us (4%)
    ppermute x2, waiting for transfers between devices, to_partner(): return lax.ppermute(data, 'expert', pairs)  29.6 us
    pallas_call x10, Pallas kernels, call(): pl.pallas_call(functools.partial(kernel, plan), out_shape=[jax.ShapeDtype...  21.8 us
    ppermute x7, waiting for transfers between devices, to_slot(): return lax.ppermute(data, 'expert', pairs)  18 us
    ppermute x7, starting transfers between devices, to_slot(): return lax.ppermute(data, 'expert', pairs)  13 us
    ppermute x6, starting transfers between devices, to_source(): return lax.ppermute(data, 'expert', pairs)  6.98 us
    ppermute x6, waiting for transfers between devices, to_source(): return lax.ppermute(data, 'expert', pairs)  6.67 us
    ppermute x9, waiting for transfers between devices, from_group(): return lax.ppermute(data, 'dp', pairs)  6.19 us
    pallas_call x1, Pallas kernels, routed(): pl.pallas_call(lambda g_ref, *refs: update_kernel(plan, *refs), grid_spec...  5.71 us
  transfers between devices with their start and end apart: 24, of which 9 were waited for; matrix products, arithmetic and copies ran while one was open for 0% of the time, Pallas kernels for 13%

profile of v3, /device:TPU:0, one launch (start us, length us, event | category | flops | bytes accessed | tf_op | source)
XLA Modules:
  0.0 122.5 jit_solution(13853362510813489770)
XLA Ops:
  0.6 3.4 %pack.1 = (bf16[16,10368]{1,0:T(8,128)(2,1)}, bf16[16,10368]{1,0:T(8,128)(2,1)}, bf16[16,10368]{1,0:T(8,128)(2,1)}, bf16[16,10368]{1,0:T(8,128)(2,1)}, bf16[8,10...) custom-call(s32[1,128]{1,0:T(1,128)} %bitcast.5, ...), custom_call_target="tpu_custom_call" | custom-call | flops 150994944 | bytes 3171328 | tf_op jit(solution)/shard_map/pack/pallas_call | solution.py:447
  4.0 3.0 %collective-permute-start = (bf16[16,10368]{1,0:T(8,128)(2,1)}, bf16[16,10368]{1,0:T(8,128)(2,1)S(1)}, u32[]{:S(2)}, u32[]{:S(2)}) collective-permute-start(bf16[16,10368]{1,0:T(8,128)(2,1)} %get-tuple-element.46), channel_id=1, source_target_pairs={{0,1},{1,0},{2,3},{3,2},{4,5},{5,4},{6,7},{7,6},{8,9},{9,8},{10,11... | collective-permute-start | bytes 995336 | tf_op jit(solution)/shard_map/ppermute | solution.py:474
  7.0 1.6 %collective-permute-start.1 = (bf16[16,10368]{1,0:T(8,128)(2,1)}, bf16[16,10368]{1,0:T(8,128)(2,1)S(1)}, u32[]{:S(2)}, u32[]{:S(2)}) collective-permute-start(bf16[16,10368]{1,0:T(8,128)(2,1)} %get-tuple-element.47), channel_id=1, source_target_pairs={{0,2},{1,3},{2,0},{3,1},{4,6},{5,7},{6,4},{7,5},{8,10},{9,11},{10,... | collective-permute-start | bytes 995336 | tf_op jit(solution)/shard_map/ppermute | solution.py:474
  8.6 3.0 %collective-permute-start.3 = (bf16[8,10368]{1,0:T(8,128)(2,1)}, bf16[8,10368]{1,0:T(8,128)(2,1)S(1)}, u32[]{:S(2)}, u32[]{:S(2)}) collective-permute-start(bf16[8,10368]{1,0:T(8,128)(2,1)} %get-tuple-element.51), channel_id=1, source_target_pairs={{0,4},{1,5},{2,6},{3,7},{4,0},{5,1},{6,2},{7,3},{8,12},{9,13},{10,... | collective-permute-start | bytes 497672 | tf_op jit(solution)/shard_map/ppermute | solution.py:474
  11.6 1.3 %collective-permute-start.4 = (bf16[8,10368]{1,0:T(8,128)(2,1)}, bf16[8,10368]{1,0:T(8,128)(2,1)S(1)}, u32[]{:S(2)}, u32[]{:S(2)}) collective-permute-start(bf16[8,10368]{1,0:T(8,128)(2,1)} %get-tuple-element.53), channel_id=1, source_target_pairs={{0,5},{1,4},{2,7},{3,6},{4,1},{5,0},{6,3},{7,2},{8,13},{9,12},{10,... | collective-permute-start | bytes 497672 | tf_op jit(solution)/shard_map/ppermute | solution.py:474
  12.9 14.9 %collective-permute-done.3.refs_2_.refs_0_ = bf16[8,10368]{1,0:T(8,128)(2,1)S(1)} collective-permute-done((bf16[8,10368]{1,0:T(8,128)(2,1)}, bf16[8,10368]{1,0:T(8,128)(2,1)S(1)}, u32[]{:S(2)}, u32[]{:S(2)}) %collective-permute-start.3) | collective-permute-done | bytes 165920 | tf_op jit(solution)/shard_map/ppermute | solution.py:474
  27.8 0.9 copy-done.4
  28.7 0.9 copy-done.5
  29.7 0.0 copy-start.3
  29.7 2.5 %collective-permute-start.5 = (bf16[8,10368]{1,0:T(8,128)(2,1)S(1)}, bf16[8,10368]{1,0:T(8,128)(2,1)S(1)}, u32[]{:S(2)}, u32[]{:S(2)}) collective-permute-start(bf16[8,10368]{1,0:T(8,128)(2,1)S(1)} %get-tuple-element.52.refs_5_), channel_id=1, source_target_pairs={{0,6},{1,7},{2,4},{3,5},{4,2},{5,3},{6,0},{7,1},{8,14},{9,15},{10,... | collective-permute-start | bytes 497672 | tf_op jit(solution)/shard_map/ppermute | solution.py:474
  32.2 3.1 %hold.1.refs_4_.weight_ref = bf16[3584,1024]{1,0:T(8,128)(2,1)S(1)} custom-call(bf16[1,3584,1024]{2,1,0:T(8,128)(2,1)} %weight_hbm.3), custom_call_target="tpu_custom_call" | custom-call | tf_op jit(solution)/shard_map/hold/pallas_call | solution.py:447
  35.3 0.0 collective-permute-done.refs_1_
  35.4 0.0 collective-permute-done.1.refs_2_
  35.4 0.0 copy-start.8
  35.4 0.3 near_columns.1
  35.7 0.1 collective-permute-start.7
  35.8 1.6 %collective-permute-start.8 = (bf16[2,72,896]{2,1,0:T(8,128)(2,1)S(1)}, bf16[2,72,896]{2,1,0:T(8,128)(2,1)S(1)}, u32[]{:S(2)}, u32[]{:S(2)}) collective-permute-start(bf16[2,72,896]{2,1,0:T(8,128)(2,1)S(1)} %get-tuple-element.59), channel_id=1, source_target_pairs={{16,0},{24,8},{0,16},{8,24},{17,1},{25,9},{1,17},{9,25},{18,2},{26... | collective-permute-start | bytes 774152 | tf_op jit(solution)/shard_map/ppermute | solution.py:491
  37.4 0.3 collective-permute-start.9
  37.6 1.6 %collective-permute-start.6 = (bf16[8,10368]{1,0:T(8,128)(2,1)S(1)}, bf16[8,10368]{1,0:T(8,128)(2,1)S(1)}, u32[]{:S(2)}, u32[]{:S(2)}) collective-permute-start(bf16[8,10368]{1,0:T(8,128)(2,1)S(1)} %get-tuple-element.57), channel_id=1, source_target_pairs={{0,7},{1,6},{2,5},{3,4},{4,3},{5,2},{6,1},{7,0},{8,15},{9,14},{10,... | collective-permute-start | bytes 497672 | tf_op jit(solution)/shard_map/ppermute | solution.py:474
  39.2 4.7 %near_rows.1 = (bf16[32,10368]{1,0:T(8,128)(2,1)S(1)}, bf16[32,8064]{1,0:T(8,128)(2,1)S(1)}, bf16[32,2304]{1,0:T(8,128)(2,1)S(1)}, bf16[32,2304]{1,0:T(8,128)(2,1)S(1)}, bf16[72,2048]{1,0:T(8,128)(2,1)S(1)}) custom-call(s32[8]{0:T(128)S(1)} %copy-done.8, bf16[3584,1024]{1,0:T(8,128)(2,1)S(1)} %hold.1.refs_4_.weight_ref, bf16[16,10368]{1,0:T(8,128)(2,1)S(1)} %copy-done.3, ...), custom_call_target="tpu_custom_call" | custom-call | flops 2113929216 | bytes 10860576 | tf_op jit(solution)/shard_map/near_rows/pallas_call | solution.py:447
  43.9 3.0 %collective-permute-done.6.refs_3_ = bf16[8,10368]{1,0:T(8,128)(2,1)S(1)} collective-permute-done((bf16[8,10368]{1,0:T(8,128)(2,1)S(1)}, bf16[8,10368]{1,0:T(8,128)(2,1)S(1)}, u32[]{:S(2)}, u32[]{:S(2)}) %collective-permute-start.6) | collective-permute-done | bytes 165920 | tf_op jit(solution)/shard_map/ppermute | solution.py:474
  46.9 2.5 %collective-permute-done.9.refs_7_.refs_3_ = bf16[2,72,896]{2,1,0:T(8,128)(2,1)S(1)} collective-permute-done((bf16[2,72,896]{2,1,0:T(8,128)(2,1)S(1)}, bf16[2,72,896]{2,1,0:T(8,128)(2,1)S(1)}, u32[]{:S(2)}, u32[]{:S(2)}) %collective-permute-start.9) | collective-permute-done | bytes 258080 | tf_op jit(solution)/shard_map/ppermute | solution.py:491
  49.5 2.5 %payload.1 = (bf16[32,2304]{1,0:T(8,128)(2,1)S(1)}, bf16[32,8064]{1,0:T(8,128)(2,1)S(1)}, bf16[72,3968]{1,0:T(8,128)(2,1)S(1)}, bf16[72,3968]{1,0:T(8,128)(2,1)S...) custom-call(s32[8]{0:T(128)S(1)} %copy-done.8, bf16[3584,1024]{1,0:T(8,128)(2,1)S(1)} %hold.1.refs_4_.weight_ref, ...), custom_call_target="tpu_custom_call" | custom-call | flops 1056964608 | bytes 12427296 | tf_op jit(solution)/shard_map/payload/pallas_call | solution.py:447
  52.0 0.3 collective-permute-start.15
  52.3 1.5 %collective-permute-start.16 = (bf16[72,3968]{1,0:T(8,128)(2,1)S(1)}, bf16[72,3968]{1,0:T(8,128)(2,1)S(1)}, u32[]{:S(2)}, u32[]{:S(2)}) collective-permute-start(bf16[72,3968]{1,0:T(8,128)(2,1)S(1)} %get-tuple-element.73), channel_id=1, source_target_pairs={{16,0},{24,8},{0,16},{8,24},{17,1},{25,9},{1,17},{9,25},{18,2},{26... | collective-permute-start | bytes 1714184 | tf_op jit(solution)/shard_map/ppermute | solution.py:491
  53.8 0.1 collective-permute-start.17
  53.9 2.4 %collective-permute-start.14 = (bf16[32,8064]{1,0:T(8,128)(2,1)S(1)}, bf16[32,8064]{1,0:T(8,128)(2,1)S(1)}, u32[]{:S(2)}, u32[]{:S(2)}) collective-permute-start(bf16[32,8064]{1,0:T(8,128)(2,1)S(1)} %get-tuple-element.68), channel_id=1, source_target_pairs={{0,4},{1,5},{2,6},{3,7},{4,0},{5,1},{6,2},{7,3},{8,12},{9,13},{10,... | collective-permute-start | bytes 1548296 | tf_op jit(solution)/shard_map/ppermute | solution.py:485
  56.3 0.5 collective-permute-start.10
  56.8 29.6 %collective-permute-done.10.small = bf16[32,2304]{1,0:T(8,128)(2,1)S(1)} collective-permute-done((bf16[32,2304]{1,0:T(8,128)(2,1)S(1)}, bf16[32,2304]{1,0:T(8,128)(2,1)S(1)}, u32[]{:S(2)}, u32[]{:S(2)}) %collective-permute-start.10) | collective-permute-done | bytes 147488 | tf_op jit(solution)/shard_map/ppermute | solution.py:485
  86.4 0.8 after_small.1
  87.2 1.3 %collective-permute-start.11 = (bf16[8,12672]{1,0:T(8,128)(2,1)S(1)}, bf16[8,12672]{1,0:T(8,128)(2,1)S(1)}, u32[]{:S(2)}, u32[]{:S(2)}) collective-permute-start(bf16[8,12672]{1,0:T(8,128)(2,1)S(1)} %get-tuple-element.65), channel_id=1, source_target_pairs={{1,0},{0,1},{3,2},{2,3},{5,4},{4,5},{7,6},{6,7},{9,8},{8,9},{11,10... | collective-permute-start | bytes 608264 | tf_op jit(solution)/shard_map/ppermute | solution.py:481
  88.5 2.2 %collective-permute-start.13 = (bf16[8,12672]{1,0:T(8,128)(2,1)S(1)}, bf16[8,12672]{1,0:T(8,128)(2,1)S(1)}, u32[]{:S(2)}, u32[]{:S(2)}) collective-permute-start(bf16[8,12672]{1,0:T(8,128)(2,1)S(1)} %get-tuple-element.67), channel_id=1, source_target_pairs={{3,0},{2,1},{1,2},{0,3},{7,4},{6,5},{5,6},{4,7},{11,8},{10,9},{9,1... | collective-permute-start | bytes 608264 | tf_op jit(solution)/shard_map/ppermute | solution.py:481
  90.7 2.6 %own_terms.1 = (f32[896,1024]{1,0:T(8,128)S(1)}, bf16[896,1024]{1,0:T(8,128)(2,1)S(1)}, bf16[72,1024]{1,0:T(8,128)(2,1)S(1)}) custom-call(bf16[1,3584,1024]{2,1,0:T(8,128)(2,1)S(1)} %bitcast.4, bf16[1,896,1024]{2,1,0:T(8,128)(2,1)S(1)} %copy-done.2, bf16[72,1024]{1,0:T(8,128)(2,1)S(1)} %get-tuple-element.70.waiting, ...), custom_call_target="tpu_custom_call" | custom-call | tf_op jit(solution)/shard_map/own_terms/pallas_call | solution.py:447
  93.3 1.6 %collective-permute-start.22 = (bf16[72,1024]{1,0:T(8,128)(2,1)S(1)}, bf16[72,1024]{1,0:T(8,128)(2,1)S(1)}, u32[]{:S(2)}, u32[]{:S(2)}) collective-permute-start(bf16[72,1024]{1,0:T(8,128)(2,1)S(1)} %get-tuple-element.82.refs_2_), channel_id=1, source_target_pairs={{16,0},{24,8},{0,16},{8,24},{17,1},{25,9},{1,17},{9,25},{18,2},{26... | collective-permute-start | bytes 442376 | tf_op jit(solution)/shard_map/ppermute | solution.py:491
  94.9 3.6 %collective-permute-done.22.refs_4_ = bf16[72,1024]{1,0:T(8,128)(2,1)S(1)} collective-permute-done((bf16[72,1024]{1,0:T(8,128)(2,1)S(1)}, bf16[72,1024]{1,0:T(8,128)(2,1)S(1)}, u32[]{:S(2)}, u32[]{:S(2)}) %collective-permute-start.22) | collective-permute-done | bytes 147488 | tf_op jit(solution)/shard_map/ppermute | solution.py:491
  98.6 0.9 collective-permute-done.13.refs_3_
  99.4 1.3 %after_large.1 = (bf16[8,8064]{1,0:T(8,128)(2,1)S(1)}, bf16[8,8064]{1,0:T(8,128)(2,1)}, bf16[8,8064]{1,0:T(8,128)(2,1)}, bf16[8,8064]{1,0:T(8,128)(2,1)}) custom-call(s32[8]{0:T(128)S(1)} %copy-done.8, bf16[32,8064]{1,0:T(8,128)(2,1)S(1)} %collective-permute-done.14.large.refs_1_, bf16[32,8064]{1,0:T(8,128)(2,1)S(1)} %get-tuple-element.69.local_back, ...), custom_call_target="tpu_custom_call" | custom-call | flops 1000000 | bytes 5826592 | tf_op jit(solution)/shard_map/after_large/pallas_call | solution.py:447
  100.8 0.6 copy-done.6
  101.4 1.6 %collective-permute-start.18 = (bf16[8,8064]{1,0:T(8,128)(2,1)}, bf16[8,8064]{1,0:T(8,128)(2,1)}, u32[]{:S(2)}, u32[]{:S(2)}) collective-permute-start(bf16[8,8064]{1,0:T(8,128)(2,1)} %get-tuple-element.77), channel_id=1, source_target_pairs={{1,0},{0,1},{3,2},{2,3},{5,4},{4,5},{7,6},{6,7},{9,8},{8,9},{11,10... | collective-permute-start | bytes 387080 | tf_op jit(solution)/shard_map/ppermute | solution.py:481
  103.0 0.3 collective-permute-start.19
  103.3 1.6 %collective-permute-start.20 = (bf16[8,8064]{1,0:T(8,128)(2,1)}, bf16[8,8064]{1,0:T(8,128)(2,1)}, u32[]{:S(2)}, u32[]{:S(2)}) collective-permute-start(bf16[8,8064]{1,0:T(8,128)(2,1)} %get-tuple-element.79), channel_id=1, source_target_pairs={{3,0},{2,1},{1,2},{0,3},{7,4},{6,5},{5,6},{4,7},{11,8},{10,9},{9,1... | collective-permute-start | bytes 387080 | tf_op jit(solution)/shard_map/ppermute | solution.py:481
  104.9 2.3 %collective-permute-done.18.refs_5_ = bf16[8,8064]{1,0:T(8,128)(2,1)} collective-permute-done((bf16[8,8064]{1,0:T(8,128)(2,1)}, bf16[8,8064]{1,0:T(8,128)(2,1)}, u32[]{:S(2)}, u32[]{:S(2)}) %collective-permute-start.18) | collective-permute-done | bytes 129056 | tf_op jit(solution)/shard_map/ppermute | solution.py:481
  107.2 2.0 %collective-permute-done.19.refs_6_ = bf16[8,8064]{1,0:T(8,128)(2,1)} collective-permute-done((bf16[8,8064]{1,0:T(8,128)(2,1)}, bf16[8,8064]{1,0:T(8,128)(2,1)}, u32[]{:S(2)}, u32[]{:S(2)}) %collective-permute-start.19) | collective-permute-done | bytes 129056 | tf_op jit(solution)/shard_map/ppermute | solution.py:481
  109.2 1.5 %collective-permute-done.20.refs_7_ = bf16[8,8064]{1,0:T(8,128)(2,1)} collective-permute-done((bf16[8,8064]{1,0:T(8,128)(2,1)}, bf16[8,8064]{1,0:T(8,128)(2,1)}, u32[]{:S(2)}, u32[]{:S(2)}) %collective-permute-start.20) | collective-permute-done | bytes 129056 | tf_op jit(solution)/shard_map/ppermute | solution.py:481
  110.7 0.9 copy-done.7
  111.6 3.1 %unpack.1 = (bf16[128,1024]{1,0:T(8,128)(2,1)}, bf16[128,3584]{1,0:T(8,128)(2,1)}) custom-call(s32[1,128]{1,0:T(1,128)S(1)} %bitcast.6, f32[1,128]{1,0:T(1,128)S(1)} %bitcast.8, bf16[8,12672]{1,0:T(8,128)(2,1)S(1)} %get-tuple-element.64.refs_0_, bf16[8,12672]{1,0:T(8,128)(2,1)S(1)} %collective-permute-done.11.refs_1_, ...), custom_call_target="tpu_custom_call" | custom-call | flops 150994944 | bytes 2507776 | tf_op jit(solution)/shard_map/unpack/pallas_call | solution.py:447
  114.7 2.0 %copy-done.1 = f32[896,1024]{1,0:T(8,128)S(1)} copy-done((f32[896,1024]{1,0:T(8,128)S(1)}, f32[896,1024]{1,0:T(8,128)}, u32[]{:S(2)}) %copy-start.1) | copy-done | bytes 3670040
  116.8 5.7 %update.1 = (bf16[1,896,1024]{2,1,0:T(8,128)(2,1)}, bf16[1,896,1024]{2,1,0:T(8,128)(2,1)}) custom-call(s32[1]{0:T(128)} %bitcast.2.g_ref, s32[8]{0:T(128)S(1)} %copy-done.8, bf16[32,8064]{1,0:T(8,128)(2,1)S(1)} %collective-permute-done.14.large.refs_1_, bf16[72,1024]{1,0:T(8,128)(2,1)S(1)} %get-tuple-element.82.refs_2_, ...), custom_call_target="tpu_custom_call" | custom-call | flops 528482304 | bytes 11010048 | tf_op jit(solution)/shard_map/update/pallas_call | solution.py:636
  (38 shorter events, 0.1 us)
Async XLA Ops:
  4.0 31.3 %collective-permute-start = (bf16[16,10368]{1,0:T(8,128)(2,1)}, bf16[16,10368]{1,0:T(8,128)(2,1)S(1)}, u32[]{:S(2)}, u32[]{:S(2)}) collective-permute-start(bf16[16,10368]{1,0:T(8,128)(2,1)} %get-tuple-element.46), channel_id=1, source_target_pairs={{0,1},{1,0},{2,3},{3,2},{4,5},{5,4},{6,7},{7,6},{8,9},{9,8},{10,11... | collective-permute-start | bytes 995336 | tf_op jit(solution)/shard_map/ppermute | solution.py:474
  7.0 28.3 %collective-permute-start.1 = (bf16[16,10368]{1,0:T(8,128)(2,1)}, bf16[16,10368]{1,0:T(8,128)(2,1)S(1)}, u32[]{:S(2)}, u32[]{:S(2)}) collective-permute-start(bf16[16,10368]{1,0:T(8,128)(2,1)} %get-tuple-element.47), channel_id=1, source_target_pairs={{0,2},{1,3},{2,0},{3,1},{4,6},{5,7},{6,4},{7,5},{8,10},{9,11},{10,... | collective-permute-start | bytes 995336 | tf_op jit(solution)/shard_map/ppermute | solution.py:474
  8.6 26.8 %collective-permute-start.2 = (bf16[16,10368]{1,0:T(8,128)(2,1)}, bf16[16,10368]{1,0:T(8,128)(2,1)S(1)}, u32[]{:S(2)}, u32[]{:S(2)}) collective-permute-start(bf16[16,10368]{1,0:T(8,128)(2,1)} %get-tuple-element.48), channel_id=1, source_target_pairs={{0,3},{1,2},{2,1},{3,0},{4,7},{5,6},{6,5},{7,4},{8,11},{9,10},{10,... | collective-permute-start | bytes 995336 | tf_op jit(solution)/shard_map/ppermute | solution.py:474
  8.6 19.2 %collective-permute-start.3 = (bf16[8,10368]{1,0:T(8,128)(2,1)}, bf16[8,10368]{1,0:T(8,128)(2,1)S(1)}, u32[]{:S(2)}, u32[]{:S(2)}) collective-permute-start(bf16[8,10368]{1,0:T(8,128)(2,1)} %get-tuple-element.51), channel_id=1, source_target_pairs={{0,4},{1,5},{2,6},{3,7},{4,0},{5,1},{6,2},{7,3},{8,12},{9,13},{10,... | collective-permute-start | bytes 497672 | tf_op jit(solution)/shard_map/ppermute | solution.py:474
  11.6 23.7 %collective-permute-start.4 = (bf16[8,10368]{1,0:T(8,128)(2,1)}, bf16[8,10368]{1,0:T(8,128)(2,1)S(1)}, u32[]{:S(2)}, u32[]{:S(2)}) collective-permute-start(bf16[8,10368]{1,0:T(8,128)(2,1)} %get-tuple-element.53), channel_id=1, source_target_pairs={{0,5},{1,4},{2,7},{3,6},{4,1},{5,0},{6,3},{7,2},{8,13},{9,12},{10,... | collective-permute-start | bytes 497672 | tf_op jit(solution)/shard_map/ppermute | solution.py:474
  27.8 0.9 copy-start.4
  28.7 0.9 copy-start.5
  29.7 5.7 %copy-start.3 = (bf16[16,10368]{1,0:T(8,128)(2,1)S(1)}, bf16[16,10368]{1,0:T(8,128)(2,1)}, u32[]{:S(2)}) copy-start(bf16[16,10368]{1,0:T(8,128)(2,1)} %get-tuple-element.45.refs_0_) | copy-start | bytes 995332
  29.7 9.5 %collective-permute-start.5 = (bf16[8,10368]{1,0:T(8,128)(2,1)S(1)}, bf16[8,10368]{1,0:T(8,128)(2,1)S(1)}, u32[]{:S(2)}, u32[]{:S(2)}) collective-permute-start(bf16[8,10368]{1,0:T(8,128)(2,1)S(1)} %get-tuple-element.52.refs_5_), channel_id=1, source_target_pairs={{0,6},{1,7},{2,4},{3,5},{4,2},{5,3},{6,0},{7,1},{8,14},{9,15},{10,... | collective-permute-start | bytes 497672 | tf_op jit(solution)/shard_map/ppermute | solution.py:474
  35.4 3.8 %copy-start.8 = (s32[8]{0:T(128)S(1)}, s32[8]{0:T(128)}, u32[]{:S(2)}) copy-start(s32[8]{0:T(128)} %refs_0_.1) | copy-start | bytes 100
  35.7 11.2 %collective-permute-start.7 = (bf16[2,72,896]{2,1,0:T(8,128)(2,1)S(1)}, bf16[2,72,896]{2,1,0:T(8,128)(2,1)S(1)}, u32[]{:S(2)}, u32[]{:S(2)}) collective-permute-start(bf16[2,72,896]{2,1,0:T(8,128)(2,1)S(1)} %get-tuple-element.58), channel_id=1, source_target_pairs={{8,0},{0,8},{24,16},{16,24},{9,1},{1,9},{25,17},{17,25},{10,2},{2,... | collective-permute-start | bytes 774152 | tf_op jit(solution)/shard_map/ppermute | solution.py:491
  35.8 11.2 %collective-permute-start.8 = (bf16[2,72,896]{2,1,0:T(8,128)(2,1)S(1)}, bf16[2,72,896]{2,1,0:T(8,128)(2,1)S(1)}, u32[]{:S(2)}, u32[]{:S(2)}) collective-permute-start(bf16[2,72,896]{2,1,0:T(8,128)(2,1)S(1)} %get-tuple-element.59), channel_id=1, source_target_pairs={{16,0},{24,8},{0,16},{8,24},{17,1},{25,9},{1,17},{9,25},{18,2},{26... | collective-permute-start | bytes 774152 | tf_op jit(solution)/shard_map/ppermute | solution.py:491
  37.4 12.1 %collective-permute-start.9 = (bf16[2,72,896]{2,1,0:T(8,128)(2,1)S(1)}, bf16[2,72,896]{2,1,0:T(8,128)(2,1)S(1)}, u32[]{:S(2)}, u32[]{:S(2)}) collective-permute-start(bf16[2,72,896]{2,1,0:T(8,128)(2,1)S(1)} %get-tuple-element.60), channel_id=1, source_target_pairs={{24,0},{16,8},{8,16},{0,24},{25,1},{17,9},{9,17},{1,25},{26,2},{18... | collective-permute-start | bytes 774152 | tf_op jit(solution)/shard_map/ppermute | solution.py:491
  37.6 9.3 %collective-permute-start.6 = (bf16[8,10368]{1,0:T(8,128)(2,1)S(1)}, bf16[8,10368]{1,0:T(8,128)(2,1)S(1)}, u32[]{:S(2)}, u32[]{:S(2)}) collective-permute-start(bf16[8,10368]{1,0:T(8,128)(2,1)S(1)} %get-tuple-element.57), channel_id=1, source_target_pairs={{0,7},{1,6},{2,5},{3,4},{4,3},{5,2},{6,1},{7,0},{8,15},{9,14},{10,... | collective-permute-start | bytes 497672 | tf_op jit(solution)/shard_map/ppermute | solution.py:474
  39.2 51.4 %slice-start = ((s8[7340032]{0:T(1024)(128)(4,1)}), s8[4194304]{0:T(1024)(128)(4,1)S(1)}, s32[]{:S(2)}) async-start(s8[7340032]{0:T(1024)(128)(4,1)} %bitcast.3), calls=%async_computation | async-start | bytes 8388608
  49.5 41.2 %slice-start.1 = ((s8[7340032]{0:T(1024)(128)(4,1)}), s8[3145728]{0:T(1024)(128)(4,1)S(1)}, s32[]{:S(2)}) async-start(s8[7340032]{0:T(1024)(128)(4,1)} %bitcast.3), calls=%async_computation.1 | async-start | bytes 6291456
  49.5 41.2 %copy-start.2 = (bf16[1,896,1024]{2,1,0:T(8,128)(2,1)S(1)}, bf16[1,896,1024]{2,1,0:T(8,128)(2,1)}, u32[]{:S(2)}) copy-start(bf16[1,896,1024]{2,1,0:T(8,128)(2,1)} %momentum_hbm.1) | copy-start | bytes 5505028
  52.0 36.5 %collective-permute-start.15 = (bf16[72,3968]{1,0:T(8,128)(2,1)S(1)}, bf16[72,3968]{1,0:T(8,128)(2,1)S(1)}, u32[]{:S(2)}, u32[]{:S(2)}) collective-permute-start(bf16[72,3968]{1,0:T(8,128)(2,1)S(1)} %get-tuple-element.72), channel_id=1, source_target_pairs={{8,0},{0,8},{24,16},{16,24},{9,1},{1,9},{25,17},{17,25},{10,2},{2,... | collective-permute-start | bytes 1714184 | tf_op jit(solution)/shard_map/ppermute | solution.py:491
  52.3 36.2 %collective-permute-start.16 = (bf16[72,3968]{1,0:T(8,128)(2,1)S(1)}, bf16[72,3968]{1,0:T(8,128)(2,1)S(1)}, u32[]{:S(2)}, u32[]{:S(2)}) collective-permute-start(bf16[72,3968]{1,0:T(8,128)(2,1)S(1)} %get-tuple-element.73), channel_id=1, source_target_pairs={{16,0},{24,8},{0,16},{8,24},{17,1},{25,9},{1,17},{9,25},{18,2},{26... | collective-permute-start | bytes 1714184 | tf_op jit(solution)/shard_map/ppermute | solution.py:491
  53.8 36.9 %collective-permute-start.17 = (bf16[72,3968]{1,0:T(8,128)(2,1)S(1)}, bf16[72,3968]{1,0:T(8,128)(2,1)S(1)}, u32[]{:S(2)}, u32[]{:S(2)}) collective-permute-start(bf16[72,3968]{1,0:T(8,128)(2,1)S(1)} %get-tuple-element.74), channel_id=1, source_target_pairs={{24,0},{16,8},{8,16},{0,24},{25,1},{17,9},{9,17},{1,25},{26,2},{18... | collective-permute-start | bytes 1714184 | tf_op jit(solution)/shard_map/ppermute | solution.py:491
  53.9 45.5 %collective-permute-start.14 = (bf16[32,8064]{1,0:T(8,128)(2,1)S(1)}, bf16[32,8064]{1,0:T(8,128)(2,1)S(1)}, u32[]{:S(2)}, u32[]{:S(2)}) collective-permute-start(bf16[32,8064]{1,0:T(8,128)(2,1)S(1)} %get-tuple-element.68), channel_id=1, source_target_pairs={{0,4},{1,5},{2,6},{3,7},{4,0},{5,1},{6,2},{7,3},{8,12},{9,13},{10,... | collective-permute-start | bytes 1548296 | tf_op jit(solution)/shard_map/ppermute | solution.py:485
  56.3 30.1 %collective-permute-start.10 = (bf16[32,2304]{1,0:T(8,128)(2,1)S(1)}, bf16[32,2304]{1,0:T(8,128)(2,1)S(1)}, u32[]{:S(2)}, u32[]{:S(2)}) collective-permute-start(bf16[32,2304]{1,0:T(8,128)(2,1)S(1)} %get-tuple-element.61), channel_id=1, source_target_pairs={{0,4},{1,5},{2,6},{3,7},{4,0},{5,1},{6,2},{7,3},{8,12},{9,13},{10,... | collective-permute-start | bytes 442376 | tf_op jit(solution)/shard_map/ppermute | solution.py:485
  87.2 7.8 %collective-permute-start.11 = (bf16[8,12672]{1,0:T(8,128)(2,1)S(1)}, bf16[8,12672]{1,0:T(8,128)(2,1)S(1)}, u32[]{:S(2)}, u32[]{:S(2)}) collective-permute-start(bf16[8,12672]{1,0:T(8,128)(2,1)S(1)} %get-tuple-element.65), channel_id=1, source_target_pairs={{1,0},{0,1},{3,2},{2,3},{5,4},{4,5},{7,6},{6,7},{9,8},{8,9},{11,10... | collective-permute-start | bytes 608264 | tf_op jit(solution)/shard_map/ppermute | solution.py:481
  88.5 10.1 %collective-permute-start.12 = (bf16[8,12672]{1,0:T(8,128)(2,1)S(1)}, bf16[8,12672]{1,0:T(8,128)(2,1)S(1)}, u32[]{:S(2)}, u32[]{:S(2)}) collective-permute-start(bf16[8,12672]{1,0:T(8,128)(2,1)S(1)} %get-tuple-element.66), channel_id=1, source_target_pairs={{2,0},{3,1},{0,2},{1,3},{6,4},{7,5},{4,6},{5,7},{10,8},{11,9},{8,1... | collective-permute-start | bytes 608264 | tf_op jit(solution)/shard_map/ppermute | solution.py:481
  88.5 10.9 %collective-permute-start.13 = (bf16[8,12672]{1,0:T(8,128)(2,1)S(1)}, bf16[8,12672]{1,0:T(8,128)(2,1)S(1)}, u32[]{:S(2)}, u32[]{:S(2)}) collective-permute-start(bf16[8,12672]{1,0:T(8,128)(2,1)S(1)} %get-tuple-element.67), channel_id=1, source_target_pairs={{3,0},{2,1},{1,2},{0,3},{7,4},{6,5},{5,6},{4,7},{11,8},{10,9},{9,1... | collective-permute-start | bytes 608264 | tf_op jit(solution)/shard_map/ppermute | solution.py:481
  93.3 7.4 %copy-start = (f32[896,1024]{1,0:T(8,128)}, f32[896,1024]{1,0:T(8,128)S(1)}, u32[]{:S(2)}) copy-start(f32[896,1024]{1,0:T(8,128)S(1)} %get-tuple-element.75.refs_0_.refs_6_) | copy-start | bytes 11010052
  93.3 5.2 %collective-permute-start.22 = (bf16[72,1024]{1,0:T(8,128)(2,1)S(1)}, bf16[72,1024]{1,0:T(8,128)(2,1)S(1)}, u32[]{:S(2)}, u32[]{:S(2)}) collective-permute-start(bf16[72,1024]{1,0:T(8,128)(2,1)S(1)} %get-tuple-element.82.refs_2_), channel_id=1, source_target_pairs={{16,0},{24,8},{0,16},{8,24},{17,1},{25,9},{1,17},{9,25},{18,2},{26... | collective-permute-start | bytes 442376 | tf_op jit(solution)/shard_map/ppermute | solution.py:491
  94.9 19.8 %collective-permute-start.21 = (bf16[72,1024]{1,0:T(8,128)(2,1)S(1)}, bf16[72,1024]{1,0:T(8,128)(2,1)}, u32[]{:S(2)}, u32[]{:S(2)}) collective-permute-start(bf16[72,1024]{1,0:T(8,128)(2,1)S(1)} %get-tuple-element.82.refs_2_), channel_id=1, source_target_pairs={{8,0},{0,8},{24,16},{16,24},{9,1},{1,9},{25,17},{17,25},{10,2},{2,... | collective-permute-start | bytes 442376 | tf_op jit(solution)/shard_map/ppermute | solution.py:491
  98.5 16.2 %collective-permute-start.23 = (bf16[72,1024]{1,0:T(8,128)(2,1)S(1)}, bf16[72,1024]{1,0:T(8,128)(2,1)}, u32[]{:S(2)}, u32[]{:S(2)}) collective-permute-start(bf16[72,1024]{1,0:T(8,128)(2,1)S(1)} %collective-permute-done.22.refs_4_), channel_id=1, source_target_pairs={{8,0},{0,8},{24,16},{16,24},{9,1},{1,9},{25,17},{17,25},{10,2},{2,... | collective-permute-start | bytes 442376 | tf_op jit(solution)/shard_map/ppermute | solution.py:491
  99.4 11.3 %copy-start.9 = (s32[128]{0:T(128)S(1)}, s32[128]{0:T(128)}, u32[]{:S(2)}) copy-start(s32[128]{0:T(128)} %param.10) | copy-start | bytes 1540
  99.4 11.3 %copy-start.10 = (f32[128]{0:T(128)S(1)}, f32[128]{0:T(128)}, u32[]{:S(2)}) copy-start(f32[128]{0:T(128)} %param.8) | copy-start | bytes 1540
  100.7 0.7 copy-start.6
  101.4 5.8 %collective-permute-start.18 = (bf16[8,8064]{1,0:T(8,128)(2,1)}, bf16[8,8064]{1,0:T(8,128)(2,1)}, u32[]{:S(2)}, u32[]{:S(2)}) collective-permute-start(bf16[8,8064]{1,0:T(8,128)(2,1)} %get-tuple-element.77), channel_id=1, source_target_pairs={{1,0},{0,1},{3,2},{2,3},{5,4},{4,5},{7,6},{6,7},{9,8},{8,9},{11,10... | collective-permute-start | bytes 387080 | tf_op jit(solution)/shard_map/ppermute | solution.py:481
  103.0 6.1 %collective-permute-start.19 = (bf16[8,8064]{1,0:T(8,128)(2,1)}, bf16[8,8064]{1,0:T(8,128)(2,1)}, u32[]{:S(2)}, u32[]{:S(2)}) collective-permute-start(bf16[8,8064]{1,0:T(8,128)(2,1)} %get-tuple-element.78), channel_id=1, source_target_pairs={{2,0},{3,1},{0,2},{1,3},{6,4},{7,5},{4,6},{5,7},{10,8},{11,9},{8,1... | collective-permute-start | bytes 387080 | tf_op jit(solution)/shard_map/ppermute | solution.py:481
  103.3 7.4 %collective-permute-start.20 = (bf16[8,8064]{1,0:T(8,128)(2,1)}, bf16[8,8064]{1,0:T(8,128)(2,1)}, u32[]{:S(2)}, u32[]{:S(2)}) collective-permute-start(bf16[8,8064]{1,0:T(8,128)(2,1)} %get-tuple-element.79), channel_id=1, source_target_pairs={{3,0},{2,1},{1,2},{0,3},{7,4},{6,5},{5,6},{4,7},{11,8},{10,9},{9,1... | collective-permute-start | bytes 387080 | tf_op jit(solution)/shard_map/ppermute | solution.py:481
  110.7 0.9 copy-start.7
  114.7 2.0 %copy-start.1 = (f32[896,1024]{1,0:T(8,128)S(1)}, f32[896,1024]{1,0:T(8,128)}, u32[]{:S(2)}) copy-start(f32[896,1024]{1,0:T(8,128)} %copy-done) | copy-start | bytes 11010052

commit v4 on v3

--- a/solution.py
+++ b/solution.py
@@ -220,12 +220,6 @@
     place(scaled, plan.DX)
 
 
-def pass_kernel(plan, *refs):
-    count = plan.half - 2
-    for source, target in zip(refs[:count], refs[-count:]):
-        target[...] = source[...]
-
-
 def hold_kernel(plan, weight_hbm, held, sem):
     copy = pltpu.make_async_copy(weight_hbm.at[0], held, sem)
     copy.start()
@@ -238,12 +232,10 @@
 
 def columns_kernel(plan, *refs):
     near, outs, held = refs[: plan.half], refs[-plan.groups - 1 : -1], refs[-1]
-    for i in range(2):
-        held[i] = unfold(plan, blocks_of(near, 0, plan.DX, i * SUB), plan.D)
+    held[...] = unfold(plan, blocks_of(near, 0, plan.DX), plan.D)
     for m in range(plan.groups):
         start = pl.multiple_of(plan.group_at(lax.axis_index("dp"), m) * plan.share, LANES)
-        for i in range(2):
-            outs[m][i] = held[i, :, pl.ds(start, plan.share)]
+        outs[m][...] = held[:, pl.ds(start, plan.share)]
 
 
 def activate(preact, scaled):
@@ -263,11 +255,12 @@
 
 def near_kernel(plan, placement_ref, weight_ref, *refs):
     near = refs[: plan.half]
-    back_near, local_back, local_act, folded_grad, grads = refs[-5:]
+    back_near, local_back, local_act, folded_grad, grads, far_rows = refs[-6:]
     x_near = unfold(plan, blocks_of(near, 0, plan.DX), plan.D)
     x_far = unfold(plan, blocks_of(near, 0, plan.DX, SUB), plan.D)
     g_near = unfold(plan, blocks_of(near, plan.DX, plan.C), plan.F)
     g_far = unfold(plan, blocks_of(near, plan.DX, plan.C, SUB), plan.F)
+    far_rows[...] = x_far
     x = jnp.concatenate([x_near.astype(F32), x_far.astype(F32)], axis=0).astype(BF16)
     g = jnp.concatenate([g_near.astype(F32), g_far.astype(F32)], axis=0).astype(BF16)
     act, grad_pre = activate(dot(x, weight_ref[...]), g)
@@ -285,46 +278,53 @@
 
 
 def payload_kernel(
-    plan, placement_ref, weight_ref, folded_grad, near_grads, *refs
+    sizes, plan, placement_ref, weight_ref, folded_grad, near_grads, far_rows, *refs
 ):
     half, groups = plan.half, plan.groups
     far, refs = refs[:half], refs[half:]
     columns, refs = refs[:groups], refs[groups:]
-    small, large, refs = refs[0], refs[1], refs[2:]
-    share, refs = refs[:groups], refs[groups:]
-    (rows,) = refs
+    small, large, refs = refs[0], refs[1 : 1 + len(sizes)], refs[1 + len(sizes) :]
+    shared, rows = refs[:groups], refs[groups]
     hot = is_hot(plan, placement_ref)
-    width = plan.share
     x = unfold(plan, blocks_of(far, 0, plan.DX), plan.D)
     g = unfold(plan, blocks_of(far, plan.DX, plan.C), plan.F)
     rows[...] = x
     act, grad_pre = activate(dot(x, weight_ref[...]), g)
 
+    def store(data, start, stop):
+        low = 0
+        for out, size in zip(large, sizes):
+            out[:, start:stop] = data[low : low + size].astype(BF16)
+            low += size
+
     @pl.when(jnp.logical_not(hot))
     def _():
-        back = dot_nt(grad_pre, weight_ref[...])
-        large[...] = fold(plan, back).astype(BF16)
+        folded = fold(plan, dot_nt(grad_pre, weight_ref[...]))
+        store(jnp.concatenate([folded[SUB:], folded[:SUB]], axis=0), 0, plan.DX)
         small[...] = fold(plan, act.astype(F32)).astype(BF16)
 
     @pl.when(hot)
     def _():
-        together = jnp.concatenate([c[0].astype(F32) for c in columns], axis=0)
+        together = jnp.concatenate([c[...].astype(F32) for c in columns], axis=0)
         block = half * SUB
         for i in range(plan.pieces):
-            large[:, i * plan.share : (i + 1) * plan.share] = together[
-                i * block : (i + 1) * block
-            ].astype(BF16)
+            store(
+                together[i * block : (i + 1) * block], i * plan.share, (i + 1) * plan.share
+            )
         small[...] = folded_grad[...]
 
     group = lax.axis_index("dp")
-    for o in range(groups):
-        start = pl.multiple_of(plan.group_at(group, o) * width, LANES)
-        share[o][:, :width] = rows[:, pl.ds(start, width)]
-        share[o][:, width : width + 2 * plan.F] = near_grads[...]
-        share[o][:, width + 2 * plan.F :] = grad_pre
-
-
-def after_small_kernel(plan, placement_ref, small, local_act, near_back, *outs):
+    width = plan.share
+    for m in range(groups):
+        start = pl.multiple_of(plan.group_at(group, m) * width, LANES)
+        shared[m][:, :width] = far_rows[:, pl.ds(start, width)]
+        shared[m][:, width : 2 * width] = rows[:, pl.ds(start, width)]
+        shared[m][:, 2 * width : 2 * width + 2 * plan.F] = near_grads[...]
+        shared[m][:, 2 * width + 2 * plan.F :] = grad_pre
+
+
+def after_small_kernel(plan, placement_ref, small, local_act, near_back, waiting, *outs):
+    outs[plan.half + 1][...] = waiting[...]
     hot = is_hot(plan, placement_ref)
     payload = small[...].astype(F32)
     chosen = jnp.where(hot, local_act[...].astype(F32), payload)
@@ -337,11 +337,15 @@
     outs[plan.half][...] = jnp.where(hot, unfold(plan, blocks, plan.F).astype(F32), 0.0).astype(BF16)
 
 
-def after_large_kernel(plan, placement_ref, large, local_back, *refs):
-    outs = refs[-plan.half :]
+def after_large_kernel(first, passing, plan, placement_ref, large, local_back, *refs):
+    count = large.shape[0] // SUB
+    outs = refs[-count - passing :]
+    for source, target in zip(refs[:passing], outs[count:]):
+        target[...] = source[...]
     hot = is_hot(plan, placement_ref)
-    chosen = jnp.where(hot, local_back[...].astype(F32), large[...].astype(F32))
-    for m in range(plan.half):
+    local = local_back[...].astype(F32)[first * SUB : (first + count) * SUB]
+    chosen = jnp.where(hot, local, large[...].astype(F32))
+    for m in range(count):
         outs[m][...] = chosen[m * SUB : (m + 1) * SUB].astype(BF16)
 
 
@@ -384,11 +388,11 @@
     return jnp.concatenate([p.astype(F32) for p in parts], axis=0).astype(BF16)
 
 
-def gather_kernel(plan, weight_hbm, momentum_hbm, waiting, *refs):
+def gather_kernel(plan, weight_hbm, momentum_hbm, *refs):
     groups, share, width = plan.groups, plan.share, plan.F
     columns, refs = refs[:groups], refs[groups:]
     shared, refs = refs[:groups], refs[groups:]
-    total, old_weight, passed, x_all, momentum, sems = refs
+    total, old_weight, x_all, momentum, sems = refs
     mine = pl.multiple_of(lax.axis_index("dp") * share, LANES)
     copies = [
         pltpu.make_async_copy(momentum_hbm.at[0], momentum, sems.at[0]),
@@ -396,11 +400,12 @@
     ]
     for copy in copies:
         copy.start()
-    passed[...] = waiting[...]
+    base = 2 * share
     x_parts, g_parts = [], []
     for m in range(groups):
-        x_parts += [columns[m][0], columns[m][1], shared[m][:, :share]]
-        g_parts += [shared[m][:, share + i * width : share + (i + 1) * width] for i in range(3)]
+        x_parts.append(columns[m][...])
+        x_parts += [shared[m][:, i * share : (i + 1) * share] for i in range(2)]
+        g_parts += [shared[m][:, base + i * width : base + (i + 1) * width] for i in range(3)]
     x_all[...] = rows_of(x_parts)
     g_all = rows_of(g_parts)
     for copy in copies:
@@ -411,7 +416,8 @@
         total[span, :] = before + dot_tn(x_all[:, span], g_all)
 
 
-def update_kernel(plan, placement_ref, large, *refs):
+def update_kernel(plan, count, placement_ref, *refs):
+    large, refs = refs[:count], refs[count:]
     other_g, refs = refs[: plan.groups], refs[plan.groups :]
     total_ref, weight_ref, new_weight, new_momentum, x_all, g_all = refs
     step = pl.program_id(0)
@@ -422,7 +428,9 @@
     def _():
         hot = is_hot(plan, placement_ref)
         pieces = [
-            large[:, i * share : (i + 1) * share].astype(F32) for i in range(plan.pieces)
+            block[:, i * share : (i + 1) * share].astype(F32)
+            for i in range(plan.pieces)
+            for block in large
         ]
         x_all[...] = jnp.where(hot, jnp.concatenate(pieces, axis=0), 0.0).astype(BF16)
         g_all[...] = rows_of([g[...] for g in other_g])
@@ -461,7 +469,7 @@
 
 
 def routed(plan, tokens, route_weight, cotangent, slot_ids, placement, weight, momentum):
-    half, groups, outer = plan.half, plan.groups, plan.outer
+    half, groups = plan.half, plan.groups
     D, F, C, rows, share = plan.D, plan.F, plan.C, plan.rows, plan.share
     slot = slot_ids.reshape(1, -1)
     gate = route_weight.reshape(1, -1)
@@ -490,15 +498,10 @@
             pairs.append((plan.group_at(d, m), d))
         return lax.ppermute(data, "dp", pairs)
 
-    def from_chips(per_chip):
-        got = [per_chip[0]]
-        for o in range(1, outer):
-            sent = o if outer & (outer - 1) == 0 else outer - o
-            got.append(from_group(per_chip[sent], INNER * o))
-        return got
-
-    def with_sisters(got):
-        return [data for own in got for data in (own, from_group(own, 1))]
+    def from_groups(per_group):
+        return [per_group[0]] + [
+            from_group(per_group[plan.group_from(m)], m) for m in range(1, groups)
+        ]
 
     packed = call(
         pack_kernel,
@@ -518,18 +521,7 @@
         limit=60,
     )
     near = [packed[0]] + [to_slot(packed[m], m) for m in range(1, half)]
-    far = [to_slot(packed[half + m], m, 1) for m in range(2)]
-    later = call(
-        pass_kernel,
-        plan,
-        list(packed[half + 2 :]) + far[:1],
-        [VMEM_SPEC] * (half - 2) + [ANY_SPEC],
-        [(SUB, C)] * (half - 2),
-        [],
-        0,
-        "pass_on",
-    )
-    far += [to_slot(later[m - 2], m, 1) for m in range(2, half)]
+    far = [to_slot(packed[half + m], m, 1) for m in range(half)]
     (held,) = call(
         hold_kernel,
         plan,
@@ -544,64 +536,86 @@
     columns = call(
         columns_kernel,
         plan,
-        near + [held] + [later[0], far[1]],
-        [VMEM_SPEC] * half + [ANY_SPEC] * 3,
-        [(2, rows, share)] * groups,
-        [pltpu.VMEM((2, rows, D), BF16)],
+        near,
+        [VMEM_SPEC] * half,
+        [(rows, share)] * groups,
+        [pltpu.VMEM((rows, D), BF16)],
         0,
         "near_columns",
     )
-    columns_here = [columns[0]] + [
-        from_group(columns[plan.group_from(m)], m) for m in range(1, groups)
-    ]
-    back_near, local_back, local_act, folded_grad, grads = call(
+    columns_here = from_groups(columns)
+    back_near, local_back, local_act, folded_grad, grads, far_rows = call(
         near_kernel,
         plan,
-        [placement, held] + near + [columns[0], far[2]],
-        [SMEM_SPEC] + [VMEM_SPEC] * (1 + half) + [ANY_SPEC] * 2,
+        [placement, held] + near + [columns[0]],
+        [SMEM_SPEC] + [VMEM_SPEC] * (1 + half) + [ANY_SPEC],
         [
             (half * SUB, C),
             (half * SUB, plan.DX),
             (half * SUB, plan.FG),
             (half * SUB, plan.FG),
             (rows, 2 * F),
+            (rows, D),
         ],
         [],
         8 * rows * D * F,
         "near_rows",
     )
+    sizes = [SUB] * half
     outs = call(
-        payload_kernel,
+        functools.partial(payload_kernel, sizes),
         plan,
-        [placement, held, folded_grad, grads] + far + columns_here,
-        [SMEM_SPEC] + [VMEM_SPEC] * (3 + half + groups),
-        [(half * SUB, plan.FG), (half * SUB, plan.DX)]
-        + [(rows, share + 3 * F)] * groups,
+        [placement, held, folded_grad, grads, far_rows] + far + columns_here,
+        [SMEM_SPEC] + [VMEM_SPEC] * (4 + half + groups),
+        [(half * SUB, plan.FG)]
+        + [(size, plan.DX) for size in sizes]
+        + [(rows, 2 * share + 3 * F)] * groups,
         [pltpu.VMEM((rows, D), BF16)],
         4 * rows * D * F,
         "payload",
     )
     small = to_partner(outs[0])
-    large = to_partner(outs[1])
-    shared = outs[2 : 2 + groups]
-    shared = [shared[0]] + [from_group(shared[plan.group_from(m)], m) for m in range(1, groups)]
+    large = [to_partner(outs[1])]
+    waiting = outs[2 : 1 + half]
+    shared = from_groups(outs[1 + half :])
     outs = call(
         after_small_kernel,
         plan,
-        [placement, small, local_act, back_near],
-        [SMEM_SPEC] + [VMEM_SPEC] * 3,
-        [(SUB, C + plan.FG)] * half + [(rows, F)],
+        [placement, small, local_act, back_near, waiting[0]],
+        [SMEM_SPEC] + [VMEM_SPEC] * 4,
+        [(SUB, C + plan.FG)] * half + [(rows, F), (sizes[1], plan.DX)],
         [],
         0,
         "after_small",
     )
     early = [outs[0]] + [to_source(outs[m], m) for m in range(1, half)]
-    total, old_weight, passed = call(
+    large.append(to_partner(outs[half + 1]))
+    other_g = from_groups([outs[half]] * groups)
+
+    def after_large(first, data, passing, before):
+        count = data.shape[0] // SUB
+        return call(
+            functools.partial(after_large_kernel, first, len(passing)),
+            plan,
+            [placement, data, local_back] + passing + before,
+            [SMEM_SPEC] + [VMEM_SPEC] * (2 + len(passing)) + [ANY_SPEC] * len(before),
+            [(SUB, plan.DX)] * count + [p.shape for p in passing],
+            [],
+            0,
+            "after_large",
+        )
+
+    far_back = []
+    for i in range(half - 2):
+        outs = after_large(i + 1, large[i], [waiting[i + 1]], [])
+        large.append(to_partner(outs[1]))
+        far_back.append(to_source(outs[0], i + 1))
+    total, old_weight = call(
         gather_kernel,
         plan,
-        [weight, momentum, outs[half]] + columns_here + shared,
-        [ANY_SPEC] * 2 + [VMEM_SPEC] * (1 + 2 * groups),
-        [(share, F), (share, F), (rows, F)],
+        [weight, momentum] + columns_here + shared,
+        [ANY_SPEC] * 2 + [VMEM_SPEC] * (2 * groups),
+        [(share, F)] * 2,
         [
             pltpu.VMEM((3 * groups * rows, share), BF16),
             pltpu.VMEM((share, F), BF16),
@@ -610,21 +624,12 @@
         0,
         "own_terms",
         limit=24,
-        dtypes=[F32, BF16, BF16],
-    )
-    other_g = with_sisters(from_chips([passed] * outer))
-    first = [total] + early[1:]
-    outs = call(
-        after_large_kernel,
-        plan,
-        [placement, large, local_back] + first,
-        [SMEM_SPEC] + [VMEM_SPEC] * 2 + [ANY_SPEC] * len(first),
-        [(SUB, plan.DX)] * half,
-        [],
-        1000000,
-        "after_large",
-    )
-    far_back = [outs[0]] + [to_source(outs[m], m) for m in range(1, half)]
+        dtypes=[F32, BF16],
+    )
+    outs = after_large(half - 1, large[-2], [], [])
+    far_back.append(to_source(outs[0], half - 1))
+    outs = after_large(0, large[-1], [], [total] + early[1:])
+    far_back = [outs[0]] + far_back
 
     tile = LANES
     steps = share // tile
@@ -634,12 +639,13 @@
         return pl.BlockSpec(shape, lambda i, g: (0,) * len(shape))
 
     new_weight, new_momentum = pl.pallas_call(
-        lambda g_ref, *refs: update_kernel(plan, *refs),
+        lambda g_ref, *refs: update_kernel(plan, len(sizes), *refs),
         grid_spec=pltpu.PrefetchScalarGridSpec(
             num_scalar_prefetch=1,
             grid=(steps,),
-            in_specs=[SMEM_SPEC, whole(half * SUB, plan.DX)]
-            + [whole(rows, F)] * groups
+            in_specs=[SMEM_SPEC]
+            + [whole(size, plan.DX) for size in sizes]
+            + [whole(*g.shape) for g in other_g]
             + [
                 pl.BlockSpec((tile, F), lambda i, g: (i, 0)),
                 pl.BlockSpec((tile, F), lambda i, g: (i, 0)),
@@ -656,7 +662,7 @@
             flops=2 * groups * rows * share * F, bytes_accessed=12 * share * F, transcendentals=0
         ),
         name="update",
-    )(group, placement, large, *other_g, total, old_weight)
+    )(group, placement, *large, *other_g, total, old_weight)
 
     expert_out, token_grad = call(
         unpack_kernel,

time: 123 us -> 122 us (level); the launches traced: 122 us -> 120 us
  waiting for transfers between devices: 60.4 us -> 24.5 us
  starting transfers between devices: 28.3 us -> 48.9 us
  local copies, waits for them, and re-layouts: 5.45 us -> 14.4 us
  Pallas kernels: 27.5 us -> 31.2 us
    ppermute x2 -> x5, waiting for transfers between devices: 29.6 us -> 11.9 us  [to_partner(): return lax.ppermute(data, 'expert', pairs)]
    ppermute x6, starting transfers between devices: 6.98 us -> 17.3 us  [to_source(): return lax.ppermute(data, 'expert', pairs)]
    unnamed x26 -> x56, local copies, waits for them, and re-layouts: 5.45 us -> 14.4 us
    ppermute x7, waiting for transfers between devices: 18 us -> 9.65 us  [to_slot(): return lax.ppermute(data, 'expert', pairs)]
    ppermute x2 -> x5, starting transfers between devices: 2.92 us -> 10 us  [to_partner(): return lax.ppermute(data, 'expert', pairs)]
    ppermute x9, waiting for transfers between devices: 6.19 us -> 0.12 us  [from_group(): return lax.ppermute(data, 'dp', pairs)]
    ppermute x6, waiting for transfers between devices: 6.67 us -> 2.83 us  [to_source(): return lax.ppermute(data, 'expert', pairs)]
    pallas_call x10 -> x12, Pallas kernels: 21.8 us -> 25.3 us  [call(): pl.pallas_call(functools.partial(kernel, plan), out_shape=[jax.ShapeDtype...]
  transfers between devices with their start and end apart: 24 -> 27, of which waited for: 9 -> 10; matrix products, arithmetic and copies ran while one was open for 0% -> 0% of each run, Pallas kernels for 13% -> 18%
where the time goes in v4:
time: 122 us; the launch traced here: 120 us
  starting transfers between devices  48.9 us (40%)
  Pallas kernels  31.2 us (26%)
  waiting for transfers between devices  24.5 us (20%)
  local copies, waits for them, and re-layouts  14.4 us (12%)
    pallas_call x12, Pallas kernels, call(): pl.pallas_call(functools.partial(kernel, plan), out_shape=[jax.ShapeDtype...  25.3 us
    ppermute x6, starting transfers between devices, to_source(): return lax.ppermute(data, 'expert', pairs)  17.3 us
    ppermute x7, starting transfers between devices, to_slot(): return lax.ppermute(data, 'expert', pairs)  16.3 us
    unnamed x56, local copies, waits for them, and re-layouts  14.4 us
    ppermute x5, waiting for transfers between devices, to_partner(): return lax.ppermute(data, 'expert', pairs)  11.9 us
    ppermute x5, starting transfers between devices, to_partner(): return lax.ppermute(data, 'expert', pairs)  10 us
    ppermute x7, waiting for transfers between devices, to_slot(): return lax.ppermute(data, 'expert', pairs)  9.65 us
    pallas_call x1, Pallas kernels, routed(): pl.pallas_call(lambda g_ref, *refs: update_kernel(plan, len(sizes), *refs...  5.9 us
  transfers between devices with their start and end apart: 27, of which 10 were waited for; matrix products, arithmetic and copies ran while one was open for 0% of the time, Pallas kernels for 18%

profile of v4, /device:TPU:0, one launch (start us, length us, event | category | flops | bytes accessed | tf_op | source)
XLA Modules:
  0.0 119.9 jit_solution(1859176232044304450)
XLA Ops:
  0.6 3.4 %pack.1 = (bf16[16,10368]{1,0:T(8,128)(2,1)}, bf16[16,10368]{1,0:T(8,128)(2,1)}, bf16[16,10368]{1,0:T(8,128)(2,1)}, bf16[16,10368]{1,0:T(8,128)(2,1)}, bf16[8,10...) custom-call(s32[1,128]{1,0:T(1,128)} %bitcast.3, ...), custom_call_target="tpu_custom_call" | custom-call | flops 150994944 | bytes 3171328 | tf_op jit(solution)/shard_map/pack/pallas_call | solution.py:455
  4.0 3.0 %collective-permute-start = (bf16[16,10368]{1,0:T(8,128)(2,1)}, bf16[16,10368]{1,0:T(8,128)(2,1)S(1)}, u32[]{:S(2)}, u32[]{:S(2)}) collective-permute-start(bf16[16,10368]{1,0:T(8,128)(2,1)} %get-tuple-element.48), channel_id=1, source_target_pairs={{0,1},{1,0},{2,3},{3,2},{4,5},{5,4},{6,7},{7,6},{8,9},{9,8},{10,11... | collective-permute-start | bytes 995336 | tf_op jit(solution)/shard_map/ppermute | solution.py:482
  7.0 1.6 %collective-permute-start.1 = (bf16[16,10368]{1,0:T(8,128)(2,1)}, bf16[16,10368]{1,0:T(8,128)(2,1)S(1)}, u32[]{:S(2)}, u32[]{:S(2)}) collective-permute-start(bf16[16,10368]{1,0:T(8,128)(2,1)} %get-tuple-element.49), channel_id=1, source_target_pairs={{0,2},{1,3},{2,0},{3,1},{4,6},{5,7},{6,4},{7,5},{8,10},{9,11},{10,... | collective-permute-start | bytes 995336 | tf_op jit(solution)/shard_map/ppermute | solution.py:482
  8.6 3.0 %collective-permute-start.3 = (bf16[8,10368]{1,0:T(8,128)(2,1)}, bf16[8,10368]{1,0:T(8,128)(2,1)S(1)}, u32[]{:S(2)}, u32[]{:S(2)}) collective-permute-start(bf16[8,10368]{1,0:T(8,128)(2,1)} %get-tuple-element.55), channel_id=1, source_target_pairs={{0,4},{1,5},{2,6},{3,7},{4,0},{5,1},{6,2},{7,3},{8,12},{9,13},{10,... | collective-permute-start | bytes 497672 | tf_op jit(solution)/shard_map/ppermute | solution.py:482
  11.6 1.3 %collective-permute-start.4 = (bf16[8,10368]{1,0:T(8,128)(2,1)}, bf16[8,10368]{1,0:T(8,128)(2,1)S(1)}, u32[]{:S(2)}, u32[]{:S(2)}) collective-permute-start(bf16[8,10368]{1,0:T(8,128)(2,1)} %get-tuple-element.56), channel_id=1, source_target_pairs={{0,5},{1,4},{2,7},{3,6},{4,1},{5,0},{6,3},{7,2},{8,13},{9,12},{10,... | collective-permute-start | bytes 497672 | tf_op jit(solution)/shard_map/ppermute | solution.py:482
  13.0 3.1 %hold.1.weight_ref = bf16[3584,1024]{1,0:T(8,128)(2,1)S(1)} custom-call(bf16[1,3584,1024]{2,1,0:T(8,128)(2,1)} %weight_hbm.3), custom_call_target="tpu_custom_call" | custom-call | tf_op jit(solution)/shard_map/hold/pallas_call | solution.py:455
  16.1 3.8 %collective-permute-start.5 = (bf16[8,10368]{1,0:T(8,128)(2,1)S(1)}, bf16[8,10368]{1,0:T(8,128)(2,1)S(1)}, u32[]{:S(2)}, u32[]{:S(2)}) collective-permute-start(bf16[8,10368]{1,0:T(8,128)(2,1)S(1)} %copy-done.27), channel_id=1, source_target_pairs={{0,6},{1,7},{2,4},{3,5},{4,2},{5,3},{6,0},{7,1},{8,14},{9,15},{10,... | collective-permute-start | bytes 497672 | tf_op jit(solution)/shard_map/ppermute | solution.py:482
  19.9 5.2 %collective-permute-done.1.refs_2_ = bf16[16,10368]{1,0:T(8,128)(2,1)S(1)} collective-permute-done((bf16[16,10368]{1,0:T(8,128)(2,1)}, bf16[16,10368]{1,0:T(8,128)(2,1)S(1)}, u32[]{:S(2)}, u32[]{:S(2)}) %collective-permute-start.1) | collective-permute-done | bytes 331808 | tf_op jit(solution)/shard_map/ppermute | solution.py:482
  25.1 3.6 %collective-permute-start.6 = (bf16[8,10368]{1,0:T(8,128)(2,1)S(1)}, bf16[8,10368]{1,0:T(8,128)(2,1)S(1)}, u32[]{:S(2)}, u32[]{:S(2)}) collective-permute-start(bf16[8,10368]{1,0:T(8,128)(2,1)S(1)} %copy-done.26), channel_id=1, source_target_pairs={{0,7},{1,6},{2,5},{3,4},{4,3},{5,2},{6,1},{7,0},{8,15},{9,14},{10,... | collective-permute-start | bytes 497672 | tf_op jit(solution)/shard_map/ppermute | solution.py:482
  28.6 1.9 %collective-permute-done.2.refs_3_ = bf16[16,10368]{1,0:T(8,128)(2,1)S(1)} collective-permute-done((bf16[16,10368]{1,0:T(8,128)(2,1)}, bf16[16,10368]{1,0:T(8,128)(2,1)S(1)}, u32[]{:S(2)}, u32[]{:S(2)}) %collective-permute-start.2) | collective-permute-done | bytes 331808 | tf_op jit(solution)/shard_map/ppermute | solution.py:482
  30.8 1.8 %collective-permute-start.8 = (bf16[72,896]{1,0:T(8,128)(2,1)S(1)}, bf16[72,896]{1,0:T(8,128)(2,1)S(1)}, u32[]{:S(2)}, u32[]{:S(2)}) collective-permute-start(bf16[72,896]{1,0:T(8,128)(2,1)S(1)} %get-tuple-element.60), channel_id=1, source_target_pairs={{16,0},{24,8},{0,16},{8,24},{17,1},{25,9},{1,17},{9,25},{18,2},{26... | collective-permute-start | bytes 387080 | tf_op jit(solution)/shard_map/ppermute | solution.py:499
  32.7 4.7 %near_rows.1 = (bf16[32,10368]{1,0:T(8,128)(2,1)S(1)}, bf16[32,8064]{1,0:T(8,128)(2,1)S(1)}, bf16[32,2304]{1,0:T(8,128)(2,1)S(1)}, bf16[32,2304]{1,0:T(8,128)(2,...) custom-call(s32[8]{0:T(128)S(1)} %copy-done.23, bf16[3584,1024]{1,0:T(8,128)(2,1)S(1)} %hold.1.weight_ref, ...), custom_call_target="tpu_custom_call" | custom-call | flops 2113929216 | bytes 11081760 | tf_op jit(solution)/shard_map/near_rows/pallas_call | solution.py:455
  37.9 2.1 %collective-permute-done.6.refs_3_ = bf16[8,10368]{1,0:T(8,128)(2,1)S(1)} collective-permute-done((bf16[8,10368]{1,0:T(8,128)(2,1)S(1)}, bf16[8,10368]{1,0:T(8,128)(2,1)S(1)}, u32[]{:S(2)}, u32[]{:S(2)}) %collective-permute-start.6) | collective-permute-done | bytes 165920 | tf_op jit(solution)/shard_map/ppermute | solution.py:482
  40.0 2.5 %payload.1 = (bf16[32,2304]{1,0:T(8,128)(2,1)S(1)}, bf16[8,8064]{1,0:T(8,128)(2,1)S(1)}, bf16[8,8064]{1,0:T(8,128)(2,1)S(1)}, bf16[8,8064]{1,0:T(8,128)(2,1)S(1)...) custom-call(s32[8]{0:T(128)S(1)} %copy-done.23, ...), custom_call_target="tpu_custom_call" | custom-call | flops 1056964608 | bytes 12943392 | tf_op jit(solution)/shard_map/payload/pallas_call | solution.py:455
  43.1 3.9 %collective-permute-start.19 = (bf16[8,8064]{1,0:T(8,128)(2,1)S(1)}, bf16[8,8064]{1,0:T(8,128)(2,1)S(1)}, u32[]{:S(2)}, u32[]{:S(2)}) collective-permute-start(bf16[8,8064]{1,0:T(8,128)(2,1)S(1)} %get-tuple-element.79), channel_id=1, source_target_pairs={{0,4},{1,5},{2,6},{3,7},{4,0},{5,1},{6,2},{7,3},{8,12},{9,13},{10,... | collective-permute-start | bytes 387080 | tf_op jit(solution)/shard_map/ppermute | solution.py:493
  47.1 1.5 %collective-permute-start.17 = (bf16[72,4864]{1,0:T(8,128)(2,1)S(1)}, bf16[72,4864]{1,0:T(8,128)(2,1)S(1)}, u32[]{:S(2)}, u32[]{:S(2)}) collective-permute-start(bf16[72,4864]{1,0:T(8,128)(2,1)S(1)} %get-tuple-element.76), channel_id=1, source_target_pairs={{16,0},{24,8},{0,16},{8,24},{17,1},{25,9},{1,17},{9,25},{18,2},{26... | collective-permute-start | bytes 2101256 | tf_op jit(solution)/shard_map/ppermute | solution.py:499
  49.0 2.1 %collective-permute-done.19.large.refs_1_ = bf16[8,8064]{1,0:T(8,128)(2,1)S(1)} collective-permute-done((bf16[8,8064]{1,0:T(8,128)(2,1)S(1)}, bf16[8,8064]{1,0:T(8,128)(2,1)S(1)}, u32[]{:S(2)}, u32[]{:S(2)}) %collective-permute-start.19) | collective-permute-done | bytes 129056 | tf_op jit(solution)/shard_map/ppermute | solution.py:493
  51.0 1.2 %after_large.6 = (bf16[8,8064]{1,0:T(8,128)(2,1)}, bf16[8,8064]{1,0:T(8,128)(2,1)S(1)}) custom-call(s32[8]{0:T(128)S(1)} %copy-done.23, bf16[8,8064]{1,0:T(8,128)(2,1)S(1)} %collective-permute-done.19.large.refs_1_, bf16[32,8064]{1,0:T(8,128)(2,1)S(1)} %get-tuple-element.71.local_back, bf16[8,8064]{1,0:T(8,128)(2,1)S(1)} %get-tuple-element.80.refs_0_), custom_call_target="tpu_custom_call" | custom-call | tf_op jit(solution)/shard_map/after_large/pallas_call | solution.py:455
  52.3 3.2 %collective-permute-start.22 = (bf16[8,8064]{1,0:T(8,128)(2,1)S(1)}, bf16[8,8064]{1,0:T(8,128)(2,1)S(1)}, u32[]{:S(2)}, u32[]{:S(2)}) collective-permute-start(bf16[8,8064]{1,0:T(8,128)(2,1)S(1)} %get-tuple-element.83), channel_id=1, source_target_pairs={{0,4},{1,5},{2,6},{3,7},{4,0},{5,1},{6,2},{7,3},{8,12},{9,13},{10,... | collective-permute-start | bytes 387080 | tf_op jit(solution)/shard_map/ppermute | solution.py:493
  55.5 1.4 %after_small.1 = (bf16[8,12672]{1,0:T(8,128)(2,1)S(1)}, bf16[8,12672]{1,0:T(8,128)(2,1)S(1)}, bf16[8,12672]{1,0:T(8,128)(2,1)S(1)}, bf16[8,12672]{1,0:T(8,128)(2...) custom-call(s32[8]{0:T(128)S(1)} %copy-done.23, bf16[32,2304]{1,0:T(8,128)(2,1)S(1)} %collective-permute-done.10.small, ...), custom_call_target="tpu_custom_call" | custom-call | tf_op jit(solution)/shard_map/after_small/pallas_call | solution.py:455
  56.9 1.0 collective-permute-start.14
  57.9 7.3 %collective-permute-done.22.large.refs_3_ = bf16[8,8064]{1,0:T(8,128)(2,1)S(1)} collective-permute-done((bf16[8,8064]{1,0:T(8,128)(2,1)S(1)}, bf16[8,8064]{1,0:T(8,128)(2,1)S(1)}, u32[]{:S(2)}, u32[]{:S(2)}) %collective-permute-start.22) | collective-permute-done | bytes 129056 | tf_op jit(solution)/shard_map/ppermute | solution.py:493
  65.2 1.5 %collective-permute-done.14.large.refs_2_ = bf16[8,8064]{1,0:T(8,128)(2,1)S(1)} collective-permute-done((bf16[8,8064]{1,0:T(8,128)(2,1)S(1)}, bf16[8,8064]{1,0:T(8,128)(2,1)S(1)}, u32[]{:S(2)}, u32[]{:S(2)}) %collective-permute-start.14) | collective-permute-done | bytes 129056 | tf_op jit(solution)/shard_map/ppermute | solution.py:493
  67.4 9.3 %collective-permute-start.12 = (bf16[8,12672]{1,0:T(8,128)(2,1)S(1)}, bf16[8,12672]{1,0:T(8,128)(2,1)S(1)}, u32[]{:S(2)}, u32[]{:S(2)}) collective-permute-start(bf16[8,12672]{1,0:T(8,128)(2,1)S(1)} %get-tuple-element.68), channel_id=1, source_target_pairs={{2,0},{3,1},{0,2},{1,3},{6,4},{7,5},{4,6},{5,7},{10,8},{11,9},{8,1... | collective-permute-start | bytes 608264 | tf_op jit(solution)/shard_map/ppermute | solution.py:489
  76.7 4.5 %collective-permute-start.13 = (bf16[8,12672]{1,0:T(8,128)(2,1)S(1)}, bf16[8,12672]{1,0:T(8,128)(2,1)S(1)}, u32[]{:S(2)}, u32[]{:S(2)}) collective-permute-start(bf16[8,12672]{1,0:T(8,128)(2,1)S(1)} %get-tuple-element.69), channel_id=1, source_target_pairs={{3,0},{2,1},{1,2},{0,3},{7,4},{6,5},{5,6},{4,7},{11,8},{10,9},{9,1... | collective-permute-start | bytes 608264 | tf_op jit(solution)/shard_map/ppermute | solution.py:489
  81.2 1.2 %after_large.4 = (bf16[8,8064]{1,0:T(8,128)(2,1)}, bf16[8,8064]{1,0:T(8,128)(2,1)S(1)}) custom-call(s32[8]{0:T(128)S(1)} %copy-done.23, bf16[8,8064]{1,0:T(8,128)(2,1)S(1)} %collective-permute-done.14.large.refs_2_, bf16[32,8064]{1,0:T(8,128)(2,1)S(1)} %get-tuple-element.71.local_back, bf16[8,8064]{1,0:T(8,128)(2,1)S(1)} %get-tuple-element.72.refs_0_), custom_call_target="tpu_custom_call" | custom-call | tf_op jit(solution)/shard_map/after_large/pallas_call | solution.py:455
  82.5 1.8 %collective-permute-start.15 = (bf16[8,8064]{1,0:T(8,128)(2,1)S(1)}, bf16[8,8064]{1,0:T(8,128)(2,1)S(1)}, u32[]{:S(2)}, u32[]{:S(2)}) collective-permute-start(bf16[8,8064]{1,0:T(8,128)(2,1)S(1)} %get-tuple-element.73), channel_id=1, source_target_pairs={{0,4},{1,5},{2,6},{3,7},{4,0},{5,1},{6,2},{7,3},{8,12},{9,13},{10,... | collective-permute-start | bytes 387080 | tf_op jit(solution)/shard_map/ppermute | solution.py:493
  84.3 2.8 %collective-permute-done.13.refs_3_ = bf16[8,12672]{1,0:T(8,128)(2,1)S(1)} collective-permute-done((bf16[8,12672]{1,0:T(8,128)(2,1)S(1)}, bf16[8,12672]{1,0:T(8,128)(2,1)S(1)}, u32[]{:S(2)}, u32[]{:S(2)}) %collective-permute-start.13) | collective-permute-done | bytes 202784 | tf_op jit(solution)/shard_map/ppermute | solution.py:489
  87.1 1.5 %collective-permute-start.25 = (bf16[72,1024]{1,0:T(8,128)(2,1)}, bf16[72,1024]{1,0:T(8,128)(2,1)}, u32[]{:S(2)}, u32[]{:S(2)}) collective-permute-start(bf16[72,1024]{1,0:T(8,128)(2,1)} %get-tuple-element.86.refs_5_), channel_id=1, source_target_pairs={{16,0},{24,8},{0,16},{8,24},{17,1},{25,9},{1,17},{9,25},{18,2},{26... | collective-permute-start | bytes 442376 | tf_op jit(solution)/shard_map/ppermute | solution.py:499
  88.7 1.1 collective-permute-done.15.large.refs_4_
  89.7 1.2 %after_large.7 = bf16[8,8064]{1,0:T(8,128)(2,1)} custom-call(s32[8]{0:T(128)S(1)} %copy-done.23, bf16[8,8064]{1,0:T(8,128)(2,1)S(1)} %collective-permute-done.22.large.refs_3_, bf16[32,8064]{1,0:T(8,128)(2,1)S(1)} %get-tuple-element.71.local_back), custom_call_target="tpu_custom_call" | custom-call | tf_op jit(solution)/shard_map/after_large/pallas_call | solution.py:455
  91.0 0.8 copy-done.5
  91.8 2.0 %collective-permute-start.20 = (bf16[8,8064]{1,0:T(8,128)(2,1)}, bf16[8,8064]{1,0:T(8,128)(2,1)}, u32[]{:S(2)}, u32[]{:S(2)}) collective-permute-start(bf16[8,8064]{1,0:T(8,128)(2,1)} %get-tuple-element.81), channel_id=1, source_target_pairs={{1,0},{0,1},{3,2},{2,3},{5,4},{4,5},{7,6},{6,7},{9,8},{8,9},{11,10... | collective-permute-start | bytes 387080 | tf_op jit(solution)/shard_map/ppermute | solution.py:489
  93.8 0.8 copy-done.7
  94.7 0.7 collective-permute-start.23
  95.4 0.9 copy-done.9
  96.3 0.8 collective-permute-start.21
  97.1 3.1 %copy-done = bf16[1,3584,1024]{2,1,0:T(8,128)(2,1)S(1)} copy-done((bf16[1,3584,1024]{2,1,0:T(8,128)(2,1)S(1)}, bf16[1,3584,1024]{2,1,0:T(8,128)(2,1)}, u32[]{:S(2)}) %copy-start) | copy-done | bytes 7340056
  100.1 1.1 copy-done.4
  101.2 1.1 copy-done.6
  102.3 1.1 copy-done.8
  103.5 1.1 copy-done.10
  104.6 0.9 copy-done.12
  105.5 0.9 copy-done.14
  106.4 0.9 copy-done.16
  107.3 2.6 %own_terms.1 = (f32[896,1024]{1,0:T(8,128)S(1)}, bf16[896,1024]{1,0:T(8,128)(2,1)S(1)}) custom-call(bf16[1,3584,1024]{2,1,0:T(8,128)(2,1)S(1)} %copy-done, bf16[1,896,1024]{2,1,0:T(8,128)(2,1)S(1)} %copy-done.1, bf16[72,896]{1,0:T(8,128)(2,1)S(1)} %get-tuple-element.51.refs_4_.refs_0_, bf16[72,896]{1,0:T(8,128)(2,1)S(1)} %copy-done.12, ...), custom_call_target="tpu_custom_call" | custom-call | tf_op jit(solution)/shard_map/own_terms/pallas_call | solution.py:455
  110.8 5.9 %update.1 = (bf16[1,896,1024]{2,1,0:T(8,128)(2,1)}, bf16[1,896,1024]{2,1,0:T(8,128)(2,1)}) custom-call(s32[1]{0:T(128)} %bitcast.2.g_ref, s32[8]{0:T(128)S(1)} %copy-done.23, bf16[8,8064]{1,0:T(8,128)(2,1)S(1)} %collective-permute-done.19.large.refs_1_, bf16[8,8064]{1,0:T(8,128)(2,1)S(1)} %collective-permute-done.14.large.refs_2_, ...), custom_call_target="tpu_custom_call" | custom-call | flops 528482304 | bytes 11010048 | tf_op jit(solution)/shard_map/update/pallas_call | solution.py:641
  116.8 3.1 %unpack.1 = (bf16[128,1024]{1,0:T(8,128)(2,1)}, bf16[128,3584]{1,0:T(8,128)(2,1)}) custom-call(s32[1,128]{1,0:T(1,128)S(1)} %bitcast.4, f32[1,128]{1,0:T(1,128)S(1)} %bitcast.6, bf16[8,12672]{1,0:T(8,128)(2,1)S(1)} %copy-done.20, bf16[8,12672]{1,0:T(8,128)(2,1)S(1)} %collective-permute-done.11.refs_1_, bf16[8,12672]{1,0:T(8,128)(2,1)S(1)} %collective-permute-done.12.refs_2_, ...), custom_call_target="tpu_custom_call" | custom-call | flops 150994944 | bytes 2507776 | tf_op jit(solution)/shard_map/unpack/pallas_call | solution.py:455
  (75 shorter events, 3.7 us)
Async XLA Ops:
  4.0 12.0 %collective-permute-start = (bf16[16,10368]{1,0:T(8,128)(2,1)}, bf16[16,10368]{1,0:T(8,128)(2,1)S(1)}, u32[]{:S(2)}, u32[]{:S(2)}) collective-permute-start(bf16[16,10368]{1,0:T(8,128)(2,1)} %get-tuple-element.48), channel_id=1, source_target_pairs={{0,1},{1,0},{2,3},{3,2},{4,5},{5,4},{6,7},{7,6},{8,9},{9,8},{10,11... | collective-permute-start | bytes 995336 | tf_op jit(solution)/shard_map/ppermute | solution.py:482
  7.0 18.0 %collective-permute-start.1 = (bf16[16,10368]{1,0:T(8,128)(2,1)}, bf16[16,10368]{1,0:T(8,128)(2,1)S(1)}, u32[]{:S(2)}, u32[]{:S(2)}) collective-permute-start(bf16[16,10368]{1,0:T(8,128)(2,1)} %get-tuple-element.49), channel_id=1, source_target_pairs={{0,2},{1,3},{2,0},{3,1},{4,6},{5,7},{6,4},{7,5},{8,10},{9,11},{10,... | collective-permute-start | bytes 995336 | tf_op jit(solution)/shard_map/ppermute | solution.py:482
  8.6 21.9 %collective-permute-start.2 = (bf16[16,10368]{1,0:T(8,128)(2,1)}, bf16[16,10368]{1,0:T(8,128)(2,1)S(1)}, u32[]{:S(2)}, u32[]{:S(2)}) collective-permute-start(bf16[16,10368]{1,0:T(8,128)(2,1)} %get-tuple-element.50), channel_id=1, source_target_pairs={{0,3},{1,2},{2,1},{3,0},{4,7},{5,6},{6,5},{7,4},{8,11},{9,10},{10,... | collective-permute-start | bytes 995336 | tf_op jit(solution)/shard_map/ppermute | solution.py:482
  8.6 22.2 %collective-permute-start.3 = (bf16[8,10368]{1,0:T(8,128)(2,1)}, bf16[8,10368]{1,0:T(8,128)(2,1)S(1)}, u32[]{:S(2)}, u32[]{:S(2)}) collective-permute-start(bf16[8,10368]{1,0:T(8,128)(2,1)} %get-tuple-element.55), channel_id=1, source_target_pairs={{0,4},{1,5},{2,6},{3,7},{4,0},{5,1},{6,2},{7,3},{8,12},{9,13},{10,... | collective-permute-start | bytes 497672 | tf_op jit(solution)/shard_map/ppermute | solution.py:482
  11.6 4.5 %copy-start.27 = (bf16[8,10368]{1,0:T(8,128)(2,1)S(1)}, bf16[8,10368]{1,0:T(8,128)(2,1)}, u32[]{:S(2)}) copy-start(bf16[8,10368]{1,0:T(8,128)(2,1)} %get-tuple-element.57) | copy-start | bytes 497668
  11.6 13.5 %copy-start.26 = (bf16[8,10368]{1,0:T(8,128)(2,1)S(1)}, bf16[8,10368]{1,0:T(8,128)(2,1)}, u32[]{:S(2)}) copy-start(bf16[8,10368]{1,0:T(8,128)(2,1)} %get-tuple-element.58) | copy-start | bytes 497668
  11.6 18.9 %copy-start.2 = (bf16[16,10368]{1,0:T(8,128)(2,1)S(1)}, bf16[16,10368]{1,0:T(8,128)(2,1)}, u32[]{:S(2)}) copy-start(bf16[16,10368]{1,0:T(8,128)(2,1)} %get-tuple-element.47.refs_0_) | copy-start | bytes 995332
  11.6 21.1 %copy-start.23 = (s32[8]{0:T(128)S(1)}, s32[8]{0:T(128)}, u32[]{:S(2)}) copy-start(s32[8]{0:T(128)} %refs_0_.1) | copy-start | bytes 100
  11.6 21.0 %collective-permute-start.4 = (bf16[8,10368]{1,0:T(8,128)(2,1)}, bf16[8,10368]{1,0:T(8,128)(2,1)S(1)}, u32[]{:S(2)}, u32[]{:S(2)}) collective-permute-start(bf16[8,10368]{1,0:T(8,128)(2,1)} %get-tuple-element.56), channel_id=1, source_target_pairs={{0,5},{1,4},{2,7},{3,6},{4,1},{5,0},{6,3},{7,2},{8,13},{9,12},{10,... | collective-permute-start | bytes 497672 | tf_op jit(solution)/shard_map/ppermute | solution.py:482
  16.1 21.8 %collective-permute-start.5 = (bf16[8,10368]{1,0:T(8,128)(2,1)S(1)}, bf16[8,10368]{1,0:T(8,128)(2,1)S(1)}, u32[]{:S(2)}, u32[]{:S(2)}) collective-permute-start(bf16[8,10368]{1,0:T(8,128)(2,1)S(1)} %copy-done.27), channel_id=1, source_target_pairs={{0,6},{1,7},{2,4},{3,5},{4,2},{5,3},{6,0},{7,1},{8,14},{9,15},{10,... | collective-permute-start | bytes 497672 | tf_op jit(solution)/shard_map/ppermute | solution.py:482
  25.1 14.8 %collective-permute-start.6 = (bf16[8,10368]{1,0:T(8,128)(2,1)S(1)}, bf16[8,10368]{1,0:T(8,128)(2,1)S(1)}, u32[]{:S(2)}, u32[]{:S(2)}) collective-permute-start(bf16[8,10368]{1,0:T(8,128)(2,1)S(1)} %copy-done.26), channel_id=1, source_target_pairs={{0,7},{1,6},{2,5},{3,4},{4,3},{5,2},{6,1},{7,0},{8,15},{9,14},{10,... | collective-permute-start | bytes 497672 | tf_op jit(solution)/shard_map/ppermute | solution.py:482
  30.7 9.2 %collective-permute-start.7 = (bf16[72,896]{1,0:T(8,128)(2,1)S(1)}, bf16[72,896]{1,0:T(8,128)(2,1)S(1)}, u32[]{:S(2)}, u32[]{:S(2)}) collective-permute-start(bf16[72,896]{1,0:T(8,128)(2,1)S(1)} %get-tuple-element.59), channel_id=1, source_target_pairs={{8,0},{0,8},{24,16},{16,24},{9,1},{1,9},{25,17},{17,25},{10,2},{2,... | collective-permute-start | bytes 387080 | tf_op jit(solution)/shard_map/ppermute | solution.py:499
  30.8 9.1 %collective-permute-start.8 = (bf16[72,896]{1,0:T(8,128)(2,1)S(1)}, bf16[72,896]{1,0:T(8,128)(2,1)S(1)}, u32[]{:S(2)}, u32[]{:S(2)}) collective-permute-start(bf16[72,896]{1,0:T(8,128)(2,1)S(1)} %get-tuple-element.60), channel_id=1, source_target_pairs={{16,0},{24,8},{0,16},{8,24},{17,1},{25,9},{1,17},{9,25},{18,2},{26... | collective-permute-start | bytes 387080 | tf_op jit(solution)/shard_map/ppermute | solution.py:499
  32.6 7.4 %collective-permute-start.9 = (bf16[72,896]{1,0:T(8,128)(2,1)S(1)}, bf16[72,896]{1,0:T(8,128)(2,1)S(1)}, u32[]{:S(2)}, u32[]{:S(2)}) collective-permute-start(bf16[72,896]{1,0:T(8,128)(2,1)S(1)} %get-tuple-element.61), channel_id=1, source_target_pairs={{24,0},{16,8},{8,16},{0,24},{25,1},{17,9},{9,17},{1,25},{26,2},{18... | collective-permute-start | bytes 387080 | tf_op jit(solution)/shard_map/ppermute | solution.py:499
  39.9 2.5 %copy-start.13 = (bf16[72,896]{1,0:T(8,128)(2,1)}, bf16[72,896]{1,0:T(8,128)(2,1)S(1)}, u32[]{:S(2)}) copy-start(bf16[72,896]{1,0:T(8,128)(2,1)S(1)} %collective-permute-done.8.refs_6_.refs_2_) | copy-start | bytes 387076
  39.9 2.5 %copy-start.15 = (bf16[72,896]{1,0:T(8,128)(2,1)}, bf16[72,896]{1,0:T(8,128)(2,1)S(1)}, u32[]{:S(2)}) copy-start(bf16[72,896]{1,0:T(8,128)(2,1)S(1)} %collective-permute-done.9.refs_7_.refs_3_) | copy-start | bytes 387076
  43.1 44.0 %copy-start.3 = (bf16[72,4864]{1,0:T(8,128)(2,1)}, bf16[72,4864]{1,0:T(8,128)(2,1)S(1)}, u32[]{:S(2)}) copy-start(bf16[72,4864]{1,0:T(8,128)(2,1)S(1)} %get-tuple-element.74.refs_4_) | copy-start | bytes 2101252
  43.1 53.9 %copy-start.1 = (bf16[1,896,1024]{2,1,0:T(8,128)(2,1)S(1)}, bf16[1,896,1024]{2,1,0:T(8,128)(2,1)}, u32[]{:S(2)}) copy-start(bf16[1,896,1024]{2,1,0:T(8,128)(2,1)} %momentum_hbm.1) | copy-start | bytes 5505028
  43.1 7.9 %collective-permute-start.19 = (bf16[8,8064]{1,0:T(8,128)(2,1)S(1)}, bf16[8,8064]{1,0:T(8,128)(2,1)S(1)}, u32[]{:S(2)}, u32[]{:S(2)}) collective-permute-start(bf16[8,8064]{1,0:T(8,128)(2,1)S(1)} %get-tuple-element.79), channel_id=1, source_target_pairs={{0,4},{1,5},{2,6},{3,7},{4,0},{5,1},{6,2},{7,3},{8,12},{9,13},{10,... | collective-permute-start | bytes 387080 | tf_op jit(solution)/shard_map/ppermute | solution.py:493
  47.1 8.5 %collective-permute-start.10 = (bf16[32,2304]{1,0:T(8,128)(2,1)S(1)}, bf16[32,2304]{1,0:T(8,128)(2,1)S(1)}, u32[]{:S(2)}, u32[]{:S(2)}) collective-permute-start(bf16[32,2304]{1,0:T(8,128)(2,1)S(1)} %get-tuple-element.62), channel_id=1, source_target_pairs={{0,4},{1,5},{2,6},{3,7},{4,0},{5,1},{6,2},{7,3},{8,12},{9,13},{10,... | collective-permute-start | bytes 442376 | tf_op jit(solution)/shard_map/ppermute | solution.py:493
  47.1 43.9 %collective-permute-start.16 = (bf16[72,4864]{1,0:T(8,128)(2,1)S(1)}, bf16[72,4864]{1,0:T(8,128)(2,1)S(1)}, u32[]{:S(2)}, u32[]{:S(2)}) collective-permute-start(bf16[72,4864]{1,0:T(8,128)(2,1)S(1)} %get-tuple-element.75), channel_id=1, source_target_pairs={{8,0},{0,8},{24,16},{16,24},{9,1},{1,9},{25,17},{17,25},{10,2},{2,... | collective-permute-start | bytes 2101256 | tf_op jit(solution)/shard_map/ppermute | solution.py:499
  47.1 46.7 %collective-permute-start.17 = (bf16[72,4864]{1,0:T(8,128)(2,1)S(1)}, bf16[72,4864]{1,0:T(8,128)(2,1)S(1)}, u32[]{:S(2)}, u32[]{:S(2)}) collective-permute-start(bf16[72,4864]{1,0:T(8,128)(2,1)S(1)} %get-tuple-element.76), channel_id=1, source_target_pairs={{16,0},{24,8},{0,16},{8,24},{17,1},{25,9},{1,17},{9,25},{18,2},{26... | collective-permute-start | bytes 2101256 | tf_op jit(solution)/shard_map/ppermute | solution.py:499
  48.6 46.7 %collective-permute-start.18 = (bf16[72,4864]{1,0:T(8,128)(2,1)S(1)}, bf16[72,4864]{1,0:T(8,128)(2,1)S(1)}, u32[]{:S(2)}, u32[]{:S(2)}) collective-permute-start(bf16[72,4864]{1,0:T(8,128)(2,1)S(1)} %get-tuple-element.77), channel_id=1, source_target_pairs={{24,0},{16,8},{8,16},{0,24},{25,1},{17,9},{9,17},{1,25},{26,2},{18... | collective-permute-start | bytes 2101256 | tf_op jit(solution)/shard_map/ppermute | solution.py:499
  52.3 12.9 %collective-permute-start.22 = (bf16[8,8064]{1,0:T(8,128)(2,1)S(1)}, bf16[8,8064]{1,0:T(8,128)(2,1)S(1)}, u32[]{:S(2)}, u32[]{:S(2)}) collective-permute-start(bf16[8,8064]{1,0:T(8,128)(2,1)S(1)} %get-tuple-element.83), channel_id=1, source_target_pairs={{0,4},{1,5},{2,6},{3,7},{4,0},{5,1},{6,2},{7,3},{8,12},{9,13},{10,... | collective-permute-start | bytes 387080 | tf_op jit(solution)/shard_map/ppermute | solution.py:493
  56.9 39.4 %copy-start.19 = (bf16[8,12672]{1,0:T(8,128)(2,1)}, bf16[8,12672]{1,0:T(8,128)(2,1)S(1)}, u32[]{:S(2)}) copy-start(bf16[8,12672]{1,0:T(8,128)(2,1)S(1)} %get-tuple-element.66.refs_0_) | copy-start | bytes 608260
  56.9 9.8 %collective-permute-start.14 = (bf16[8,8064]{1,0:T(8,128)(2,1)S(1)}, bf16[8,8064]{1,0:T(8,128)(2,1)S(1)}, u32[]{:S(2)}, u32[]{:S(2)}) collective-permute-start(bf16[8,8064]{1,0:T(8,128)(2,1)S(1)} %get-tuple-element.70), channel_id=1, source_target_pairs={{0,4},{1,5},{2,6},{3,7},{4,0},{5,1},{6,2},{7,3},{8,12},{9,13},{10,... | collective-permute-start | bytes 387080 | tf_op jit(solution)/shard_map/ppermute | solution.py:493
  65.2 1.6 %collective-permute-start.24 = (bf16[72,1024]{1,0:T(8,128)(2,1)}, bf16[72,1024]{1,0:T(8,128)(2,1)S(1)}, u32[]{:S(2)}, u32[]{:S(2)}) collective-permute-start(bf16[72,1024]{1,0:T(8,128)(2,1)} %get-tuple-element.86.refs_5_), channel_id=1, source_target_pairs={{8,0},{0,8},{24,16},{16,24},{9,1},{1,9},{25,17},{17,25},{10,2},{2,... | collective-permute-start | bytes 442376 | tf_op jit(solution)/shard_map/ppermute | solution.py:499
  66.7 10.1 %collective-permute-start.11 = (bf16[8,12672]{1,0:T(8,128)(2,1)S(1)}, bf16[8,12672]{1,0:T(8,128)(2,1)S(1)}, u32[]{:S(2)}, u32[]{:S(2)}) collective-permute-start(bf16[8,12672]{1,0:T(8,128)(2,1)S(1)} %get-tuple-element.67), channel_id=1, source_target_pairs={{1,0},{0,1},{3,2},{2,3},{5,4},{4,5},{7,6},{6,7},{9,8},{8,9},{11,10... | collective-permute-start | bytes 608264 | tf_op jit(solution)/shard_map/ppermute | solution.py:489
  67.4 15.0 %collective-permute-start.12 = (bf16[8,12672]{1,0:T(8,128)(2,1)S(1)}, bf16[8,12672]{1,0:T(8,128)(2,1)S(1)}, u32[]{:S(2)}, u32[]{:S(2)}) collective-permute-start(bf16[8,12672]{1,0:T(8,128)(2,1)S(1)} %get-tuple-element.68), channel_id=1, source_target_pairs={{2,0},{3,1},{0,2},{1,3},{6,4},{7,5},{4,6},{5,7},{10,8},{11,9},{8,1... | collective-permute-start | bytes 608264 | tf_op jit(solution)/shard_map/ppermute | solution.py:489
  76.7 10.4 %collective-permute-start.13 = (bf16[8,12672]{1,0:T(8,128)(2,1)S(1)}, bf16[8,12672]{1,0:T(8,128)(2,1)S(1)}, u32[]{:S(2)}, u32[]{:S(2)}) collective-permute-start(bf16[8,12672]{1,0:T(8,128)(2,1)S(1)} %get-tuple-element.69), channel_id=1, source_target_pairs={{3,0},{2,1},{1,2},{0,3},{7,4},{6,5},{5,6},{4,7},{11,8},{10,9},{9,1... | collective-permute-start | bytes 608264 | tf_op jit(solution)/shard_map/ppermute | solution.py:489
  82.5 7.2 %collective-permute-start.15 = (bf16[8,8064]{1,0:T(8,128)(2,1)S(1)}, bf16[8,8064]{1,0:T(8,128)(2,1)S(1)}, u32[]{:S(2)}, u32[]{:S(2)}) collective-permute-start(bf16[8,8064]{1,0:T(8,128)(2,1)S(1)} %get-tuple-element.73), channel_id=1, source_target_pairs={{0,4},{1,5},{2,6},{3,7},{4,0},{5,1},{6,2},{7,3},{8,12},{9,13},{10,... | collective-permute-start | bytes 387080 | tf_op jit(solution)/shard_map/ppermute | solution.py:493
  87.1 23.3 %collective-permute-start.25 = (bf16[72,1024]{1,0:T(8,128)(2,1)}, bf16[72,1024]{1,0:T(8,128)(2,1)}, u32[]{:S(2)}, u32[]{:S(2)}) collective-permute-start(bf16[72,1024]{1,0:T(8,128)(2,1)} %get-tuple-element.86.refs_5_), channel_id=1, source_target_pairs={{16,0},{24,8},{0,16},{8,24},{17,1},{25,9},{1,17},{9,25},{18,2},{26... | collective-permute-start | bytes 442376 | tf_op jit(solution)/shard_map/ppermute | solution.py:499
  89.7 5.6 %copy-start.17 = (bf16[8,8064]{1,0:T(8,128)(2,1)}, bf16[8,8064]{1,0:T(8,128)(2,1)S(1)}, u32[]{:S(2)}) copy-start(bf16[8,8064]{1,0:T(8,128)(2,1)S(1)} %collective-permute-done.15.large.refs_4_) | copy-start | bytes 387076
  89.7 20.8 %collective-permute-start.26 = (bf16[72,1024]{1,0:T(8,128)(2,1)}, bf16[72,1024]{1,0:T(8,128)(2,1)}, u32[]{:S(2)}, u32[]{:S(2)}) collective-permute-start(bf16[72,1024]{1,0:T(8,128)(2,1)} %get-tuple-element.86.refs_5_), channel_id=1, source_target_pairs={{24,0},{16,8},{8,16},{0,24},{25,1},{17,9},{9,17},{1,25},{26,2},{18... | collective-permute-start | bytes 442376 | tf_op jit(solution)/shard_map/ppermute | solution.py:499
  91.8 24.9 %collective-permute-start.20 = (bf16[8,8064]{1,0:T(8,128)(2,1)}, bf16[8,8064]{1,0:T(8,128)(2,1)}, u32[]{:S(2)}, u32[]{:S(2)}) collective-permute-start(bf16[8,8064]{1,0:T(8,128)(2,1)} %get-tuple-element.81), channel_id=1, source_target_pairs={{1,0},{0,1},{3,2},{2,3},{5,4},{4,5},{7,6},{6,7},{9,8},{8,9},{11,10... | collective-permute-start | bytes 387080 | tf_op jit(solution)/shard_map/ppermute | solution.py:489
  94.7 22.0 %collective-permute-start.23 = (bf16[8,8064]{1,0:T(8,128)(2,1)}, bf16[8,8064]{1,0:T(8,128)(2,1)}, u32[]{:S(2)}, u32[]{:S(2)}) collective-permute-start(bf16[8,8064]{1,0:T(8,128)(2,1)} %after_large.7), channel_id=1, source_target_pairs={{3,0},{2,1},{1,2},{0,3},{7,4},{6,5},{5,6},{4,7},{11,8},{10,9},{9,1... | collective-permute-start | bytes 387080 | tf_op jit(solution)/shard_map/ppermute | solution.py:489
  96.3 20.5 %collective-permute-start.21 = (bf16[8,8064]{1,0:T(8,128)(2,1)}, bf16[8,8064]{1,0:T(8,128)(2,1)}, u32[]{:S(2)}, u32[]{:S(2)}) collective-permute-start(bf16[8,8064]{1,0:T(8,128)(2,1)} %get-tuple-element.82), channel_id=1, source_target_pairs={{2,0},{3,1},{0,2},{1,3},{6,4},{7,5},{4,6},{5,7},{10,8},{11,9},{8,1... | collective-permute-start | bytes 387080 | tf_op jit(solution)/shard_map/ppermute | solution.py:489
  97.1 3.1 %copy-start = (bf16[1,3584,1024]{2,1,0:T(8,128)(2,1)S(1)}, bf16[1,3584,1024]{2,1,0:T(8,128)(2,1)}, u32[]{:S(2)}) copy-start(bf16[1,3584,1024]{2,1,0:T(8,128)(2,1)} %weight_hbm.3) | copy-start | bytes 22020100
  100.1 1.1 copy-start.4
  101.2 1.1 copy-start.6
  102.3 1.1 copy-start.8
  103.4 1.1 copy-start.10
  104.6 0.9 copy-start.12
  107.3 2.6 %copy-start.18 = (bf16[8,8064]{1,0:T(8,128)(2,1)S(1)}, bf16[8,8064]{1,0:T(8,128)(2,1)}, u32[]{:S(2)}) copy-start(bf16[8,8064]{1,0:T(8,128)(2,1)} %copy-done.17) | copy-start | bytes 387076
  109.9 0.9 copy-start.22
  110.8 5.9 %copy-start.20 = (bf16[8,12672]{1,0:T(8,128)(2,1)S(1)}, bf16[8,12672]{1,0:T(8,128)(2,1)}, u32[]{:S(2)}) copy-start(bf16[8,12672]{1,0:T(8,128)(2,1)} %copy-done.19) | copy-start | bytes 608260
  110.8 5.9 %copy-start.24 = (s32[128]{0:T(128)S(1)}, s32[128]{0:T(128)}, u32[]{:S(2)}) copy-start(s32[128]{0:T(128)} %param.10) | copy-start | bytes 1540
  110.8 5.9 %copy-start.25 = (f32[128]{0:T(128)S(1)}, f32[128]{0:T(128)}, u32[]{:S(2)}) copy-start(f32[128]{0:T(128)} %param.8) | copy-start | bytes 1540
  (7 other events, 5.7 us)

commit v5 on v4

--- a/solution.py
+++ b/solution.py
@@ -220,10 +220,16 @@
     place(scaled, plan.DX)
 
 
-def hold_kernel(plan, weight_hbm, held, sem):
-    copy = pltpu.make_async_copy(weight_hbm.at[0], held, sem)
-    copy.start()
-    copy.wait()
+def hold_kernel(plan, weight_hbm, held, mine, sems):
+    start = pl.multiple_of(lax.axis_index("dp") * plan.share, LANES)
+    copies = [
+        pltpu.make_async_copy(weight_hbm.at[0], held, sems.at[0]),
+        pltpu.make_async_copy(weight_hbm.at[0, pl.ds(start, plan.share), :], mine, sems.at[1]),
+    ]
+    for copy in copies:
+        copy.start()
+    for copy in copies:
+        copy.wait()
 
 
 def blocks_of(refs, start, stop, low=0):
@@ -255,7 +261,7 @@
 
 def near_kernel(plan, placement_ref, weight_ref, *refs):
     near = refs[: plan.half]
-    back_near, local_back, local_act, folded_grad, grads, far_rows = refs[-6:]
+    back_near, local, folded_grad, grads, far_rows = refs[-5:]
     x_near = unfold(plan, blocks_of(near, 0, plan.DX), plan.D)
     x_far = unfold(plan, blocks_of(near, 0, plan.DX, SUB), plan.D)
     g_near = unfold(plan, blocks_of(near, plan.DX, plan.C), plan.F)
@@ -268,8 +274,8 @@
     act, grad32 = act.astype(F32), grad_pre.astype(F32)
     back_near[:, : plan.DX] = fold(plan, back[: plan.rows]).astype(BF16)
     back_near[:, plan.DX :] = fold(plan, act[: plan.rows]).astype(BF16)
-    local_back[...] = fold(plan, back[plan.rows :]).astype(BF16)
-    local_act[...] = fold(plan, act[plan.rows :]).astype(BF16)
+    local[:, : plan.DX] = fold(plan, back[plan.rows :]).astype(BF16)
+    local[:, plan.DX :] = fold(plan, act[plan.rows :]).astype(BF16)
     grad_near = grad32[: plan.rows]
     grad_far = jnp.where(is_hot(plan, placement_ref), grad32[plan.rows :], 0.0)
     folded_grad[...] = fold(plan, grad_near).astype(BF16)
@@ -278,40 +284,36 @@
 
 
 def payload_kernel(
-    sizes, plan, placement_ref, weight_ref, folded_grad, near_grads, far_rows, *refs
+    plan, placement_ref, weight_ref, folded_grad, near_grads, far_rows, near_back, *refs
 ):
     half, groups = plan.half, plan.groups
     far, refs = refs[:half], refs[half:]
     columns, refs = refs[:groups], refs[groups:]
-    small, large, refs = refs[0], refs[1 : 1 + len(sizes)], refs[1 + len(sizes) :]
-    shared, rows = refs[:groups], refs[groups]
+    first, last, refs = refs[0], refs[1], refs[2:]
+    shared, early, rows = refs[:groups], refs[groups : groups + half], refs[groups + half]
     hot = is_hot(plan, placement_ref)
     x = unfold(plan, blocks_of(far, 0, plan.DX), plan.D)
     g = unfold(plan, blocks_of(far, plan.DX, plan.C), plan.F)
     rows[...] = x
     act, grad_pre = activate(dot(x, weight_ref[...]), g)
 
-    def store(data, start, stop):
-        low = 0
-        for out, size in zip(large, sizes):
-            out[:, start:stop] = data[low : low + size].astype(BF16)
-            low += size
+    def store(data, start):
+        stop = start + data.shape[1]
+        first[:, start:stop] = data[SUB:].astype(BF16)
+        last[:, start:stop] = data[:SUB].astype(BF16)
 
     @pl.when(jnp.logical_not(hot))
     def _():
-        folded = fold(plan, dot_nt(grad_pre, weight_ref[...]))
-        store(jnp.concatenate([folded[SUB:], folded[:SUB]], axis=0), 0, plan.DX)
-        small[...] = fold(plan, act.astype(F32)).astype(BF16)
+        store(fold(plan, dot_nt(grad_pre, weight_ref[...])), 0)
+        store(fold(plan, act.astype(F32)), plan.DX)
 
     @pl.when(hot)
     def _():
         together = jnp.concatenate([c[...].astype(F32) for c in columns], axis=0)
         block = half * SUB
         for i in range(plan.pieces):
-            store(
-                together[i * block : (i + 1) * block], i * plan.share, (i + 1) * plan.share
-            )
-        small[...] = folded_grad[...]
+            store(together[i * block : (i + 1) * block], i * plan.share)
+        store(folded_grad[...].astype(F32), plan.DX)
 
     group = lax.axis_index("dp")
     width = plan.share
@@ -321,32 +323,31 @@
         shared[m][:, width : 2 * width] = rows[:, pl.ds(start, width)]
         shared[m][:, 2 * width : 2 * width + 2 * plan.F] = near_grads[...]
         shared[m][:, 2 * width + 2 * plan.F :] = grad_pre
-
-
-def after_small_kernel(plan, placement_ref, small, local_act, near_back, waiting, *outs):
-    outs[plan.half + 1][...] = waiting[...]
+    back = near_back[...].astype(F32)
+    for m in range(half):
+        early[m][...] = back[m * SUB : (m + 1) * SUB].astype(BF16)
+
+
+def choose(plan, placement_ref, local, got):
     hot = is_hot(plan, placement_ref)
-    payload = small[...].astype(F32)
-    chosen = jnp.where(hot, local_act[...].astype(F32), payload)
-    back = near_back[...].astype(F32)
-    for m in range(plan.half):
-        span = slice(m * SUB, (m + 1) * SUB)
-        outs[m][:, : plan.C] = back[span].astype(BF16)
-        outs[m][:, plan.C :] = chosen[span].astype(BF16)
-    blocks = [payload[m * SUB : (m + 1) * SUB] for m in range(plan.half)]
-    outs[plan.half][...] = jnp.where(hot, unfold(plan, blocks, plan.F).astype(F32), 0.0).astype(BF16)
-
-
-def after_large_kernel(first, passing, plan, placement_ref, large, local_back, *refs):
-    count = large.shape[0] // SUB
-    outs = refs[-count - passing :]
-    for source, target in zip(refs[:passing], outs[count:]):
-        target[...] = source[...]
+    return jnp.where(hot, local, got[...].astype(F32))
+
+
+def after_first_kernel(plan, placement_ref, first, local, *refs):
+    outs = refs[1 - plan.half :]
+    chosen = choose(plan, placement_ref, local[...].astype(F32)[SUB:], first)
+    for m in range(plan.half - 1):
+        outs[m][...] = chosen[m * SUB : (m + 1) * SUB].astype(BF16)
+
+
+def after_last_kernel(plan, placement_ref, last, local, first, total, back, grad):
+    chosen = choose(plan, placement_ref, local[...].astype(F32)[:SUB], last)
+    back[...] = chosen.astype(BF16)
+    got = first[:, plan.DX :].astype(F32)
+    blocks = [last[:, plan.DX :].astype(F32)]
+    blocks += [got[m * SUB : (m + 1) * SUB] for m in range(plan.half - 1)]
     hot = is_hot(plan, placement_ref)
-    local = local_back[...].astype(F32)[first * SUB : (first + count) * SUB]
-    chosen = jnp.where(hot, local, large[...].astype(F32))
-    for m in range(count):
-        outs[m][...] = chosen[m * SUB : (m + 1) * SUB].astype(BF16)
+    grad[...] = jnp.where(hot, unfold(plan, blocks, plan.F).astype(F32), 0.0).astype(BF16)
 
 
 def unpack_kernel(plan, slot_ref, gate_ref, *refs):
@@ -377,29 +378,25 @@
             total = term if total is None else total + term
         return total
 
-    near = blocks_of(early, 0, plan.DX)
-    grad_ref[...] = gather(near, blocks_of(late, 0, plan.DX), plan.D).astype(BF16)
-    near = blocks_of(early, plan.DX, plan.C)
-    far = blocks_of(early, plan.C, plan.C + plan.FG)
-    out_ref[...] = (to_column(gate_ref[...]) * gather(near, far, plan.F)).astype(BF16)
+    def both(start, stop):
+        return blocks_of(early, start, stop), blocks_of(late, start, stop)
+
+    grad_ref[...] = gather(*both(0, plan.DX), plan.D).astype(BF16)
+    gate = to_column(gate_ref[...])
+    out_ref[...] = (gate * gather(*both(plan.DX, plan.C), plan.F)).astype(BF16)
 
 
 def rows_of(parts):
     return jnp.concatenate([p.astype(F32) for p in parts], axis=0).astype(BF16)
 
 
-def gather_kernel(plan, weight_hbm, momentum_hbm, *refs):
+def gather_kernel(plan, momentum_hbm, *refs):
     groups, share, width = plan.groups, plan.share, plan.F
     columns, refs = refs[:groups], refs[groups:]
     shared, refs = refs[:groups], refs[groups:]
-    total, old_weight, x_all, momentum, sems = refs
-    mine = pl.multiple_of(lax.axis_index("dp") * share, LANES)
-    copies = [
-        pltpu.make_async_copy(momentum_hbm.at[0], momentum, sems.at[0]),
-        pltpu.make_async_copy(weight_hbm.at[0, pl.ds(mine, share), :], old_weight, sems.at[1]),
-    ]
-    for copy in copies:
-        copy.start()
+    total, x_all, momentum, sem = refs
+    copy = pltpu.make_async_copy(momentum_hbm.at[0], momentum, sem)
+    copy.start()
     base = 2 * share
     x_parts, g_parts = [], []
     for m in range(groups):
@@ -408,16 +405,14 @@
         g_parts += [shared[m][:, base + i * width : base + (i + 1) * width] for i in range(3)]
     x_all[...] = rows_of(x_parts)
     g_all = rows_of(g_parts)
-    for copy in copies:
-        copy.wait()
+    copy.wait()
     for i in range(share // LANES):
         span = slice(i * LANES, (i + 1) * LANES)
         before = decay_rate * momentum[span, :].astype(F32)
         total[span, :] = before + dot_tn(x_all[:, span], g_all)
 
 
-def update_kernel(plan, count, placement_ref, *refs):
-    large, refs = refs[:count], refs[count:]
+def update_kernel(plan, placement_ref, last, first, *refs):
     other_g, refs = refs[: plan.groups], refs[plan.groups :]
     total_ref, weight_ref, new_weight, new_momentum, x_all, g_all = refs
     step = pl.program_id(0)
@@ -430,7 +425,7 @@
         pieces = [
             block[:, i * share : (i + 1) * share].astype(F32)
             for i in range(plan.pieces)
-            for block in large
+            for block in (last, first)
         ]
         x_all[...] = jnp.where(hot, jnp.concatenate(pieces, axis=0), 0.0).astype(BF16)
         g_all[...] = rows_of([g[...] for g in other_g])
@@ -522,13 +517,13 @@
     )
     near = [packed[0]] + [to_slot(packed[m], m) for m in range(1, half)]
     far = [to_slot(packed[half + m], m, 1) for m in range(half)]
-    (held,) = call(
+    held, old_weight = call(
         hold_kernel,
         plan,
         [weight],
         [ANY_SPEC],
-        [(D, F)],
-        [pltpu.SemaphoreType.DMA],
+        [(D, F), (share, F)],
+        [pltpu.SemaphoreType.DMA((2,))],
         0,
         "hold",
         limit=40,
@@ -544,15 +539,14 @@
         "near_columns",
     )
     columns_here = from_groups(columns)
-    back_near, local_back, local_act, folded_grad, grads, far_rows = call(
+    back_near, local, folded_grad, grads, far_rows = call(
         near_kernel,
         plan,
         [placement, held] + near + [columns[0]],
         [SMEM_SPEC] + [VMEM_SPEC] * (1 + half) + [ANY_SPEC],
         [
             (half * SUB, C),
-            (half * SUB, plan.DX),
-            (half * SUB, plan.FG),
+            (half * SUB, C),
             (half * SUB, plan.FG),
             (rows, 2 * F),
             (rows, D),
@@ -561,75 +555,59 @@
         8 * rows * D * F,
         "near_rows",
     )
-    sizes = [SUB] * half
     outs = call(
-        functools.partial(payload_kernel, sizes),
-        plan,
-        [placement, held, folded_grad, grads, far_rows] + far + columns_here,
-        [SMEM_SPEC] + [VMEM_SPEC] * (4 + half + groups),
-        [(half * SUB, plan.FG)]
-        + [(size, plan.DX) for size in sizes]
-        + [(rows, 2 * share + 3 * F)] * groups,
+        payload_kernel,
+        plan,
+        [placement, held, folded_grad, grads, far_rows, back_near] + far + columns_here,
+        [SMEM_SPEC] + [VMEM_SPEC] * (5 + half + groups),
+        [((half - 1) * SUB, C), (SUB, C)]
+        + [(rows, 2 * share + 3 * F)] * groups
+        + [(SUB, C)] * half,
         [pltpu.VMEM((rows, D), BF16)],
         4 * rows * D * F,
         "payload",
     )
-    small = to_partner(outs[0])
-    large = [to_partner(outs[1])]
-    waiting = outs[2 : 1 + half]
-    shared = from_groups(outs[1 + half :])
+    first, last = to_partner(outs[0]), to_partner(outs[1])
+    shared, outs = from_groups(outs[2 : 2 + groups]), outs[2 + groups :]
+    early = [outs[0]] + [to_source(outs[m], m) for m in range(1, half)]
     outs = call(
-        after_small_kernel,
-        plan,
-        [placement, small, local_act, back_near, waiting[0]],
-        [SMEM_SPEC] + [VMEM_SPEC] * 4,
-        [(SUB, C + plan.FG)] * half + [(rows, F), (sizes[1], plan.DX)],
+        after_first_kernel,
+        plan,
+        [placement, first, local] + early[1:],
+        [SMEM_SPEC] + [VMEM_SPEC] * 2 + [ANY_SPEC] * (half - 1),
+        [(SUB, C)] * (half - 1),
         [],
         0,
-        "after_small",
-    )
-    early = [outs[0]] + [to_source(outs[m], m) for m in range(1, half)]
-    large.append(to_partner(outs[half + 1]))
-    other_g = from_groups([outs[half]] * groups)
-
-    def after_large(first, data, passing, before):
-        count = data.shape[0] // SUB
-        return call(
-            functools.partial(after_large_kernel, first, len(passing)),
-            plan,
-            [placement, data, local_back] + passing + before,
-            [SMEM_SPEC] + [VMEM_SPEC] * (2 + len(passing)) + [ANY_SPEC] * len(before),
-            [(SUB, plan.DX)] * count + [p.shape for p in passing],
-            [],
-            0,
-            "after_large",
-        )
-
-    far_back = []
-    for i in range(half - 2):
-        outs = after_large(i + 1, large[i], [waiting[i + 1]], [])
-        large.append(to_partner(outs[1]))
-        far_back.append(to_source(outs[0], i + 1))
-    total, old_weight = call(
+        "after_first",
+    )
+    late = [to_source(out, m + 1) for m, out in enumerate(outs)]
+    (total,) = call(
         gather_kernel,
         plan,
-        [weight, momentum] + columns_here + shared,
-        [ANY_SPEC] * 2 + [VMEM_SPEC] * (2 * groups),
-        [(share, F)] * 2,
+        [momentum] + columns_here + shared,
+        [ANY_SPEC] + [VMEM_SPEC] * (2 * groups),
+        [(share, F)],
         [
             pltpu.VMEM((3 * groups * rows, share), BF16),
             pltpu.VMEM((share, F), BF16),
-            pltpu.SemaphoreType.DMA((2,)),
+            pltpu.SemaphoreType.DMA,
         ],
         0,
         "own_terms",
-        limit=24,
-        dtypes=[F32, BF16],
-    )
-    outs = after_large(half - 1, large[-2], [], [])
-    far_back.append(to_source(outs[0], half - 1))
-    outs = after_large(0, large[-1], [], [total] + early[1:])
-    far_back = [outs[0]] + far_back
+        dtypes=[F32],
+    )
+    back, grad = call(
+        after_last_kernel,
+        plan,
+        [placement, last, local, first, total],
+        [SMEM_SPEC] + [VMEM_SPEC] * 3 + [ANY_SPEC],
+        [(SUB, C), (rows, F)],
+        [],
+        0,
+        "after_last",
+    )
+    late = [back] + late
+    other_g = from_groups([grad] * groups)
 
     tile = LANES
     steps = share // tile
@@ -639,12 +617,12 @@
         return pl.BlockSpec(shape, lambda i, g: (0,) * len(shape))
 
     new_weight, new_momentum = pl.pallas_call(
-        lambda g_ref, *refs: update_kernel(plan, len(sizes), *refs),
+        lambda g_ref, *refs: update_kernel(plan, *refs),
         grid_spec=pltpu.PrefetchScalarGridSpec(
             num_scalar_prefetch=1,
             grid=(steps,),
             in_specs=[SMEM_SPEC]
-            + [whole(size, plan.DX) for size in sizes]
+            + [whole(*p.shape) for p in (last, first)]
             + [whole(*g.shape) for g in other_g]
             + [
                 pl.BlockSpec((tile, F), lambda i, g: (i, 0)),
@@ -662,12 +640,12 @@
             flops=2 * groups * rows * share * F, bytes_accessed=12 * share * F, transcendentals=0
         ),
         name="update",
-    )(group, placement, *large, *other_g, total, old_weight)
+    )(group, placement, last, first, *other_g, total, old_weight)
 
     expert_out, token_grad = call(
         unpack_kernel,
         plan,
-        [slot, gate] + early + far_back,
+        [slot, gate] + early + late,
         [VMEM_SPEC] * (2 + 2 * half),
         [(plan.tokens, F), (plan.tokens, D)],
         [],

time: 122 us -> 114 us (0.934); the launches traced: 120 us -> 113 us
  local copies, waits for them, and re-layouts: 14.4 us -> 3.65 us
  waiting for transfers between devices: 24.5 us -> 32.9 us
  Pallas kernels: 31.2 us -> 28.9 us
  starting transfers between devices: 48.9 us -> 47.2 us
    ppermute x6, waiting for transfers between devices: 2.83 us -> 20 us  [to_source(): return lax.ppermute(data, 'expert', pairs)]
    ppermute x5 -> x2, waiting for transfers between devices: 11.9 us -> 0.01 us  [to_partner(): return lax.ppermute(data, 'expert', pairs)]
    unnamed x56 -> x22, local copies, waits for them, and re-layouts: 14.4 us -> 3.65 us
    ppermute x6, starting transfers between devices: 17.3 us -> 13.3 us  [to_source(): return lax.ppermute(data, 'expert', pairs)]
    ppermute x9, waiting for transfers between devices: 0.12 us -> 3.54 us  [from_group(): return lax.ppermute(data, 'dp', pairs)]
    pallas_call x12 -> x9, Pallas kernels: 25.3 us -> 23 us  [call(): pl.pallas_call(functools.partial(kernel, plan), out_shape=[jax.ShapeDtype...]
    ppermute x5 -> x2, starting transfers between devices: 10 us -> 11.9 us  [to_partner(): return lax.ppermute(data, 'expert', pairs)]
  transfers between devices with their start and end apart: 27 -> 24, of which waited for: 10 -> 9; matrix products, arithmetic and copies ran while one was open for 0% -> 0% of each run, Pallas kernels for 18% -> 15%
where the time goes in v5:
time: 114 us; the launch traced here: 113 us
  starting transfers between devices  47.2 us (41%)
  waiting for transfers between devices  32.9 us (29%)
  Pallas kernels  28.9 us (25%)
  local copies, waits for them, and re-layouts  3.65 us (3%)
    pallas_call x9, Pallas kernels, call(): pl.pallas_call(functools.partial(kernel, plan), out_shape=[jax.ShapeDtype...  23 us
    ppermute x6, waiting for transfers between devices, to_source(): return lax.ppermute(data, 'expert', pairs)  20 us
    ppermute x7, starting transfers between devices, to_slot(): return lax.ppermute(data, 'expert', pairs)  16.2 us
    ppermute x6, starting transfers between devices, to_source(): return lax.ppermute(data, 'expert', pairs)  13.3 us
    ppermute x2, starting transfers between devices, to_partner(): return lax.ppermute(data, 'expert', pairs)  11.9 us
    ppermute x7, waiting for transfers between devices, to_slot(): return lax.ppermute(data, 'expert', pairs)  9.26 us
    pallas_call x1, Pallas kernels, routed(): pl.pallas_call(lambda g_ref, *refs: update_kernel(plan, *refs), grid_spec...  5.86 us
    ppermute x9, starting transfers between devices, from_group(): return lax.ppermute(data, 'dp', pairs)  5.72 us
  transfers between devices with their start and end apart: 24, of which 9 were waited for; matrix products, arithmetic and copies ran while one was open for 0% of the time, Pallas kernels for 15%

profile of v5, /device:TPU:0, one launch (start us, length us, event | category | flops | bytes accessed | tf_op | source)
XLA Modules:
  0.0 113.4 jit_solution(16768884637830341255)
XLA Ops:
  0.6 3.4 %pack.1 = (bf16[16,10368]{1,0:T(8,128)(2,1)}, bf16[16,10368]{1,0:T(8,128)(2,1)}, bf16[16,10368]{1,0:T(8,128)(2,1)}, bf16[16,10368]{1,0:T(8,128)(2,1)}, bf16[8,10...) custom-call(s32[1,128]{1,0:T(1,128)} %bitcast.3, ...), custom_call_target="tpu_custom_call" | custom-call | flops 150994944 | bytes 3171328 | tf_op jit(solution)/shard_map/pack/pallas_call | solution.py:450
  4.0 3.0 %collective-permute-start = (bf16[16,10368]{1,0:T(8,128)(2,1)}, bf16[16,10368]{1,0:T(8,128)(2,1)S(1)}, u32[]{:S(2)}, u32[]{:S(2)}) collective-permute-start(bf16[16,10368]{1,0:T(8,128)(2,1)} %get-tuple-element.44), channel_id=1, source_target_pairs={{0,1},{1,0},{2,3},{3,2},{4,5},{5,4},{6,7},{7,6},{8,9},{9,8},{10,11... | collective-permute-start | bytes 995336 | tf_op jit(solution)/shard_map/ppermute | solution.py:477
  7.0 1.6 %collective-permute-start.1 = (bf16[16,10368]{1,0:T(8,128)(2,1)}, bf16[16,10368]{1,0:T(8,128)(2,1)S(1)}, u32[]{:S(2)}, u32[]{:S(2)}) collective-permute-start(bf16[16,10368]{1,0:T(8,128)(2,1)} %get-tuple-element.45), channel_id=1, source_target_pairs={{0,2},{1,3},{2,0},{3,1},{4,6},{5,7},{6,4},{7,5},{8,10},{9,11},{10,... | collective-permute-start | bytes 995336 | tf_op jit(solution)/shard_map/ppermute | solution.py:477
  8.6 3.0 %collective-permute-start.3 = (bf16[8,10368]{1,0:T(8,128)(2,1)}, bf16[8,10368]{1,0:T(8,128)(2,1)S(1)}, u32[]{:S(2)}, u32[]{:S(2)}) collective-permute-start(bf16[8,10368]{1,0:T(8,128)(2,1)} %get-tuple-element.52), channel_id=1, source_target_pairs={{0,4},{1,5},{2,6},{3,7},{4,0},{5,1},{6,2},{7,3},{8,12},{9,13},{10,... | collective-permute-start | bytes 497672 | tf_op jit(solution)/shard_map/ppermute | solution.py:477
  11.6 1.3 %collective-permute-start.4 = (bf16[8,10368]{1,0:T(8,128)(2,1)}, bf16[8,10368]{1,0:T(8,128)(2,1)S(1)}, u32[]{:S(2)}, u32[]{:S(2)}) collective-permute-start(bf16[8,10368]{1,0:T(8,128)(2,1)} %get-tuple-element.53), channel_id=1, source_target_pairs={{0,5},{1,4},{2,7},{3,6},{4,1},{5,0},{6,3},{7,2},{8,13},{9,12},{10,... | collective-permute-start | bytes 497672 | tf_op jit(solution)/shard_map/ppermute | solution.py:477
  13.0 3.6 %hold.1 = (bf16[3584,1024]{1,0:T(8,128)(2,1)S(1)}, bf16[896,1024]{1,0:T(8,128)(2,1)S(1)}) custom-call(bf16[1,3584,1024]{2,1,0:T(8,128)(2,1)} %weight_hbm.1), custom_call_target="tpu_custom_call" | custom-call | tf_op jit(solution)/shard_map/hold/pallas_call | solution.py:450
  16.6 3.7 %collective-permute-start.5 = (bf16[8,10368]{1,0:T(8,128)(2,1)S(1)}, bf16[8,10368]{1,0:T(8,128)(2,1)S(1)}, u32[]{:S(2)}, u32[]{:S(2)}) collective-permute-start(bf16[8,10368]{1,0:T(8,128)(2,1)S(1)} %copy-done.10), channel_id=1, source_target_pairs={{0,6},{1,7},{2,4},{3,5},{4,2},{5,3},{6,0},{7,1},{8,14},{9,15},{10,... | collective-permute-start | bytes 497672 | tf_op jit(solution)/shard_map/ppermute | solution.py:477
  20.3 4.8 %collective-permute-done.1.refs_2_ = bf16[16,10368]{1,0:T(8,128)(2,1)S(1)} collective-permute-done((bf16[16,10368]{1,0:T(8,128)(2,1)}, bf16[16,10368]{1,0:T(8,128)(2,1)S(1)}, u32[]{:S(2)}, u32[]{:S(2)}) %collective-permute-start.1) | collective-permute-done | bytes 331808 | tf_op jit(solution)/shard_map/ppermute | solution.py:477
  25.1 3.6 %collective-permute-start.6 = (bf16[8,10368]{1,0:T(8,128)(2,1)S(1)}, bf16[8,10368]{1,0:T(8,128)(2,1)S(1)}, u32[]{:S(2)}, u32[]{:S(2)}) collective-permute-start(bf16[8,10368]{1,0:T(8,128)(2,1)S(1)} %copy-done.9), channel_id=1, source_target_pairs={{0,7},{1,6},{2,5},{3,4},{4,3},{5,2},{6,1},{7,0},{8,15},{9,14},{10,... | collective-permute-start | bytes 497672 | tf_op jit(solution)/shard_map/ppermute | solution.py:477
  28.7 1.9 %collective-permute-done.2.refs_3_ = bf16[16,10368]{1,0:T(8,128)(2,1)S(1)} collective-permute-done((bf16[16,10368]{1,0:T(8,128)(2,1)}, bf16[16,10368]{1,0:T(8,128)(2,1)S(1)}, u32[]{:S(2)}, u32[]{:S(2)}) %collective-permute-start.2) | collective-permute-done | bytes 331808 | tf_op jit(solution)/shard_map/ppermute | solution.py:477
  30.5 0.2 near_columns.1
  30.8 0.1 collective-permute-start.7
  30.8 0.0 collective-permute-done.3.refs_0_
  30.8 1.8 %collective-permute-start.8 = (bf16[72,896]{1,0:T(8,128)(2,1)S(1)}, bf16[72,896]{1,0:T(8,128)(2,1)S(1)}, u32[]{:S(2)}, u32[]{:S(2)}) collective-permute-start(bf16[72,896]{1,0:T(8,128)(2,1)S(1)} %get-tuple-element.57), channel_id=1, source_target_pairs={{16,0},{24,8},{0,16},{8,24},{17,1},{25,9},{1,17},{9,25},{18,2},{26... | collective-permute-start | bytes 387080 | tf_op jit(solution)/shard_map/ppermute | solution.py:494
  32.6 0.1 collective-permute-start.9
  32.7 4.7 %near_rows.1 = (bf16[32,10368]{1,0:T(8,128)(2,1)S(1)}, bf16[32,10368]{1,0:T(8,128)(2,1)S(1)}, bf16[32,2304]{1,0:T(8,128)(2,1)S(1)}, bf16[72,2048]{1,0:T(8,128)(2,1)S(1)}, bf16[72,3584]{1,0:T(8,128)(2,1)S(1)}) custom-call(s32[8]{0:T(128)S(1)} %copy-done.6, bf16[3584,1024]{1,0:T(8,128)(2,1)S(1)} %get-tuple-element.42.weight_ref, ...), custom_call_target="tpu_custom_call" | custom-call | flops 2113929216 | bytes 11081760 | tf_op jit(solution)/shard_map/near_rows/pallas_call | solution.py:450
  37.4 0.5 collective-permute-done.5.refs_2_
  37.9 2.1 %collective-permute-done.6.refs_3_ = bf16[8,10368]{1,0:T(8,128)(2,1)S(1)} collective-permute-done((bf16[8,10368]{1,0:T(8,128)(2,1)S(1)}, bf16[8,10368]{1,0:T(8,128)(2,1)S(1)}, u32[]{:S(2)}, u32[]{:S(2)}) %collective-permute-start.6) | collective-permute-done | bytes 165920 | tf_op jit(solution)/shard_map/ppermute | solution.py:477
  39.9 0.0 collective-permute-done.7.refs_5_.refs_1_
  40.0 0.0 copy-start.2
  40.0 2.6 %payload.1 = (bf16[24,10368]{1,0:T(8,128)(2,1)S(1)}, bf16[8,10368]{1,0:T(8,128)(2,1)S(1)}, bf16[72,4864]{1,0:T(8,128)(2,1)S(1)}, bf16[72,4864]{1,0:T(8,128)(2,1)...) custom-call(s32[8]{0:T(128)S(1)} %copy-done.6, ...), custom_call_target="tpu_custom_call" | custom-call | flops 1056964608 | bytes 14270496 | tf_op jit(solution)/shard_map/payload/pallas_call | solution.py:450
  42.5 0.1 collective-permute-start.15
  42.6 1.6 %collective-permute-start.16 = (bf16[72,4864]{1,0:T(8,128)(2,1)S(1)}, bf16[72,4864]{1,0:T(8,128)(2,1)S(1)}, u32[]{:S(2)}, u32[]{:S(2)}) collective-permute-start(bf16[72,4864]{1,0:T(8,128)(2,1)S(1)} %get-tuple-element.68), channel_id=1, source_target_pairs={{16,0},{24,8},{0,16},{8,24},{17,1},{25,9},{1,17},{9,25},{18,2},{26... | collective-permute-start | bytes 2101256 | tf_op jit(solution)/shard_map/ppermute | solution.py:494
  44.2 0.3 collective-permute-start.17
  44.5 3.9 %collective-permute-start.10 = (bf16[8,10368]{1,0:T(8,128)(2,1)S(1)}, bf16[8,10368]{1,0:T(8,128)(2,1)S(1)}, u32[]{:S(2)}, u32[]{:S(2)}) collective-permute-start(bf16[8,10368]{1,0:T(8,128)(2,1)S(1)} %get-tuple-element.60), channel_id=1, source_target_pairs={{1,0},{0,1},{3,2},{2,3},{5,4},{4,5},{7,6},{6,7},{9,8},{8,9},{11,10... | collective-permute-start | bytes 497672 | tf_op jit(solution)/shard_map/ppermute | solution.py:484
  48.4 3.4 %collective-permute-start.14 = (bf16[24,10368]{1,0:T(8,128)(2,1)S(1)}, bf16[24,10368]{1,0:T(8,128)(2,1)S(1)}, u32[]{:S(2)}, u32[]{:S(2)}) collective-permute-start(bf16[24,10368]{1,0:T(8,128)(2,1)S(1)} %get-tuple-element.65), channel_id=1, source_target_pairs={{0,4},{1,5},{2,6},{3,7},{4,0},{5,1},{6,2},{7,3},{8,12},{9,13},{10,... | collective-permute-start | bytes 1493000 | tf_op jit(solution)/shard_map/ppermute | solution.py:488
  51.7 1.4 %collective-permute-done.10.refs_0_.refs_1_ = bf16[8,10368]{1,0:T(8,128)(2,1)S(1)} collective-permute-done((bf16[8,10368]{1,0:T(8,128)(2,1)S(1)}, bf16[8,10368]{1,0:T(8,128)(2,1)S(1)}, u32[]{:S(2)}, u32[]{:S(2)}) %collective-permute-start.10) | collective-permute-done | bytes 165920 | tf_op jit(solution)/shard_map/ppermute | solution.py:484
  53.1 3.3 %collective-permute-start.11 = (bf16[8,10368]{1,0:T(8,128)(2,1)S(1)}, bf16[8,10368]{1,0:T(8,128)(2,1)S(1)}, u32[]{:S(2)}, u32[]{:S(2)}) collective-permute-start(bf16[8,10368]{1,0:T(8,128)(2,1)S(1)} %get-tuple-element.61), channel_id=1, source_target_pairs={{2,0},{3,1},{0,2},{1,3},{6,4},{7,5},{4,6},{5,7},{10,8},{11,9},{8,1... | collective-permute-start | bytes 497672 | tf_op jit(solution)/shard_map/ppermute | solution.py:484
  56.4 9.8 %collective-permute-done.11.refs_1_.refs_2_ = bf16[8,10368]{1,0:T(8,128)(2,1)S(1)} collective-permute-done((bf16[8,10368]{1,0:T(8,128)(2,1)S(1)}, bf16[8,10368]{1,0:T(8,128)(2,1)S(1)}, u32[]{:S(2)}, u32[]{:S(2)}) %collective-permute-start.11) | collective-permute-done | bytes 165920 | tf_op jit(solution)/shard_map/ppermute | solution.py:484
  66.2 2.2 %collective-permute-start.12 = (bf16[8,10368]{1,0:T(8,128)(2,1)S(1)}, bf16[8,10368]{1,0:T(8,128)(2,1)S(1)}, u32[]{:S(2)}, u32[]{:S(2)}) collective-permute-start(bf16[8,10368]{1,0:T(8,128)(2,1)S(1)} %get-tuple-element.62), channel_id=1, source_target_pairs={{3,0},{2,1},{1,2},{0,3},{7,4},{6,5},{5,6},{4,7},{11,8},{10,9},{9,1... | collective-permute-start | bytes 497672 | tf_op jit(solution)/shard_map/ppermute | solution.py:484
  68.4 8.9 %collective-permute-done.12.refs_2_.refs_3_ = bf16[8,10368]{1,0:T(8,128)(2,1)S(1)} collective-permute-done((bf16[8,10368]{1,0:T(8,128)(2,1)S(1)}, bf16[8,10368]{1,0:T(8,128)(2,1)S(1)}, u32[]{:S(2)}, u32[]{:S(2)}) %collective-permute-start.12) | collective-permute-done | bytes 165920 | tf_op jit(solution)/shard_map/ppermute | solution.py:484
  77.3 8.6 %collective-permute-start.13 = (bf16[8,10368]{1,0:T(8,128)(2,1)S(1)}, bf16[8,10368]{1,0:T(8,128)(2,1)S(1)}, u32[]{:S(2)}, u32[]{:S(2)}) collective-permute-start(bf16[8,10368]{1,0:T(8,128)(2,1)S(1)} %get-tuple-element.63), channel_id=1, source_target_pairs={{0,4},{1,5},{2,6},{3,7},{4,0},{5,1},{6,2},{7,3},{8,12},{9,13},{10,... | collective-permute-start | bytes 497672 | tf_op jit(solution)/shard_map/ppermute | solution.py:488
  85.8 1.3 %after_first.1 = (bf16[8,10368]{1,0:T(8,128)(2,1)S(1)}, bf16[8,10368]{1,0:T(8,128)(2,1)}, bf16[8,10368]{1,0:T(8,128)(2,1)}) custom-call(s32[8]{0:T(128)S(1)} %copy-done.6, bf16[24,10368]{1,0:T(8,128)(2,1)S(1)} %collective-permute-done.14.first.refs_2_, bf16[32,10368]{1,0:T(8,128)(2,1)S(1)} %get-tuple-element.64.local, ...), custom_call_target="tpu_custom_call" | custom-call | tf_op jit(solution)/shard_map/after_first/pallas_call | solution.py:450
  87.2 0.1 collective-permute-start.18
  87.3 3.8 %collective-permute-start.19 = (bf16[8,10368]{1,0:T(8,128)(2,1)}, bf16[8,10368]{1,0:T(8,128)(2,1)S(1)}, u32[]{:S(2)}, u32[]{:S(2)}) collective-permute-start(bf16[8,10368]{1,0:T(8,128)(2,1)} %get-tuple-element.72), channel_id=1, source_target_pairs={{2,0},{3,1},{0,2},{1,3},{6,4},{7,5},{4,6},{5,7},{10,8},{11,9},{8,1... | collective-permute-start | bytes 497672 | tf_op jit(solution)/shard_map/ppermute | solution.py:484
  91.1 2.5 %own_terms.1.total.refs_7_ = f32[896,1024]{1,0:T(8,128)S(1)} custom-call(bf16[1,896,1024]{2,1,0:T(8,128)(2,1)S(1)} %copy-done.2, bf16[72,896]{1,0:T(8,128)(2,1)S(1)} %get-tuple-element.47.refs_4_.refs_0_, bf16[72,896]{1,0:T(8,128)(2,1)S(1)} %collective-permute-done.7.refs_5_.refs_1_, bf16[72,896]{1,0:T(8,128)(2,1)S(1)} %collective-permute-done.8.refs_6_.refs_2_, ...), custom_call_target="tpu_custom_call" | custom-call | tf_op jit(solution)/shard_map/own_terms/pallas_call | solution.py:450
  93.6 0.0 copy-start.7
  93.6 0.0 copy-start.8
  93.7 1.8 %after_last.1 = (bf16[8,10368]{1,0:T(8,128)(2,1)S(1)}, bf16[72,1024]{1,0:T(8,128)(2,1)}) custom-call(s32[8]{0:T(128)S(1)} %copy-done.6, bf16[8,10368]{1,0:T(8,128)(2,1)S(1)} %collective-permute-done.13.last.refs_1_, bf16[32,10368]{1,0:T(8,128)(2,1)S(1)} %get-tuple-element.64.local, bf16[24,10368]{1,0:T(8,128)(2,1)S(1)} %collective-permute-done.14.first.refs_2_, ...), custom_call_target="tpu_custom_call" | custom-call | tf_op jit(solution)/shard_map/after_last/pallas_call | solution.py:450
  95.5 0.7 copy-done.4
  96.1 1.5 %collective-permute-start.22 = (bf16[72,1024]{1,0:T(8,128)(2,1)}, bf16[72,1024]{1,0:T(8,128)(2,1)}, u32[]{:S(2)}, u32[]{:S(2)}) collective-permute-start(bf16[72,1024]{1,0:T(8,128)(2,1)} %get-tuple-element.76.refs_3_), channel_id=1, source_target_pairs={{16,0},{24,8},{0,16},{8,24},{17,1},{25,9},{1,17},{9,25},{18,2},{26... | collective-permute-start | bytes 442376 | tf_op jit(solution)/shard_map/ppermute | solution.py:494
  97.6 0.4 collective-permute-start.23
  98.0 0.9 copy-done.5
  98.9 3.0 %unpack.1 = (bf16[128,1024]{1,0:T(8,128)(2,1)}, bf16[128,3584]{1,0:T(8,128)(2,1)}) custom-call(s32[1,128]{1,0:T(1,128)S(1)} %bitcast.4, f32[1,128]{1,0:T(1,128)S(1)} %bitcast.6, bf16[8,10368]{1,0:T(8,128)(2,1)S(1)} %get-tuple-element.59.refs_0_, bf16[8,10368]{1,0:T(8,128)(2,1)S(1)} %collective-permute-done.10.refs_0_.refs_1_, ...), custom_call_target="tpu_custom_call" | custom-call | flops 150994944 | bytes 2507776 | tf_op jit(solution)/shard_map/unpack/pallas_call | solution.py:450
  102.0 1.1 %collective-permute-done.22.refs_5_ = bf16[72,1024]{1,0:T(8,128)(2,1)} collective-permute-done((bf16[72,1024]{1,0:T(8,128)(2,1)}, bf16[72,1024]{1,0:T(8,128)(2,1)}, u32[]{:S(2)}, u32[]{:S(2)}) %collective-permute-start.22) | collective-permute-done | bytes 147488 | tf_op jit(solution)/shard_map/ppermute | solution.py:494
  103.1 2.4 %collective-permute-done.23.refs_6_ = bf16[72,1024]{1,0:T(8,128)(2,1)} collective-permute-done((bf16[72,1024]{1,0:T(8,128)(2,1)}, bf16[72,1024]{1,0:T(8,128)(2,1)}, u32[]{:S(2)}, u32[]{:S(2)}) %collective-permute-start.23) | collective-permute-done | bytes 147488 | tf_op jit(solution)/shard_map/ppermute | solution.py:494
  105.5 2.0 %copy-done.1 = f32[896,1024]{1,0:T(8,128)S(1)} copy-done((f32[896,1024]{1,0:T(8,128)S(1)}, f32[896,1024]{1,0:T(8,128)}, u32[]{:S(2)}) %copy-start.1) | copy-done | bytes 3670040
  107.5 5.9 %update.1 = (bf16[1,896,1024]{2,1,0:T(8,128)(2,1)}, bf16[1,896,1024]{2,1,0:T(8,128)(2,1)}) custom-call(s32[1]{0:T(128)} %bitcast.2.g_ref, s32[8]{0:T(128)S(1)} %copy-done.6, bf16[8,10368]{1,0:T(8,128)(2,1)S(1)} %collective-permute-done.13.last.refs_1_, bf16[24,10368]{1,0:T(8,128)(2,1)S(1)} %collective-permute-done.14.first.refs_2_, ...), custom_call_target="tpu_custom_call" | custom-call | flops 528482304 | bytes 11010048 | tf_op jit(solution)/shard_map/update/pallas_call | solution.py:619
  (32 shorter events, 0.1 us)
Async XLA Ops:
  4.0 12.5 %collective-permute-start = (bf16[16,10368]{1,0:T(8,128)(2,1)}, bf16[16,10368]{1,0:T(8,128)(2,1)S(1)}, u32[]{:S(2)}, u32[]{:S(2)}) collective-permute-start(bf16[16,10368]{1,0:T(8,128)(2,1)} %get-tuple-element.44), channel_id=1, source_target_pairs={{0,1},{1,0},{2,3},{3,2},{4,5},{5,4},{6,7},{7,6},{8,9},{9,8},{10,11... | collective-permute-start | bytes 995336 | tf_op jit(solution)/shard_map/ppermute | solution.py:477
  7.0 18.0 %collective-permute-start.1 = (bf16[16,10368]{1,0:T(8,128)(2,1)}, bf16[16,10368]{1,0:T(8,128)(2,1)S(1)}, u32[]{:S(2)}, u32[]{:S(2)}) collective-permute-start(bf16[16,10368]{1,0:T(8,128)(2,1)} %get-tuple-element.45), channel_id=1, source_target_pairs={{0,2},{1,3},{2,0},{3,1},{4,6},{5,7},{6,4},{7,5},{8,10},{9,11},{10,... | collective-permute-start | bytes 995336 | tf_op jit(solution)/shard_map/ppermute | solution.py:477
  8.6 21.9 %collective-permute-start.2 = (bf16[16,10368]{1,0:T(8,128)(2,1)}, bf16[16,10368]{1,0:T(8,128)(2,1)S(1)}, u32[]{:S(2)}, u32[]{:S(2)}) collective-permute-start(bf16[16,10368]{1,0:T(8,128)(2,1)} %get-tuple-element.46), channel_id=1, source_target_pairs={{0,3},{1,2},{2,1},{3,0},{4,7},{5,6},{6,5},{7,4},{8,11},{9,10},{10,... | collective-permute-start | bytes 995336 | tf_op jit(solution)/shard_map/ppermute | solution.py:477
  8.6 22.2 %collective-permute-start.3 = (bf16[8,10368]{1,0:T(8,128)(2,1)}, bf16[8,10368]{1,0:T(8,128)(2,1)S(1)}, u32[]{:S(2)}, u32[]{:S(2)}) collective-permute-start(bf16[8,10368]{1,0:T(8,128)(2,1)} %get-tuple-element.52), channel_id=1, source_target_pairs={{0,4},{1,5},{2,6},{3,7},{4,0},{5,1},{6,2},{7,3},{8,12},{9,13},{10,... | collective-permute-start | bytes 497672 | tf_op jit(solution)/shard_map/ppermute | solution.py:477
  11.6 5.0 %copy-start.10 = (bf16[8,10368]{1,0:T(8,128)(2,1)S(1)}, bf16[8,10368]{1,0:T(8,128)(2,1)}, u32[]{:S(2)}) copy-start(bf16[8,10368]{1,0:T(8,128)(2,1)} %get-tuple-element.54) | copy-start | bytes 497668
  11.6 13.5 %copy-start.9 = (bf16[8,10368]{1,0:T(8,128)(2,1)S(1)}, bf16[8,10368]{1,0:T(8,128)(2,1)}, u32[]{:S(2)}) copy-start(bf16[8,10368]{1,0:T(8,128)(2,1)} %get-tuple-element.55) | copy-start | bytes 497668
  11.6 18.9 %copy-start.3 = (bf16[16,10368]{1,0:T(8,128)(2,1)S(1)}, bf16[16,10368]{1,0:T(8,128)(2,1)}, u32[]{:S(2)}) copy-start(bf16[16,10368]{1,0:T(8,128)(2,1)} %get-tuple-element.43.refs_0_) | copy-start | bytes 995332
  11.6 21.1 %copy-start.6 = (s32[8]{0:T(128)S(1)}, s32[8]{0:T(128)}, u32[]{:S(2)}) copy-start(s32[8]{0:T(128)} %refs_0_.1) | copy-start | bytes 100
  11.6 21.0 %collective-permute-start.4 = (bf16[8,10368]{1,0:T(8,128)(2,1)}, bf16[8,10368]{1,0:T(8,128)(2,1)S(1)}, u32[]{:S(2)}, u32[]{:S(2)}) collective-permute-start(bf16[8,10368]{1,0:T(8,128)(2,1)} %get-tuple-element.53), channel_id=1, source_target_pairs={{0,5},{1,4},{2,7},{3,6},{4,1},{5,0},{6,3},{7,2},{8,13},{9,12},{10,... | collective-permute-start | bytes 497672 | tf_op jit(solution)/shard_map/ppermute | solution.py:477
  16.6 21.3 %collective-permute-start.5 = (bf16[8,10368]{1,0:T(8,128)(2,1)S(1)}, bf16[8,10368]{1,0:T(8,128)(2,1)S(1)}, u32[]{:S(2)}, u32[]{:S(2)}) collective-permute-start(bf16[8,10368]{1,0:T(8,128)(2,1)S(1)} %copy-done.10), channel_id=1, source_target_pairs={{0,6},{1,7},{2,4},{3,5},{4,2},{5,3},{6,0},{7,1},{8,14},{9,15},{10,... | collective-permute-start | bytes 497672 | tf_op jit(solution)/shard_map/ppermute | solution.py:477
  25.1 14.8 %collective-permute-start.6 = (bf16[8,10368]{1,0:T(8,128)(2,1)S(1)}, bf16[8,10368]{1,0:T(8,128)(2,1)S(1)}, u32[]{:S(2)}, u32[]{:S(2)}) collective-permute-start(bf16[8,10368]{1,0:T(8,128)(2,1)S(1)} %copy-done.9), channel_id=1, source_target_pairs={{0,7},{1,6},{2,5},{3,4},{4,3},{5,2},{6,1},{7,0},{8,15},{9,14},{10,... | collective-permute-start | bytes 497672 | tf_op jit(solution)/shard_map/ppermute | solution.py:477
  30.8 9.2 %collective-permute-start.7 = (bf16[72,896]{1,0:T(8,128)(2,1)S(1)}, bf16[72,896]{1,0:T(8,128)(2,1)S(1)}, u32[]{:S(2)}, u32[]{:S(2)}) collective-permute-start(bf16[72,896]{1,0:T(8,128)(2,1)S(1)} %get-tuple-element.56), channel_id=1, source_target_pairs={{8,0},{0,8},{24,16},{16,24},{9,1},{1,9},{25,17},{17,25},{10,2},{2,... | collective-permute-start | bytes 387080 | tf_op jit(solution)/shard_map/ppermute | solution.py:494
  30.8 9.1 %collective-permute-start.8 = (bf16[72,896]{1,0:T(8,128)(2,1)S(1)}, bf16[72,896]{1,0:T(8,128)(2,1)S(1)}, u32[]{:S(2)}, u32[]{:S(2)}) collective-permute-start(bf16[72,896]{1,0:T(8,128)(2,1)S(1)} %get-tuple-element.57), channel_id=1, source_target_pairs={{16,0},{24,8},{0,16},{8,24},{17,1},{25,9},{1,17},{9,25},{18,2},{26... | collective-permute-start | bytes 387080 | tf_op jit(solution)/shard_map/ppermute | solution.py:494
  32.6 7.3 %collective-permute-start.9 = (bf16[72,896]{1,0:T(8,128)(2,1)S(1)}, bf16[72,896]{1,0:T(8,128)(2,1)S(1)}, u32[]{:S(2)}, u32[]{:S(2)}) collective-permute-start(bf16[72,896]{1,0:T(8,128)(2,1)S(1)} %get-tuple-element.58), channel_id=1, source_target_pairs={{24,0},{16,8},{8,16},{0,24},{25,1},{17,9},{9,17},{1,25},{26,2},{18... | collective-permute-start | bytes 387080 | tf_op jit(solution)/shard_map/ppermute | solution.py:494
  40.0 51.2 %copy-start.2 = (bf16[1,896,1024]{2,1,0:T(8,128)(2,1)S(1)}, bf16[1,896,1024]{2,1,0:T(8,128)(2,1)}, u32[]{:S(2)}) copy-start(bf16[1,896,1024]{2,1,0:T(8,128)(2,1)} %momentum_hbm.1) | copy-start | bytes 5505028
  42.5 44.8 %collective-permute-start.15 = (bf16[72,4864]{1,0:T(8,128)(2,1)S(1)}, bf16[72,4864]{1,0:T(8,128)(2,1)S(1)}, u32[]{:S(2)}, u32[]{:S(2)}) collective-permute-start(bf16[72,4864]{1,0:T(8,128)(2,1)S(1)} %get-tuple-element.67), channel_id=1, source_target_pairs={{8,0},{0,8},{24,16},{16,24},{9,1},{1,9},{25,17},{17,25},{10,2},{2,... | collective-permute-start | bytes 2101256 | tf_op jit(solution)/shard_map/ppermute | solution.py:494
  42.6 48.5 %collective-permute-start.16 = (bf16[72,4864]{1,0:T(8,128)(2,1)S(1)}, bf16[72,4864]{1,0:T(8,128)(2,1)S(1)}, u32[]{:S(2)}, u32[]{:S(2)}) collective-permute-start(bf16[72,4864]{1,0:T(8,128)(2,1)S(1)} %get-tuple-element.68), channel_id=1, source_target_pairs={{16,0},{24,8},{0,16},{8,24},{17,1},{25,9},{1,17},{9,25},{18,2},{26... | collective-permute-start | bytes 2101256 | tf_op jit(solution)/shard_map/ppermute | solution.py:494
  44.2 46.9 %collective-permute-start.17 = (bf16[72,4864]{1,0:T(8,128)(2,1)S(1)}, bf16[72,4864]{1,0:T(8,128)(2,1)S(1)}, u32[]{:S(2)}, u32[]{:S(2)}) collective-permute-start(bf16[72,4864]{1,0:T(8,128)(2,1)S(1)} %get-tuple-element.69), channel_id=1, source_target_pairs={{24,0},{16,8},{8,16},{0,24},{25,1},{17,9},{9,17},{1,25},{26,2},{18... | collective-permute-start | bytes 2101256 | tf_op jit(solution)/shard_map/ppermute | solution.py:494
  44.5 8.7 %collective-permute-start.10 = (bf16[8,10368]{1,0:T(8,128)(2,1)S(1)}, bf16[8,10368]{1,0:T(8,128)(2,1)S(1)}, u32[]{:S(2)}, u32[]{:S(2)}) collective-permute-start(bf16[8,10368]{1,0:T(8,128)(2,1)S(1)} %get-tuple-element.60), channel_id=1, source_target_pairs={{1,0},{0,1},{3,2},{2,3},{5,4},{4,5},{7,6},{6,7},{9,8},{8,9},{11,10... | collective-permute-start | bytes 497672 | tf_op jit(solution)/shard_map/ppermute | solution.py:484
  48.4 37.5 %collective-permute-start.14 = (bf16[24,10368]{1,0:T(8,128)(2,1)S(1)}, bf16[24,10368]{1,0:T(8,128)(2,1)S(1)}, u32[]{:S(2)}, u32[]{:S(2)}) collective-permute-start(bf16[24,10368]{1,0:T(8,128)(2,1)S(1)} %get-tuple-element.65), channel_id=1, source_target_pairs={{0,4},{1,5},{2,6},{3,7},{4,0},{5,1},{6,2},{7,3},{8,12},{9,13},{10,... | collective-permute-start | bytes 1493000 | tf_op jit(solution)/shard_map/ppermute | solution.py:488
  53.1 13.1 %collective-permute-start.11 = (bf16[8,10368]{1,0:T(8,128)(2,1)S(1)}, bf16[8,10368]{1,0:T(8,128)(2,1)S(1)}, u32[]{:S(2)}, u32[]{:S(2)}) collective-permute-start(bf16[8,10368]{1,0:T(8,128)(2,1)S(1)} %get-tuple-element.61), channel_id=1, source_target_pairs={{2,0},{3,1},{0,2},{1,3},{6,4},{7,5},{4,6},{5,7},{10,8},{11,9},{8,1... | collective-permute-start | bytes 497672 | tf_op jit(solution)/shard_map/ppermute | solution.py:484
  66.2 11.1 %collective-permute-start.12 = (bf16[8,10368]{1,0:T(8,128)(2,1)S(1)}, bf16[8,10368]{1,0:T(8,128)(2,1)S(1)}, u32[]{:S(2)}, u32[]{:S(2)}) collective-permute-start(bf16[8,10368]{1,0:T(8,128)(2,1)S(1)} %get-tuple-element.62), channel_id=1, source_target_pairs={{3,0},{2,1},{1,2},{0,3},{7,4},{6,5},{5,6},{4,7},{11,8},{10,9},{9,1... | collective-permute-start | bytes 497672 | tf_op jit(solution)/shard_map/ppermute | solution.py:484
  77.3 16.4 %collective-permute-start.13 = (bf16[8,10368]{1,0:T(8,128)(2,1)S(1)}, bf16[8,10368]{1,0:T(8,128)(2,1)S(1)}, u32[]{:S(2)}, u32[]{:S(2)}) collective-permute-start(bf16[8,10368]{1,0:T(8,128)(2,1)S(1)} %get-tuple-element.63), channel_id=1, source_target_pairs={{0,4},{1,5},{2,6},{3,7},{4,0},{5,1},{6,2},{7,3},{8,12},{9,13},{10,... | collective-permute-start | bytes 497672 | tf_op jit(solution)/shard_map/ppermute | solution.py:488
  87.2 10.5 %collective-permute-start.18 = (bf16[8,10368]{1,0:T(8,128)(2,1)S(1)}, bf16[8,10368]{1,0:T(8,128)(2,1)S(1)}, u32[]{:S(2)}, u32[]{:S(2)}) collective-permute-start(bf16[8,10368]{1,0:T(8,128)(2,1)S(1)} %get-tuple-element.71), channel_id=1, source_target_pairs={{1,0},{0,1},{3,2},{2,3},{5,4},{4,5},{7,6},{6,7},{9,8},{8,9},{11,10... | collective-permute-start | bytes 497672 | tf_op jit(solution)/shard_map/ppermute | solution.py:484
  87.3 10.7 %collective-permute-start.19 = (bf16[8,10368]{1,0:T(8,128)(2,1)}, bf16[8,10368]{1,0:T(8,128)(2,1)S(1)}, u32[]{:S(2)}, u32[]{:S(2)}) collective-permute-start(bf16[8,10368]{1,0:T(8,128)(2,1)} %get-tuple-element.72), channel_id=1, source_target_pairs={{2,0},{3,1},{0,2},{1,3},{6,4},{7,5},{4,6},{5,7},{10,8},{11,9},{8,1... | collective-permute-start | bytes 497672 | tf_op jit(solution)/shard_map/ppermute | solution.py:484
  91.1 6.9 %collective-permute-start.20 = (bf16[8,10368]{1,0:T(8,128)(2,1)}, bf16[8,10368]{1,0:T(8,128)(2,1)}, u32[]{:S(2)}, u32[]{:S(2)}) collective-permute-start(bf16[8,10368]{1,0:T(8,128)(2,1)} %get-tuple-element.73), channel_id=1, source_target_pairs={{3,0},{2,1},{1,2},{0,3},{7,4},{6,5},{5,6},{4,7},{11,8},{10,9},{9,1... | collective-permute-start | bytes 497672 | tf_op jit(solution)/shard_map/ppermute | solution.py:484
  93.6 1.8 %copy-start = (f32[896,1024]{1,0:T(8,128)}, f32[896,1024]{1,0:T(8,128)S(1)}, u32[]{:S(2)}) copy-start(f32[896,1024]{1,0:T(8,128)S(1)} %own_terms.1.total.refs_7_) | copy-start | bytes 11010052
  93.6 4.4 %copy-start.7 = (s32[128]{0:T(128)S(1)}, s32[128]{0:T(128)}, u32[]{:S(2)}) copy-start(s32[128]{0:T(128)} %param.10) | copy-start | bytes 1540
  93.6 4.4 %copy-start.8 = (f32[128]{0:T(128)S(1)}, f32[128]{0:T(128)}, u32[]{:S(2)}) copy-start(f32[128]{0:T(128)} %param.8) | copy-start | bytes 1540
  95.5 0.7 copy-start.4
  96.1 5.8 %collective-permute-start.21 = (bf16[72,1024]{1,0:T(8,128)(2,1)}, bf16[72,1024]{1,0:T(8,128)(2,1)}, u32[]{:S(2)}, u32[]{:S(2)}) collective-permute-start(bf16[72,1024]{1,0:T(8,128)(2,1)} %get-tuple-element.76.refs_3_), channel_id=1, source_target_pairs={{8,0},{0,8},{24,16},{16,24},{9,1},{1,9},{25,17},{17,25},{10,2},{2,... | collective-permute-start | bytes 442376 | tf_op jit(solution)/shard_map/ppermute | solution.py:494
  96.1 7.0 %collective-permute-start.22 = (bf16[72,1024]{1,0:T(8,128)(2,1)}, bf16[72,1024]{1,0:T(8,128)(2,1)}, u32[]{:S(2)}, u32[]{:S(2)}) collective-permute-start(bf16[72,1024]{1,0:T(8,128)(2,1)} %get-tuple-element.76.refs_3_), channel_id=1, source_target_pairs={{16,0},{24,8},{0,16},{8,24},{17,1},{25,9},{1,17},{9,25},{18,2},{26... | collective-permute-start | bytes 442376 | tf_op jit(solution)/shard_map/ppermute | solution.py:494
  97.6 7.9 %collective-permute-start.23 = (bf16[72,1024]{1,0:T(8,128)(2,1)}, bf16[72,1024]{1,0:T(8,128)(2,1)}, u32[]{:S(2)}, u32[]{:S(2)}) collective-permute-start(bf16[72,1024]{1,0:T(8,128)(2,1)} %get-tuple-element.76.refs_3_), channel_id=1, source_target_pairs={{24,0},{16,8},{8,16},{0,24},{25,1},{17,9},{9,17},{1,25},{26,2},{18... | collective-permute-start | bytes 442376 | tf_op jit(solution)/shard_map/ppermute | solution.py:494
  98.0 0.9 copy-start.5
  105.5 2.0 %copy-start.1 = (f32[896,1024]{1,0:T(8,128)S(1)}, f32[896,1024]{1,0:T(8,128)}, u32[]{:S(2)}) copy-start(f32[896,1024]{1,0:T(8,128)} %copy-done) | copy-start | bytes 11010052

commit v6 on v5

--- a/solution.py
+++ b/solution.py
@@ -284,36 +284,33 @@
 
 
 def payload_kernel(
-    plan, placement_ref, weight_ref, folded_grad, near_grads, far_rows, near_back, *refs
+    plan, placement_ref, weight_ref, folded_grad, near_grads, far_rows, *refs
 ):
     half, groups = plan.half, plan.groups
     far, refs = refs[:half], refs[half:]
     columns, refs = refs[:groups], refs[groups:]
-    first, last, refs = refs[0], refs[1], refs[2:]
-    shared, early, rows = refs[:groups], refs[groups : groups + half], refs[groups + half]
+    payload, refs = refs[0], refs[1:]
+    shared, rows = refs[:groups], refs[groups]
     hot = is_hot(plan, placement_ref)
     x = unfold(plan, blocks_of(far, 0, plan.DX), plan.D)
     g = unfold(plan, blocks_of(far, plan.DX, plan.C), plan.F)
     rows[...] = x
     act, grad_pre = activate(dot(x, weight_ref[...]), g)
 
-    def store(data, start):
-        stop = start + data.shape[1]
-        first[:, start:stop] = data[SUB:].astype(BF16)
-        last[:, start:stop] = data[:SUB].astype(BF16)
-
     @pl.when(jnp.logical_not(hot))
     def _():
-        store(fold(plan, dot_nt(grad_pre, weight_ref[...])), 0)
-        store(fold(plan, act.astype(F32)), plan.DX)
+        payload[:, : plan.DX] = fold(plan, dot_nt(grad_pre, weight_ref[...])).astype(BF16)
+        payload[:, plan.DX :] = fold(plan, act.astype(F32)).astype(BF16)
 
     @pl.when(hot)
     def _():
         together = jnp.concatenate([c[...].astype(F32) for c in columns], axis=0)
         block = half * SUB
         for i in range(plan.pieces):
-            store(together[i * block : (i + 1) * block], i * plan.share)
-        store(folded_grad[...].astype(F32), plan.DX)
+            payload[:, i * plan.share : (i + 1) * plan.share] = together[
+                i * block : (i + 1) * block
+            ].astype(BF16)
+        payload[:, plan.DX :] = folded_grad[...]
 
     group = lax.axis_index("dp")
     width = plan.share
@@ -323,67 +320,62 @@
         shared[m][:, width : 2 * width] = rows[:, pl.ds(start, width)]
         shared[m][:, 2 * width : 2 * width + 2 * plan.F] = near_grads[...]
         shared[m][:, 2 * width + 2 * plan.F :] = grad_pre
+
+
+def early_kernel(plan, near_back, *refs):
     back = near_back[...].astype(F32)
-    for m in range(half):
-        early[m][...] = back[m * SUB : (m + 1) * SUB].astype(BF16)
-
-
-def choose(plan, placement_ref, local, got):
+    for m, out in enumerate(refs[-plan.half :]):
+        out[...] = back[m * SUB : (m + 1) * SUB].astype(BF16)
+
+
+def after_kernel(plan, placement_ref, payload, local, *refs):
+    outs = refs[-plan.half - 1 :]
     hot = is_hot(plan, placement_ref)
-    return jnp.where(hot, local, got[...].astype(F32))
-
-
-def after_first_kernel(plan, placement_ref, first, local, *refs):
-    outs = refs[1 - plan.half :]
-    chosen = choose(plan, placement_ref, local[...].astype(F32)[SUB:], first)
-    for m in range(plan.half - 1):
+    got = payload[...].astype(F32)
+    chosen = jnp.where(hot, local[...].astype(F32), got)
+    for m in range(plan.half):
         outs[m][...] = chosen[m * SUB : (m + 1) * SUB].astype(BF16)
-
-
-def after_last_kernel(plan, placement_ref, last, local, first, total, back, grad):
-    chosen = choose(plan, placement_ref, local[...].astype(F32)[:SUB], last)
-    back[...] = chosen.astype(BF16)
-    got = first[:, plan.DX :].astype(F32)
-    blocks = [last[:, plan.DX :].astype(F32)]
-    blocks += [got[m * SUB : (m + 1) * SUB] for m in range(plan.half - 1)]
-    hot = is_hot(plan, placement_ref)
-    grad[...] = jnp.where(hot, unfold(plan, blocks, plan.F).astype(F32), 0.0).astype(BF16)
+    blocks = [got[m * SUB : (m + 1) * SUB, plan.DX :] for m in range(plan.half)]
+    outs[plan.half][...] = jnp.where(hot, unfold(plan, blocks, plan.F).astype(F32), 0.0).astype(BF16)
 
 
 def unpack_kernel(plan, slot_ref, gate_ref, *refs):
-    early, refs = refs[: plan.half], refs[plan.half :]
-    late, refs = refs[: plan.half], refs[plan.half :]
-    out_ref, grad_ref = refs
+    count = 2 * plan.half
+    got, refs = refs[:count], refs[count:]
+    out_ref, grad_ref, held, sems = refs
+    copies = [
+        pltpu.make_async_copy(source, held.at[i], sems.at[i]) for i, source in enumerate(got)
+    ]
+    for copy in copies:
+        copy.start()
     block, rank = token_places(plan, slot_ref[...])
-    width = 2 * plan.half * SUB
+    width = count * SUB
     picks = []
     for target in row_targets(plan, block, rank):
         column = to_column(target).astype(jnp.int32)
         picks.append((iota((plan.tokens, width), 1) == column).astype(BF16))
-
-    def gather(near, far, size):
-        stacked = []
-        for m in range(plan.half):
-            stacked += [near[m], far[m]]
-        stacked = jnp.concatenate(stacked, axis=0).astype(BF16)
-        total = None
-        for i in range(plan.full):
-            term = dot(picks[i], stacked[:, i * size : (i + 1) * size])
-            total = term if total is None else total + term
-        if plan.rest:
-            tail = stacked[:, plan.full * size :]
-            term = jnp.concatenate(
-                [dot(picks[plan.full + q], tail) for q in range(plan.cuts)], axis=1
-            )
-            total = term if total is None else total + term
-        return total
-
-    def both(start, stop):
-        return blocks_of(early, start, stop), blocks_of(late, start, stop)
-
-    grad_ref[...] = gather(*both(0, plan.DX), plan.D).astype(BF16)
     gate = to_column(gate_ref[...])
-    out_ref[...] = (gate * gather(*both(plan.DX, plan.C), plan.F)).astype(BF16)
+    for copy in copies:
+        copy.wait()
+
+    def gather(base, size):
+        rows = [held[i, :, base : base + size * plan.cap // SUB].astype(F32) for i in range(count)]
+        rows = jnp.concatenate(rows, axis=0).astype(BF16)
+        piece = size // plan.cuts
+        parts = []
+        for q in range(plan.cuts):
+            lhs, rhs = list(picks[: plan.full]), []
+            for i in range(plan.full):
+                start = i * size + q * piece
+                rhs.append(rows[:, start : start + piece])
+            if plan.rest:
+                lhs.append(picks[plan.full + q])
+                rhs.append(rows[:, plan.full * size :])
+            parts.append(dot(jnp.concatenate(lhs, axis=1), jnp.concatenate(rhs, axis=0)))
+        return jnp.concatenate(parts, axis=1)
+
+    grad_ref[...] = gather(0, plan.D).astype(BF16)
+    out_ref[...] = (gate * gather(plan.DX, plan.F)).astype(BF16)
 
 
 def rows_of(parts):
@@ -412,31 +404,43 @@
         total[span, :] = before + dot_tn(x_all[:, span], g_all)
 
 
-def update_kernel(plan, placement_ref, last, first, *refs):
-    other_g, refs = refs[: plan.groups], refs[plan.groups :]
-    total_ref, weight_ref, new_weight, new_momentum, x_all, g_all = refs
-    step = pl.program_id(0)
-    share = plan.share
-    tile = new_weight.shape[1]
-
-    @pl.when(step == 0)
-    def _():
-        hot = is_hot(plan, placement_ref)
-        pieces = [
-            block[:, i * share : (i + 1) * share].astype(F32)
-            for i in range(plan.pieces)
-            for block in (last, first)
-        ]
-        x_all[...] = jnp.where(hot, jnp.concatenate(pieces, axis=0), 0.0).astype(BF16)
-        g_all[...] = rows_of([g[...] for g in other_g])
-
-    start = pl.multiple_of(step * tile, LANES)
-    total = total_ref[...] + dot_tn(x_all[:, pl.ds(start, tile)], g_all[...])
-    momentum = total.astype(BF16)
-    new_momentum[0] = momentum
-    new_weight[0] = (
-        weight_ref[...].astype(F32) - learning_rate * momentum.astype(F32)
-    ).astype(BF16)
+def update_kernel(plan, placement_ref, *refs):
+    groups, share = plan.groups, plan.share
+    sources, refs = refs[: groups + 3], refs[groups + 3 :]
+    new_weight, new_momentum, payload, other_g, total, weight, momentum, sems, out_sems = refs
+    targets = [payload] + [other_g.at[m] for m in range(groups)] + [total, weight]
+    copies = [
+        pltpu.make_async_copy(source, target, sems.at[i])
+        for i, (source, target) in enumerate(zip(sources, targets))
+    ]
+    for copy in copies:
+        copy.start()
+    hot = is_hot(plan, placement_ref)
+    for copy in copies[: groups + 1]:
+        copy.wait()
+    pieces = [payload[:, i * share : (i + 1) * share] for i in range(plan.pieces)]
+    x = jnp.concatenate(pieces, axis=0)
+    x = jnp.where(hot, x.astype(F32), 0.0).astype(BF16)
+    g = rows_of([other_g[m] for m in range(groups)])
+    for copy in copies[groups + 1 :]:
+        copy.wait()
+    done = []
+    for i in range(share // LANES):
+        span = pl.ds(i * LANES, LANES)
+        value = total[span, :] + dot_tn(x[:, i * LANES : (i + 1) * LANES], g)
+        value = value.astype(BF16)
+        momentum[span, :] = value
+        weight[span, :] = (
+            weight[span, :].astype(F32) - learning_rate * value.astype(F32)
+        ).astype(BF16)
+        for j, (source, target) in enumerate(((momentum, new_momentum), (weight, new_weight))):
+            copy = pltpu.make_async_copy(
+                source.at[span, :], target.at[0, span, :], out_sems.at[i, j]
+            )
+            copy.start()
+            done.append(copy)
+    for copy in done:
+        copy.wait()
 
 
 MIB = 1024 * 1024
@@ -558,29 +562,27 @@
     outs = call(
         payload_kernel,
         plan,
-        [placement, held, folded_grad, grads, far_rows, back_near] + far + columns_here,
-        [SMEM_SPEC] + [VMEM_SPEC] * (5 + half + groups),
-        [((half - 1) * SUB, C), (SUB, C)]
-        + [(rows, 2 * share + 3 * F)] * groups
-        + [(SUB, C)] * half,
+        [placement, held, folded_grad, grads, far_rows] + far + columns_here,
+        [SMEM_SPEC] + [VMEM_SPEC] * (4 + half + groups),
+        [(half * SUB, C)] + [(rows, 2 * share + 3 * F)] * groups,
         [pltpu.VMEM((rows, D), BF16)],
         4 * rows * D * F,
         "payload",
     )
-    first, last = to_partner(outs[0]), to_partner(outs[1])
-    shared, outs = from_groups(outs[2 : 2 + groups]), outs[2 + groups :]
-    early = [outs[0]] + [to_source(outs[m], m) for m in range(1, half)]
+    payload = to_partner(outs[0])
+    shared = from_groups(outs[1:])
     outs = call(
-        after_first_kernel,
-        plan,
-        [placement, first, local] + early[1:],
-        [SMEM_SPEC] + [VMEM_SPEC] * 2 + [ANY_SPEC] * (half - 1),
-        [(SUB, C)] * (half - 1),
+        early_kernel,
+        plan,
+        [back_near, shared[1]],
+        [VMEM_SPEC, ANY_SPEC],
+        [(SUB, C)] * half,
         [],
         0,
-        "after_first",
-    )
-    late = [to_source(out, m + 1) for m, out in enumerate(outs)]
+        "early",
+        limit=4,
+    )
+    early = [outs[0]] + [to_source(outs[m], m) for m in range(1, half)]
     (total,) = call(
         gather_kernel,
         plan,
@@ -596,61 +598,54 @@
         "own_terms",
         dtypes=[F32],
     )
-    back, grad = call(
-        after_last_kernel,
-        plan,
-        [placement, last, local, first, total],
-        [SMEM_SPEC] + [VMEM_SPEC] * 3 + [ANY_SPEC],
-        [(SUB, C), (rows, F)],
+    outs = call(
+        after_kernel,
+        plan,
+        [placement, payload, local, total] + early[1:-1],
+        [SMEM_SPEC] + [VMEM_SPEC] * 2 + [ANY_SPEC] * (half - 1),
+        [(SUB, C)] * half + [(rows, F)],
         [],
         0,
-        "after_last",
-    )
-    late = [back] + late
-    other_g = from_groups([grad] * groups)
-
-    tile = LANES
-    steps = share // tile
-    group = lax.axis_index("dp").reshape(1)
-
-    def whole(*shape):
-        return pl.BlockSpec(shape, lambda i, g: (0,) * len(shape))
+        "after_swap",
+        limit=8,
+    )
+    late = [outs[0]] + [to_source(outs[m], m) for m in range(1, half)]
+    other_g = from_groups([outs[half]] * groups)
 
     new_weight, new_momentum = pl.pallas_call(
-        lambda g_ref, *refs: update_kernel(plan, *refs),
-        grid_spec=pltpu.PrefetchScalarGridSpec(
-            num_scalar_prefetch=1,
-            grid=(steps,),
-            in_specs=[SMEM_SPEC]
-            + [whole(*p.shape) for p in (last, first)]
-            + [whole(*g.shape) for g in other_g]
-            + [
-                pl.BlockSpec((tile, F), lambda i, g: (i, 0)),
-                pl.BlockSpec((tile, F), lambda i, g: (i, 0)),
-            ],
-            out_specs=[pl.BlockSpec((1, tile, F), lambda i, g: (0, i, 0))] * 2,
-            scratch_shapes=[
-                pltpu.VMEM((groups * rows, share), BF16),
-                pltpu.VMEM((groups * rows, F), BF16),
-            ],
-        ),
+        functools.partial(update_kernel, plan),
         out_shape=[jax.ShapeDtypeStruct((1, share, F), BF16)] * 2,
-        compiler_params=pltpu.CompilerParams(vmem_limit_bytes=16 * MIB),
+        in_specs=[SMEM_SPEC] + [ANY_SPEC] * (groups + 3),
+        out_specs=[ANY_SPEC] * 2,
+        scratch_shapes=[
+            pltpu.VMEM((half * SUB, C), BF16),
+            pltpu.VMEM((groups, rows, F), BF16),
+            pltpu.VMEM((share, F), F32),
+            pltpu.VMEM((share, F), BF16),
+            pltpu.VMEM((share, F), BF16),
+            pltpu.SemaphoreType.DMA((groups + 3,)),
+            pltpu.SemaphoreType.DMA((share // LANES, 2)),
+        ],
+        compiler_params=pltpu.CompilerParams(vmem_limit_bytes=20 * MIB),
         cost_estimate=pl.CostEstimate(
             flops=2 * groups * rows * share * F, bytes_accessed=12 * share * F, transcendentals=0
         ),
         name="update",
-    )(group, placement, last, first, *other_g, total, old_weight)
+    )(placement, payload, *other_g, total, old_weight)
 
     expert_out, token_grad = call(
         unpack_kernel,
         plan,
-        [slot, gate] + early + late,
-        [VMEM_SPEC] * (2 + 2 * half),
+        [slot, gate] + [data for pair in zip(early, late) for data in pair],
+        [VMEM_SPEC] * 2 + [ANY_SPEC] * (2 * half),
         [(plan.tokens, F), (plan.tokens, D)],
-        [],
+        [
+            pltpu.VMEM((2 * half, SUB, C), BF16),
+            pltpu.SemaphoreType.DMA((2 * half,)),
+        ],
         2 * 4 * half * SUB * plan.tokens * (D + F),
         "unpack",
+        limit=12,
     )
     return expert_out, token_grad, new_weight, new_momentum
 

time: 114 us -> 105 us (0.921)
  the two profiles are of different devices: /device:TPU:0 before, /device:TPU:25 now
where the time goes in v6:
time: 105 us
  waiting for transfers between devices  53.6 us (51%)
  Pallas kernels  25.8 us (25%)
  starting transfers between devices  24.3 us (23%)
    ppermute x9, waiting for transfers between devices, from_group(): return lax.ppermute(data, 'dp', pairs)  35.6 us
    pallas_call x9, Pallas kernels, call(): pl.pallas_call(functools.partial(kernel, plan), out_shape=[jax.ShapeDtype...  21.4 us
    ppermute x9, starting transfers between devices, from_group(): return lax.ppermute(data, 'dp', pairs)  15 us
    ppermute x7, waiting for transfers between devices, to_slot(): return lax.ppermute(data, 'expert', pairs)  14.3 us
    ppermute x7, starting transfers between devices, to_slot(): return lax.ppermute(data, 'expert', pairs)  6.21 us
    pallas_call x1, Pallas kernels, routed(): pl.pallas_call(functools.partial(update_kernel, plan), out_shape=[jax.Sha...  4.42 us
    ppermute x6, waiting for transfers between devices, to_source(): return lax.ppermute(data, 'expert', pairs)  3.67 us
    ppermute x6, starting transfers between devices, to_source(): return lax.ppermute(data, 'expert', pairs)  3.05 us
  transfers between devices with their start and end apart: 23, of which 8 were waited for; matrix products, arithmetic and copies ran while one was open for 0% of the time, Pallas kernels for 15%

profile of v6, /device:TPU:25, one launch (start us, length us, event | category | flops | bytes accessed | tf_op | source)
XLA Modules:
  0.0 104.6 jit_solution(5697306280213450609)
XLA Ops:
  0.6 3.4 %pack.1 = (bf16[16,10368]{1,0:T(8,128)(2,1)}, bf16[16,10368]{1,0:T(8,128)(2,1)}, bf16[16,10368]{1,0:T(8,128)(2,1)}, bf16[16,10368]{1,0:T(8,128)(2,1)}, bf16[8,10...) custom-call(s32[1,128]{1,0:T(1,128)} %bitcast.2, ...), custom_call_target="tpu_custom_call" | custom-call | flops 150994944 | bytes 3171328 | tf_op jit(solution)/shard_map/pack/pallas_call | solution.py:454
  4.0 1.3 %collective-permute-start = (bf16[16,10368]{1,0:T(8,128)(2,1)}, bf16[16,10368]{1,0:T(8,128)(2,1)S(1)}, u32[]{:S(2)}, u32[]{:S(2)}) collective-permute-start(bf16[16,10368]{1,0:T(8,128)(2,1)} %get-tuple-element.43), channel_id=1, source_target_pairs={{0,1},{1,0},{2,3},{3,2},{4,5},{5,4},{6,7},{7,6},{8,9},{9,8},{10,11... | collective-permute-start | bytes 995336 | tf_op jit(solution)/shard_map/ppermute | solution.py:481
  5.3 0.2 collective-permute-start.1
  5.5 1.3 %collective-permute-start.2 = (bf16[16,10368]{1,0:T(8,128)(2,1)}, bf16[16,10368]{1,0:T(8,128)(2,1)S(1)}, u32[]{:S(2)}, u32[]{:S(2)}) collective-permute-start(bf16[16,10368]{1,0:T(8,128)(2,1)} %get-tuple-element.45), channel_id=1, source_target_pairs={{0,3},{1,2},{2,1},{3,0},{4,7},{5,6},{6,5},{7,4},{8,11},{9,10},{10,... | collective-permute-start | bytes 995336 | tf_op jit(solution)/shard_map/ppermute | solution.py:481
  6.7 0.1 collective-permute-start.3
  6.8 3.3 %collective-permute-start.4 = (bf16[8,10368]{1,0:T(8,128)(2,1)}, bf16[8,10368]{1,0:T(8,128)(2,1)S(1)}, u32[]{:S(2)}, u32[]{:S(2)}) collective-permute-start(bf16[8,10368]{1,0:T(8,128)(2,1)} %get-tuple-element.52), channel_id=1, source_target_pairs={{0,5},{1,4},{2,7},{3,6},{4,1},{5,0},{6,3},{7,2},{8,13},{9,12},{10,... | collective-permute-start | bytes 497672 | tf_op jit(solution)/shard_map/ppermute | solution.py:481
  10.1 3.6 %hold.1 = (bf16[3584,1024]{1,0:T(8,128)(2,1)S(1)}, bf16[896,1024]{1,0:T(8,128)(2,1)S(1)}) custom-call(bf16[1,3584,1024]{2,1,0:T(8,128)(2,1)} %weight_hbm.1), custom_call_target="tpu_custom_call" | custom-call | tf_op jit(solution)/shard_map/hold/pallas_call | solution.py:454
  13.7 0.0 collective-permute-done.refs_1_
  13.7 0.1 collective-permute-start.5
  13.8 7.1 %collective-permute-done.1.refs_2_ = bf16[16,10368]{1,0:T(8,128)(2,1)S(1)} collective-permute-done((bf16[16,10368]{1,0:T(8,128)(2,1)}, bf16[16,10368]{1,0:T(8,128)(2,1)S(1)}, u32[]{:S(2)}, u32[]{:S(2)}) %collective-permute-start.1) | collective-permute-done | bytes 331808 | tf_op jit(solution)/shard_map/ppermute | solution.py:481
  21.0 0.1 collective-permute-start.6
  21.0 7.1 %collective-permute-done.2.refs_3_ = bf16[16,10368]{1,0:T(8,128)(2,1)S(1)} collective-permute-done((bf16[16,10368]{1,0:T(8,128)(2,1)}, bf16[16,10368]{1,0:T(8,128)(2,1)S(1)}, u32[]{:S(2)}, u32[]{:S(2)}) %collective-permute-start.2) | collective-permute-done | bytes 331808 | tf_op jit(solution)/shard_map/ppermute | solution.py:481
  28.2 0.2 near_columns.1
  28.4 8.9 %collective-permute-start.7 = (bf16[72,896]{1,0:T(8,128)(2,1)S(1)}, bf16[72,896]{1,0:T(8,128)(2,1)S(1)}, u32[]{:S(2)}, u32[]{:S(2)}) collective-permute-start(bf16[72,896]{1,0:T(8,128)(2,1)S(1)} %get-tuple-element.55), channel_id=1, source_target_pairs={{8,0},{0,8},{24,16},{16,24},{9,1},{1,9},{25,17},{17,25},{10,2},{2,... | collective-permute-start | bytes 387080 | tf_op jit(solution)/shard_map/ppermute | solution.py:498
  37.3 0.0 collective-permute-done.3.refs_0_
  37.3 1.3 %collective-permute-start.8 = (bf16[72,896]{1,0:T(8,128)(2,1)S(1)}, bf16[72,896]{1,0:T(8,128)(2,1)S(1)}, u32[]{:S(2)}, u32[]{:S(2)}) collective-permute-start(bf16[72,896]{1,0:T(8,128)(2,1)S(1)} %get-tuple-element.56), channel_id=1, source_target_pairs={{16,0},{24,8},{0,16},{8,24},{17,1},{25,9},{1,17},{9,25},{18,2},{26... | collective-permute-start | bytes 387080 | tf_op jit(solution)/shard_map/ppermute | solution.py:498
  38.6 0.0 collective-permute-done.4.refs_1_
  38.6 0.5 collective-permute-start.9
  39.0 4.7 %near_rows.1 = (bf16[32,10368]{1,0:T(8,128)(2,1)S(1)}, bf16[32,10368]{1,0:T(8,128)(2,1)S(1)}, bf16[32,2304]{1,0:T(8,128)(2,1)S(1)}, bf16[72,2048]{1,0:T(8,128)(2,1)S(1)}, bf16[72,3584]{1,0:T(8,128)(2,1)S(1)}) custom-call(s32[8]{0:T(128)S(1)} %copy-done.2, bf16[3584,1024]{1,0:T(8,128)(2,1)S(1)} %get-tuple-element.41.weight_ref, ...), custom_call_target="tpu_custom_call" | custom-call | flops 2113929216 | bytes 11081760 | tf_op jit(solution)/shard_map/near_rows/pallas_call | solution.py:454
  43.7 0.0 collective-permute-done.5.refs_2_
  43.7 0.0 collective-permute-done.6.refs_3_
  43.7 0.0 collective-permute-done.7.refs_5_.refs_1_
  43.7 1.5 %collective-permute-done.9.refs_7_.refs_3_ = bf16[72,896]{1,0:T(8,128)(2,1)S(1)} collective-permute-done((bf16[72,896]{1,0:T(8,128)(2,1)S(1)}, bf16[72,896]{1,0:T(8,128)(2,1)S(1)}, u32[]{:S(2)}, u32[]{:S(2)}) %collective-permute-start.9) | collective-permute-done | bytes 129056 | tf_op jit(solution)/shard_map/ppermute | solution.py:498
  45.3 2.5 %payload.1 = (bf16[32,10368]{1,0:T(8,128)(2,1)S(1)}, bf16[72,4864]{1,0:T(8,128)(2,1)S(1)}, bf16[72,4864]{1,0:T(8,128)(2,1)S(1)}, bf16[72,4864]{1,0:T(8,128)(2,1)S(1)}, bf16[72,4864]{1,0:T(8,128)(2,1)S(1)}) custom-call(s32[8]{0:T(128)S(1)} %copy-done.2, bf16[3584,1024]{1,0:T(8,128)(2,1)S(1)} %get-tuple-element.41.weight_ref, ...), custom_call_target="tpu_custom_call" | custom-call | flops 1056964608 | bytes 12943392 | tf_op jit(solution)/shard_map/payload/pallas_call | solution.py:454
  47.8 0.3 collective-permute-start.10
  48.1 1.2 %collective-permute-start.12 = (bf16[72,4864]{1,0:T(8,128)(2,1)S(1)}, bf16[72,4864]{1,0:T(8,128)(2,1)S(1)}, u32[]{:S(2)}, u32[]{:S(2)}) collective-permute-start(bf16[72,4864]{1,0:T(8,128)(2,1)S(1)} %get-tuple-element.63), channel_id=1, source_target_pairs={{16,0},{24,8},{0,16},{8,24},{17,1},{25,9},{1,17},{9,25},{18,2},{26... | collective-permute-start | bytes 2101256 | tf_op jit(solution)/shard_map/ppermute | solution.py:498
  49.3 0.7 collective-permute-start.13
  50.0 0.0 collective-permute-start.11
  50.0 0.0 collective-permute-done.10.refs_0_.refs_5_
  50.1 1.3 %collective-permute-start.14 = (bf16[8,10368]{1,0:T(8,128)(2,1)S(1)}, bf16[8,10368]{1,0:T(8,128)(2,1)S(1)}, u32[]{:S(2)}, u32[]{:S(2)}) collective-permute-start(bf16[8,10368]{1,0:T(8,128)(2,1)S(1)} %get-tuple-element.65), channel_id=1, source_target_pairs={{1,0},{0,1},{3,2},{2,3},{5,4},{4,5},{7,6},{6,7},{9,8},{8,9},{11,10... | collective-permute-start | bytes 497672 | tf_op jit(solution)/shard_map/ppermute | solution.py:488
  51.3 0.0 collective-permute-start.15
  51.3 13.7 %collective-permute-done.12.refs_6_ = bf16[72,4864]{1,0:T(8,128)(2,1)S(1)} collective-permute-done((bf16[72,4864]{1,0:T(8,128)(2,1)S(1)}, bf16[72,4864]{1,0:T(8,128)(2,1)S(1)}, u32[]{:S(2)}, u32[]{:S(2)}) %collective-permute-start.12) | collective-permute-done | bytes 700448 | tf_op jit(solution)/shard_map/ppermute | solution.py:498
  65.1 15.4 %collective-permute-done.13.refs_7_ = bf16[72,4864]{1,0:T(8,128)(2,1)S(1)} collective-permute-done((bf16[72,4864]{1,0:T(8,128)(2,1)S(1)}, bf16[72,4864]{1,0:T(8,128)(2,1)S(1)}, u32[]{:S(2)}, u32[]{:S(2)}) %collective-permute-start.13) | collective-permute-done | bytes 700448 | tf_op jit(solution)/shard_map/ppermute | solution.py:498
  80.5 2.5 %own_terms.1.refs_0_.refs_5_ = f32[896,1024]{1,0:T(8,128)S(1)} custom-call(bf16[1,896,1024]{2,1,0:T(8,128)(2,1)S(1)} %copy-done, bf16[72,896]{1,0:T(8,128)(2,1)S(1)} %get-tuple-element.46.refs_4_.refs_0_, bf16[72,896]{1,0:T(8,128)(2,1)S(1)} %collective-permute-done.7.refs_5_.refs_1_, bf16[72,896]{1,0:T(8,128)(2,1)S(1)} %collective-permute-done.8.refs_6_.refs_2_, ...), custom_call_target="tpu_custom_call" | custom-call | tf_op jit(solution)/shard_map/own_terms/pallas_call | solution.py:454
  83.0 0.0 collective-permute-done.11.payload.refs_0_
  83.0 0.0 collective-permute-done.14.refs_1_.refs_2_
  83.0 1.0 after_swap.1
  84.0 1.1 %collective-permute-start.22 = (bf16[72,1024]{1,0:T(8,128)(2,1)S(1)}, bf16[72,1024]{1,0:T(8,128)(2,1)S(1)}, u32[]{:S(2)}, u32[]{:S(2)}) collective-permute-start(bf16[72,1024]{1,0:T(8,128)(2,1)S(1)} %get-tuple-element.74.refs_1_), channel_id=1, source_target_pairs={{24,0},{16,8},{8,16},{0,24},{25,1},{17,9},{9,17},{1,25},{26,2},{18... | collective-permute-start | bytes 442376 | tf_op jit(solution)/shard_map/ppermute | solution.py:498
  85.1 0.2 collective-permute-start.21
  85.3 0.8 collective-permute-start.20
  86.1 0.0 collective-permute-start.18
  86.1 1.2 %collective-permute-start.16 = (bf16[8,10368]{1,0:T(8,128)(2,1)S(1)}, bf16[8,10368]{1,0:T(8,128)(2,1)S(1)}, u32[]{:S(2)}, u32[]{:S(2)}) collective-permute-start(bf16[8,10368]{1,0:T(8,128)(2,1)S(1)} %get-tuple-element.68), channel_id=1, source_target_pairs={{1,0},{0,1},{3,2},{2,3},{5,4},{4,5},{7,6},{6,7},{9,8},{8,9},{11,10... | collective-permute-start | bytes 497672 | tf_op jit(solution)/shard_map/ppermute | solution.py:488
  87.3 3.0 %collective-permute-done.22.refs_4_ = bf16[72,1024]{1,0:T(8,128)(2,1)S(1)} collective-permute-done((bf16[72,1024]{1,0:T(8,128)(2,1)S(1)}, bf16[72,1024]{1,0:T(8,128)(2,1)S(1)}, u32[]{:S(2)}, u32[]{:S(2)}) %collective-permute-start.22) | collective-permute-done | bytes 147488 | tf_op jit(solution)/shard_map/ppermute | solution.py:498
  90.4 1.8 %collective-permute-done.21.refs_3_ = bf16[72,1024]{1,0:T(8,128)(2,1)S(1)} collective-permute-done((bf16[72,1024]{1,0:T(8,128)(2,1)S(1)}, bf16[72,1024]{1,0:T(8,128)(2,1)S(1)}, u32[]{:S(2)}, u32[]{:S(2)}) %collective-permute-start.21) | collective-permute-done | bytes 147488 | tf_op jit(solution)/shard_map/ppermute | solution.py:498
  92.2 0.6 collective-permute-start.19
  92.8 4.4 %update.1 = (bf16[1,896,1024]{2,1,0:T(8,128)(2,1)}, bf16[1,896,1024]{2,1,0:T(8,128)(2,1)}) custom-call(s32[8]{0:T(128)S(1)} %copy-done.2, bf16[32,10368]{1,0:T(8,128)(2,1)S(1)} %collective-permute-done.11.payload.refs_0_, bf16[72,1024]{1,0:T(8,128)(2,1)S(1)} %get-tuple-element.74.refs_1_, bf16[72,1024]{1,0:T(8,128)(2,1)S(1)} %collective-permute-done.20.refs_2_, ...), custom_call_target="tpu_custom_call" | custom-call | flops 528482304 | bytes 11010048 | tf_op jit(solution)/shard_map/update/pallas_call | solution.py:615
  97.2 3.7 %collective-permute-done.19.refs_7_ = bf16[8,10368]{1,0:T(8,128)(2,1)S(1)} collective-permute-done((bf16[8,10368]{1,0:T(8,128)(2,1)S(1)}, bf16[8,10368]{1,0:T(8,128)(2,1)S(1)}, u32[]{:S(2)}, u32[]{:S(2)}) %collective-permute-start.19) | collective-permute-done | bytes 165920 | tf_op jit(solution)/shard_map/ppermute | solution.py:488
  100.9 3.6 %unpack.1 = (bf16[128,1024]{1,0:T(8,128)(2,1)}, bf16[128,3584]{1,0:T(8,128)(2,1)}) custom-call(s32[1,128]{1,0:T(1,128)S(1)} %bitcast.3, f32[1,128]{1,0:T(1,128)S(1)} %bitcast.5, bf16[8,10368]{1,0:T(8,128)(2,1)S(1)} %get-tuple-element.59.refs_0_, bf16[8,10368]{1,0:T(8,128)(2,1)S(1)} %get-tuple-element.67.refs_1_, ...), custom_call_target="tpu_custom_call" | custom-call | flops 150994944 | bytes 2507776 | tf_op jit(solution)/shard_map/unpack/pallas_call | solution.py:454
  (22 shorter events, 0.1 us)
Async XLA Ops:
  4.0 9.7 %collective-permute-start = (bf16[16,10368]{1,0:T(8,128)(2,1)}, bf16[16,10368]{1,0:T(8,128)(2,1)S(1)}, u32[]{:S(2)}, u32[]{:S(2)}) collective-permute-start(bf16[16,10368]{1,0:T(8,128)(2,1)} %get-tuple-element.43), channel_id=1, source_target_pairs={{0,1},{1,0},{2,3},{3,2},{4,5},{5,4},{6,7},{7,6},{8,9},{9,8},{10,11... | collective-permute-start | bytes 995336 | tf_op jit(solution)/shard_map/ppermute | solution.py:481
  5.3 15.7 %collective-permute-start.1 = (bf16[16,10368]{1,0:T(8,128)(2,1)}, bf16[16,10368]{1,0:T(8,128)(2,1)S(1)}, u32[]{:S(2)}, u32[]{:S(2)}) collective-permute-start(bf16[16,10368]{1,0:T(8,128)(2,1)} %get-tuple-element.44), channel_id=1, source_target_pairs={{0,2},{1,3},{2,0},{3,1},{4,6},{5,7},{6,4},{7,5},{8,10},{9,11},{10,... | collective-permute-start | bytes 995336 | tf_op jit(solution)/shard_map/ppermute | solution.py:481
  5.5 22.7 %collective-permute-start.2 = (bf16[16,10368]{1,0:T(8,128)(2,1)}, bf16[16,10368]{1,0:T(8,128)(2,1)S(1)}, u32[]{:S(2)}, u32[]{:S(2)}) collective-permute-start(bf16[16,10368]{1,0:T(8,128)(2,1)} %get-tuple-element.45), channel_id=1, source_target_pairs={{0,3},{1,2},{2,1},{3,0},{4,7},{5,6},{6,5},{7,4},{8,11},{9,10},{10,... | collective-permute-start | bytes 995336 | tf_op jit(solution)/shard_map/ppermute | solution.py:481
  6.7 30.6 %collective-permute-start.3 = (bf16[8,10368]{1,0:T(8,128)(2,1)}, bf16[8,10368]{1,0:T(8,128)(2,1)S(1)}, u32[]{:S(2)}, u32[]{:S(2)}) collective-permute-start(bf16[8,10368]{1,0:T(8,128)(2,1)} %get-tuple-element.51), channel_id=1, source_target_pairs={{0,4},{1,5},{2,6},{3,7},{4,0},{5,1},{6,2},{7,3},{8,12},{9,13},{10,... | collective-permute-start | bytes 497672 | tf_op jit(solution)/shard_map/ppermute | solution.py:481
  6.8 6.9 %copy-start.6 = (bf16[8,10368]{1,0:T(8,128)(2,1)S(1)}, bf16[8,10368]{1,0:T(8,128)(2,1)}, u32[]{:S(2)}) copy-start(bf16[8,10368]{1,0:T(8,128)(2,1)} %get-tuple-element.53) | copy-start | bytes 497668
  6.8 14.2 %copy-start.5 = (bf16[8,10368]{1,0:T(8,128)(2,1)S(1)}, bf16[8,10368]{1,0:T(8,128)(2,1)}, u32[]{:S(2)}) copy-start(bf16[8,10368]{1,0:T(8,128)(2,1)} %get-tuple-element.54) | copy-start | bytes 497668
  6.8 21.4 %copy-start.1 = (bf16[16,10368]{1,0:T(8,128)(2,1)S(1)}, bf16[16,10368]{1,0:T(8,128)(2,1)}, u32[]{:S(2)}) copy-start(bf16[16,10368]{1,0:T(8,128)(2,1)} %get-tuple-element.42.refs_0_) | copy-start | bytes 995332
  6.8 32.2 %copy-start.2 = (s32[8]{0:T(128)S(1)}, s32[8]{0:T(128)}, u32[]{:S(2)}) copy-start(s32[8]{0:T(128)} %placement_ref.7) | copy-start | bytes 100
  6.8 31.8 %collective-permute-start.4 = (bf16[8,10368]{1,0:T(8,128)(2,1)}, bf16[8,10368]{1,0:T(8,128)(2,1)S(1)}, u32[]{:S(2)}, u32[]{:S(2)}) collective-permute-start(bf16[8,10368]{1,0:T(8,128)(2,1)} %get-tuple-element.52), channel_id=1, source_target_pairs={{0,5},{1,4},{2,7},{3,6},{4,1},{5,0},{6,3},{7,2},{8,13},{9,12},{10,... | collective-permute-start | bytes 497672 | tf_op jit(solution)/shard_map/ppermute | solution.py:481
  13.7 30.0 %collective-permute-start.5 = (bf16[8,10368]{1,0:T(8,128)(2,1)S(1)}, bf16[8,10368]{1,0:T(8,128)(2,1)S(1)}, u32[]{:S(2)}, u32[]{:S(2)}) collective-permute-start(bf16[8,10368]{1,0:T(8,128)(2,1)S(1)} %copy-done.6), channel_id=1, source_target_pairs={{0,6},{1,7},{2,4},{3,5},{4,2},{5,3},{6,0},{7,1},{8,14},{9,15},{10,... | collective-permute-start | bytes 497672 | tf_op jit(solution)/shard_map/ppermute | solution.py:481
  21.0 22.7 %collective-permute-start.6 = (bf16[8,10368]{1,0:T(8,128)(2,1)S(1)}, bf16[8,10368]{1,0:T(8,128)(2,1)S(1)}, u32[]{:S(2)}, u32[]{:S(2)}) collective-permute-start(bf16[8,10368]{1,0:T(8,128)(2,1)S(1)} %copy-done.5), channel_id=1, source_target_pairs={{0,7},{1,6},{2,5},{3,4},{4,3},{5,2},{6,1},{7,0},{8,15},{9,14},{10,... | collective-permute-start | bytes 497672 | tf_op jit(solution)/shard_map/ppermute | solution.py:481
  28.4 15.3 %collective-permute-start.7 = (bf16[72,896]{1,0:T(8,128)(2,1)S(1)}, bf16[72,896]{1,0:T(8,128)(2,1)S(1)}, u32[]{:S(2)}, u32[]{:S(2)}) collective-permute-start(bf16[72,896]{1,0:T(8,128)(2,1)S(1)} %get-tuple-element.55), channel_id=1, source_target_pairs={{8,0},{0,8},{24,16},{16,24},{9,1},{1,9},{25,17},{17,25},{10,2},{2,... | collective-permute-start | bytes 387080 | tf_op jit(solution)/shard_map/ppermute | solution.py:498
  37.3 6.4 %collective-permute-start.8 = (bf16[72,896]{1,0:T(8,128)(2,1)S(1)}, bf16[72,896]{1,0:T(8,128)(2,1)S(1)}, u32[]{:S(2)}, u32[]{:S(2)}) collective-permute-start(bf16[72,896]{1,0:T(8,128)(2,1)S(1)} %get-tuple-element.56), channel_id=1, source_target_pairs={{16,0},{24,8},{0,16},{8,24},{17,1},{25,9},{1,17},{9,25},{18,2},{26... | collective-permute-start | bytes 387080 | tf_op jit(solution)/shard_map/ppermute | solution.py:498
  38.6 6.7 %collective-permute-start.9 = (bf16[72,896]{1,0:T(8,128)(2,1)S(1)}, bf16[72,896]{1,0:T(8,128)(2,1)S(1)}, u32[]{:S(2)}, u32[]{:S(2)}) collective-permute-start(bf16[72,896]{1,0:T(8,128)(2,1)S(1)} %get-tuple-element.57), channel_id=1, source_target_pairs={{24,0},{16,8},{8,16},{0,24},{25,1},{17,9},{9,17},{1,25},{26,2},{18... | collective-permute-start | bytes 387080 | tf_op jit(solution)/shard_map/ppermute | solution.py:498
  45.3 35.2 %copy-start = (bf16[1,896,1024]{2,1,0:T(8,128)(2,1)S(1)}, bf16[1,896,1024]{2,1,0:T(8,128)(2,1)}, u32[]{:S(2)}) copy-start(bf16[1,896,1024]{2,1,0:T(8,128)(2,1)} %momentum_hbm.1) | copy-start | bytes 5505028
  47.8 2.2 %collective-permute-start.10 = (bf16[72,4864]{1,0:T(8,128)(2,1)S(1)}, bf16[72,4864]{1,0:T(8,128)(2,1)S(1)}, u32[]{:S(2)}, u32[]{:S(2)}) collective-permute-start(bf16[72,4864]{1,0:T(8,128)(2,1)S(1)} %get-tuple-element.58), channel_id=1, source_target_pairs={{8,0},{0,8},{24,16},{16,24},{9,1},{1,9},{25,17},{17,25},{10,2},{2,... | collective-permute-start | bytes 2101256 | tf_op jit(solution)/shard_map/ppermute | solution.py:498
  48.1 17.0 %collective-permute-start.12 = (bf16[72,4864]{1,0:T(8,128)(2,1)S(1)}, bf16[72,4864]{1,0:T(8,128)(2,1)S(1)}, u32[]{:S(2)}, u32[]{:S(2)}) collective-permute-start(bf16[72,4864]{1,0:T(8,128)(2,1)S(1)} %get-tuple-element.63), channel_id=1, source_target_pairs={{16,0},{24,8},{0,16},{8,24},{17,1},{25,9},{1,17},{9,25},{18,2},{26... | collective-permute-start | bytes 2101256 | tf_op jit(solution)/shard_map/ppermute | solution.py:498
  49.3 31.2 %collective-permute-start.13 = (bf16[72,4864]{1,0:T(8,128)(2,1)S(1)}, bf16[72,4864]{1,0:T(8,128)(2,1)S(1)}, u32[]{:S(2)}, u32[]{:S(2)}) collective-permute-start(bf16[72,4864]{1,0:T(8,128)(2,1)S(1)} %get-tuple-element.64), channel_id=1, source_target_pairs={{24,0},{16,8},{8,16},{0,24},{25,1},{17,9},{9,17},{1,25},{26,2},{18... | collective-permute-start | bytes 2101256 | tf_op jit(solution)/shard_map/ppermute | solution.py:498
  50.0 33.0 %collective-permute-start.11 = (bf16[32,10368]{1,0:T(8,128)(2,1)S(1)}, bf16[32,10368]{1,0:T(8,128)(2,1)S(1)}, u32[]{:S(2)}, u32[]{:S(2)}) collective-permute-start(bf16[32,10368]{1,0:T(8,128)(2,1)S(1)} %get-tuple-element.60), channel_id=1, source_target_pairs={{0,4},{1,5},{2,6},{3,7},{4,0},{5,1},{6,2},{7,3},{8,12},{9,13},{10,... | collective-permute-start | bytes 1990664 | tf_op jit(solution)/shard_map/ppermute | solution.py:492
  50.1 32.9 %collective-permute-start.14 = (bf16[8,10368]{1,0:T(8,128)(2,1)S(1)}, bf16[8,10368]{1,0:T(8,128)(2,1)S(1)}, u32[]{:S(2)}, u32[]{:S(2)}) collective-permute-start(bf16[8,10368]{1,0:T(8,128)(2,1)S(1)} %get-tuple-element.65), channel_id=1, source_target_pairs={{1,0},{0,1},{3,2},{2,3},{5,4},{4,5},{7,6},{6,7},{9,8},{8,9},{11,10... | collective-permute-start | bytes 497672 | tf_op jit(solution)/shard_map/ppermute | solution.py:488
  51.3 31.7 %collective-permute-start.15 = (bf16[8,10368]{1,0:T(8,128)(2,1)S(1)}, bf16[8,10368]{1,0:T(8,128)(2,1)S(1)}, u32[]{:S(2)}, u32[]{:S(2)}) collective-permute-start(bf16[8,10368]{1,0:T(8,128)(2,1)S(1)} %get-tuple-element.66), channel_id=1, source_target_pairs={{2,0},{3,1},{0,2},{1,3},{6,4},{7,5},{4,6},{5,7},{10,8},{11,9},{8,1... | collective-permute-start | bytes 497672 | tf_op jit(solution)/shard_map/ppermute | solution.py:488
  84.0 6.4 %collective-permute-start.22 = (bf16[72,1024]{1,0:T(8,128)(2,1)S(1)}, bf16[72,1024]{1,0:T(8,128)(2,1)S(1)}, u32[]{:S(2)}, u32[]{:S(2)}) collective-permute-start(bf16[72,1024]{1,0:T(8,128)(2,1)S(1)} %get-tuple-element.74.refs_1_), channel_id=1, source_target_pairs={{24,0},{16,8},{8,16},{0,24},{25,1},{17,9},{9,17},{1,25},{26,2},{18... | collective-permute-start | bytes 442376 | tf_op jit(solution)/shard_map/ppermute | solution.py:498
  85.1 7.1 %collective-permute-start.21 = (bf16[72,1024]{1,0:T(8,128)(2,1)S(1)}, bf16[72,1024]{1,0:T(8,128)(2,1)S(1)}, u32[]{:S(2)}, u32[]{:S(2)}) collective-permute-start(bf16[72,1024]{1,0:T(8,128)(2,1)S(1)} %get-tuple-element.74.refs_1_), channel_id=1, source_target_pairs={{16,0},{24,8},{0,16},{8,24},{17,1},{25,9},{1,17},{9,25},{18,2},{26... | collective-permute-start | bytes 442376 | tf_op jit(solution)/shard_map/ppermute | solution.py:498
  85.3 7.5 %collective-permute-start.20 = (bf16[72,1024]{1,0:T(8,128)(2,1)S(1)}, bf16[72,1024]{1,0:T(8,128)(2,1)S(1)}, u32[]{:S(2)}, u32[]{:S(2)}) collective-permute-start(bf16[72,1024]{1,0:T(8,128)(2,1)S(1)} %get-tuple-element.74.refs_1_), channel_id=1, source_target_pairs={{8,0},{0,8},{24,16},{16,24},{9,1},{1,9},{25,17},{17,25},{10,2},{2,... | collective-permute-start | bytes 442376 | tf_op jit(solution)/shard_map/ppermute | solution.py:498
  86.1 11.1 %collective-permute-start.18 = (bf16[8,10368]{1,0:T(8,128)(2,1)S(1)}, bf16[8,10368]{1,0:T(8,128)(2,1)S(1)}, u32[]{:S(2)}, u32[]{:S(2)}) collective-permute-start(bf16[8,10368]{1,0:T(8,128)(2,1)S(1)} %get-tuple-element.70), channel_id=1, source_target_pairs={{3,0},{2,1},{1,2},{0,3},{7,4},{6,5},{5,6},{4,7},{11,8},{10,9},{9,1... | collective-permute-start | bytes 497672 | tf_op jit(solution)/shard_map/ppermute | solution.py:488
  86.1 11.1 %collective-permute-start.16 = (bf16[8,10368]{1,0:T(8,128)(2,1)S(1)}, bf16[8,10368]{1,0:T(8,128)(2,1)S(1)}, u32[]{:S(2)}, u32[]{:S(2)}) collective-permute-start(bf16[8,10368]{1,0:T(8,128)(2,1)S(1)} %get-tuple-element.68), channel_id=1, source_target_pairs={{1,0},{0,1},{3,2},{2,3},{5,4},{4,5},{7,6},{6,7},{9,8},{8,9},{11,10... | collective-permute-start | bytes 497672 | tf_op jit(solution)/shard_map/ppermute | solution.py:488
  90.4 6.9 %collective-permute-start.17 = (bf16[8,10368]{1,0:T(8,128)(2,1)S(1)}, bf16[8,10368]{1,0:T(8,128)(2,1)S(1)}, u32[]{:S(2)}, u32[]{:S(2)}) collective-permute-start(bf16[8,10368]{1,0:T(8,128)(2,1)S(1)} %get-tuple-element.69), channel_id=1, source_target_pairs={{2,0},{3,1},{0,2},{1,3},{6,4},{7,5},{4,6},{5,7},{10,8},{11,9},{8,1... | collective-permute-start | bytes 497672 | tf_op jit(solution)/shard_map/ppermute | solution.py:488
  92.2 8.7 %collective-permute-start.19 = (bf16[8,10368]{1,0:T(8,128)(2,1)S(1)}, bf16[8,10368]{1,0:T(8,128)(2,1)S(1)}, u32[]{:S(2)}, u32[]{:S(2)}) collective-permute-start(bf16[8,10368]{1,0:T(8,128)(2,1)S(1)} %get-tuple-element.71), channel_id=1, source_target_pairs={{3,0},{2,1},{1,2},{0,3},{7,4},{6,5},{5,6},{4,7},{11,8},{10,9},{9,1... | collective-permute-start | bytes 497672 | tf_op jit(solution)/shard_map/ppermute | solution.py:488
  92.8 8.1 %copy-start.3 = (s32[128]{0:T(128)S(1)}, s32[128]{0:T(128)}, u32[]{:S(2)}) copy-start(s32[128]{0:T(128)} %param.10) | copy-start | bytes 1540
  92.8 8.1 %copy-start.4 = (f32[128]{0:T(128)S(1)}, f32[128]{0:T(128)}, u32[]{:S(2)}) copy-start(f32[128]{0:T(128)} %param.8) | copy-start | bytes 1540

commit v7 on v6

--- a/solution.py
+++ b/solution.py
@@ -33,6 +33,8 @@
         self.C = self.DX + self.FG
         self.pieces = self.cap * groups // SUB
         self.outer = groups // INNER
+        self.ahead = self.pieces // 2
+        self.cut = self.ahead * self.share
 
     def group_at(self, group, step):
         chip, core = group // INNER, group % INNER
@@ -41,6 +43,11 @@
         return away_traced(chip, step // INNER, self.outer) * INNER + jnp.bitwise_xor(
             core, step % INNER
         )
+
+    def place_of_piece(self, piece, first, second):
+        if piece < self.ahead:
+            return first, self.FG + piece * self.share
+        return second, (piece - self.ahead) * self.share
 
     def group_from(self, step):
         chips = step // INNER
@@ -289,7 +296,7 @@
     half, groups = plan.half, plan.groups
     far, refs = refs[:half], refs[half:]
     columns, refs = refs[:groups], refs[groups:]
-    payload, refs = refs[0], refs[1:]
+    first, second, refs = refs[0], refs[1], refs[2:]
     shared, rows = refs[:groups], refs[groups]
     hot = is_hot(plan, placement_ref)
     x = unfold(plan, blocks_of(far, 0, plan.DX), plan.D)
@@ -299,27 +306,30 @@
 
     @pl.when(jnp.logical_not(hot))
     def _():
-        payload[:, : plan.DX] = fold(plan, dot_nt(grad_pre, weight_ref[...])).astype(BF16)
-        payload[:, plan.DX :] = fold(plan, act.astype(F32)).astype(BF16)
+        back = fold(plan, dot_nt(grad_pre, weight_ref[...])).astype(BF16)
+        first[:, : plan.FG] = fold(plan, act.astype(F32)).astype(BF16)
+        first[:, plan.FG :] = back[:, : plan.cut]
+        second[...] = back[:, plan.cut :]
 
     @pl.when(hot)
     def _():
         together = jnp.concatenate([c[...].astype(F32) for c in columns], axis=0)
         block = half * SUB
         for i in range(plan.pieces):
-            payload[:, i * plan.share : (i + 1) * plan.share] = together[
+            target, start = plan.place_of_piece(i, first, second)
+            target[:, start : start + plan.share] = together[
                 i * block : (i + 1) * block
             ].astype(BF16)
-        payload[:, plan.DX :] = folded_grad[...]
+        first[:, : plan.FG] = folded_grad[...]
 
     group = lax.axis_index("dp")
     width = plan.share
-    for m in range(groups):
-        start = pl.multiple_of(plan.group_at(group, m) * width, LANES)
-        shared[m][:, :width] = far_rows[:, pl.ds(start, width)]
-        shared[m][:, width : 2 * width] = rows[:, pl.ds(start, width)]
-        shared[m][:, 2 * width : 2 * width + 2 * plan.F] = near_grads[...]
-        shared[m][:, 2 * width + 2 * plan.F :] = grad_pre
+    for o in range(groups):
+        start = pl.multiple_of(plan.group_at(group, o) * width, LANES)
+        shared[o][:, :width] = far_rows[:, pl.ds(start, width)]
+        shared[o][:, width : 2 * width] = rows[:, pl.ds(start, width)]
+        shared[o][:, 2 * width : 2 * width + 2 * plan.F] = near_grads[...]
+        shared[o][:, 2 * width + 2 * plan.F :] = grad_pre
 
 
 def early_kernel(plan, near_back, *refs):
@@ -328,15 +338,28 @@
         out[...] = back[m * SUB : (m + 1) * SUB].astype(BF16)
 
 
-def after_kernel(plan, placement_ref, payload, local, *refs):
-    outs = refs[-plan.half - 1 :]
+def after_first_kernel(plan, placement_ref, first, *refs):
+    grad = refs[-1]
+    got = first[:, : plan.FG].astype(F32)
+    blocks = [got[m * SUB : (m + 1) * SUB] for m in range(plan.half)]
+    rows = unfold(plan, blocks, plan.F).astype(F32)
+    grad[...] = jnp.where(is_hot(plan, placement_ref), rows, 0.0).astype(BF16)
+
+
+def after_second_kernel(plan, placement_ref, first, second, local, *refs):
+    outs = refs[-plan.half :]
     hot = is_hot(plan, placement_ref)
-    got = payload[...].astype(F32)
-    chosen = jnp.where(hot, local[...].astype(F32), got)
-    for m in range(plan.half):
-        outs[m][...] = chosen[m * SUB : (m + 1) * SUB].astype(BF16)
-    blocks = [got[m * SUB : (m + 1) * SUB, plan.DX :] for m in range(plan.half)]
-    outs[plan.half][...] = jnp.where(hot, unfold(plan, blocks, plan.F).astype(F32), 0.0).astype(BF16)
+    for source, low, high, start in (
+        (first, plan.FG, plan.FG + plan.cut, 0),
+        (second, 0, plan.DX - plan.cut, plan.cut),
+        (first, 0, plan.FG, plan.DX),
+    ):
+        stop = start + high - low
+        chosen = jnp.where(
+            hot, local[:, start:stop].astype(F32), source[:, low:high].astype(F32)
+        )
+        for m in range(plan.half):
+            outs[m][:, start:stop] = chosen[m * SUB : (m + 1) * SUB].astype(BF16)
 
 
 def unpack_kernel(plan, slot_ref, gate_ref, *refs):
@@ -406,9 +429,10 @@
 
 def update_kernel(plan, placement_ref, *refs):
     groups, share = plan.groups, plan.share
-    sources, refs = refs[: groups + 3], refs[groups + 3 :]
-    new_weight, new_momentum, payload, other_g, total, weight, momentum, sems, out_sems = refs
-    targets = [payload] + [other_g.at[m] for m in range(groups)] + [total, weight]
+    sources, refs = refs[: groups + 4], refs[groups + 4 :]
+    new_weight, new_momentum, first, second, other_g = refs[:5]
+    total, weight, momentum, sems, out_sems = refs[5:]
+    targets = [first, second] + [other_g.at[m] for m in range(groups)] + [total, weight]
     copies = [
         pltpu.make_async_copy(source, target, sems.at[i])
         for i, (source, target) in enumerate(zip(sources, targets))
@@ -416,13 +440,16 @@
     for copy in copies:
         copy.start()
     hot = is_hot(plan, placement_ref)
-    for copy in copies[: groups + 1]:
+    for copy in copies[: groups + 2]:
         copy.wait()
-    pieces = [payload[:, i * share : (i + 1) * share] for i in range(plan.pieces)]
+    pieces = []
+    for i in range(plan.pieces):
+        source, start = plan.place_of_piece(i, first, second)
+        pieces.append(source[:, start : start + share])
     x = jnp.concatenate(pieces, axis=0)
     x = jnp.where(hot, x.astype(F32), 0.0).astype(BF16)
     g = rows_of([other_g[m] for m in range(groups)])
-    for copy in copies[groups + 1 :]:
+    for copy in copies[groups + 2 :]:
         copy.wait()
     done = []
     for i in range(share // LANES):
@@ -468,7 +495,7 @@
 
 
 def routed(plan, tokens, route_weight, cotangent, slot_ids, placement, weight, momentum):
-    half, groups = plan.half, plan.groups
+    half, groups, outer = plan.half, plan.groups, plan.outer
     D, F, C, rows, share = plan.D, plan.F, plan.C, plan.rows, plan.share
     slot = slot_ids.reshape(1, -1)
     gate = route_weight.reshape(1, -1)
@@ -496,6 +523,15 @@
         for d in range(groups):
             pairs.append((plan.group_at(d, m), d))
         return lax.ppermute(data, "dp", pairs)
+
+    def from_chips(per_chip):
+        return [per_chip[0]] + [
+            from_group(per_chip[plan.group_from(INNER * o) // INNER], INNER * o)
+            for o in range(1, outer)
+        ]
+
+    def with_sisters(got):
+        return [data for own in got for data in (own, from_group(own, 1))]
 
     def from_groups(per_group):
         return [per_group[0]] + [
@@ -564,13 +600,14 @@
         plan,
         [placement, held, folded_grad, grads, far_rows] + far + columns_here,
         [SMEM_SPEC] + [VMEM_SPEC] * (4 + half + groups),
-        [(half * SUB, C)] + [(rows, 2 * share + 3 * F)] * groups,
+        [(half * SUB, plan.FG + plan.cut), (half * SUB, plan.DX - plan.cut)]
+        + [(rows, 2 * share + 3 * F)] * groups,
         [pltpu.VMEM((rows, D), BF16)],
         4 * rows * D * F,
         "payload",
     )
-    payload = to_partner(outs[0])
-    shared = from_groups(outs[1:])
+    first, second = to_partner(outs[0]), to_partner(outs[1])
+    shared = from_groups(outs[2:])
     outs = call(
         early_kernel,
         plan,
@@ -583,6 +620,18 @@
         limit=4,
     )
     early = [outs[0]] + [to_source(outs[m], m) for m in range(1, half)]
+    (grad,) = call(
+        after_first_kernel,
+        plan,
+        [placement, first] + early[1:2],
+        [SMEM_SPEC, VMEM_SPEC] + [ANY_SPEC],
+        [(rows, F)],
+        [],
+        0,
+        "after_first",
+        limit=4,
+    )
+    other_g = from_chips([grad] * outer)
     (total,) = call(
         gather_kernel,
         plan,
@@ -598,32 +647,34 @@
         "own_terms",
         dtypes=[F32],
     )
+    before = other_g[1:] + early[2:3]
+    other_g = with_sisters(other_g)
     outs = call(
-        after_kernel,
-        plan,
-        [placement, payload, local, total] + early[1:-1],
-        [SMEM_SPEC] + [VMEM_SPEC] * 2 + [ANY_SPEC] * (half - 1),
-        [(SUB, C)] * half + [(rows, F)],
+        after_second_kernel,
+        plan,
+        [placement, first, second, local] + before,
+        [SMEM_SPEC] + [VMEM_SPEC] * 3 + [ANY_SPEC] * len(before),
+        [(SUB, C)] * half,
         [],
         0,
-        "after_swap",
+        "after_second",
         limit=8,
     )
     late = [outs[0]] + [to_source(outs[m], m) for m in range(1, half)]
-    other_g = from_groups([outs[half]] * groups)
 
     new_weight, new_momentum = pl.pallas_call(
         functools.partial(update_kernel, plan),
         out_shape=[jax.ShapeDtypeStruct((1, share, F), BF16)] * 2,
-        in_specs=[SMEM_SPEC] + [ANY_SPEC] * (groups + 3),
+        in_specs=[SMEM_SPEC] + [ANY_SPEC] * (groups + 4),
         out_specs=[ANY_SPEC] * 2,
         scratch_shapes=[
-            pltpu.VMEM((half * SUB, C), BF16),
+            pltpu.VMEM(first.shape, BF16),
+            pltpu.VMEM(second.shape, BF16),
             pltpu.VMEM((groups, rows, F), BF16),
             pltpu.VMEM((share, F), F32),
             pltpu.VMEM((share, F), BF16),
             pltpu.VMEM((share, F), BF16),
-            pltpu.SemaphoreType.DMA((groups + 3,)),
+            pltpu.SemaphoreType.DMA((groups + 4,)),
             pltpu.SemaphoreType.DMA((share // LANES, 2)),
         ],
         compiler_params=pltpu.CompilerParams(vmem_limit_bytes=20 * MIB),
@@ -631,7 +682,7 @@
             flops=2 * groups * rows * share * F, bytes_accessed=12 * share * F, transcendentals=0
         ),
         name="update",
-    )(placement, payload, *other_g, total, old_weight)
+    )(placement, first, second, *other_g, total, old_weight)
 
     expert_out, token_grad = call(
         unpack_kernel,

time: 105 us -> 105 us (level)
  the two profiles are of different devices: /device:TPU:25 before, /device:TPU:28 now
where the time goes in v7:
time: 105 us
  waiting for transfers between devices  55.9 us (53%)
  Pallas kernels  28.7 us (27%)
  starting transfers between devices  18.9 us (18%)
    pallas_call x10, Pallas kernels, call(): pl.pallas_call(functools.partial(kernel, plan), out_shape=[jax.ShapeDtype...  24.3 us
    ppermute x7, waiting for transfers between devices, to_slot(): return lax.ppermute(data, 'expert', pairs)  20.7 us
    ppermute x2, waiting for transfers between devices, to_partner(): return lax.ppermute(data, 'expert', pairs)  20.6 us
    ppermute x9, waiting for transfers between devices, from_group(): return lax.ppermute(data, 'dp', pairs)  11.2 us
    ppermute x7, starting transfers between devices, to_slot(): return lax.ppermute(data, 'expert', pairs)  7.95 us
    pallas_call x1, Pallas kernels, routed(): pl.pallas_call(functools.partial(update_kernel, plan), out_shape=[jax.Sha...  4.43 us
    ppermute x9, starting transfers between devices, from_group(): return lax.ppermute(data, 'dp', pairs)  4.4 us
    ppermute x6, starting transfers between devices, to_source(): return lax.ppermute(data, 'expert', pairs)  3.62 us
  transfers between devices with their start and end apart: 24, of which 7 were waited for; matrix products, arithmetic and copies ran while one was open for 0% of the time, Pallas kernels for 16%

profile of v7, /device:TPU:28, one launch (start us, length us, event | category | flops | bytes accessed | tf_op | source)
XLA Modules:
  0.0 104.6 jit_solution(5909257857876579269)
XLA Ops:
  0.6 3.4 %pack.1 = (bf16[16,10368]{1,0:T(8,128)(2,1)}, bf16[16,10368]{1,0:T(8,128)(2,1)}, bf16[16,10368]{1,0:T(8,128)(2,1)}, bf16[16,10368]{1,0:T(8,128)(2,1)}, bf16[8,10...) custom-call(s32[1,128]{1,0:T(1,128)} %bitcast.2, ...), custom_call_target="tpu_custom_call" | custom-call | flops 150994944 | bytes 3171328 | tf_op jit(solution)/shard_map/pack/pallas_call | solution.py:481
  4.0 1.6 %collective-permute-start = (bf16[16,10368]{1,0:T(8,128)(2,1)}, bf16[16,10368]{1,0:T(8,128)(2,1)S(1)}, u32[]{:S(2)}, u32[]{:S(2)}) collective-permute-start(bf16[16,10368]{1,0:T(8,128)(2,1)} %get-tuple-element.43), channel_id=1, source_target_pairs={{0,1},{1,0},{2,3},{3,2},{4,5},{5,4},{6,7},{7,6},{8,9},{9,8},{10,11... | collective-permute-start | bytes 995336 | tf_op jit(solution)/shard_map/ppermute | solution.py:508
  5.6 0.4 collective-permute-start.1
  6.1 1.5 %collective-permute-start.2 = (bf16[16,10368]{1,0:T(8,128)(2,1)}, bf16[16,10368]{1,0:T(8,128)(2,1)S(1)}, u32[]{:S(2)}, u32[]{:S(2)}) collective-permute-start(bf16[16,10368]{1,0:T(8,128)(2,1)} %get-tuple-element.45), channel_id=1, source_target_pairs={{0,3},{1,2},{2,1},{3,0},{4,7},{5,6},{6,5},{7,4},{8,11},{9,10},{10,... | collective-permute-start | bytes 995336 | tf_op jit(solution)/shard_map/ppermute | solution.py:508
  7.6 0.3 collective-permute-start.3
  8.0 3.6 %collective-permute-start.4 = (bf16[8,10368]{1,0:T(8,128)(2,1)}, bf16[8,10368]{1,0:T(8,128)(2,1)S(1)}, u32[]{:S(2)}, u32[]{:S(2)}) collective-permute-start(bf16[8,10368]{1,0:T(8,128)(2,1)} %get-tuple-element.52), channel_id=1, source_target_pairs={{0,5},{1,4},{2,7},{3,6},{4,1},{5,0},{6,3},{7,2},{8,13},{9,12},{10,... | collective-permute-start | bytes 497672 | tf_op jit(solution)/shard_map/ppermute | solution.py:508
  11.5 3.6 %hold.1 = (bf16[3584,1024]{1,0:T(8,128)(2,1)S(1)}, bf16[896,1024]{1,0:T(8,128)(2,1)S(1)}) custom-call(bf16[1,3584,1024]{2,1,0:T(8,128)(2,1)} %weight_hbm.1), custom_call_target="tpu_custom_call" | custom-call | tf_op jit(solution)/shard_map/hold/pallas_call | solution.py:481
  15.1 0.0 collective-permute-done.refs_1_
  15.2 0.3 collective-permute-start.5
  15.5 8.2 %collective-permute-done.1.refs_2_ = bf16[16,10368]{1,0:T(8,128)(2,1)S(1)} collective-permute-done((bf16[16,10368]{1,0:T(8,128)(2,1)}, bf16[16,10368]{1,0:T(8,128)(2,1)S(1)}, u32[]{:S(2)}, u32[]{:S(2)}) %collective-permute-start.1) | collective-permute-done | bytes 331808 | tf_op jit(solution)/shard_map/ppermute | solution.py:508
  23.7 0.2 collective-permute-start.6
  23.8 12.5 %collective-permute-done.2.refs_3_ = bf16[16,10368]{1,0:T(8,128)(2,1)S(1)} collective-permute-done((bf16[16,10368]{1,0:T(8,128)(2,1)}, bf16[16,10368]{1,0:T(8,128)(2,1)S(1)}, u32[]{:S(2)}, u32[]{:S(2)}) %collective-permute-start.2) | collective-permute-done | bytes 331808 | tf_op jit(solution)/shard_map/ppermute | solution.py:508
  36.4 0.2 near_columns.1
  36.6 0.1 collective-permute-start.7
  36.7 0.0 collective-permute-done.3.refs_0_
  36.7 0.6 collective-permute-start.8
  37.3 1.3 %collective-permute-start.9 = (bf16[72,896]{1,0:T(8,128)(2,1)S(1)}, bf16[72,896]{1,0:T(8,128)(2,1)S(1)}, u32[]{:S(2)}, u32[]{:S(2)}) collective-permute-start(bf16[72,896]{1,0:T(8,128)(2,1)S(1)} %get-tuple-element.57), channel_id=1, source_target_pairs={{24,0},{16,8},{8,16},{0,24},{25,1},{17,9},{9,17},{1,25},{26,2},{18... | collective-permute-start | bytes 387080 | tf_op jit(solution)/shard_map/ppermute | solution.py:525
  38.5 4.7 %near_rows.1 = (bf16[32,10368]{1,0:T(8,128)(2,1)S(1)}, bf16[32,10368]{1,0:T(8,128)(2,1)S(1)}, bf16[32,2304]{1,0:T(8,128)(2,1)S(1)}, bf16[72,2048]{1,0:T(8,128)(2,1)S(1)}, bf16[72,3584]{1,0:T(8,128)(2,1)S(1)}) custom-call(s32[8]{0:T(128)S(1)} %copy-done.2, bf16[3584,1024]{1,0:T(8,128)(2,1)S(1)} %get-tuple-element.41.weight_ref, ...), custom_call_target="tpu_custom_call" | custom-call | flops 2113929216 | bytes 11081760 | tf_op jit(solution)/shard_map/near_rows/pallas_call | solution.py:481
  43.2 0.0 collective-permute-done.5.refs_2_
  43.2 0.0 collective-permute-done.6.refs_3_
  43.2 0.0 collective-permute-done.7.refs_5_.refs_1_
  43.2 1.6 %collective-permute-done.9.refs_7_.refs_3_ = bf16[72,896]{1,0:T(8,128)(2,1)S(1)} collective-permute-done((bf16[72,896]{1,0:T(8,128)(2,1)S(1)}, bf16[72,896]{1,0:T(8,128)(2,1)S(1)}, u32[]{:S(2)}, u32[]{:S(2)}) %collective-permute-start.9) | collective-permute-done | bytes 129056 | tf_op jit(solution)/shard_map/ppermute | solution.py:525
  44.8 4.9 %payload.1 = (bf16[32,5888]{1,0:T(8,128)(2,1)S(1)}, bf16[32,4480]{1,0:T(8,128)(2,1)S(1)}, bf16[72,4864]{1,0:T(8,128)(2,1)S(1)}, bf16[72,4864]{1,0:T(8,128)(2,1)S...) custom-call(s32[8]{0:T(128)S(1)} %copy-done.2, bf16[3584,1024]{1,0:T(8,128)(2,1)S(1)} %get-tuple-element.41.weight_ref, ...), custom_call_target="tpu_custom_call" | custom-call | flops 1056964608 | bytes 12943392 | tf_op jit(solution)/shard_map/payload/pallas_call | solution.py:481
  49.8 0.4 collective-permute-start.10
  50.1 0.5 collective-permute-start.22
  50.6 1.1 %collective-permute-start.23 = (bf16[72,4864]{1,0:T(8,128)(2,1)S(1)}, bf16[72,4864]{1,0:T(8,128)(2,1)S(1)}, u32[]{:S(2)}, u32[]{:S(2)}) collective-permute-start(bf16[72,4864]{1,0:T(8,128)(2,1)S(1)} %get-tuple-element.74), channel_id=1, source_target_pairs={{24,0},{16,8},{8,16},{0,24},{25,1},{17,9},{9,17},{1,25},{26,2},{18... | collective-permute-start | bytes 2101256 | tf_op jit(solution)/shard_map/ppermute | solution.py:525
  51.7 2.9 %collective-permute-start.12 = (bf16[32,4480]{1,0:T(8,128)(2,1)S(1)}, bf16[32,4480]{1,0:T(8,128)(2,1)S(1)}, u32[]{:S(2)}, u32[]{:S(2)}) collective-permute-start(bf16[32,4480]{1,0:T(8,128)(2,1)S(1)} %get-tuple-element.61), channel_id=1, source_target_pairs={{0,4},{1,5},{2,6},{3,7},{4,0},{5,1},{6,2},{7,3},{8,12},{9,13},{10,... | collective-permute-start | bytes 860168 | tf_op jit(solution)/shard_map/ppermute | solution.py:519
  54.6 0.0 collective-permute-done.10.refs_0_.refs_5_
  54.7 0.1 collective-permute-start.13
  54.8 15.6 %collective-permute-done.11.first.refs_0_ = bf16[32,5888]{1,0:T(8,128)(2,1)S(1)} collective-permute-done((bf16[32,5888]{1,0:T(8,128)(2,1)S(1)}, bf16[32,5888]{1,0:T(8,128)(2,1)S(1)}, u32[]{:S(2)}, u32[]{:S(2)}) %collective-permute-start.11) | collective-permute-done | bytes 376864 | tf_op jit(solution)/shard_map/ppermute | solution.py:519
  70.3 0.0 collective-permute-done.13.refs_0_.refs_2_
  70.3 0.7 after_first.1.refs_2_
  71.0 0.5 collective-permute-start.14
  71.5 5.0 %collective-permute-done.12.second.refs_1_ = bf16[32,4480]{1,0:T(8,128)(2,1)S(1)} collective-permute-done((bf16[32,4480]{1,0:T(8,128)(2,1)S(1)}, bf16[32,4480]{1,0:T(8,128)(2,1)S(1)}, u32[]{:S(2)}, u32[]{:S(2)}) %collective-permute-start.12) | collective-permute-done | bytes 286752 | tf_op jit(solution)/shard_map/ppermute | solution.py:519
  76.6 0.0 collective-permute-start.20
  76.6 9.5 %collective-permute-done.14.refs_0_.refs_4_ = bf16[72,1024]{1,0:T(8,128)(2,1)S(1)} collective-permute-done((bf16[72,1024]{1,0:T(8,128)(2,1)S(1)}, bf16[72,1024]{1,0:T(8,128)(2,1)S(1)}, u32[]{:S(2)}, u32[]{:S(2)}) %collective-permute-start.14) | collective-permute-done | bytes 147488 | tf_op jit(solution)/shard_map/ppermute | solution.py:525
  86.1 0.0 collective-permute-start.21
  86.1 0.7 after_second.1
  86.9 0.0 collective-permute-done.22.refs_6_
  86.9 0.1 collective-permute-start.16
  87.0 3.5 %collective-permute-start.17 = (bf16[8,10368]{1,0:T(8,128)(2,1)S(1)}, bf16[8,10368]{1,0:T(8,128)(2,1)S(1)}, u32[]{:S(2)}, u32[]{:S(2)}) collective-permute-start(bf16[8,10368]{1,0:T(8,128)(2,1)S(1)} %get-tuple-element.67), channel_id=1, source_target_pairs={{2,0},{3,1},{0,2},{1,3},{6,4},{7,5},{4,6},{5,7},{10,8},{11,9},{8,1... | collective-permute-start | bytes 497672 | tf_op jit(solution)/shard_map/ppermute | solution.py:515
  90.4 0.0 collective-permute-start.19
  90.4 2.5 %own_terms.1.refs_6_ = f32[896,1024]{1,0:T(8,128)S(1)} custom-call(bf16[1,896,1024]{2,1,0:T(8,128)(2,1)S(1)} %copy-done, bf16[72,896]{1,0:T(8,128)(2,1)S(1)} %get-tuple-element.46.refs_4_.refs_0_, bf16[72,896]{1,0:T(8,128)(2,1)S(1)} %collective-permute-done.7.refs_5_.refs_1_, bf16[72,896]{1,0:T(8,128)(2,1)S(1)} %collective-permute-done.8.refs_6_.refs_2_, ...), custom_call_target="tpu_custom_call" | custom-call | tf_op jit(solution)/shard_map/own_terms/pallas_call | solution.py:481
  92.9 0.0 copy-start.3
  92.9 0.0 copy-start.4
  92.9 4.4 %update.1 = (bf16[1,896,1024]{2,1,0:T(8,128)(2,1)}, bf16[1,896,1024]{2,1,0:T(8,128)(2,1)}) custom-call(s32[8]{0:T(128)S(1)} %copy-done.2, bf16[32,5888]{1,0:T(8,128)(2,1)S(1)} %collective-permute-done.11.first.refs_0_, bf16[32,4480]{1,0:T(8,128)(2,1)S(1)} %collective-permute-done.12.second.refs_1_, bf16[72,1024]{1,0:T(8,128)(2,1)S(1)} %after_first.1.refs_2_, ...), custom_call_target="tpu_custom_call" | custom-call | flops 528482304 | bytes 11010048 | tf_op jit(solution)/shard_map/update/pallas_call | solution.py:665
  97.4 3.4 %collective-permute-done.19.refs_7_ = bf16[8,10368]{1,0:T(8,128)(2,1)S(1)} collective-permute-done((bf16[8,10368]{1,0:T(8,128)(2,1)S(1)}, bf16[8,10368]{1,0:T(8,128)(2,1)S(1)}, u32[]{:S(2)}, u32[]{:S(2)}) %collective-permute-start.19) | collective-permute-done | bytes 165920 | tf_op jit(solution)/shard_map/ppermute | solution.py:515
  100.8 3.6 %unpack.1 = (bf16[128,1024]{1,0:T(8,128)(2,1)}, bf16[128,3584]{1,0:T(8,128)(2,1)}) custom-call(s32[1,128]{1,0:T(1,128)S(1)} %bitcast.3, f32[1,128]{1,0:T(1,128)S(1)} %bitcast.5, bf16[8,10368]{1,0:T(8,128)(2,1)S(1)} %get-tuple-element.59.refs_0_, bf16[8,10368]{1,0:T(8,128)(2,1)S(1)} %get-tuple-element.65.refs_1_, ...), custom_call_target="tpu_custom_call" | custom-call | flops 150994944 | bytes 2507776 | tf_op jit(solution)/shard_map/unpack/pallas_call | solution.py:481
  (25 shorter events, 0.1 us)
Async XLA Ops:
  4.0 11.1 %collective-permute-start = (bf16[16,10368]{1,0:T(8,128)(2,1)}, bf16[16,10368]{1,0:T(8,128)(2,1)S(1)}, u32[]{:S(2)}, u32[]{:S(2)}) collective-permute-start(bf16[16,10368]{1,0:T(8,128)(2,1)} %get-tuple-element.43), channel_id=1, source_target_pairs={{0,1},{1,0},{2,3},{3,2},{4,5},{5,4},{6,7},{7,6},{8,9},{9,8},{10,11... | collective-permute-start | bytes 995336 | tf_op jit(solution)/shard_map/ppermute | solution.py:508
  5.6 18.0 %collective-permute-start.1 = (bf16[16,10368]{1,0:T(8,128)(2,1)}, bf16[16,10368]{1,0:T(8,128)(2,1)S(1)}, u32[]{:S(2)}, u32[]{:S(2)}) collective-permute-start(bf16[16,10368]{1,0:T(8,128)(2,1)} %get-tuple-element.44), channel_id=1, source_target_pairs={{0,2},{1,3},{2,0},{3,1},{4,6},{5,7},{6,4},{7,5},{8,10},{9,11},{10,... | collective-permute-start | bytes 995336 | tf_op jit(solution)/shard_map/ppermute | solution.py:508
  6.1 30.3 %collective-permute-start.2 = (bf16[16,10368]{1,0:T(8,128)(2,1)}, bf16[16,10368]{1,0:T(8,128)(2,1)S(1)}, u32[]{:S(2)}, u32[]{:S(2)}) collective-permute-start(bf16[16,10368]{1,0:T(8,128)(2,1)} %get-tuple-element.45), channel_id=1, source_target_pairs={{0,3},{1,2},{2,1},{3,0},{4,7},{5,6},{6,5},{7,4},{8,11},{9,10},{10,... | collective-permute-start | bytes 995336 | tf_op jit(solution)/shard_map/ppermute | solution.py:508
  7.6 29.1 %collective-permute-start.3 = (bf16[8,10368]{1,0:T(8,128)(2,1)}, bf16[8,10368]{1,0:T(8,128)(2,1)S(1)}, u32[]{:S(2)}, u32[]{:S(2)}) collective-permute-start(bf16[8,10368]{1,0:T(8,128)(2,1)} %get-tuple-element.51), channel_id=1, source_target_pairs={{0,4},{1,5},{2,6},{3,7},{4,0},{5,1},{6,2},{7,3},{8,12},{9,13},{10,... | collective-permute-start | bytes 497672 | tf_op jit(solution)/shard_map/ppermute | solution.py:508
  7.9 7.2 %copy-start.6 = (bf16[8,10368]{1,0:T(8,128)(2,1)S(1)}, bf16[8,10368]{1,0:T(8,128)(2,1)}, u32[]{:S(2)}) copy-start(bf16[8,10368]{1,0:T(8,128)(2,1)} %get-tuple-element.53) | copy-start | bytes 497668
  7.9 15.7 %copy-start.5 = (bf16[8,10368]{1,0:T(8,128)(2,1)S(1)}, bf16[8,10368]{1,0:T(8,128)(2,1)}, u32[]{:S(2)}) copy-start(bf16[8,10368]{1,0:T(8,128)(2,1)} %get-tuple-element.54) | copy-start | bytes 497668
  7.9 28.4 %copy-start.1 = (bf16[16,10368]{1,0:T(8,128)(2,1)S(1)}, bf16[16,10368]{1,0:T(8,128)(2,1)}, u32[]{:S(2)}) copy-start(bf16[16,10368]{1,0:T(8,128)(2,1)} %get-tuple-element.42.refs_0_) | copy-start | bytes 995332
  8.0 30.6 %copy-start.2 = (s32[8]{0:T(128)S(1)}, s32[8]{0:T(128)}, u32[]{:S(2)}) copy-start(s32[8]{0:T(128)} %placement_ref.9) | copy-start | bytes 100
  8.0 29.3 %collective-permute-start.4 = (bf16[8,10368]{1,0:T(8,128)(2,1)}, bf16[8,10368]{1,0:T(8,128)(2,1)S(1)}, u32[]{:S(2)}, u32[]{:S(2)}) collective-permute-start(bf16[8,10368]{1,0:T(8,128)(2,1)} %get-tuple-element.52), channel_id=1, source_target_pairs={{0,5},{1,4},{2,7},{3,6},{4,1},{5,0},{6,3},{7,2},{8,13},{9,12},{10,... | collective-permute-start | bytes 497672 | tf_op jit(solution)/shard_map/ppermute | solution.py:508
  15.2 28.0 %collective-permute-start.5 = (bf16[8,10368]{1,0:T(8,128)(2,1)S(1)}, bf16[8,10368]{1,0:T(8,128)(2,1)S(1)}, u32[]{:S(2)}, u32[]{:S(2)}) collective-permute-start(bf16[8,10368]{1,0:T(8,128)(2,1)S(1)} %copy-done.6), channel_id=1, source_target_pairs={{0,6},{1,7},{2,4},{3,5},{4,2},{5,3},{6,0},{7,1},{8,14},{9,15},{10,... | collective-permute-start | bytes 497672 | tf_op jit(solution)/shard_map/ppermute | solution.py:508
  23.7 19.6 %collective-permute-start.6 = (bf16[8,10368]{1,0:T(8,128)(2,1)S(1)}, bf16[8,10368]{1,0:T(8,128)(2,1)S(1)}, u32[]{:S(2)}, u32[]{:S(2)}) collective-permute-start(bf16[8,10368]{1,0:T(8,128)(2,1)S(1)} %copy-done.5), channel_id=1, source_target_pairs={{0,7},{1,6},{2,5},{3,4},{4,3},{5,2},{6,1},{7,0},{8,15},{9,14},{10,... | collective-permute-start | bytes 497672 | tf_op jit(solution)/shard_map/ppermute | solution.py:508
  36.6 6.6 %collective-permute-start.7 = (bf16[72,896]{1,0:T(8,128)(2,1)S(1)}, bf16[72,896]{1,0:T(8,128)(2,1)S(1)}, u32[]{:S(2)}, u32[]{:S(2)}) collective-permute-start(bf16[72,896]{1,0:T(8,128)(2,1)S(1)} %get-tuple-element.55), channel_id=1, source_target_pairs={{8,0},{0,8},{24,16},{16,24},{9,1},{1,9},{25,17},{17,25},{10,2},{2,... | collective-permute-start | bytes 387080 | tf_op jit(solution)/shard_map/ppermute | solution.py:525
  36.7 6.6 %collective-permute-start.8 = (bf16[72,896]{1,0:T(8,128)(2,1)S(1)}, bf16[72,896]{1,0:T(8,128)(2,1)S(1)}, u32[]{:S(2)}, u32[]{:S(2)}) collective-permute-start(bf16[72,896]{1,0:T(8,128)(2,1)S(1)} %get-tuple-element.56), channel_id=1, source_target_pairs={{16,0},{24,8},{0,16},{8,24},{17,1},{25,9},{1,17},{9,25},{18,2},{26... | collective-permute-start | bytes 387080 | tf_op jit(solution)/shard_map/ppermute | solution.py:525
  37.3 7.6 %collective-permute-start.9 = (bf16[72,896]{1,0:T(8,128)(2,1)S(1)}, bf16[72,896]{1,0:T(8,128)(2,1)S(1)}, u32[]{:S(2)}, u32[]{:S(2)}) collective-permute-start(bf16[72,896]{1,0:T(8,128)(2,1)S(1)} %get-tuple-element.57), channel_id=1, source_target_pairs={{24,0},{16,8},{8,16},{0,24},{25,1},{17,9},{9,17},{1,25},{26,2},{18... | collective-permute-start | bytes 387080 | tf_op jit(solution)/shard_map/ppermute | solution.py:525
  49.8 4.9 %collective-permute-start.10 = (bf16[72,4864]{1,0:T(8,128)(2,1)S(1)}, bf16[72,4864]{1,0:T(8,128)(2,1)S(1)}, u32[]{:S(2)}, u32[]{:S(2)}) collective-permute-start(bf16[72,4864]{1,0:T(8,128)(2,1)S(1)} %get-tuple-element.58), channel_id=1, source_target_pairs={{8,0},{0,8},{24,16},{16,24},{9,1},{1,9},{25,17},{17,25},{10,2},{2,... | collective-permute-start | bytes 2101256 | tf_op jit(solution)/shard_map/ppermute | solution.py:525
  50.1 36.7 %collective-permute-start.22 = (bf16[72,4864]{1,0:T(8,128)(2,1)S(1)}, bf16[72,4864]{1,0:T(8,128)(2,1)S(1)}, u32[]{:S(2)}, u32[]{:S(2)}) collective-permute-start(bf16[72,4864]{1,0:T(8,128)(2,1)S(1)} %get-tuple-element.73), channel_id=1, source_target_pairs={{16,0},{24,8},{0,16},{8,24},{17,1},{25,9},{1,17},{9,25},{18,2},{26... | collective-permute-start | bytes 2101256 | tf_op jit(solution)/shard_map/ppermute | solution.py:525
  50.6 36.3 %collective-permute-start.23 = (bf16[72,4864]{1,0:T(8,128)(2,1)S(1)}, bf16[72,4864]{1,0:T(8,128)(2,1)S(1)}, u32[]{:S(2)}, u32[]{:S(2)}) collective-permute-start(bf16[72,4864]{1,0:T(8,128)(2,1)S(1)} %get-tuple-element.74), channel_id=1, source_target_pairs={{24,0},{16,8},{8,16},{0,24},{25,1},{17,9},{9,17},{1,25},{26,2},{18... | collective-permute-start | bytes 2101256 | tf_op jit(solution)/shard_map/ppermute | solution.py:525
  51.7 18.6 %collective-permute-start.11 = (bf16[32,5888]{1,0:T(8,128)(2,1)S(1)}, bf16[32,5888]{1,0:T(8,128)(2,1)S(1)}, u32[]{:S(2)}, u32[]{:S(2)}) collective-permute-start(bf16[32,5888]{1,0:T(8,128)(2,1)S(1)} %get-tuple-element.60), channel_id=1, source_target_pairs={{0,4},{1,5},{2,6},{3,7},{4,0},{5,1},{6,2},{7,3},{8,12},{9,13},{10,... | collective-permute-start | bytes 1130504 | tf_op jit(solution)/shard_map/ppermute | solution.py:519
  51.7 24.9 %collective-permute-start.12 = (bf16[32,4480]{1,0:T(8,128)(2,1)S(1)}, bf16[32,4480]{1,0:T(8,128)(2,1)S(1)}, u32[]{:S(2)}, u32[]{:S(2)}) collective-permute-start(bf16[32,4480]{1,0:T(8,128)(2,1)S(1)} %get-tuple-element.61), channel_id=1, source_target_pairs={{0,4},{1,5},{2,6},{3,7},{4,0},{5,1},{6,2},{7,3},{8,12},{9,13},{10,... | collective-permute-start | bytes 860168 | tf_op jit(solution)/shard_map/ppermute | solution.py:519
  54.6 35.8 %copy-start = (bf16[1,896,1024]{2,1,0:T(8,128)(2,1)S(1)}, bf16[1,896,1024]{2,1,0:T(8,128)(2,1)}, u32[]{:S(2)}) copy-start(bf16[1,896,1024]{2,1,0:T(8,128)(2,1)} %momentum_hbm.1) | copy-start | bytes 5505028
  54.7 15.7 %collective-permute-start.13 = (bf16[8,10368]{1,0:T(8,128)(2,1)S(1)}, bf16[8,10368]{1,0:T(8,128)(2,1)S(1)}, u32[]{:S(2)}, u32[]{:S(2)}) collective-permute-start(bf16[8,10368]{1,0:T(8,128)(2,1)S(1)} %get-tuple-element.63), channel_id=1, source_target_pairs={{1,0},{0,1},{3,2},{2,3},{5,4},{4,5},{7,6},{6,7},{9,8},{8,9},{11,10... | collective-permute-start | bytes 497672 | tf_op jit(solution)/shard_map/ppermute | solution.py:515
  71.0 15.1 %collective-permute-start.14 = (bf16[72,1024]{1,0:T(8,128)(2,1)S(1)}, bf16[72,1024]{1,0:T(8,128)(2,1)S(1)}, u32[]{:S(2)}, u32[]{:S(2)}) collective-permute-start(bf16[72,1024]{1,0:T(8,128)(2,1)S(1)} %after_first.1.refs_2_), channel_id=1, source_target_pairs={{16,0},{24,8},{0,16},{8,24},{17,1},{25,9},{1,17},{9,25},{18,2},{26... | collective-permute-start | bytes 442376 | tf_op jit(solution)/shard_map/ppermute | solution.py:525
  71.5 14.6 %collective-permute-start.15 = (bf16[8,10368]{1,0:T(8,128)(2,1)S(1)}, bf16[8,10368]{1,0:T(8,128)(2,1)S(1)}, u32[]{:S(2)}, u32[]{:S(2)}) collective-permute-start(bf16[8,10368]{1,0:T(8,128)(2,1)S(1)} %get-tuple-element.64), channel_id=1, source_target_pairs={{2,0},{3,1},{0,2},{1,3},{6,4},{7,5},{4,6},{5,7},{10,8},{11,9},{8,1... | collective-permute-start | bytes 497672 | tf_op jit(solution)/shard_map/ppermute | solution.py:515
  76.6 13.9 %collective-permute-start.20 = (bf16[72,1024]{1,0:T(8,128)(2,1)S(1)}, bf16[72,1024]{1,0:T(8,128)(2,1)S(1)}, u32[]{:S(2)}, u32[]{:S(2)}) collective-permute-start(bf16[72,1024]{1,0:T(8,128)(2,1)S(1)} %after_first.1.refs_2_), channel_id=1, source_target_pairs={{8,0},{0,8},{24,16},{16,24},{9,1},{1,9},{25,17},{17,25},{10,2},{2,... | collective-permute-start | bytes 442376 | tf_op jit(solution)/shard_map/ppermute | solution.py:525
  86.1 6.8 %collective-permute-start.21 = (bf16[72,1024]{1,0:T(8,128)(2,1)S(1)}, bf16[72,1024]{1,0:T(8,128)(2,1)S(1)}, u32[]{:S(2)}, u32[]{:S(2)}) collective-permute-start(bf16[72,1024]{1,0:T(8,128)(2,1)S(1)} %collective-permute-done.14.refs_0_.refs_4_), channel_id=1, source_target_pairs={{8,0},{0,8},{24,16},{16,24},{9,1},{1,9},{25,17},{17,25},{10,2},{2,... | collective-permute-start | bytes 442376 | tf_op jit(solution)/shard_map/ppermute | solution.py:525
  86.1 11.3 %collective-permute-start.18 = (bf16[8,10368]{1,0:T(8,128)(2,1)S(1)}, bf16[8,10368]{1,0:T(8,128)(2,1)S(1)}, u32[]{:S(2)}, u32[]{:S(2)}) collective-permute-start(bf16[8,10368]{1,0:T(8,128)(2,1)S(1)} %get-tuple-element.68), channel_id=1, source_target_pairs={{3,0},{2,1},{1,2},{0,3},{7,4},{6,5},{5,6},{4,7},{11,8},{10,9},{9,1... | collective-permute-start | bytes 497672 | tf_op jit(solution)/shard_map/ppermute | solution.py:515
  86.9 10.5 %collective-permute-start.16 = (bf16[8,10368]{1,0:T(8,128)(2,1)S(1)}, bf16[8,10368]{1,0:T(8,128)(2,1)S(1)}, u32[]{:S(2)}, u32[]{:S(2)}) collective-permute-start(bf16[8,10368]{1,0:T(8,128)(2,1)S(1)} %get-tuple-element.66), channel_id=1, source_target_pairs={{1,0},{0,1},{3,2},{2,3},{5,4},{4,5},{7,6},{6,7},{9,8},{8,9},{11,10... | collective-permute-start | bytes 497672 | tf_op jit(solution)/shard_map/ppermute | solution.py:515
  87.0 10.4 %collective-permute-start.17 = (bf16[8,10368]{1,0:T(8,128)(2,1)S(1)}, bf16[8,10368]{1,0:T(8,128)(2,1)S(1)}, u32[]{:S(2)}, u32[]{:S(2)}) collective-permute-start(bf16[8,10368]{1,0:T(8,128)(2,1)S(1)} %get-tuple-element.67), channel_id=1, source_target_pairs={{2,0},{3,1},{0,2},{1,3},{6,4},{7,5},{4,6},{5,7},{10,8},{11,9},{8,1... | collective-permute-start | bytes 497672 | tf_op jit(solution)/shard_map/ppermute | solution.py:515
  90.4 10.4 %collective-permute-start.19 = (bf16[8,10368]{1,0:T(8,128)(2,1)S(1)}, bf16[8,10368]{1,0:T(8,128)(2,1)S(1)}, u32[]{:S(2)}, u32[]{:S(2)}) collective-permute-start(bf16[8,10368]{1,0:T(8,128)(2,1)S(1)} %get-tuple-element.69), channel_id=1, source_target_pairs={{3,0},{2,1},{1,2},{0,3},{7,4},{6,5},{5,6},{4,7},{11,8},{10,9},{9,1... | collective-permute-start | bytes 497672 | tf_op jit(solution)/shard_map/ppermute | solution.py:515
  92.9 7.9 %copy-start.3 = (s32[128]{0:T(128)S(1)}, s32[128]{0:T(128)}, u32[]{:S(2)}) copy-start(s32[128]{0:T(128)} %param.10) | copy-start | bytes 1540
  92.9 7.9 %copy-start.4 = (f32[128]{0:T(128)S(1)}, f32[128]{0:T(128)}, u32[]{:S(2)}) copy-start(f32[128]{0:T(128)} %param.8) | copy-start | bytes 1540

commit v8 on v7

--- a/solution.py
+++ b/solution.py
@@ -647,7 +647,7 @@
         "own_terms",
         dtypes=[F32],
     )
-    before = other_g[1:] + early[2:3]
+    before = early[2:3]
     other_g = with_sisters(other_g)
     outs = call(
         after_second_kernel,

time: 105 us -> 102 us (0.971)
  the two profiles are of different devices: /device:TPU:28 before, /device:TPU:0 now
where the time goes in v8:
time: 102 us; the launch traced here: 103 us
  starting transfers between devices  39.2 us (38%)
  waiting for transfers between devices  36.7 us (36%)
  Pallas kernels  26.3 us (26%)
    pallas_call x10, Pallas kernels, call(): pl.pallas_call(functools.partial(kernel, plan), out_shape=[jax.ShapeDtype...  21.8 us
    ppermute x2, waiting for transfers between devices, to_partner(): return lax.ppermute(data, 'expert', pairs)  20.7 us
    ppermute x7, starting transfers between devices, to_slot(): return lax.ppermute(data, 'expert', pairs)  16.2 us
    ppermute x6, starting transfers between devices, to_source(): return lax.ppermute(data, 'expert', pairs)  13.2 us
    ppermute x7, waiting for transfers between devices, to_slot(): return lax.ppermute(data, 'expert', pairs)  9.26 us
    ppermute x6, waiting for transfers between devices, to_source(): return lax.ppermute(data, 'expert', pairs)  6.7 us
    ppermute x9, starting transfers between devices, from_group(): return lax.ppermute(data, 'dp', pairs)  5.89 us
    pallas_call x1, Pallas kernels, routed(): pl.pallas_call(functools.partial(update_kernel, plan), out_shape=[jax.Sha...  4.44 us
  transfers between devices with their start and end apart: 24, of which 11 were waited for; matrix products, arithmetic and copies ran while one was open for 0% of the time, Pallas kernels for 15%

profile of v8, /device:TPU:0, one launch (start us, length us, event | category | flops | bytes accessed | tf_op | source)
XLA Modules:
  0.0 103.2 jit_solution(1505273518635806120)
XLA Ops:
  0.6 3.4 %pack.1 = (bf16[16,10368]{1,0:T(8,128)(2,1)}, bf16[16,10368]{1,0:T(8,128)(2,1)}, bf16[16,10368]{1,0:T(8,128)(2,1)}, bf16[16,10368]{1,0:T(8,128)(2,1)}, bf16[8,10...) custom-call(s32[1,128]{1,0:T(1,128)} %bitcast.2, ...), custom_call_target="tpu_custom_call" | custom-call | flops 150994944 | bytes 3171328 | tf_op jit(solution)/shard_map/pack/pallas_call | solution.py:481
  4.0 3.0 %collective-permute-start = (bf16[16,10368]{1,0:T(8,128)(2,1)}, bf16[16,10368]{1,0:T(8,128)(2,1)S(1)}, u32[]{:S(2)}, u32[]{:S(2)}) collective-permute-start(bf16[16,10368]{1,0:T(8,128)(2,1)} %get-tuple-element.43), channel_id=1, source_target_pairs={{0,1},{1,0},{2,3},{3,2},{4,5},{5,4},{6,7},{7,6},{8,9},{9,8},{10,11... | collective-permute-start | bytes 995336 | tf_op jit(solution)/shard_map/ppermute | solution.py:508
  7.1 1.6 %collective-permute-start.1 = (bf16[16,10368]{1,0:T(8,128)(2,1)}, bf16[16,10368]{1,0:T(8,128)(2,1)S(1)}, u32[]{:S(2)}, u32[]{:S(2)}) collective-permute-start(bf16[16,10368]{1,0:T(8,128)(2,1)} %get-tuple-element.44), channel_id=1, source_target_pairs={{0,2},{1,3},{2,0},{3,1},{4,6},{5,7},{6,4},{7,5},{8,10},{9,11},{10,... | collective-permute-start | bytes 995336 | tf_op jit(solution)/shard_map/ppermute | solution.py:508
  8.6 3.0 %collective-permute-start.3 = (bf16[8,10368]{1,0:T(8,128)(2,1)}, bf16[8,10368]{1,0:T(8,128)(2,1)S(1)}, u32[]{:S(2)}, u32[]{:S(2)}) collective-permute-start(bf16[8,10368]{1,0:T(8,128)(2,1)} %get-tuple-element.51), channel_id=1, source_target_pairs={{0,4},{1,5},{2,6},{3,7},{4,0},{5,1},{6,2},{7,3},{8,12},{9,13},{10,... | collective-permute-start | bytes 497672 | tf_op jit(solution)/shard_map/ppermute | solution.py:508
  11.6 1.3 %collective-permute-start.4 = (bf16[8,10368]{1,0:T(8,128)(2,1)}, bf16[8,10368]{1,0:T(8,128)(2,1)S(1)}, u32[]{:S(2)}, u32[]{:S(2)}) collective-permute-start(bf16[8,10368]{1,0:T(8,128)(2,1)} %get-tuple-element.52), channel_id=1, source_target_pairs={{0,5},{1,4},{2,7},{3,6},{4,1},{5,0},{6,3},{7,2},{8,13},{9,12},{10,... | collective-permute-start | bytes 497672 | tf_op jit(solution)/shard_map/ppermute | solution.py:508
  13.0 3.6 %hold.1 = (bf16[3584,1024]{1,0:T(8,128)(2,1)S(1)}, bf16[896,1024]{1,0:T(8,128)(2,1)S(1)}) custom-call(bf16[1,3584,1024]{2,1,0:T(8,128)(2,1)} %weight_hbm.1), custom_call_target="tpu_custom_call" | custom-call | tf_op jit(solution)/shard_map/hold/pallas_call | solution.py:481
  16.6 3.7 %collective-permute-start.5 = (bf16[8,10368]{1,0:T(8,128)(2,1)S(1)}, bf16[8,10368]{1,0:T(8,128)(2,1)S(1)}, u32[]{:S(2)}, u32[]{:S(2)}) collective-permute-start(bf16[8,10368]{1,0:T(8,128)(2,1)S(1)} %copy-done.6), channel_id=1, source_target_pairs={{0,6},{1,7},{2,4},{3,5},{4,2},{5,3},{6,0},{7,1},{8,14},{9,15},{10,... | collective-permute-start | bytes 497672 | tf_op jit(solution)/shard_map/ppermute | solution.py:508
  20.3 4.8 %collective-permute-done.1.refs_2_ = bf16[16,10368]{1,0:T(8,128)(2,1)S(1)} collective-permute-done((bf16[16,10368]{1,0:T(8,128)(2,1)}, bf16[16,10368]{1,0:T(8,128)(2,1)S(1)}, u32[]{:S(2)}, u32[]{:S(2)}) %collective-permute-start.1) | collective-permute-done | bytes 331808 | tf_op jit(solution)/shard_map/ppermute | solution.py:508
  25.1 3.6 %collective-permute-start.6 = (bf16[8,10368]{1,0:T(8,128)(2,1)S(1)}, bf16[8,10368]{1,0:T(8,128)(2,1)S(1)}, u32[]{:S(2)}, u32[]{:S(2)}) collective-permute-start(bf16[8,10368]{1,0:T(8,128)(2,1)S(1)} %copy-done.5), channel_id=1, source_target_pairs={{0,7},{1,6},{2,5},{3,4},{4,3},{5,2},{6,1},{7,0},{8,15},{9,14},{10,... | collective-permute-start | bytes 497672 | tf_op jit(solution)/shard_map/ppermute | solution.py:508
  28.7 1.9 %collective-permute-done.2.refs_3_ = bf16[16,10368]{1,0:T(8,128)(2,1)S(1)} collective-permute-done((bf16[16,10368]{1,0:T(8,128)(2,1)}, bf16[16,10368]{1,0:T(8,128)(2,1)S(1)}, u32[]{:S(2)}, u32[]{:S(2)}) %collective-permute-start.2) | collective-permute-done | bytes 331808 | tf_op jit(solution)/shard_map/ppermute | solution.py:508
  30.5 0.2 near_columns.1
  30.8 0.1 collective-permute-start.7
  30.8 1.8 %collective-permute-start.8 = (bf16[72,896]{1,0:T(8,128)(2,1)S(1)}, bf16[72,896]{1,0:T(8,128)(2,1)S(1)}, u32[]{:S(2)}, u32[]{:S(2)}) collective-permute-start(bf16[72,896]{1,0:T(8,128)(2,1)S(1)} %get-tuple-element.56), channel_id=1, source_target_pairs={{16,0},{24,8},{0,16},{8,24},{17,1},{25,9},{1,17},{9,25},{18,2},{26... | collective-permute-start | bytes 387080 | tf_op jit(solution)/shard_map/ppermute | solution.py:525
  32.6 0.1 collective-permute-start.9
  32.7 4.7 %near_rows.1 = (bf16[32,10368]{1,0:T(8,128)(2,1)S(1)}, bf16[32,10368]{1,0:T(8,128)(2,1)S(1)}, bf16[32,2304]{1,0:T(8,128)(2,1)S(1)}, bf16[72,2048]{1,0:T(8,128)(2,1)S(1)}, bf16[72,3584]{1,0:T(8,128)(2,1)S(1)}) custom-call(s32[8]{0:T(128)S(1)} %copy-done.2, bf16[3584,1024]{1,0:T(8,128)(2,1)S(1)} %get-tuple-element.41.weight_ref, ...), custom_call_target="tpu_custom_call" | custom-call | flops 2113929216 | bytes 11081760 | tf_op jit(solution)/shard_map/near_rows/pallas_call | solution.py:481
  37.4 0.5 collective-permute-done.5.refs_2_
  37.9 2.1 %collective-permute-done.6.refs_3_ = bf16[8,10368]{1,0:T(8,128)(2,1)S(1)} collective-permute-done((bf16[8,10368]{1,0:T(8,128)(2,1)S(1)}, bf16[8,10368]{1,0:T(8,128)(2,1)S(1)}, u32[]{:S(2)}, u32[]{:S(2)}) %collective-permute-start.6) | collective-permute-done | bytes 165920 | tf_op jit(solution)/shard_map/ppermute | solution.py:508
  39.9 0.0 collective-permute-done.7.refs_5_.refs_1_
  39.9 0.0 collective-permute-done.8.refs_6_.refs_2_
  40.0 2.5 %payload.1 = (bf16[32,5888]{1,0:T(8,128)(2,1)S(1)}, bf16[32,4480]{1,0:T(8,128)(2,1)S(1)}, bf16[72,4864]{1,0:T(8,128)(2,1)S(1)}, bf16[72,4864]{1,0:T(8,128)(2,1)S...) custom-call(s32[8]{0:T(128)S(1)} %copy-done.2, bf16[3584,1024]{1,0:T(8,128)(2,1)S(1)} %get-tuple-element.41.weight_ref, ...), custom_call_target="tpu_custom_call" | custom-call | flops 1056964608 | bytes 12943392 | tf_op jit(solution)/shard_map/payload/pallas_call | solution.py:481
  42.5 0.0 copy-start
  42.5 0.1 collective-permute-start.10
  42.6 1.6 %collective-permute-start.22 = (bf16[72,4864]{1,0:T(8,128)(2,1)S(1)}, bf16[72,4864]{1,0:T(8,128)(2,1)S(1)}, u32[]{:S(2)}, u32[]{:S(2)}) collective-permute-start(bf16[72,4864]{1,0:T(8,128)(2,1)S(1)} %get-tuple-element.73), channel_id=1, source_target_pairs={{16,0},{24,8},{0,16},{8,24},{17,1},{25,9},{1,17},{9,25},{18,2},{26... | collective-permute-start | bytes 2101256 | tf_op jit(solution)/shard_map/ppermute | solution.py:525
  44.1 0.3 collective-permute-start.23
  44.4 3.9 %collective-permute-start.11 = (bf16[32,5888]{1,0:T(8,128)(2,1)S(1)}, bf16[32,5888]{1,0:T(8,128)(2,1)S(1)}, u32[]{:S(2)}, u32[]{:S(2)}) collective-permute-start(bf16[32,5888]{1,0:T(8,128)(2,1)S(1)} %get-tuple-element.60), channel_id=1, source_target_pairs={{0,4},{1,5},{2,6},{3,7},{4,0},{5,1},{6,2},{7,3},{8,12},{9,13},{10,... | collective-permute-start | bytes 1130504 | tf_op jit(solution)/shard_map/ppermute | solution.py:519
  48.4 0.0 collective-permute-start.12
  48.4 0.0 collective-permute-done.10.refs_0_.refs_5_
  48.4 3.4 %collective-permute-start.14 = (bf16[8,10368]{1,0:T(8,128)(2,1)S(1)}, bf16[8,10368]{1,0:T(8,128)(2,1)S(1)}, u32[]{:S(2)}, u32[]{:S(2)}) collective-permute-start(bf16[8,10368]{1,0:T(8,128)(2,1)S(1)} %get-tuple-element.65), channel_id=1, source_target_pairs={{1,0},{0,1},{3,2},{2,3},{5,4},{4,5},{7,6},{6,7},{9,8},{8,9},{11,10... | collective-permute-start | bytes 497672 | tf_op jit(solution)/shard_map/ppermute | solution.py:515
  51.9 20.3 %collective-permute-done.11.first.refs_0_ = bf16[32,5888]{1,0:T(8,128)(2,1)S(1)} collective-permute-done((bf16[32,5888]{1,0:T(8,128)(2,1)S(1)}, bf16[32,5888]{1,0:T(8,128)(2,1)S(1)}, u32[]{:S(2)}, u32[]{:S(2)}) %collective-permute-start.11) | collective-permute-done | bytes 376864 | tf_op jit(solution)/shard_map/ppermute | solution.py:519
  72.2 0.4 collective-permute-start.13
  72.6 0.0 collective-permute-done.14.refs_2_.refs_0_
  72.6 4.4 %collective-permute-start.17 = (bf16[8,10368]{1,0:T(8,128)(2,1)S(1)}, bf16[8,10368]{1,0:T(8,128)(2,1)S(1)}, u32[]{:S(2)}, u32[]{:S(2)}) collective-permute-start(bf16[8,10368]{1,0:T(8,128)(2,1)S(1)} %get-tuple-element.68), channel_id=1, source_target_pairs={{3,0},{2,1},{1,2},{0,3},{7,4},{6,5},{5,6},{4,7},{11,8},{10,9},{9,1... | collective-permute-start | bytes 497672 | tf_op jit(solution)/shard_map/ppermute | solution.py:515
  77.0 0.7 after_first.1.refs_2_
  77.7 0.4 collective-permute-done.12.second.refs_1_
  78.1 1.5 %collective-permute-start.20 = (bf16[72,1024]{1,0:T(8,128)(2,1)S(1)}, bf16[72,1024]{1,0:T(8,128)(2,1)S(1)}, u32[]{:S(2)}, u32[]{:S(2)}) collective-permute-start(bf16[72,1024]{1,0:T(8,128)(2,1)S(1)} %after_first.1.refs_2_), channel_id=1, source_target_pairs={{16,0},{24,8},{0,16},{8,24},{17,1},{25,9},{1,17},{9,25},{18,2},{26... | collective-permute-start | bytes 442376 | tf_op jit(solution)/shard_map/ppermute | solution.py:525
  79.6 2.0 %collective-permute-done.13.refs_0_.refs_4_ = bf16[8,10368]{1,0:T(8,128)(2,1)S(1)} collective-permute-done((bf16[8,10368]{1,0:T(8,128)(2,1)S(1)}, bf16[8,10368]{1,0:T(8,128)(2,1)S(1)}, u32[]{:S(2)}, u32[]{:S(2)}) %collective-permute-start.13) | collective-permute-done | bytes 165920 | tf_op jit(solution)/shard_map/ppermute | solution.py:515
  81.6 0.7 after_second.1
  82.3 3.4 %collective-permute-start.15 = (bf16[8,10368]{1,0:T(8,128)(2,1)S(1)}, bf16[8,10368]{1,0:T(8,128)(2,1)S(1)}, u32[]{:S(2)}, u32[]{:S(2)}) collective-permute-start(bf16[8,10368]{1,0:T(8,128)(2,1)S(1)} %get-tuple-element.66), channel_id=1, source_target_pairs={{1,0},{0,1},{3,2},{2,3},{5,4},{4,5},{7,6},{6,7},{9,8},{8,9},{11,10... | collective-permute-start | bytes 497672 | tf_op jit(solution)/shard_map/ppermute | solution.py:515
  85.8 0.0 collective-permute-done.22.refs_6_
  85.8 1.5 %collective-permute-start.18 = (bf16[8,10368]{1,0:T(8,128)(2,1)S(1)}, bf16[8,10368]{1,0:T(8,128)(2,1)S(1)}, u32[]{:S(2)}, u32[]{:S(2)}) collective-permute-start(bf16[8,10368]{1,0:T(8,128)(2,1)S(1)} %get-tuple-element.69), channel_id=1, source_target_pairs={{3,0},{2,1},{1,2},{0,3},{7,4},{6,5},{5,6},{4,7},{11,8},{10,9},{9,1... | collective-permute-start | bytes 497672 | tf_op jit(solution)/shard_map/ppermute | solution.py:515
  87.3 0.7 collective-permute-done.17.refs_6_
  88.0 0.5 collective-permute-start.21
  88.5 2.5 %own_terms.1.refs_6_ = f32[896,1024]{1,0:T(8,128)S(1)} custom-call(bf16[1,896,1024]{2,1,0:T(8,128)(2,1)S(1)} %copy-done, bf16[72,896]{1,0:T(8,128)(2,1)S(1)} %get-tuple-element.46.refs_4_.refs_0_, bf16[72,896]{1,0:T(8,128)(2,1)S(1)} %collective-permute-done.7.refs_5_.refs_1_, bf16[72,896]{1,0:T(8,128)(2,1)S(1)} %collective-permute-done.8.refs_6_.refs_2_, ...), custom_call_target="tpu_custom_call" | custom-call | tf_op jit(solution)/shard_map/own_terms/pallas_call | solution.py:481
  91.0 1.4 %collective-permute-done.15.refs_3_ = bf16[8,10368]{1,0:T(8,128)(2,1)S(1)} collective-permute-done((bf16[8,10368]{1,0:T(8,128)(2,1)S(1)}, bf16[8,10368]{1,0:T(8,128)(2,1)S(1)}, u32[]{:S(2)}, u32[]{:S(2)}) %collective-permute-start.15) | collective-permute-done | bytes 165920 | tf_op jit(solution)/shard_map/ppermute | solution.py:515
  92.4 0.5 collective-permute-done.16.refs_5_
  92.9 2.1 %collective-permute-done.18.refs_7_ = bf16[8,10368]{1,0:T(8,128)(2,1)S(1)} collective-permute-done((bf16[8,10368]{1,0:T(8,128)(2,1)S(1)}, bf16[8,10368]{1,0:T(8,128)(2,1)S(1)}, u32[]{:S(2)}, u32[]{:S(2)}) %collective-permute-start.18) | collective-permute-done | bytes 165920 | tf_op jit(solution)/shard_map/ppermute | solution.py:515
  95.0 3.6 %unpack.1 = (bf16[128,1024]{1,0:T(8,128)(2,1)}, bf16[128,3584]{1,0:T(8,128)(2,1)}) custom-call(s32[1,128]{1,0:T(1,128)S(1)} %bitcast.3, f32[1,128]{1,0:T(1,128)S(1)} %bitcast.5, bf16[8,10368]{1,0:T(8,128)(2,1)S(1)} %get-tuple-element.59.refs_0_, bf16[8,10368]{1,0:T(8,128)(2,1)S(1)} %get-tuple-element.64.refs_1_, ...), custom_call_target="tpu_custom_call" | custom-call | flops 150994944 | bytes 2507776 | tf_op jit(solution)/shard_map/unpack/pallas_call | solution.py:481
  98.6 4.4 %update.1 = (bf16[1,896,1024]{2,1,0:T(8,128)(2,1)}, bf16[1,896,1024]{2,1,0:T(8,128)(2,1)}) custom-call(s32[8]{0:T(128)S(1)} %copy-done.2, bf16[32,5888]{1,0:T(8,128)(2,1)S(1)} %collective-permute-done.11.first.refs_0_, bf16[32,4480]{1,0:T(8,128)(2,1)S(1)} %collective-permute-done.12.second.refs_1_, bf16[72,1024]{1,0:T(8,128)(2,1)S(1)} %after_first.1.refs_2_, ...), custom_call_target="tpu_custom_call" | custom-call | flops 528482304 | bytes 11010048 | tf_op jit(solution)/shard_map/update/pallas_call | solution.py:665
  (25 shorter events, 0.1 us)
Async XLA Ops:
  4.0 12.5 %collective-permute-start = (bf16[16,10368]{1,0:T(8,128)(2,1)}, bf16[16,10368]{1,0:T(8,128)(2,1)S(1)}, u32[]{:S(2)}, u32[]{:S(2)}) collective-permute-start(bf16[16,10368]{1,0:T(8,128)(2,1)} %get-tuple-element.43), channel_id=1, source_target_pairs={{0,1},{1,0},{2,3},{3,2},{4,5},{5,4},{6,7},{7,6},{8,9},{9,8},{10,11... | collective-permute-start | bytes 995336 | tf_op jit(solution)/shard_map/ppermute | solution.py:508
  7.1 18.0 %collective-permute-start.1 = (bf16[16,10368]{1,0:T(8,128)(2,1)}, bf16[16,10368]{1,0:T(8,128)(2,1)S(1)}, u32[]{:S(2)}, u32[]{:S(2)}) collective-permute-start(bf16[16,10368]{1,0:T(8,128)(2,1)} %get-tuple-element.44), channel_id=1, source_target_pairs={{0,2},{1,3},{2,0},{3,1},{4,6},{5,7},{6,4},{7,5},{8,10},{9,11},{10,... | collective-permute-start | bytes 995336 | tf_op jit(solution)/shard_map/ppermute | solution.py:508
  8.6 21.9 %collective-permute-start.2 = (bf16[16,10368]{1,0:T(8,128)(2,1)}, bf16[16,10368]{1,0:T(8,128)(2,1)S(1)}, u32[]{:S(2)}, u32[]{:S(2)}) collective-permute-start(bf16[16,10368]{1,0:T(8,128)(2,1)} %get-tuple-element.45), channel_id=1, source_target_pairs={{0,3},{1,2},{2,1},{3,0},{4,7},{5,6},{6,5},{7,4},{8,11},{9,10},{10,... | collective-permute-start | bytes 995336 | tf_op jit(solution)/shard_map/ppermute | solution.py:508
  8.6 22.2 %collective-permute-start.3 = (bf16[8,10368]{1,0:T(8,128)(2,1)}, bf16[8,10368]{1,0:T(8,128)(2,1)S(1)}, u32[]{:S(2)}, u32[]{:S(2)}) collective-permute-start(bf16[8,10368]{1,0:T(8,128)(2,1)} %get-tuple-element.51), channel_id=1, source_target_pairs={{0,4},{1,5},{2,6},{3,7},{4,0},{5,1},{6,2},{7,3},{8,12},{9,13},{10,... | collective-permute-start | bytes 497672 | tf_op jit(solution)/shard_map/ppermute | solution.py:508
  11.6 5.0 %copy-start.6 = (bf16[8,10368]{1,0:T(8,128)(2,1)S(1)}, bf16[8,10368]{1,0:T(8,128)(2,1)}, u32[]{:S(2)}) copy-start(bf16[8,10368]{1,0:T(8,128)(2,1)} %get-tuple-element.53) | copy-start | bytes 497668
  11.6 13.5 %copy-start.5 = (bf16[8,10368]{1,0:T(8,128)(2,1)S(1)}, bf16[8,10368]{1,0:T(8,128)(2,1)}, u32[]{:S(2)}) copy-start(bf16[8,10368]{1,0:T(8,128)(2,1)} %get-tuple-element.54) | copy-start | bytes 497668
  11.6 18.9 %copy-start.1 = (bf16[16,10368]{1,0:T(8,128)(2,1)S(1)}, bf16[16,10368]{1,0:T(8,128)(2,1)}, u32[]{:S(2)}) copy-start(bf16[16,10368]{1,0:T(8,128)(2,1)} %get-tuple-element.42.refs_0_) | copy-start | bytes 995332
  11.6 21.1 %copy-start.2 = (s32[8]{0:T(128)S(1)}, s32[8]{0:T(128)}, u32[]{:S(2)}) copy-start(s32[8]{0:T(128)} %placement_ref.9) | copy-start | bytes 100
  11.6 21.0 %collective-permute-start.4 = (bf16[8,10368]{1,0:T(8,128)(2,1)}, bf16[8,10368]{1,0:T(8,128)(2,1)S(1)}, u32[]{:S(2)}, u32[]{:S(2)}) collective-permute-start(bf16[8,10368]{1,0:T(8,128)(2,1)} %get-tuple-element.52), channel_id=1, source_target_pairs={{0,5},{1,4},{2,7},{3,6},{4,1},{5,0},{6,3},{7,2},{8,13},{9,12},{10,... | collective-permute-start | bytes 497672 | tf_op jit(solution)/shard_map/ppermute | solution.py:508
  16.6 21.3 %collective-permute-start.5 = (bf16[8,10368]{1,0:T(8,128)(2,1)S(1)}, bf16[8,10368]{1,0:T(8,128)(2,1)S(1)}, u32[]{:S(2)}, u32[]{:S(2)}) collective-permute-start(bf16[8,10368]{1,0:T(8,128)(2,1)S(1)} %copy-done.6), channel_id=1, source_target_pairs={{0,6},{1,7},{2,4},{3,5},{4,2},{5,3},{6,0},{7,1},{8,14},{9,15},{10,... | collective-permute-start | bytes 497672 | tf_op jit(solution)/shard_map/ppermute | solution.py:508
  25.1 14.8 %collective-permute-start.6 = (bf16[8,10368]{1,0:T(8,128)(2,1)S(1)}, bf16[8,10368]{1,0:T(8,128)(2,1)S(1)}, u32[]{:S(2)}, u32[]{:S(2)}) collective-permute-start(bf16[8,10368]{1,0:T(8,128)(2,1)S(1)} %copy-done.5), channel_id=1, source_target_pairs={{0,7},{1,6},{2,5},{3,4},{4,3},{5,2},{6,1},{7,0},{8,15},{9,14},{10,... | collective-permute-start | bytes 497672 | tf_op jit(solution)/shard_map/ppermute | solution.py:508
  30.8 9.2 %collective-permute-start.7 = (bf16[72,896]{1,0:T(8,128)(2,1)S(1)}, bf16[72,896]{1,0:T(8,128)(2,1)S(1)}, u32[]{:S(2)}, u32[]{:S(2)}) collective-permute-start(bf16[72,896]{1,0:T(8,128)(2,1)S(1)} %get-tuple-element.55), channel_id=1, source_target_pairs={{8,0},{0,8},{24,16},{16,24},{9,1},{1,9},{25,17},{17,25},{10,2},{2,... | collective-permute-start | bytes 387080 | tf_op jit(solution)/shard_map/ppermute | solution.py:525
  30.8 9.1 %collective-permute-start.8 = (bf16[72,896]{1,0:T(8,128)(2,1)S(1)}, bf16[72,896]{1,0:T(8,128)(2,1)S(1)}, u32[]{:S(2)}, u32[]{:S(2)}) collective-permute-start(bf16[72,896]{1,0:T(8,128)(2,1)S(1)} %get-tuple-element.56), channel_id=1, source_target_pairs={{16,0},{24,8},{0,16},{8,24},{17,1},{25,9},{1,17},{9,25},{18,2},{26... | collective-permute-start | bytes 387080 | tf_op jit(solution)/shard_map/ppermute | solution.py:525
  32.6 7.3 %collective-permute-start.9 = (bf16[72,896]{1,0:T(8,128)(2,1)S(1)}, bf16[72,896]{1,0:T(8,128)(2,1)S(1)}, u32[]{:S(2)}, u32[]{:S(2)}) collective-permute-start(bf16[72,896]{1,0:T(8,128)(2,1)S(1)} %get-tuple-element.57), channel_id=1, source_target_pairs={{24,0},{16,8},{8,16},{0,24},{25,1},{17,9},{9,17},{1,25},{26,2},{18... | collective-permute-start | bytes 387080 | tf_op jit(solution)/shard_map/ppermute | solution.py:525
  42.5 46.0 %copy-start = (bf16[1,896,1024]{2,1,0:T(8,128)(2,1)S(1)}, bf16[1,896,1024]{2,1,0:T(8,128)(2,1)}, u32[]{:S(2)}) copy-start(bf16[1,896,1024]{2,1,0:T(8,128)(2,1)} %momentum_hbm.1) | copy-start | bytes 5505028
  42.5 5.9 %collective-permute-start.10 = (bf16[72,4864]{1,0:T(8,128)(2,1)S(1)}, bf16[72,4864]{1,0:T(8,128)(2,1)S(1)}, u32[]{:S(2)}, u32[]{:S(2)}) collective-permute-start(bf16[72,4864]{1,0:T(8,128)(2,1)S(1)} %get-tuple-element.58), channel_id=1, source_target_pairs={{8,0},{0,8},{24,16},{16,24},{9,1},{1,9},{25,17},{17,25},{10,2},{2,... | collective-permute-start | bytes 2101256 | tf_op jit(solution)/shard_map/ppermute | solution.py:525
  42.6 43.2 %collective-permute-start.22 = (bf16[72,4864]{1,0:T(8,128)(2,1)S(1)}, bf16[72,4864]{1,0:T(8,128)(2,1)S(1)}, u32[]{:S(2)}, u32[]{:S(2)}) collective-permute-start(bf16[72,4864]{1,0:T(8,128)(2,1)S(1)} %get-tuple-element.73), channel_id=1, source_target_pairs={{16,0},{24,8},{0,16},{8,24},{17,1},{25,9},{1,17},{9,25},{18,2},{26... | collective-permute-start | bytes 2101256 | tf_op jit(solution)/shard_map/ppermute | solution.py:525
  44.1 41.6 %collective-permute-start.23 = (bf16[72,4864]{1,0:T(8,128)(2,1)S(1)}, bf16[72,4864]{1,0:T(8,128)(2,1)S(1)}, u32[]{:S(2)}, u32[]{:S(2)}) collective-permute-start(bf16[72,4864]{1,0:T(8,128)(2,1)S(1)} %get-tuple-element.74), channel_id=1, source_target_pairs={{24,0},{16,8},{8,16},{0,24},{25,1},{17,9},{9,17},{1,25},{26,2},{18... | collective-permute-start | bytes 2101256 | tf_op jit(solution)/shard_map/ppermute | solution.py:525
  44.4 27.7 %collective-permute-start.11 = (bf16[32,5888]{1,0:T(8,128)(2,1)S(1)}, bf16[32,5888]{1,0:T(8,128)(2,1)S(1)}, u32[]{:S(2)}, u32[]{:S(2)}) collective-permute-start(bf16[32,5888]{1,0:T(8,128)(2,1)S(1)} %get-tuple-element.60), channel_id=1, source_target_pairs={{0,4},{1,5},{2,6},{3,7},{4,0},{5,1},{6,2},{7,3},{8,12},{9,13},{10,... | collective-permute-start | bytes 1130504 | tf_op jit(solution)/shard_map/ppermute | solution.py:519
  48.4 29.7 %collective-permute-start.12 = (bf16[32,4480]{1,0:T(8,128)(2,1)S(1)}, bf16[32,4480]{1,0:T(8,128)(2,1)S(1)}, u32[]{:S(2)}, u32[]{:S(2)}) collective-permute-start(bf16[32,4480]{1,0:T(8,128)(2,1)S(1)} %get-tuple-element.61), channel_id=1, source_target_pairs={{0,4},{1,5},{2,6},{3,7},{4,0},{5,1},{6,2},{7,3},{8,12},{9,13},{10,... | collective-permute-start | bytes 860168 | tf_op jit(solution)/shard_map/ppermute | solution.py:519
  48.4 24.2 %collective-permute-start.14 = (bf16[8,10368]{1,0:T(8,128)(2,1)S(1)}, bf16[8,10368]{1,0:T(8,128)(2,1)S(1)}, u32[]{:S(2)}, u32[]{:S(2)}) collective-permute-start(bf16[8,10368]{1,0:T(8,128)(2,1)S(1)} %get-tuple-element.65), channel_id=1, source_target_pairs={{1,0},{0,1},{3,2},{2,3},{5,4},{4,5},{7,6},{6,7},{9,8},{8,9},{11,10... | collective-permute-start | bytes 497672 | tf_op jit(solution)/shard_map/ppermute | solution.py:515
  72.2 9.5 %collective-permute-start.13 = (bf16[8,10368]{1,0:T(8,128)(2,1)S(1)}, bf16[8,10368]{1,0:T(8,128)(2,1)S(1)}, u32[]{:S(2)}, u32[]{:S(2)}) collective-permute-start(bf16[8,10368]{1,0:T(8,128)(2,1)S(1)} %get-tuple-element.63), channel_id=1, source_target_pairs={{2,0},{3,1},{0,2},{1,3},{6,4},{7,5},{4,6},{5,7},{10,8},{11,9},{8,1... | collective-permute-start | bytes 497672 | tf_op jit(solution)/shard_map/ppermute | solution.py:515
  72.6 15.4 %collective-permute-start.17 = (bf16[8,10368]{1,0:T(8,128)(2,1)S(1)}, bf16[8,10368]{1,0:T(8,128)(2,1)S(1)}, u32[]{:S(2)}, u32[]{:S(2)}) collective-permute-start(bf16[8,10368]{1,0:T(8,128)(2,1)S(1)} %get-tuple-element.68), channel_id=1, source_target_pairs={{3,0},{2,1},{1,2},{0,3},{7,4},{6,5},{5,6},{4,7},{11,8},{10,9},{9,1... | collective-permute-start | bytes 497672 | tf_op jit(solution)/shard_map/ppermute | solution.py:515
  78.1 9.9 %collective-permute-start.20 = (bf16[72,1024]{1,0:T(8,128)(2,1)S(1)}, bf16[72,1024]{1,0:T(8,128)(2,1)S(1)}, u32[]{:S(2)}, u32[]{:S(2)}) collective-permute-start(bf16[72,1024]{1,0:T(8,128)(2,1)S(1)} %after_first.1.refs_2_), channel_id=1, source_target_pairs={{16,0},{24,8},{0,16},{8,24},{17,1},{25,9},{1,17},{9,25},{18,2},{26... | collective-permute-start | bytes 442376 | tf_op jit(solution)/shard_map/ppermute | solution.py:525
  82.3 10.1 %collective-permute-start.15 = (bf16[8,10368]{1,0:T(8,128)(2,1)S(1)}, bf16[8,10368]{1,0:T(8,128)(2,1)S(1)}, u32[]{:S(2)}, u32[]{:S(2)}) collective-permute-start(bf16[8,10368]{1,0:T(8,128)(2,1)S(1)} %get-tuple-element.66), channel_id=1, source_target_pairs={{1,0},{0,1},{3,2},{2,3},{5,4},{4,5},{7,6},{6,7},{9,8},{8,9},{11,10... | collective-permute-start | bytes 497672 | tf_op jit(solution)/shard_map/ppermute | solution.py:515
  85.8 7.2 %collective-permute-start.16 = (bf16[8,10368]{1,0:T(8,128)(2,1)S(1)}, bf16[8,10368]{1,0:T(8,128)(2,1)S(1)}, u32[]{:S(2)}, u32[]{:S(2)}) collective-permute-start(bf16[8,10368]{1,0:T(8,128)(2,1)S(1)} %get-tuple-element.67), channel_id=1, source_target_pairs={{2,0},{3,1},{0,2},{1,3},{6,4},{7,5},{4,6},{5,7},{10,8},{11,9},{8,1... | collective-permute-start | bytes 497672 | tf_op jit(solution)/shard_map/ppermute | solution.py:515
  85.8 9.2 %collective-permute-start.18 = (bf16[8,10368]{1,0:T(8,128)(2,1)S(1)}, bf16[8,10368]{1,0:T(8,128)(2,1)S(1)}, u32[]{:S(2)}, u32[]{:S(2)}) collective-permute-start(bf16[8,10368]{1,0:T(8,128)(2,1)S(1)} %get-tuple-element.69), channel_id=1, source_target_pairs={{3,0},{2,1},{1,2},{0,3},{7,4},{6,5},{5,6},{4,7},{11,8},{10,9},{9,1... | collective-permute-start | bytes 497672 | tf_op jit(solution)/shard_map/ppermute | solution.py:515
  88.0 10.6 %collective-permute-start.19 = (bf16[72,1024]{1,0:T(8,128)(2,1)S(1)}, bf16[72,1024]{1,0:T(8,128)(2,1)S(1)}, u32[]{:S(2)}, u32[]{:S(2)}) collective-permute-start(bf16[72,1024]{1,0:T(8,128)(2,1)S(1)} %after_first.1.refs_2_), channel_id=1, source_target_pairs={{8,0},{0,8},{24,16},{16,24},{9,1},{1,9},{25,17},{17,25},{10,2},{2,... | collective-permute-start | bytes 442376 | tf_op jit(solution)/shard_map/ppermute | solution.py:525
  88.0 10.6 %collective-permute-start.21 = (bf16[72,1024]{1,0:T(8,128)(2,1)S(1)}, bf16[72,1024]{1,0:T(8,128)(2,1)S(1)}, u32[]{:S(2)}, u32[]{:S(2)}) collective-permute-start(bf16[72,1024]{1,0:T(8,128)(2,1)S(1)} %collective-permute-done.20.refs_4_), channel_id=1, source_target_pairs={{8,0},{0,8},{24,16},{16,24},{9,1},{1,9},{25,17},{17,25},{10,2},{2,... | collective-permute-start | bytes 442376 | tf_op jit(solution)/shard_map/ppermute | solution.py:525
  88.5 6.5 %copy-start.3 = (s32[128]{0:T(128)S(1)}, s32[128]{0:T(128)}, u32[]{:S(2)}) copy-start(s32[128]{0:T(128)} %param.10) | copy-start | bytes 1540
  88.5 6.5 %copy-start.4 = (f32[128]{0:T(128)S(1)}, f32[128]{0:T(128)}, u32[]{:S(2)}) copy-start(f32[128]{0:T(128)} %param.8) | copy-start | bytes 1540

commit v9 on v6

--- a/solution.py
+++ b/solution.py
@@ -339,9 +339,10 @@
     outs[plan.half][...] = jnp.where(hot, unfold(plan, blocks, plan.F).astype(F32), 0.0).astype(BF16)
 
 
-def unpack_kernel(plan, slot_ref, gate_ref, *refs):
-    count = 2 * plan.half
-    got, refs = refs[:count], refs[count:]
+def unpack_kernel(far, plan, slot_ref, gate_ref, *refs):
+    half = plan.half
+    got, refs = refs[:half], refs[half:]
+    before, refs = (refs[:2], refs[2:]) if far else ((None, None), refs)
     out_ref, grad_ref, held, sems = refs
     copies = [
         pltpu.make_async_copy(source, held.at[i], sems.at[i]) for i, source in enumerate(got)
@@ -349,7 +350,8 @@
     for copy in copies:
         copy.start()
     block, rank = token_places(plan, slot_ref[...])
-    width = count * SUB
+    block = jnp.where(lax.rem(block, 2) == far, block // 2, -2)
+    width = half * SUB
     picks = []
     for target in row_targets(plan, block, rank):
         column = to_column(target).astype(jnp.int32)
@@ -358,24 +360,27 @@
     for copy in copies:
         copy.wait()
 
-    def gather(base, size):
-        rows = [held[i, :, base : base + size * plan.cap // SUB].astype(F32) for i in range(count)]
+    def gather(base, size, scale, placed, out):
+        rows = [held[i, :, base : base + size * plan.cap // SUB].astype(F32) for i in range(half)]
         rows = jnp.concatenate(rows, axis=0).astype(BF16)
         piece = size // plan.cuts
-        parts = []
         for q in range(plan.cuts):
+            span = slice(q * piece, (q + 1) * piece)
             lhs, rhs = list(picks[: plan.full]), []
             for i in range(plan.full):
-                start = i * size + q * piece
-                rhs.append(rows[:, start : start + piece])
+                rhs.append(rows[:, i * size + q * piece : i * size + (q + 1) * piece])
             if plan.rest:
                 lhs.append(picks[plan.full + q])
                 rhs.append(rows[:, plan.full * size :])
-            parts.append(dot(jnp.concatenate(lhs, axis=1), jnp.concatenate(rhs, axis=0)))
-        return jnp.concatenate(parts, axis=1)
-
-    grad_ref[...] = gather(0, plan.D).astype(BF16)
-    out_ref[...] = (gate * gather(plan.DX, plan.F)).astype(BF16)
+            value = dot(jnp.concatenate(lhs, axis=1), jnp.concatenate(rhs, axis=0))
+            if scale is not None:
+                value = scale * value
+            if placed is not None:
+                value = value + placed[:, span].astype(F32)
+            out[:, span] = value.astype(BF16)
+
+    gather(0, plan.D, None, before[1], grad_ref)
+    gather(plan.DX, plan.F, gate, before[0], out_ref)
 
 
 def rows_of(parts):
@@ -404,29 +409,35 @@
         total[span, :] = before + dot_tn(x_all[:, span], g_all)
 
 
-def update_kernel(plan, placement_ref, *refs):
+def update_kernel(plan, placement_ref, payload_hbm, *refs):
     groups, share = plan.groups, plan.share
-    sources, refs = refs[: groups + 3], refs[groups + 3 :]
-    new_weight, new_momentum, payload, other_g, total, weight, momentum, sems, out_sems = refs
-    targets = [payload] + [other_g.at[m] for m in range(groups)] + [total, weight]
-    copies = [
-        pltpu.make_async_copy(source, target, sems.at[i])
-        for i, (source, target) in enumerate(zip(sources, targets))
+    other_hbm, refs = refs[:groups], refs[groups:]
+    total_hbm, weight_hbm, new_weight, new_momentum, payload, other_g = refs[:6]
+    total, weight, momentum, sems, tile_sems, out_sems = refs[6:]
+    first = [pltpu.make_async_copy(payload_hbm, payload, sems.at[groups])]
+    for m in range(groups):
+        first.append(pltpu.make_async_copy(other_hbm[m], other_g.at[m], sems.at[m]))
+    spans = [pl.ds(i * LANES, LANES) for i in range(share // LANES)]
+    tiles = [
+        [
+            pltpu.make_async_copy(source.at[span, :], target.at[span, :], tile_sems.at[i, j])
+            for j, (source, target) in enumerate(((total_hbm, total), (weight_hbm, weight)))
+        ]
+        for i, span in enumerate(spans)
     ]
-    for copy in copies:
+    for copy in first + [copy for pair in tiles for copy in pair]:
         copy.start()
     hot = is_hot(plan, placement_ref)
-    for copy in copies[: groups + 1]:
+    for copy in first:
         copy.wait()
     pieces = [payload[:, i * share : (i + 1) * share] for i in range(plan.pieces)]
     x = jnp.concatenate(pieces, axis=0)
     x = jnp.where(hot, x.astype(F32), 0.0).astype(BF16)
     g = rows_of([other_g[m] for m in range(groups)])
-    for copy in copies[groups + 1 :]:
-        copy.wait()
     done = []
-    for i in range(share // LANES):
-        span = pl.ds(i * LANES, LANES)
+    for i, span in enumerate(spans):
+        for copy in tiles[i]:
+            copy.wait()
         value = total[span, :] + dot_tn(x[:, i * LANES : (i + 1) * LANES], g)
         value = value.astype(BF16)
         momentum[span, :] = value
@@ -468,7 +479,7 @@
 
 
 def routed(plan, tokens, route_weight, cotangent, slot_ids, placement, weight, momentum):
-    half, groups = plan.half, plan.groups
+    half, groups, outer = plan.half, plan.groups, plan.outer
     D, F, C, rows, share = plan.D, plan.F, plan.C, plan.rows, plan.share
     slot = slot_ids.reshape(1, -1)
     gate = route_weight.reshape(1, -1)
@@ -496,6 +507,15 @@
         for d in range(groups):
             pairs.append((plan.group_at(d, m), d))
         return lax.ppermute(data, "dp", pairs)
+
+    def from_chips(per_chip):
+        return [per_chip[0]] + [
+            from_group(per_chip[plan.group_from(INNER * o) // INNER], INNER * o)
+            for o in range(1, outer)
+        ]
+
+    def with_sisters(got):
+        return [data for own in got for data in (own, from_group(own, 1))]
 
     def from_groups(per_group):
         return [per_group[0]] + [
@@ -598,11 +618,25 @@
         "own_terms",
         dtypes=[F32],
     )
+    def place(far, got, placed, name):
+        return call(
+            functools.partial(unpack_kernel, far),
+            plan,
+            [slot, gate] + got + placed,
+            [VMEM_SPEC] * 2 + [ANY_SPEC] * half + [VMEM_SPEC] * len(placed),
+            [(plan.tokens, F), (plan.tokens, D)],
+            [pltpu.VMEM((half, SUB, C), BF16), pltpu.SemaphoreType.DMA((half,))],
+            0,
+            name,
+            limit=12,
+        )
+
+    placed = list(place(0, early, [], "near_results"))
     outs = call(
         after_kernel,
         plan,
-        [placement, payload, local, total] + early[1:-1],
-        [SMEM_SPEC] + [VMEM_SPEC] * 2 + [ANY_SPEC] * (half - 1),
+        [placement, payload, local] + early[1:3],
+        [SMEM_SPEC] + [VMEM_SPEC] * 2 + [ANY_SPEC] * 2,
         [(SUB, C)] * half + [(rows, F)],
         [],
         0,
@@ -610,7 +644,7 @@
         limit=8,
     )
     late = [outs[0]] + [to_source(outs[m], m) for m in range(1, half)]
-    other_g = from_groups([outs[half]] * groups)
+    other_g = with_sisters(from_chips([outs[half]] * outer))
 
     new_weight, new_momentum = pl.pallas_call(
         functools.partial(update_kernel, plan),
@@ -623,7 +657,8 @@
             pltpu.VMEM((share, F), F32),
             pltpu.VMEM((share, F), BF16),
             pltpu.VMEM((share, F), BF16),
-            pltpu.SemaphoreType.DMA((groups + 3,)),
+            pltpu.SemaphoreType.DMA((groups + 1,)),
+            pltpu.SemaphoreType.DMA((share // LANES, 2)),
             pltpu.SemaphoreType.DMA((share // LANES, 2)),
         ],
         compiler_params=pltpu.CompilerParams(vmem_limit_bytes=20 * MIB),
@@ -633,20 +668,7 @@
         name="update",
     )(placement, payload, *other_g, total, old_weight)
 
-    expert_out, token_grad = call(
-        unpack_kernel,
-        plan,
-        [slot, gate] + [data for pair in zip(early, late) for data in pair],
-        [VMEM_SPEC] * 2 + [ANY_SPEC] * (2 * half),
-        [(plan.tokens, F), (plan.tokens, D)],
-        [
-            pltpu.VMEM((2 * half, SUB, C), BF16),
-            pltpu.SemaphoreType.DMA((2 * half,)),
-        ],
-        2 * 4 * half * SUB * plan.tokens * (D + F),
-        "unpack",
-        limit=12,
-    )
+    expert_out, token_grad = place(1, late, placed, "far_results")
     return expert_out, token_grad, new_weight, new_momentum
 
 

time: 105 us -> 102 us (0.971)
  the two profiles are of different devices: /device:TPU:25 before, /device:TPU:0 now
where the time goes in v9:
time: 102 us; the launch traced here: 100 us
  starting transfers between devices  43.5 us (43%)
  waiting for transfers between devices  28.1 us (28%)
  Pallas kernels  27.8 us (27%)
    pallas_call x10, Pallas kernels, call(): pl.pallas_call(functools.partial(kernel, plan), out_shape=[jax.ShapeDtype...  22.3 us
    ppermute x1, waiting for transfers between devices, to_partner(): return lax.ppermute(data, 'expert', pairs)  18.8 us
    ppermute x6, starting transfers between devices, to_source(): return lax.ppermute(data, 'expert', pairs)  17.4 us
    ppermute x7, starting transfers between devices, to_slot(): return lax.ppermute(data, 'expert', pairs)  16.2 us
    ppermute x7, waiting for transfers between devices, to_slot(): return lax.ppermute(data, 'expert', pairs)  9.26 us
    ppermute x9, starting transfers between devices, from_group(): return lax.ppermute(data, 'dp', pairs)  5.95 us
    pallas_call x1, Pallas kernels, routed(): pl.pallas_call(functools.partial(update_kernel, plan), out_shape=[jax.Sha...  5.58 us
    ppermute x1, starting transfers between devices, to_partner(): return lax.ppermute(data, 'expert', pairs)  3.98 us
  transfers between devices with their start and end apart: 23, of which 5 were waited for; matrix products, arithmetic and copies ran while one was open for 0% of the time, Pallas kernels for 16%

profile of v9, /device:TPU:0, one launch (start us, length us, event | category | flops | bytes accessed | tf_op | source)
XLA Modules:
  0.0 100.5 jit_solution(14196215592351286022)
XLA Ops:
  0.6 3.4 %pack.1 = (bf16[16,10368]{1,0:T(8,128)(2,1)}, bf16[16,10368]{1,0:T(8,128)(2,1)}, bf16[16,10368]{1,0:T(8,128)(2,1)}, bf16[16,10368]{1,0:T(8,128)(2,1)}, bf16[8,10...) custom-call(s32[1,128]{1,0:T(1,128)} %bitcast.2, ...), custom_call_target="tpu_custom_call" | custom-call | flops 150994944 | bytes 3171328 | tf_op jit(solution)/shard_map/pack/pallas_call | solution.py:465
  4.0 3.0 %collective-permute-start = (bf16[16,10368]{1,0:T(8,128)(2,1)}, bf16[16,10368]{1,0:T(8,128)(2,1)S(1)}, u32[]{:S(2)}, u32[]{:S(2)}) collective-permute-start(bf16[16,10368]{1,0:T(8,128)(2,1)} %get-tuple-element.45), channel_id=1, source_target_pairs={{0,1},{1,0},{2,3},{3,2},{4,5},{5,4},{6,7},{7,6},{8,9},{9,8},{10,11... | collective-permute-start | bytes 995336 | tf_op jit(solution)/shard_map/ppermute | solution.py:492
  7.1 1.6 %collective-permute-start.1 = (bf16[16,10368]{1,0:T(8,128)(2,1)}, bf16[16,10368]{1,0:T(8,128)(2,1)S(1)}, u32[]{:S(2)}, u32[]{:S(2)}) collective-permute-start(bf16[16,10368]{1,0:T(8,128)(2,1)} %get-tuple-element.46), channel_id=1, source_target_pairs={{0,2},{1,3},{2,0},{3,1},{4,6},{5,7},{6,4},{7,5},{8,10},{9,11},{10,... | collective-permute-start | bytes 995336 | tf_op jit(solution)/shard_map/ppermute | solution.py:492
  8.6 0.0 collective-permute-start.2
  8.6 3.0 %collective-permute-start.3 = (bf16[8,10368]{1,0:T(8,128)(2,1)}, bf16[8,10368]{1,0:T(8,128)(2,1)S(1)}, u32[]{:S(2)}, u32[]{:S(2)}) collective-permute-start(bf16[8,10368]{1,0:T(8,128)(2,1)} %get-tuple-element.52), channel_id=1, source_target_pairs={{0,4},{1,5},{2,6},{3,7},{4,0},{5,1},{6,2},{7,3},{8,12},{9,13},{10,... | collective-permute-start | bytes 497672 | tf_op jit(solution)/shard_map/ppermute | solution.py:492
  11.6 1.3 %collective-permute-start.4 = (bf16[8,10368]{1,0:T(8,128)(2,1)}, bf16[8,10368]{1,0:T(8,128)(2,1)S(1)}, u32[]{:S(2)}, u32[]{:S(2)}) collective-permute-start(bf16[8,10368]{1,0:T(8,128)(2,1)} %get-tuple-element.53), channel_id=1, source_target_pairs={{0,5},{1,4},{2,7},{3,6},{4,1},{5,0},{6,3},{7,2},{8,13},{9,12},{10,... | collective-permute-start | bytes 497672 | tf_op jit(solution)/shard_map/ppermute | solution.py:492
  13.0 3.6 %hold.1 = (bf16[3584,1024]{1,0:T(8,128)(2,1)S(1)}, bf16[896,1024]{1,0:T(8,128)(2,1)S(1)}) custom-call(bf16[1,3584,1024]{2,1,0:T(8,128)(2,1)} %weight_hbm.1), custom_call_target="tpu_custom_call" | custom-call | tf_op jit(solution)/shard_map/hold/pallas_call | solution.py:465
  16.6 0.0 collective-permute-done.refs_1_
  16.6 3.7 %collective-permute-start.5 = (bf16[8,10368]{1,0:T(8,128)(2,1)S(1)}, bf16[8,10368]{1,0:T(8,128)(2,1)S(1)}, u32[]{:S(2)}, u32[]{:S(2)}) collective-permute-start(bf16[8,10368]{1,0:T(8,128)(2,1)S(1)} %copy-done.6), channel_id=1, source_target_pairs={{0,6},{1,7},{2,4},{3,5},{4,2},{5,3},{6,0},{7,1},{8,14},{9,15},{10,... | collective-permute-start | bytes 497672 | tf_op jit(solution)/shard_map/ppermute | solution.py:492
  20.3 4.8 %collective-permute-done.1.refs_2_ = bf16[16,10368]{1,0:T(8,128)(2,1)S(1)} collective-permute-done((bf16[16,10368]{1,0:T(8,128)(2,1)}, bf16[16,10368]{1,0:T(8,128)(2,1)S(1)}, u32[]{:S(2)}, u32[]{:S(2)}) %collective-permute-start.1) | collective-permute-done | bytes 331808 | tf_op jit(solution)/shard_map/ppermute | solution.py:492
  25.1 3.6 %collective-permute-start.6 = (bf16[8,10368]{1,0:T(8,128)(2,1)S(1)}, bf16[8,10368]{1,0:T(8,128)(2,1)S(1)}, u32[]{:S(2)}, u32[]{:S(2)}) collective-permute-start(bf16[8,10368]{1,0:T(8,128)(2,1)S(1)} %copy-done.5), channel_id=1, source_target_pairs={{0,7},{1,6},{2,5},{3,4},{4,3},{5,2},{6,1},{7,0},{8,15},{9,14},{10,... | collective-permute-start | bytes 497672 | tf_op jit(solution)/shard_map/ppermute | solution.py:492
  28.7 1.9 %collective-permute-done.2.refs_3_ = bf16[16,10368]{1,0:T(8,128)(2,1)S(1)} collective-permute-done((bf16[16,10368]{1,0:T(8,128)(2,1)}, bf16[16,10368]{1,0:T(8,128)(2,1)S(1)}, u32[]{:S(2)}, u32[]{:S(2)}) %collective-permute-start.2) | collective-permute-done | bytes 331808 | tf_op jit(solution)/shard_map/ppermute | solution.py:492
  30.5 0.2 near_columns.1
  30.8 0.1 collective-permute-start.7
  30.8 0.0 collective-permute-done.3.refs_0_
  30.8 1.8 %collective-permute-start.8 = (bf16[72,896]{1,0:T(8,128)(2,1)S(1)}, bf16[72,896]{1,0:T(8,128)(2,1)S(1)}, u32[]{:S(2)}, u32[]{:S(2)}) collective-permute-start(bf16[72,896]{1,0:T(8,128)(2,1)S(1)} %get-tuple-element.57), channel_id=1, source_target_pairs={{16,0},{24,8},{0,16},{8,24},{17,1},{25,9},{1,17},{9,25},{18,2},{26... | collective-permute-start | bytes 387080 | tf_op jit(solution)/shard_map/ppermute | solution.py:509
  32.6 0.0 collective-permute-done.4.refs_1_
  32.6 0.1 collective-permute-start.9
  32.7 4.7 %near_rows.1 = (bf16[32,10368]{1,0:T(8,128)(2,1)S(1)}, bf16[32,10368]{1,0:T(8,128)(2,1)S(1)}, bf16[32,2304]{1,0:T(8,128)(2,1)S(1)}, bf16[72,2048]{1,0:T(8,128)(2,1)S(1)}, bf16[72,3584]{1,0:T(8,128)(2,1)S(1)}) custom-call(s32[8]{0:T(128)S(1)} %copy-done.2, bf16[3584,1024]{1,0:T(8,128)(2,1)S(1)} %get-tuple-element.43.weight_ref, ...), custom_call_target="tpu_custom_call" | custom-call | flops 2113929216 | bytes 11081760 | tf_op jit(solution)/shard_map/near_rows/pallas_call | solution.py:465
  37.4 0.5 collective-permute-done.5.refs_2_
  37.9 2.1 %collective-permute-done.6.refs_3_ = bf16[8,10368]{1,0:T(8,128)(2,1)S(1)} collective-permute-done((bf16[8,10368]{1,0:T(8,128)(2,1)S(1)}, bf16[8,10368]{1,0:T(8,128)(2,1)S(1)}, u32[]{:S(2)}, u32[]{:S(2)}) %collective-permute-start.6) | collective-permute-done | bytes 165920 | tf_op jit(solution)/shard_map/ppermute | solution.py:492
  39.9 0.0 collective-permute-done.7.refs_5_.refs_1_
  39.9 0.0 collective-permute-done.8.refs_6_.refs_2_
  40.0 0.0 collective-permute-done.9.refs_7_.refs_3_
  40.0 2.5 %payload.1 = (bf16[32,10368]{1,0:T(8,128)(2,1)S(1)}, bf16[72,4864]{1,0:T(8,128)(2,1)S(1)}, bf16[72,4864]{1,0:T(8,128)(2,1)S(1)}, bf16[72,4864]{1,0:T(8,128)(2,1)S(1)}, bf16[72,4864]{1,0:T(8,128)(2,1)S(1)}) custom-call(s32[8]{0:T(128)S(1)} %copy-done.2, bf16[3584,1024]{1,0:T(8,128)(2,1)S(1)} %get-tuple-element.43.weight_ref, ...), custom_call_target="tpu_custom_call" | custom-call | flops 1056964608 | bytes 12943392 | tf_op jit(solution)/shard_map/payload/pallas_call | solution.py:465
  42.5 0.0 copy-start
  42.5 0.1 collective-permute-start.11
  42.6 4.0 %collective-permute-start.10 = (bf16[32,10368]{1,0:T(8,128)(2,1)S(1)}, bf16[32,10368]{1,0:T(8,128)(2,1)S(1)}, u32[]{:S(2)}, u32[]{:S(2)}) collective-permute-start(bf16[32,10368]{1,0:T(8,128)(2,1)S(1)} %get-tuple-element.59), channel_id=1, source_target_pairs={{0,4},{1,5},{2,6},{3,7},{4,0},{5,1},{6,2},{7,3},{8,12},{9,13},{10,... | collective-permute-start | bytes 1990664 | tf_op jit(solution)/shard_map/ppermute | solution.py:503
  46.5 1.6 %collective-permute-start.21 = (bf16[72,4864]{1,0:T(8,128)(2,1)S(1)}, bf16[72,4864]{1,0:T(8,128)(2,1)S(1)}, u32[]{:S(2)}, u32[]{:S(2)}) collective-permute-start(bf16[72,4864]{1,0:T(8,128)(2,1)S(1)} %get-tuple-element.77), channel_id=1, source_target_pairs={{16,0},{24,8},{0,16},{8,24},{17,1},{25,9},{1,17},{9,25},{18,2},{26... | collective-permute-start | bytes 2101256 | tf_op jit(solution)/shard_map/ppermute | solution.py:509
  48.1 0.0 collective-permute-start.22
  48.1 0.0 collective-permute-done.11.refs_0_.refs_5_
  48.1 1.0 collective-permute-start.12
  49.2 8.3 %collective-permute-start.13 = (bf16[8,10368]{1,0:T(8,128)(2,1)S(1)}, bf16[8,10368]{1,0:T(8,128)(2,1)S(1)}, u32[]{:S(2)}, u32[]{:S(2)}) collective-permute-start(bf16[8,10368]{1,0:T(8,128)(2,1)S(1)} %get-tuple-element.64), channel_id=1, source_target_pairs={{2,0},{3,1},{0,2},{1,3},{6,4},{7,5},{4,6},{5,7},{10,8},{11,9},{8,1... | collective-permute-start | bytes 497672 | tf_op jit(solution)/shard_map/ppermute | solution.py:499
  57.5 18.8 %collective-permute-done.10.payload.payload_hbm = bf16[32,10368]{1,0:T(8,128)(2,1)S(1)} collective-permute-done((bf16[32,10368]{1,0:T(8,128)(2,1)S(1)}, bf16[32,10368]{1,0:T(8,128)(2,1)S(1)}, u32[]{:S(2)}, u32[]{:S(2)}) %collective-permute-start.10) | collective-permute-done | bytes 663584 | tf_op jit(solution)/shard_map/ppermute | solution.py:503
  76.3 1.1 %collective-permute-start.17 = (bf16[8,10368]{1,0:T(8,128)(2,1)S(1)}, bf16[8,10368]{1,0:T(8,128)(2,1)S(1)}, u32[]{:S(2)}, u32[]{:S(2)}) collective-permute-start(bf16[8,10368]{1,0:T(8,128)(2,1)S(1)} %get-tuple-element.70), channel_id=1, source_target_pairs={{3,0},{2,1},{1,2},{0,3},{7,4},{6,5},{5,6},{4,7},{11,8},{10,9},{9,1... | collective-permute-start | bytes 497672 | tf_op jit(solution)/shard_map/ppermute | solution.py:499
  77.4 0.0 collective-permute-done.12.refs_0_.refs_1_
  77.4 0.0 collective-permute-done.13.refs_1_.refs_2_
  77.4 0.9 after_swap.1
  78.3 1.5 %collective-permute-start.19 = (bf16[72,1024]{1,0:T(8,128)(2,1)S(1)}, bf16[72,1024]{1,0:T(8,128)(2,1)S(1)}, u32[]{:S(2)}, u32[]{:S(2)}) collective-permute-start(bf16[72,1024]{1,0:T(8,128)(2,1)S(1)} %get-tuple-element.75.refs_0_), channel_id=1, source_target_pairs={{16,0},{24,8},{0,16},{8,24},{17,1},{25,9},{1,17},{9,25},{18,2},{26... | collective-permute-start | bytes 442376 | tf_op jit(solution)/shard_map/ppermute | solution.py:509
  79.9 1.1 %collective-permute-start.14 = (bf16[8,10368]{1,0:T(8,128)(2,1)S(1)}, bf16[8,10368]{1,0:T(8,128)(2,1)S(1)}, u32[]{:S(2)}, u32[]{:S(2)}) collective-permute-start(bf16[8,10368]{1,0:T(8,128)(2,1)S(1)} %get-tuple-element.66), channel_id=1, source_target_pairs={{1,0},{0,1},{3,2},{2,3},{5,4},{4,5},{7,6},{6,7},{9,8},{8,9},{11,10... | collective-permute-start | bytes 497672 | tf_op jit(solution)/shard_map/ppermute | solution.py:499
  80.9 1.3 %collective-permute-start.15 = (bf16[8,10368]{1,0:T(8,128)(2,1)S(1)}, bf16[8,10368]{1,0:T(8,128)(2,1)S(1)}, u32[]{:S(2)}, u32[]{:S(2)}) collective-permute-start(bf16[8,10368]{1,0:T(8,128)(2,1)S(1)} %get-tuple-element.67), channel_id=1, source_target_pairs={{2,0},{3,1},{0,2},{1,3},{6,4},{7,5},{4,6},{5,7},{10,8},{11,9},{8,1... | collective-permute-start | bytes 497672 | tf_op jit(solution)/shard_map/ppermute | solution.py:499
  82.2 4.6 %collective-permute-start.16 = (bf16[8,10368]{1,0:T(8,128)(2,1)S(1)}, bf16[8,10368]{1,0:T(8,128)(2,1)S(1)}, u32[]{:S(2)}, u32[]{:S(2)}) collective-permute-start(bf16[8,10368]{1,0:T(8,128)(2,1)S(1)} %get-tuple-element.68), channel_id=1, source_target_pairs={{3,0},{2,1},{1,2},{0,3},{7,4},{6,5},{5,6},{4,7},{11,8},{10,9},{9,1... | collective-permute-start | bytes 497672 | tf_op jit(solution)/shard_map/ppermute | solution.py:499
  86.9 0.8 collective-permute-start.18
  87.7 0.1 collective-permute-start.20
  87.8 2.5 %own_terms.1.refs_4_ = f32[896,1024]{1,0:T(8,128)S(1)} custom-call(bf16[1,896,1024]{2,1,0:T(8,128)(2,1)S(1)} %copy-done, bf16[72,896]{1,0:T(8,128)(2,1)S(1)} %get-tuple-element.48.refs_4_.refs_0_, bf16[72,896]{1,0:T(8,128)(2,1)S(1)} %collective-permute-done.7.refs_5_.refs_1_, bf16[72,896]{1,0:T(8,128)(2,1)S(1)} %collective-permute-done.8.refs_6_.refs_2_, ...), custom_call_target="tpu_custom_call" | custom-call | tf_op jit(solution)/shard_map/own_terms/pallas_call | solution.py:465
  90.2 1.7 %near_results.1 = (bf16[128,1024]{1,0:T(8,128)(2,1)S(1)}, bf16[128,3584]{1,0:T(8,128)(2,1)S(1)}) custom-call(s32[1,128]{1,0:T(1,128)S(1)} %bitcast.3, f32[1,128]{1,0:T(1,128)S(1)} %bitcast.6, bf16[8,10368]{1,0:T(8,128)(2,1)S(1)} %get-tuple-element.69.refs_0_, bf16[8,10368]{1,0:T(8,128)(2,1)S(1)} %collective-permute-done.12.refs_0_.refs_1_, ...), custom_call_target="tpu_custom_call" | custom-call | tf_op jit(solution)/shard_map/near_results/pallas_call | solution.py:465
  92.0 2.7 %far_results.1 = (bf16[128,1024]{1,0:T(8,128)(2,1)}, bf16[128,3584]{1,0:T(8,128)(2,1)}) custom-call(s32[1,128]{1,0:T(1,128)S(1)} %bitcast.4, f32[1,128]{1,0:T(1,128)S(1)} %bitcast.7, bf16[8,10368]{1,0:T(8,128)(2,1)S(1)} %get-tuple-element.65.refs_0_, bf16[8,10368]{1,0:T(8,128)(2,1)S(1)} %collective-permute-done.14.refs_1_, ...), custom_call_target="tpu_custom_call" | custom-call | tf_op jit(solution)/shard_map/far_results/pallas_call | solution.py:465
  94.7 5.6 %update.1 = (bf16[1,896,1024]{2,1,0:T(8,128)(2,1)}, bf16[1,896,1024]{2,1,0:T(8,128)(2,1)}) custom-call(s32[8]{0:T(128)S(1)} %copy-done.2, bf16[32,10368]{1,0:T(8,128)(2,1)S(1)} %collective-permute-done.10.payload.payload_hbm, bf16[72,1024]{1,0:T(8,128)(2,1)S(1)} %get-tuple-element.75.refs_0_, bf16[72,1024]{1,0:T(8,128)(2,1)S(1)} %collective-permute-done.18.refs_1_, ...), custom_call_target="tpu_custom_call" | custom-call | flops 528482304 | bytes 11010048 | tf_op jit(solution)/shard_map/update/pallas_call | solution.py:649
  (23 shorter events, 0.1 us)
Async XLA Ops:
  4.0 12.5 %collective-permute-start = (bf16[16,10368]{1,0:T(8,128)(2,1)}, bf16[16,10368]{1,0:T(8,128)(2,1)S(1)}, u32[]{:S(2)}, u32[]{:S(2)}) collective-permute-start(bf16[16,10368]{1,0:T(8,128)(2,1)} %get-tuple-element.45), channel_id=1, source_target_pairs={{0,1},{1,0},{2,3},{3,2},{4,5},{5,4},{6,7},{7,6},{8,9},{9,8},{10,11... | collective-permute-start | bytes 995336 | tf_op jit(solution)/shard_map/ppermute | solution.py:492
  7.1 18.0 %collective-permute-start.1 = (bf16[16,10368]{1,0:T(8,128)(2,1)}, bf16[16,10368]{1,0:T(8,128)(2,1)S(1)}, u32[]{:S(2)}, u32[]{:S(2)}) collective-permute-start(bf16[16,10368]{1,0:T(8,128)(2,1)} %get-tuple-element.46), channel_id=1, source_target_pairs={{0,2},{1,3},{2,0},{3,1},{4,6},{5,7},{6,4},{7,5},{8,10},{9,11},{10,... | collective-permute-start | bytes 995336 | tf_op jit(solution)/shard_map/ppermute | solution.py:492
  8.6 21.9 %collective-permute-start.2 = (bf16[16,10368]{1,0:T(8,128)(2,1)}, bf16[16,10368]{1,0:T(8,128)(2,1)S(1)}, u32[]{:S(2)}, u32[]{:S(2)}) collective-permute-start(bf16[16,10368]{1,0:T(8,128)(2,1)} %get-tuple-element.47), channel_id=1, source_target_pairs={{0,3},{1,2},{2,1},{3,0},{4,7},{5,6},{6,5},{7,4},{8,11},{9,10},{10,... | collective-permute-start | bytes 995336 | tf_op jit(solution)/shard_map/ppermute | solution.py:492
  8.6 22.2 %collective-permute-start.3 = (bf16[8,10368]{1,0:T(8,128)(2,1)}, bf16[8,10368]{1,0:T(8,128)(2,1)S(1)}, u32[]{:S(2)}, u32[]{:S(2)}) collective-permute-start(bf16[8,10368]{1,0:T(8,128)(2,1)} %get-tuple-element.52), channel_id=1, source_target_pairs={{0,4},{1,5},{2,6},{3,7},{4,0},{5,1},{6,2},{7,3},{8,12},{9,13},{10,... | collective-permute-start | bytes 497672 | tf_op jit(solution)/shard_map/ppermute | solution.py:492
  11.6 5.0 %copy-start.6 = (bf16[8,10368]{1,0:T(8,128)(2,1)S(1)}, bf16[8,10368]{1,0:T(8,128)(2,1)}, u32[]{:S(2)}) copy-start(bf16[8,10368]{1,0:T(8,128)(2,1)} %get-tuple-element.54) | copy-start | bytes 497668
  11.6 13.5 %copy-start.5 = (bf16[8,10368]{1,0:T(8,128)(2,1)S(1)}, bf16[8,10368]{1,0:T(8,128)(2,1)}, u32[]{:S(2)}) copy-start(bf16[8,10368]{1,0:T(8,128)(2,1)} %get-tuple-element.55) | copy-start | bytes 497668
  11.6 18.9 %copy-start.1 = (bf16[16,10368]{1,0:T(8,128)(2,1)S(1)}, bf16[16,10368]{1,0:T(8,128)(2,1)}, u32[]{:S(2)}) copy-start(bf16[16,10368]{1,0:T(8,128)(2,1)} %get-tuple-element.44.refs_0_) | copy-start | bytes 995332
  11.6 21.1 %copy-start.2 = (s32[8]{0:T(128)S(1)}, s32[8]{0:T(128)}, u32[]{:S(2)}) copy-start(s32[8]{0:T(128)} %placement_ref.7) | copy-start | bytes 100
  11.6 21.0 %collective-permute-start.4 = (bf16[8,10368]{1,0:T(8,128)(2,1)}, bf16[8,10368]{1,0:T(8,128)(2,1)S(1)}, u32[]{:S(2)}, u32[]{:S(2)}) collective-permute-start(bf16[8,10368]{1,0:T(8,128)(2,1)} %get-tuple-element.53), channel_id=1, source_target_pairs={{0,5},{1,4},{2,7},{3,6},{4,1},{5,0},{6,3},{7,2},{8,13},{9,12},{10,... | collective-permute-start | bytes 497672 | tf_op jit(solution)/shard_map/ppermute | solution.py:492
  16.6 21.3 %collective-permute-start.5 = (bf16[8,10368]{1,0:T(8,128)(2,1)S(1)}, bf16[8,10368]{1,0:T(8,128)(2,1)S(1)}, u32[]{:S(2)}, u32[]{:S(2)}) collective-permute-start(bf16[8,10368]{1,0:T(8,128)(2,1)S(1)} %copy-done.6), channel_id=1, source_target_pairs={{0,6},{1,7},{2,4},{3,5},{4,2},{5,3},{6,0},{7,1},{8,14},{9,15},{10,... | collective-permute-start | bytes 497672 | tf_op jit(solution)/shard_map/ppermute | solution.py:492
  25.1 14.8 %collective-permute-start.6 = (bf16[8,10368]{1,0:T(8,128)(2,1)S(1)}, bf16[8,10368]{1,0:T(8,128)(2,1)S(1)}, u32[]{:S(2)}, u32[]{:S(2)}) collective-permute-start(bf16[8,10368]{1,0:T(8,128)(2,1)S(1)} %copy-done.5), channel_id=1, source_target_pairs={{0,7},{1,6},{2,5},{3,4},{4,3},{5,2},{6,1},{7,0},{8,15},{9,14},{10,... | collective-permute-start | bytes 497672 | tf_op jit(solution)/shard_map/ppermute | solution.py:492
  30.8 9.2 %collective-permute-start.7 = (bf16[72,896]{1,0:T(8,128)(2,1)S(1)}, bf16[72,896]{1,0:T(8,128)(2,1)S(1)}, u32[]{:S(2)}, u32[]{:S(2)}) collective-permute-start(bf16[72,896]{1,0:T(8,128)(2,1)S(1)} %get-tuple-element.56), channel_id=1, source_target_pairs={{8,0},{0,8},{24,16},{16,24},{9,1},{1,9},{25,17},{17,25},{10,2},{2,... | collective-permute-start | bytes 387080 | tf_op jit(solution)/shard_map/ppermute | solution.py:509
  30.8 9.1 %collective-permute-start.8 = (bf16[72,896]{1,0:T(8,128)(2,1)S(1)}, bf16[72,896]{1,0:T(8,128)(2,1)S(1)}, u32[]{:S(2)}, u32[]{:S(2)}) collective-permute-start(bf16[72,896]{1,0:T(8,128)(2,1)S(1)} %get-tuple-element.57), channel_id=1, source_target_pairs={{16,0},{24,8},{0,16},{8,24},{17,1},{25,9},{1,17},{9,25},{18,2},{26... | collective-permute-start | bytes 387080 | tf_op jit(solution)/shard_map/ppermute | solution.py:509
  32.6 7.3 %collective-permute-start.9 = (bf16[72,896]{1,0:T(8,128)(2,1)S(1)}, bf16[72,896]{1,0:T(8,128)(2,1)S(1)}, u32[]{:S(2)}, u32[]{:S(2)}) collective-permute-start(bf16[72,896]{1,0:T(8,128)(2,1)S(1)} %get-tuple-element.58), channel_id=1, source_target_pairs={{24,0},{16,8},{8,16},{0,24},{25,1},{17,9},{9,17},{1,25},{26,2},{18... | collective-permute-start | bytes 387080 | tf_op jit(solution)/shard_map/ppermute | solution.py:509
  42.5 45.3 %copy-start = (bf16[1,896,1024]{2,1,0:T(8,128)(2,1)S(1)}, bf16[1,896,1024]{2,1,0:T(8,128)(2,1)}, u32[]{:S(2)}) copy-start(bf16[1,896,1024]{2,1,0:T(8,128)(2,1)} %momentum_hbm.1) | copy-start | bytes 5505028
  42.5 5.6 %collective-permute-start.11 = (bf16[72,4864]{1,0:T(8,128)(2,1)S(1)}, bf16[72,4864]{1,0:T(8,128)(2,1)S(1)}, u32[]{:S(2)}, u32[]{:S(2)}) collective-permute-start(bf16[72,4864]{1,0:T(8,128)(2,1)S(1)} %get-tuple-element.62), channel_id=1, source_target_pairs={{8,0},{0,8},{24,16},{16,24},{9,1},{1,9},{25,17},{17,25},{10,2},{2,... | collective-permute-start | bytes 2101256 | tf_op jit(solution)/shard_map/ppermute | solution.py:509
  42.6 33.7 %collective-permute-start.10 = (bf16[32,10368]{1,0:T(8,128)(2,1)S(1)}, bf16[32,10368]{1,0:T(8,128)(2,1)S(1)}, u32[]{:S(2)}, u32[]{:S(2)}) collective-permute-start(bf16[32,10368]{1,0:T(8,128)(2,1)S(1)} %get-tuple-element.59), channel_id=1, source_target_pairs={{0,4},{1,5},{2,6},{3,7},{4,0},{5,1},{6,2},{7,3},{8,12},{9,13},{10,... | collective-permute-start | bytes 1990664 | tf_op jit(solution)/shard_map/ppermute | solution.py:503
  46.5 34.4 %collective-permute-start.21 = (bf16[72,4864]{1,0:T(8,128)(2,1)S(1)}, bf16[72,4864]{1,0:T(8,128)(2,1)S(1)}, u32[]{:S(2)}, u32[]{:S(2)}) collective-permute-start(bf16[72,4864]{1,0:T(8,128)(2,1)S(1)} %get-tuple-element.77), channel_id=1, source_target_pairs={{16,0},{24,8},{0,16},{8,24},{17,1},{25,9},{1,17},{9,25},{18,2},{26... | collective-permute-start | bytes 2101256 | tf_op jit(solution)/shard_map/ppermute | solution.py:509
  48.1 34.1 %collective-permute-start.22 = (bf16[72,4864]{1,0:T(8,128)(2,1)S(1)}, bf16[72,4864]{1,0:T(8,128)(2,1)S(1)}, u32[]{:S(2)}, u32[]{:S(2)}) collective-permute-start(bf16[72,4864]{1,0:T(8,128)(2,1)S(1)} %get-tuple-element.78), channel_id=1, source_target_pairs={{24,0},{16,8},{8,16},{0,24},{25,1},{17,9},{9,17},{1,25},{26,2},{18... | collective-permute-start | bytes 2101256 | tf_op jit(solution)/shard_map/ppermute | solution.py:509
  48.1 29.2 %collective-permute-start.12 = (bf16[8,10368]{1,0:T(8,128)(2,1)S(1)}, bf16[8,10368]{1,0:T(8,128)(2,1)S(1)}, u32[]{:S(2)}, u32[]{:S(2)}) collective-permute-start(bf16[8,10368]{1,0:T(8,128)(2,1)S(1)} %get-tuple-element.63), channel_id=1, source_target_pairs={{1,0},{0,1},{3,2},{2,3},{5,4},{4,5},{7,6},{6,7},{9,8},{8,9},{11,10... | collective-permute-start | bytes 497672 | tf_op jit(solution)/shard_map/ppermute | solution.py:499
  49.2 28.2 %collective-permute-start.13 = (bf16[8,10368]{1,0:T(8,128)(2,1)S(1)}, bf16[8,10368]{1,0:T(8,128)(2,1)S(1)}, u32[]{:S(2)}, u32[]{:S(2)}) collective-permute-start(bf16[8,10368]{1,0:T(8,128)(2,1)S(1)} %get-tuple-element.64), channel_id=1, source_target_pairs={{2,0},{3,1},{0,2},{1,3},{6,4},{7,5},{4,6},{5,7},{10,8},{11,9},{8,1... | collective-permute-start | bytes 497672 | tf_op jit(solution)/shard_map/ppermute | solution.py:499
  76.3 10.6 %collective-permute-start.17 = (bf16[8,10368]{1,0:T(8,128)(2,1)S(1)}, bf16[8,10368]{1,0:T(8,128)(2,1)S(1)}, u32[]{:S(2)}, u32[]{:S(2)}) collective-permute-start(bf16[8,10368]{1,0:T(8,128)(2,1)S(1)} %get-tuple-element.70), channel_id=1, source_target_pairs={{3,0},{2,1},{1,2},{0,3},{7,4},{6,5},{5,6},{4,7},{11,8},{10,9},{9,1... | collective-permute-start | bytes 497672 | tf_op jit(solution)/shard_map/ppermute | solution.py:499
  78.3 9.3 %collective-permute-start.19 = (bf16[72,1024]{1,0:T(8,128)(2,1)S(1)}, bf16[72,1024]{1,0:T(8,128)(2,1)S(1)}, u32[]{:S(2)}, u32[]{:S(2)}) collective-permute-start(bf16[72,1024]{1,0:T(8,128)(2,1)S(1)} %get-tuple-element.75.refs_0_), channel_id=1, source_target_pairs={{16,0},{24,8},{0,16},{8,24},{17,1},{25,9},{1,17},{9,25},{18,2},{26... | collective-permute-start | bytes 442376 | tf_op jit(solution)/shard_map/ppermute | solution.py:509
  79.9 12.1 %collective-permute-start.14 = (bf16[8,10368]{1,0:T(8,128)(2,1)S(1)}, bf16[8,10368]{1,0:T(8,128)(2,1)S(1)}, u32[]{:S(2)}, u32[]{:S(2)}) collective-permute-start(bf16[8,10368]{1,0:T(8,128)(2,1)S(1)} %get-tuple-element.66), channel_id=1, source_target_pairs={{1,0},{0,1},{3,2},{2,3},{5,4},{4,5},{7,6},{6,7},{9,8},{8,9},{11,10... | collective-permute-start | bytes 497672 | tf_op jit(solution)/shard_map/ppermute | solution.py:499
  80.9 11.1 %collective-permute-start.15 = (bf16[8,10368]{1,0:T(8,128)(2,1)S(1)}, bf16[8,10368]{1,0:T(8,128)(2,1)S(1)}, u32[]{:S(2)}, u32[]{:S(2)}) collective-permute-start(bf16[8,10368]{1,0:T(8,128)(2,1)S(1)} %get-tuple-element.67), channel_id=1, source_target_pairs={{2,0},{3,1},{0,2},{1,3},{6,4},{7,5},{4,6},{5,7},{10,8},{11,9},{8,1... | collective-permute-start | bytes 497672 | tf_op jit(solution)/shard_map/ppermute | solution.py:499
  82.2 9.8 %collective-permute-start.16 = (bf16[8,10368]{1,0:T(8,128)(2,1)S(1)}, bf16[8,10368]{1,0:T(8,128)(2,1)S(1)}, u32[]{:S(2)}, u32[]{:S(2)}) collective-permute-start(bf16[8,10368]{1,0:T(8,128)(2,1)S(1)} %get-tuple-element.68), channel_id=1, source_target_pairs={{3,0},{2,1},{1,2},{0,3},{7,4},{6,5},{5,6},{4,7},{11,8},{10,9},{9,1... | collective-permute-start | bytes 497672 | tf_op jit(solution)/shard_map/ppermute | solution.py:499
  86.9 7.8 %collective-permute-start.18 = (bf16[72,1024]{1,0:T(8,128)(2,1)S(1)}, bf16[72,1024]{1,0:T(8,128)(2,1)S(1)}, u32[]{:S(2)}, u32[]{:S(2)}) collective-permute-start(bf16[72,1024]{1,0:T(8,128)(2,1)S(1)} %get-tuple-element.75.refs_0_), channel_id=1, source_target_pairs={{8,0},{0,8},{24,16},{16,24},{9,1},{1,9},{25,17},{17,25},{10,2},{2,... | collective-permute-start | bytes 442376 | tf_op jit(solution)/shard_map/ppermute | solution.py:509
  87.7 7.0 %collective-permute-start.20 = (bf16[72,1024]{1,0:T(8,128)(2,1)S(1)}, bf16[72,1024]{1,0:T(8,128)(2,1)S(1)}, u32[]{:S(2)}, u32[]{:S(2)}) collective-permute-start(bf16[72,1024]{1,0:T(8,128)(2,1)S(1)} %collective-permute-done.19.refs_2_), channel_id=1, source_target_pairs={{8,0},{0,8},{24,16},{16,24},{9,1},{1,9},{25,17},{17,25},{10,2},{2,... | collective-permute-start | bytes 442376 | tf_op jit(solution)/shard_map/ppermute | solution.py:509
  87.7 2.5 %copy-start.3 = (s32[128]{0:T(128)S(1)}, s32[128]{0:T(128)}, u32[]{:S(2)}) copy-start(s32[128]{0:T(128)} %param.10) | copy-start | bytes 1540
  87.7 2.5 %copy-start.4 = (f32[128]{0:T(128)S(1)}, f32[128]{0:T(128)}, u32[]{:S(2)}) copy-start(f32[128]{0:T(128)} %param.8) | copy-start | bytes 1540

commit v10 on v9

--- a/solution.py
+++ b/solution.py
@@ -286,11 +286,11 @@
 def payload_kernel(
     plan, placement_ref, weight_ref, folded_grad, near_grads, far_rows, *refs
 ):
-    half, groups = plan.half, plan.groups
+    half, groups, outer = plan.half, plan.groups, plan.outer
     far, refs = refs[:half], refs[half:]
     columns, refs = refs[:groups], refs[groups:]
     payload, refs = refs[0], refs[1:]
-    shared, rows = refs[:groups], refs[groups]
+    shared, rows = refs[:outer], refs[outer]
     hot = is_hot(plan, placement_ref)
     x = unfold(plan, blocks_of(far, 0, plan.DX), plan.D)
     g = unfold(plan, blocks_of(far, plan.DX, plan.C), plan.F)
@@ -312,14 +312,20 @@
             ].astype(BF16)
         payload[:, plan.DX :] = folded_grad[...]
 
-    group = lax.axis_index("dp")
-    width = plan.share
-    for m in range(groups):
-        start = pl.multiple_of(plan.group_at(group, m) * width, LANES)
-        shared[m][:, :width] = far_rows[:, pl.ds(start, width)]
-        shared[m][:, width : 2 * width] = rows[:, pl.ds(start, width)]
-        shared[m][:, 2 * width : 2 * width + 2 * plan.F] = near_grads[...]
-        shared[m][:, 2 * width + 2 * plan.F :] = grad_pre
+    chip = lax.axis_index("dp") // INNER
+    width = INNER * plan.share
+    for o in range(outer):
+        start = pl.multiple_of(away_traced(chip, o, outer) * width, LANES)
+        shared[o][:, :width] = far_rows[:, pl.ds(start, width)]
+        shared[o][:, width : 2 * width] = rows[:, pl.ds(start, width)]
+        shared[o][:, 2 * width : 2 * width + 2 * plan.F] = near_grads[...]
+        shared[o][:, 2 * width + 2 * plan.F :] = grad_pre
+
+
+def relay_kernel(plan, *refs):
+    count = plan.outer - 1
+    for source, target in zip(refs[:count], refs[-count:]):
+        target[...] = source[...]
 
 
 def early_kernel(plan, near_back, *refs):
@@ -394,11 +400,14 @@
     total, x_all, momentum, sem = refs
     copy = pltpu.make_async_copy(momentum_hbm.at[0], momentum, sem)
     copy.start()
-    base = 2 * share
+    core = lax.rem(lax.axis_index("dp"), INNER)
+    base = 2 * INNER * share
     x_parts, g_parts = [], []
     for m in range(groups):
         x_parts.append(columns[m][...])
-        x_parts += [shared[m][:, i * share : (i + 1) * share] for i in range(2)]
+        for i in range(2):
+            start = pl.multiple_of((i * INNER + core) * share, LANES)
+            x_parts.append(shared[m][:, pl.ds(start, share)])
         g_parts += [shared[m][:, base + i * width : base + (i + 1) * width] for i in range(3)]
     x_all[...] = rows_of(x_parts)
     g_all = rows_of(g_parts)
@@ -409,40 +418,30 @@
         total[span, :] = before + dot_tn(x_all[:, span], g_all)
 
 
-def update_kernel(plan, placement_ref, payload_hbm, *refs):
+def update_kernel(plan, placement_ref, total, old_weight, payload_hbm, *refs):
     groups, share = plan.groups, plan.share
     other_hbm, refs = refs[:groups], refs[groups:]
-    total_hbm, weight_hbm, new_weight, new_momentum, payload, other_g = refs[:6]
-    total, weight, momentum, sems, tile_sems, out_sems = refs[6:]
-    first = [pltpu.make_async_copy(payload_hbm, payload, sems.at[groups])]
+    new_weight, new_momentum, payload, other_g, weight, momentum, sems, out_sems = refs
+    copies = [pltpu.make_async_copy(payload_hbm, payload, sems.at[groups])]
     for m in range(groups):
-        first.append(pltpu.make_async_copy(other_hbm[m], other_g.at[m], sems.at[m]))
-    spans = [pl.ds(i * LANES, LANES) for i in range(share // LANES)]
-    tiles = [
-        [
-            pltpu.make_async_copy(source.at[span, :], target.at[span, :], tile_sems.at[i, j])
-            for j, (source, target) in enumerate(((total_hbm, total), (weight_hbm, weight)))
-        ]
-        for i, span in enumerate(spans)
-    ]
-    for copy in first + [copy for pair in tiles for copy in pair]:
+        copies.append(pltpu.make_async_copy(other_hbm[m], other_g.at[m], sems.at[m]))
+    for copy in copies:
         copy.start()
     hot = is_hot(plan, placement_ref)
-    for copy in first:
+    for copy in copies:
         copy.wait()
     pieces = [payload[:, i * share : (i + 1) * share] for i in range(plan.pieces)]
     x = jnp.concatenate(pieces, axis=0)
     x = jnp.where(hot, x.astype(F32), 0.0).astype(BF16)
     g = rows_of([other_g[m] for m in range(groups)])
     done = []
-    for i, span in enumerate(spans):
-        for copy in tiles[i]:
-            copy.wait()
+    for i in range(share // LANES):
+        span = pl.ds(i * LANES, LANES)
         value = total[span, :] + dot_tn(x[:, i * LANES : (i + 1) * LANES], g)
         value = value.astype(BF16)
         momentum[span, :] = value
         weight[span, :] = (
-            weight[span, :].astype(F32) - learning_rate * value.astype(F32)
+            old_weight[span, :].astype(F32) - learning_rate * value.astype(F32)
         ).astype(BF16)
         for j, (source, target) in enumerate(((momentum, new_momentum), (weight, new_weight))):
             copy = pltpu.make_async_copy(
@@ -584,17 +583,18 @@
         plan,
         [placement, held, folded_grad, grads, far_rows] + far + columns_here,
         [SMEM_SPEC] + [VMEM_SPEC] * (4 + half + groups),
-        [(half * SUB, C)] + [(rows, 2 * share + 3 * F)] * groups,
+        [(half * SUB, C)] + [(rows, 2 * INNER * share + 3 * F)] * outer,
         [pltpu.VMEM((rows, D), BF16)],
         4 * rows * D * F,
         "payload",
     )
     payload = to_partner(outs[0])
-    shared = from_groups(outs[1:])
+    shared = from_chips(outs[1:])
+    sister = from_group(shared[0], 1)
     outs = call(
         early_kernel,
         plan,
-        [back_near, shared[1]],
+        [back_near, sister],
         [VMEM_SPEC, ANY_SPEC],
         [(SUB, C)] * half,
         [],
@@ -603,6 +603,20 @@
         limit=4,
     )
     early = [outs[0]] + [to_source(outs[m], m) for m in range(1, half)]
+    gate_by = early[1:]
+    relayed = call(
+        relay_kernel,
+        plan,
+        shared[1:] + gate_by,
+        [VMEM_SPEC] * (outer - 1) + [ANY_SPEC] * len(gate_by),
+        [data.shape for data in shared[1:]],
+        [],
+        0,
+        "relay",
+        limit=8,
+    )
+    sisters = [sister] + [from_group(data, 1) for data in relayed]
+    shared = [data for pair in zip(shared, sisters) for data in pair]
     (total,) = call(
         gather_kernel,
         plan,
@@ -635,8 +649,8 @@
     outs = call(
         after_kernel,
         plan,
-        [placement, payload, local] + early[1:3],
-        [SMEM_SPEC] + [VMEM_SPEC] * 2 + [ANY_SPEC] * 2,
+        [placement, payload, local] + placed[:1],
+        [SMEM_SPEC] + [VMEM_SPEC] * 2 + [ANY_SPEC] * 1,
         [(SUB, C)] * half + [(rows, F)],
         [],
         0,
@@ -649,16 +663,14 @@
     new_weight, new_momentum = pl.pallas_call(
         functools.partial(update_kernel, plan),
         out_shape=[jax.ShapeDtypeStruct((1, share, F), BF16)] * 2,
-        in_specs=[SMEM_SPEC] + [ANY_SPEC] * (groups + 3),
+        in_specs=[SMEM_SPEC] + [VMEM_SPEC] * 2 + [ANY_SPEC] * (groups + 1),
         out_specs=[ANY_SPEC] * 2,
         scratch_shapes=[
             pltpu.VMEM((half * SUB, C), BF16),
             pltpu.VMEM((groups, rows, F), BF16),
-            pltpu.VMEM((share, F), F32),
             pltpu.VMEM((share, F), BF16),
             pltpu.VMEM((share, F), BF16),
             pltpu.SemaphoreType.DMA((groups + 1,)),
-            pltpu.SemaphoreType.DMA((share // LANES, 2)),
             pltpu.SemaphoreType.DMA((share // LANES, 2)),
         ],
         compiler_params=pltpu.CompilerParams(vmem_limit_bytes=20 * MIB),
@@ -666,7 +678,7 @@
             flops=2 * groups * rows * share * F, bytes_accessed=12 * share * F, transcendentals=0
         ),
         name="update",
-    )(placement, payload, *other_g, total, old_weight)
+    )(placement, total, old_weight, payload, *other_g)
 
     expert_out, token_grad = place(1, late, placed, "far_results")
     return expert_out, token_grad, new_weight, new_momentum

time: 102 us -> 108 us (1.059); the launches traced: 100 us -> 108 us
  waiting for transfers between devices: 28.1 us -> 43.5 us
  starting transfers between devices: 43.5 us -> 37.4 us
  Pallas kernels: 27.8 us -> 26.1 us
    ppermute x9, waiting for transfers between devices: 0.02 us -> 11.5 us  [from_group(): return lax.ppermute(data, 'dp', pairs)]
    ppermute x6, starting transfers between devices: 17.4 us -> 9.01 us  [to_source(): return lax.ppermute(data, 'expert', pairs)]
    ppermute x6, waiting for transfers between devices: 0.02 us -> 4.6 us  [to_source(): return lax.ppermute(data, 'expert', pairs)]
    ppermute x1, starting transfers between devices: 3.98 us -> 6.53 us  [to_partner(): return lax.ppermute(data, 'expert', pairs)]
    pallas_call x1, Pallas kernels: 5.58 us -> 3.9 us  [routed(): pl.pallas_call(functools.partial(update_kernel, plan), out_shape=[jax.Sha...]
    pallas_call x10 -> x11, Pallas kernels: 22.3 us -> 22.2 us  [call(): pl.pallas_call(functools.partial(kernel, plan), out_shape=[jax.ShapeDtype...]
  transfers between devices with their start and end apart: 23 -> 23, of which waited for: 5 -> 10; matrix products, arithmetic and copies ran while one was open for 0% -> 0% of each run, Pallas kernels for 16% -> 15%
where the time goes in v10:
time: 108 us
  waiting for transfers between devices  43.5 us (40%)
  starting transfers between devices  37.4 us (35%)
  Pallas kernels  26.1 us (24%)
    pallas_call x11, Pallas kernels, call(): pl.pallas_call(functools.partial(kernel, plan), out_shape=[jax.ShapeDtype...  22.2 us
    ppermute x1, waiting for transfers between devices, to_partner(): return lax.ppermute(data, 'expert', pairs)  18.1 us
    ppermute x7, starting transfers between devices, to_slot(): return lax.ppermute(data, 'expert', pairs)  16.2 us
    ppermute x9, waiting for transfers between devices, from_group(): return lax.ppermute(data, 'dp', pairs)  11.5 us
    ppermute x7, waiting for transfers between devices, to_slot(): return lax.ppermute(data, 'expert', pairs)  9.26 us
    ppermute x6, starting transfers between devices, to_source(): return lax.ppermute(data, 'expert', pairs)  9.01 us
    ppermute x1, starting transfers between devices, to_partner(): return lax.ppermute(data, 'expert', pairs)  6.53 us
    ppermute x9, starting transfers between devices, from_group(): return lax.ppermute(data, 'dp', pairs)  5.68 us
  transfers between devices with their start and end apart: 23, of which 10 were waited for; matrix products, arithmetic and copies ran while one was open for 0% of the time, Pallas kernels for 15%

profile of v10, /device:TPU:0, one launch (start us, length us, event | category | flops | bytes accessed | tf_op | source)
XLA Modules:
  0.0 108.0 jit_solution(8838809473014168011)
XLA Ops:
  0.6 3.4 %pack.1 = (bf16[16,10368]{1,0:T(8,128)(2,1)}, bf16[16,10368]{1,0:T(8,128)(2,1)}, bf16[16,10368]{1,0:T(8,128)(2,1)}, bf16[16,10368]{1,0:T(8,128)(2,1)}, bf16[8,10...) custom-call(s32[1,128]{1,0:T(1,128)} %bitcast.2, ...), custom_call_target="tpu_custom_call" | custom-call | flops 150994944 | bytes 3171328 | tf_op jit(solution)/shard_map/pack/pallas_call | solution.py:464
  4.0 3.0 %collective-permute-start = (bf16[16,10368]{1,0:T(8,128)(2,1)}, bf16[16,10368]{1,0:T(8,128)(2,1)S(1)}, u32[]{:S(2)}, u32[]{:S(2)}) collective-permute-start(bf16[16,10368]{1,0:T(8,128)(2,1)} %get-tuple-element.43), channel_id=1, source_target_pairs={{0,1},{1,0},{2,3},{3,2},{4,5},{5,4},{6,7},{7,6},{8,9},{9,8},{10,11... | collective-permute-start | bytes 995336 | tf_op jit(solution)/shard_map/ppermute | solution.py:491
  7.1 1.6 %collective-permute-start.1 = (bf16[16,10368]{1,0:T(8,128)(2,1)}, bf16[16,10368]{1,0:T(8,128)(2,1)S(1)}, u32[]{:S(2)}, u32[]{:S(2)}) collective-permute-start(bf16[16,10368]{1,0:T(8,128)(2,1)} %get-tuple-element.44), channel_id=1, source_target_pairs={{0,2},{1,3},{2,0},{3,1},{4,6},{5,7},{6,4},{7,5},{8,10},{9,11},{10,... | collective-permute-start | bytes 995336 | tf_op jit(solution)/shard_map/ppermute | solution.py:491
  8.6 0.0 collective-permute-start.2
  8.6 3.0 %collective-permute-start.3 = (bf16[8,10368]{1,0:T(8,128)(2,1)}, bf16[8,10368]{1,0:T(8,128)(2,1)S(1)}, u32[]{:S(2)}, u32[]{:S(2)}) collective-permute-start(bf16[8,10368]{1,0:T(8,128)(2,1)} %get-tuple-element.50), channel_id=1, source_target_pairs={{0,4},{1,5},{2,6},{3,7},{4,0},{5,1},{6,2},{7,3},{8,12},{9,13},{10,... | collective-permute-start | bytes 497672 | tf_op jit(solution)/shard_map/ppermute | solution.py:491
  11.6 1.3 %collective-permute-start.4 = (bf16[8,10368]{1,0:T(8,128)(2,1)}, bf16[8,10368]{1,0:T(8,128)(2,1)S(1)}, u32[]{:S(2)}, u32[]{:S(2)}) collective-permute-start(bf16[8,10368]{1,0:T(8,128)(2,1)} %get-tuple-element.51), channel_id=1, source_target_pairs={{0,5},{1,4},{2,7},{3,6},{4,1},{5,0},{6,3},{7,2},{8,13},{9,12},{10,... | collective-permute-start | bytes 497672 | tf_op jit(solution)/shard_map/ppermute | solution.py:491
  13.0 3.6 %hold.1 = (bf16[3584,1024]{1,0:T(8,128)(2,1)S(1)}, bf16[896,1024]{1,0:T(8,128)(2,1)S(1)}) custom-call(bf16[1,3584,1024]{2,1,0:T(8,128)(2,1)} %weight_hbm.1), custom_call_target="tpu_custom_call" | custom-call | tf_op jit(solution)/shard_map/hold/pallas_call | solution.py:464
  16.6 0.0 collective-permute-done.refs_1_
  16.6 3.7 %collective-permute-start.5 = (bf16[8,10368]{1,0:T(8,128)(2,1)S(1)}, bf16[8,10368]{1,0:T(8,128)(2,1)S(1)}, u32[]{:S(2)}, u32[]{:S(2)}) collective-permute-start(bf16[8,10368]{1,0:T(8,128)(2,1)S(1)} %copy-done.6), channel_id=1, source_target_pairs={{0,6},{1,7},{2,4},{3,5},{4,2},{5,3},{6,0},{7,1},{8,14},{9,15},{10,... | collective-permute-start | bytes 497672 | tf_op jit(solution)/shard_map/ppermute | solution.py:491
  20.3 4.8 %collective-permute-done.1.refs_2_ = bf16[16,10368]{1,0:T(8,128)(2,1)S(1)} collective-permute-done((bf16[16,10368]{1,0:T(8,128)(2,1)}, bf16[16,10368]{1,0:T(8,128)(2,1)S(1)}, u32[]{:S(2)}, u32[]{:S(2)}) %collective-permute-start.1) | collective-permute-done | bytes 331808 | tf_op jit(solution)/shard_map/ppermute | solution.py:491
  25.1 3.6 %collective-permute-start.6 = (bf16[8,10368]{1,0:T(8,128)(2,1)S(1)}, bf16[8,10368]{1,0:T(8,128)(2,1)S(1)}, u32[]{:S(2)}, u32[]{:S(2)}) collective-permute-start(bf16[8,10368]{1,0:T(8,128)(2,1)S(1)} %copy-done.5), channel_id=1, source_target_pairs={{0,7},{1,6},{2,5},{3,4},{4,3},{5,2},{6,1},{7,0},{8,15},{9,14},{10,... | collective-permute-start | bytes 497672 | tf_op jit(solution)/shard_map/ppermute | solution.py:491
  28.7 1.9 %collective-permute-done.2.refs_3_ = bf16[16,10368]{1,0:T(8,128)(2,1)S(1)} collective-permute-done((bf16[16,10368]{1,0:T(8,128)(2,1)}, bf16[16,10368]{1,0:T(8,128)(2,1)S(1)}, u32[]{:S(2)}, u32[]{:S(2)}) %collective-permute-start.2) | collective-permute-done | bytes 331808 | tf_op jit(solution)/shard_map/ppermute | solution.py:491
  30.5 0.2 near_columns.1
  30.8 0.1 collective-permute-start.7
  30.8 0.0 collective-permute-done.3.refs_0_
  30.8 1.8 %collective-permute-start.8 = (bf16[72,896]{1,0:T(8,128)(2,1)S(1)}, bf16[72,896]{1,0:T(8,128)(2,1)S(1)}, u32[]{:S(2)}, u32[]{:S(2)}) collective-permute-start(bf16[72,896]{1,0:T(8,128)(2,1)S(1)} %get-tuple-element.55), channel_id=1, source_target_pairs={{16,0},{24,8},{0,16},{8,24},{17,1},{25,9},{1,17},{9,25},{18,2},{26... | collective-permute-start | bytes 387080 | tf_op jit(solution)/shard_map/ppermute | solution.py:508
  32.6 0.0 collective-permute-done.4.refs_1_
  32.6 0.1 collective-permute-start.9
  32.7 4.7 %near_rows.1 = (bf16[32,10368]{1,0:T(8,128)(2,1)S(1)}, bf16[32,10368]{1,0:T(8,128)(2,1)S(1)}, bf16[32,2304]{1,0:T(8,128)(2,1)S(1)}, bf16[72,2048]{1,0:T(8,128)(2,1)S(1)}, bf16[72,3584]{1,0:T(8,128)(2,1)S(1)}) custom-call(s32[8]{0:T(128)S(1)} %copy-done.2, bf16[3584,1024]{1,0:T(8,128)(2,1)S(1)} %get-tuple-element.41.weight_ref, ...), custom_call_target="tpu_custom_call" | custom-call | flops 2113929216 | bytes 11081760 | tf_op jit(solution)/shard_map/near_rows/pallas_call | solution.py:464
  37.4 0.5 collective-permute-done.5.refs_2_
  37.9 2.1 %collective-permute-done.6.refs_3_ = bf16[8,10368]{1,0:T(8,128)(2,1)S(1)} collective-permute-done((bf16[8,10368]{1,0:T(8,128)(2,1)S(1)}, bf16[8,10368]{1,0:T(8,128)(2,1)S(1)}, u32[]{:S(2)}, u32[]{:S(2)}) %collective-permute-start.6) | collective-permute-done | bytes 165920 | tf_op jit(solution)/shard_map/ppermute | solution.py:491
  39.9 0.0 collective-permute-done.7.refs_5_.refs_1_
  40.0 2.4 %payload.1 = (bf16[32,10368]{1,0:T(8,128)(2,1)S(1)}, bf16[72,6656]{1,0:T(8,128)(2,1)S(1)}, bf16[72,6656]{1,0:T(8,128)(2,1)S(1)}) custom-call(s32[8]{0:T(128)S(1)} %copy-done.2, bf16[3584,1024]{1,0:T(8,128)(2,1)S(1)} %get-tuple-element.41.weight_ref, bf16[32,2304]{1,0:T(8,128)(2,1)S(1)} %get-tuple-element.47.folded_grad, ...), custom_call_target="tpu_custom_call" | custom-call | flops 1056964608 | bytes 12058656 | tf_op jit(solution)/shard_map/payload/pallas_call | solution.py:464
  42.4 0.1 collective-permute-start.11
  42.5 1.6 %collective-permute-start.18 = (bf16[72,6656]{1,0:T(8,128)(2,1)S(1)}, bf16[72,6656]{1,0:T(8,128)(2,1)S(1)}, u32[]{:S(2)}, u32[]{:S(2)}) collective-permute-start(bf16[72,6656]{1,0:T(8,128)(2,1)S(1)} %get-tuple-element.73), channel_id=1, source_target_pairs={{16,0},{24,8},{0,16},{8,24},{17,1},{25,9},{1,17},{9,25},{18,2},{26... | collective-permute-start | bytes 2875400 | tf_op jit(solution)/shard_map/ppermute | solution.py:508
  44.1 0.9 collective-permute-done.11.refs_0_.refs_5_
  45.0 4.0 %collective-permute-start.12 = (bf16[8,10368]{1,0:T(8,128)(2,1)S(1)}, bf16[8,10368]{1,0:T(8,128)(2,1)S(1)}, u32[]{:S(2)}, u32[]{:S(2)}) collective-permute-start(bf16[8,10368]{1,0:T(8,128)(2,1)S(1)} %get-tuple-element.62), channel_id=1, source_target_pairs={{1,0},{0,1},{3,2},{2,3},{5,4},{4,5},{7,6},{6,7},{9,8},{8,9},{11,10... | collective-permute-start | bytes 497672 | tf_op jit(solution)/shard_map/ppermute | solution.py:498
  49.0 0.5 collective-permute-start.13
  49.5 1.1 collective-permute-start.14
  50.6 6.5 %collective-permute-start.10 = (bf16[32,10368]{1,0:T(8,128)(2,1)S(1)}, bf16[32,10368]{1,0:T(8,128)(2,1)S(1)}, u32[]{:S(2)}, u32[]{:S(2)}) collective-permute-start(bf16[32,10368]{1,0:T(8,128)(2,1)S(1)} %get-tuple-element.57), channel_id=1, source_target_pairs={{0,4},{1,5},{2,6},{3,7},{4,0},{5,1},{6,2},{7,3},{8,12},{9,13},{10,... | collective-permute-start | bytes 1990664 | tf_op jit(solution)/shard_map/ppermute | solution.py:502
  57.1 9.0 %collective-permute-done.18.refs_0_.refs_6_ = bf16[72,6656]{1,0:T(8,128)(2,1)S(1)} collective-permute-done((bf16[72,6656]{1,0:T(8,128)(2,1)S(1)}, bf16[72,6656]{1,0:T(8,128)(2,1)S(1)}, u32[]{:S(2)}, u32[]{:S(2)}) %collective-permute-start.18) | collective-permute-done | bytes 958496 | tf_op jit(solution)/shard_map/ppermute | solution.py:508
  66.1 0.1 relay.1
  66.2 0.1 collective-permute-start.19
  66.3 1.7 %near_results.1 = (bf16[128,1024]{1,0:T(8,128)(2,1)S(1)}, bf16[128,3584]{1,0:T(8,128)(2,1)S(1)}) custom-call(s32[1,128]{1,0:T(1,128)S(1)} %bitcast.3, f32[1,128]{1,0:T(1,128)S(1)} %bitcast.6, bf16[8,10368]{1,0:T(8,128)(2,1)S(1)} %get-tuple-element.61.refs_0_, bf16[8,10368]{1,0:T(8,128)(2,1)S(1)} %collective-permute-done.12.refs_1_, ...), custom_call_target="tpu_custom_call" | custom-call | tf_op jit(solution)/shard_map/near_results/pallas_call | solution.py:464
  68.0 0.0 copy-start
  68.1 18.1 %collective-permute-done.10.payload.payload_hbm = bf16[32,10368]{1,0:T(8,128)(2,1)S(1)} collective-permute-done((bf16[32,10368]{1,0:T(8,128)(2,1)S(1)}, bf16[32,10368]{1,0:T(8,128)(2,1)S(1)}, u32[]{:S(2)}, u32[]{:S(2)}) %collective-permute-start.10) | collective-permute-done | bytes 663584 | tf_op jit(solution)/shard_map/ppermute | solution.py:502
  86.2 0.9 after_swap.1
  87.1 1.4 %collective-permute-start.15 = (bf16[8,10368]{1,0:T(8,128)(2,1)S(1)}, bf16[8,10368]{1,0:T(8,128)(2,1)S(1)}, u32[]{:S(2)}, u32[]{:S(2)}) collective-permute-start(bf16[8,10368]{1,0:T(8,128)(2,1)S(1)} %get-tuple-element.67), channel_id=1, source_target_pairs={{1,0},{0,1},{3,2},{2,3},{5,4},{4,5},{7,6},{6,7},{9,8},{8,9},{11,10... | collective-permute-start | bytes 497672 | tf_op jit(solution)/shard_map/ppermute | solution.py:498
  88.5 1.5 %collective-permute-start.21 = (bf16[72,1024]{1,0:T(8,128)(2,1)S(1)}, bf16[72,1024]{1,0:T(8,128)(2,1)S(1)}, u32[]{:S(2)}, u32[]{:S(2)}) collective-permute-start(bf16[72,1024]{1,0:T(8,128)(2,1)S(1)} %get-tuple-element.75.refs_0_), channel_id=1, source_target_pairs={{16,0},{24,8},{0,16},{8,24},{17,1},{25,9},{1,17},{9,25},{18,2},{26... | collective-permute-start | bytes 442376 | tf_op jit(solution)/shard_map/ppermute | solution.py:508
  90.0 0.7 collective-permute-start.16
  90.8 1.3 %collective-permute-start.17 = (bf16[8,10368]{1,0:T(8,128)(2,1)S(1)}, bf16[8,10368]{1,0:T(8,128)(2,1)S(1)}, u32[]{:S(2)}, u32[]{:S(2)}) collective-permute-start(bf16[8,10368]{1,0:T(8,128)(2,1)S(1)} %get-tuple-element.69), channel_id=1, source_target_pairs={{3,0},{2,1},{1,2},{0,3},{7,4},{6,5},{5,6},{4,7},{11,8},{10,9},{9,1... | collective-permute-start | bytes 497672 | tf_op jit(solution)/shard_map/ppermute | solution.py:498
  92.1 1.6 %collective-permute-done.21.refs_2_ = bf16[72,1024]{1,0:T(8,128)(2,1)S(1)} collective-permute-done((bf16[72,1024]{1,0:T(8,128)(2,1)S(1)}, bf16[72,1024]{1,0:T(8,128)(2,1)S(1)}, u32[]{:S(2)}, u32[]{:S(2)}) %collective-permute-start.21) | collective-permute-done | bytes 147488 | tf_op jit(solution)/shard_map/ppermute | solution.py:508
  93.7 0.5 collective-permute-start.22
  94.2 2.4 %collective-permute-done.16.refs_2_ = bf16[8,10368]{1,0:T(8,128)(2,1)S(1)} collective-permute-done((bf16[8,10368]{1,0:T(8,128)(2,1)S(1)}, bf16[8,10368]{1,0:T(8,128)(2,1)S(1)}, u32[]{:S(2)}, u32[]{:S(2)}) %collective-permute-start.16) | collective-permute-done | bytes 165920 | tf_op jit(solution)/shard_map/ppermute | solution.py:498
  96.6 2.2 %collective-permute-done.17.refs_3_ = bf16[8,10368]{1,0:T(8,128)(2,1)S(1)} collective-permute-done((bf16[8,10368]{1,0:T(8,128)(2,1)S(1)}, bf16[8,10368]{1,0:T(8,128)(2,1)S(1)}, u32[]{:S(2)}, u32[]{:S(2)}) %collective-permute-start.17) | collective-permute-done | bytes 165920 | tf_op jit(solution)/shard_map/ppermute | solution.py:498
  98.8 2.6 %far_results.1 = (bf16[128,1024]{1,0:T(8,128)(2,1)}, bf16[128,3584]{1,0:T(8,128)(2,1)}) custom-call(s32[1,128]{1,0:T(1,128)S(1)} %bitcast.4, f32[1,128]{1,0:T(1,128)S(1)} %bitcast.7, bf16[8,10368]{1,0:T(8,128)(2,1)S(1)} %get-tuple-element.66.refs_0_, bf16[8,10368]{1,0:T(8,128)(2,1)S(1)} %collective-permute-done.15.refs_1_, ...), custom_call_target="tpu_custom_call" | custom-call | tf_op jit(solution)/shard_map/far_results/pallas_call | solution.py:464
  101.4 2.5 %own_terms.1.total = f32[896,1024]{1,0:T(8,128)S(1)} custom-call(bf16[1,896,1024]{2,1,0:T(8,128)(2,1)S(1)} %copy-done, bf16[72,896]{1,0:T(8,128)(2,1)S(1)} %get-tuple-element.46.refs_4_.refs_0_, bf16[72,896]{1,0:T(8,128)(2,1)S(1)} %collective-permute-done.7.refs_5_.refs_1_, bf16[72,896]{1,0:T(8,128)(2,1)S(1)} %collective-permute-done.8.refs_6_.refs_2_, ...), custom_call_target="tpu_custom_call" | custom-call | tf_op jit(solution)/shard_map/own_terms/pallas_call | solution.py:464
  103.9 3.9 %update.1 = (bf16[1,896,1024]{2,1,0:T(8,128)(2,1)}, bf16[1,896,1024]{2,1,0:T(8,128)(2,1)}) custom-call(s32[8]{0:T(128)S(1)} %copy-done.2, f32[896,1024]{1,0:T(8,128)S(1)} %own_terms.1.total, bf16[896,1024]{1,0:T(8,128)(2,1)S(1)} %get-tuple-element.74.old_weight, bf16[32,10368]{1,0:T(8,128)(2,1)S(1)} %collective-permute-done.10.payload.payload_hbm, ...), custom_call_target="tpu_custom_call" | custom-call | flops 528482304 | bytes 11010048 | tf_op jit(solution)/shard_map/update/pallas_call | solution.py:663
  (24 shorter events, 0.1 us)
Async XLA Ops:
  4.0 12.5 %collective-permute-start = (bf16[16,10368]{1,0:T(8,128)(2,1)}, bf16[16,10368]{1,0:T(8,128)(2,1)S(1)}, u32[]{:S(2)}, u32[]{:S(2)}) collective-permute-start(bf16[16,10368]{1,0:T(8,128)(2,1)} %get-tuple-element.43), channel_id=1, source_target_pairs={{0,1},{1,0},{2,3},{3,2},{4,5},{5,4},{6,7},{7,6},{8,9},{9,8},{10,11... | collective-permute-start | bytes 995336 | tf_op jit(solution)/shard_map/ppermute | solution.py:491
  7.1 18.0 %collective-permute-start.1 = (bf16[16,10368]{1,0:T(8,128)(2,1)}, bf16[16,10368]{1,0:T(8,128)(2,1)S(1)}, u32[]{:S(2)}, u32[]{:S(2)}) collective-permute-start(bf16[16,10368]{1,0:T(8,128)(2,1)} %get-tuple-element.44), channel_id=1, source_target_pairs={{0,2},{1,3},{2,0},{3,1},{4,6},{5,7},{6,4},{7,5},{8,10},{9,11},{10,... | collective-permute-start | bytes 995336 | tf_op jit(solution)/shard_map/ppermute | solution.py:491
  8.6 21.9 %collective-permute-start.2 = (bf16[16,10368]{1,0:T(8,128)(2,1)}, bf16[16,10368]{1,0:T(8,128)(2,1)S(1)}, u32[]{:S(2)}, u32[]{:S(2)}) collective-permute-start(bf16[16,10368]{1,0:T(8,128)(2,1)} %get-tuple-element.45), channel_id=1, source_target_pairs={{0,3},{1,2},{2,1},{3,0},{4,7},{5,6},{6,5},{7,4},{8,11},{9,10},{10,... | collective-permute-start | bytes 995336 | tf_op jit(solution)/shard_map/ppermute | solution.py:491
  8.6 22.2 %collective-permute-start.3 = (bf16[8,10368]{1,0:T(8,128)(2,1)}, bf16[8,10368]{1,0:T(8,128)(2,1)S(1)}, u32[]{:S(2)}, u32[]{:S(2)}) collective-permute-start(bf16[8,10368]{1,0:T(8,128)(2,1)} %get-tuple-element.50), channel_id=1, source_target_pairs={{0,4},{1,5},{2,6},{3,7},{4,0},{5,1},{6,2},{7,3},{8,12},{9,13},{10,... | collective-permute-start | bytes 497672 | tf_op jit(solution)/shard_map/ppermute | solution.py:491
  11.6 5.0 %copy-start.6 = (bf16[8,10368]{1,0:T(8,128)(2,1)S(1)}, bf16[8,10368]{1,0:T(8,128)(2,1)}, u32[]{:S(2)}) copy-start(bf16[8,10368]{1,0:T(8,128)(2,1)} %get-tuple-element.52) | copy-start | bytes 497668
  11.6 13.5 %copy-start.5 = (bf16[8,10368]{1,0:T(8,128)(2,1)S(1)}, bf16[8,10368]{1,0:T(8,128)(2,1)}, u32[]{:S(2)}) copy-start(bf16[8,10368]{1,0:T(8,128)(2,1)} %get-tuple-element.53) | copy-start | bytes 497668
  11.6 18.9 %copy-start.1 = (bf16[16,10368]{1,0:T(8,128)(2,1)S(1)}, bf16[16,10368]{1,0:T(8,128)(2,1)}, u32[]{:S(2)}) copy-start(bf16[16,10368]{1,0:T(8,128)(2,1)} %get-tuple-element.42.refs_0_) | copy-start | bytes 995332
  11.6 21.1 %copy-start.2 = (s32[8]{0:T(128)S(1)}, s32[8]{0:T(128)}, u32[]{:S(2)}) copy-start(s32[8]{0:T(128)} %placement_ref.7) | copy-start | bytes 100
  11.6 21.0 %collective-permute-start.4 = (bf16[8,10368]{1,0:T(8,128)(2,1)}, bf16[8,10368]{1,0:T(8,128)(2,1)S(1)}, u32[]{:S(2)}, u32[]{:S(2)}) collective-permute-start(bf16[8,10368]{1,0:T(8,128)(2,1)} %get-tuple-element.51), channel_id=1, source_target_pairs={{0,5},{1,4},{2,7},{3,6},{4,1},{5,0},{6,3},{7,2},{8,13},{9,12},{10,... | collective-permute-start | bytes 497672 | tf_op jit(solution)/shard_map/ppermute | solution.py:491
  16.6 21.3 %collective-permute-start.5 = (bf16[8,10368]{1,0:T(8,128)(2,1)S(1)}, bf16[8,10368]{1,0:T(8,128)(2,1)S(1)}, u32[]{:S(2)}, u32[]{:S(2)}) collective-permute-start(bf16[8,10368]{1,0:T(8,128)(2,1)S(1)} %copy-done.6), channel_id=1, source_target_pairs={{0,6},{1,7},{2,4},{3,5},{4,2},{5,3},{6,0},{7,1},{8,14},{9,15},{10,... | collective-permute-start | bytes 497672 | tf_op jit(solution)/shard_map/ppermute | solution.py:491
  25.1 14.8 %collective-permute-start.6 = (bf16[8,10368]{1,0:T(8,128)(2,1)S(1)}, bf16[8,10368]{1,0:T(8,128)(2,1)S(1)}, u32[]{:S(2)}, u32[]{:S(2)}) collective-permute-start(bf16[8,10368]{1,0:T(8,128)(2,1)S(1)} %copy-done.5), channel_id=1, source_target_pairs={{0,7},{1,6},{2,5},{3,4},{4,3},{5,2},{6,1},{7,0},{8,15},{9,14},{10,... | collective-permute-start | bytes 497672 | tf_op jit(solution)/shard_map/ppermute | solution.py:491
  30.8 9.2 %collective-permute-start.7 = (bf16[72,896]{1,0:T(8,128)(2,1)S(1)}, bf16[72,896]{1,0:T(8,128)(2,1)S(1)}, u32[]{:S(2)}, u32[]{:S(2)}) collective-permute-start(bf16[72,896]{1,0:T(8,128)(2,1)S(1)} %get-tuple-element.54), channel_id=1, source_target_pairs={{8,0},{0,8},{24,16},{16,24},{9,1},{1,9},{25,17},{17,25},{10,2},{2,... | collective-permute-start | bytes 387080 | tf_op jit(solution)/shard_map/ppermute | solution.py:508
  30.8 9.1 %collective-permute-start.8 = (bf16[72,896]{1,0:T(8,128)(2,1)S(1)}, bf16[72,896]{1,0:T(8,128)(2,1)S(1)}, u32[]{:S(2)}, u32[]{:S(2)}) collective-permute-start(bf16[72,896]{1,0:T(8,128)(2,1)S(1)} %get-tuple-element.55), channel_id=1, source_target_pairs={{16,0},{24,8},{0,16},{8,24},{17,1},{25,9},{1,17},{9,25},{18,2},{26... | collective-permute-start | bytes 387080 | tf_op jit(solution)/shard_map/ppermute | solution.py:508
  32.6 7.3 %collective-permute-start.9 = (bf16[72,896]{1,0:T(8,128)(2,1)S(1)}, bf16[72,896]{1,0:T(8,128)(2,1)S(1)}, u32[]{:S(2)}, u32[]{:S(2)}) collective-permute-start(bf16[72,896]{1,0:T(8,128)(2,1)S(1)} %get-tuple-element.56), channel_id=1, source_target_pairs={{24,0},{16,8},{8,16},{0,24},{25,1},{17,9},{9,17},{1,25},{26,2},{18... | collective-permute-start | bytes 387080 | tf_op jit(solution)/shard_map/ppermute | solution.py:508
  42.4 2.6 %collective-permute-start.11 = (bf16[72,6656]{1,0:T(8,128)(2,1)S(1)}, bf16[72,6656]{1,0:T(8,128)(2,1)S(1)}, u32[]{:S(2)}, u32[]{:S(2)}) collective-permute-start(bf16[72,6656]{1,0:T(8,128)(2,1)S(1)} %get-tuple-element.60.refs_4_), channel_id=1, source_target_pairs={{8,0},{0,8},{24,16},{16,24},{9,1},{1,9},{25,17},{17,25},{10,2},{2,... | collective-permute-start | bytes 2875400 | tf_op jit(solution)/shard_map/ppermute | solution.py:508
  42.5 23.6 %collective-permute-start.18 = (bf16[72,6656]{1,0:T(8,128)(2,1)S(1)}, bf16[72,6656]{1,0:T(8,128)(2,1)S(1)}, u32[]{:S(2)}, u32[]{:S(2)}) collective-permute-start(bf16[72,6656]{1,0:T(8,128)(2,1)S(1)} %get-tuple-element.73), channel_id=1, source_target_pairs={{16,0},{24,8},{0,16},{8,24},{17,1},{25,9},{1,17},{9,25},{18,2},{26... | collective-permute-start | bytes 2875400 | tf_op jit(solution)/shard_map/ppermute | solution.py:508
  45.0 21.3 %copy-start.3 = (s32[128]{0:T(128)S(1)}, s32[128]{0:T(128)}, u32[]{:S(2)}) copy-start(s32[128]{0:T(128)} %param.10) | copy-start | bytes 1540
  45.0 21.3 %copy-start.4 = (f32[128]{0:T(128)S(1)}, f32[128]{0:T(128)}, u32[]{:S(2)}) copy-start(f32[128]{0:T(128)} %param.8) | copy-start | bytes 1540
  45.0 21.1 %collective-permute-start.12 = (bf16[8,10368]{1,0:T(8,128)(2,1)S(1)}, bf16[8,10368]{1,0:T(8,128)(2,1)S(1)}, u32[]{:S(2)}, u32[]{:S(2)}) collective-permute-start(bf16[8,10368]{1,0:T(8,128)(2,1)S(1)} %get-tuple-element.62), channel_id=1, source_target_pairs={{1,0},{0,1},{3,2},{2,3},{5,4},{4,5},{7,6},{6,7},{9,8},{8,9},{11,10... | collective-permute-start | bytes 497672 | tf_op jit(solution)/shard_map/ppermute | solution.py:498
  49.0 17.1 %collective-permute-start.13 = (bf16[8,10368]{1,0:T(8,128)(2,1)S(1)}, bf16[8,10368]{1,0:T(8,128)(2,1)S(1)}, u32[]{:S(2)}, u32[]{:S(2)}) collective-permute-start(bf16[8,10368]{1,0:T(8,128)(2,1)S(1)} %get-tuple-element.63), channel_id=1, source_target_pairs={{2,0},{3,1},{0,2},{1,3},{6,4},{7,5},{4,6},{5,7},{10,8},{11,9},{8,1... | collective-permute-start | bytes 497672 | tf_op jit(solution)/shard_map/ppermute | solution.py:498
  49.5 16.6 %collective-permute-start.14 = (bf16[8,10368]{1,0:T(8,128)(2,1)S(1)}, bf16[8,10368]{1,0:T(8,128)(2,1)S(1)}, u32[]{:S(2)}, u32[]{:S(2)}) collective-permute-start(bf16[8,10368]{1,0:T(8,128)(2,1)S(1)} %get-tuple-element.64), channel_id=1, source_target_pairs={{3,0},{2,1},{1,2},{0,3},{7,4},{6,5},{5,6},{4,7},{11,8},{10,9},{9,1... | collective-permute-start | bytes 497672 | tf_op jit(solution)/shard_map/ppermute | solution.py:498
  50.6 35.6 %collective-permute-start.10 = (bf16[32,10368]{1,0:T(8,128)(2,1)S(1)}, bf16[32,10368]{1,0:T(8,128)(2,1)S(1)}, u32[]{:S(2)}, u32[]{:S(2)}) collective-permute-start(bf16[32,10368]{1,0:T(8,128)(2,1)S(1)} %get-tuple-element.57), channel_id=1, source_target_pairs={{0,4},{1,5},{2,6},{3,7},{4,0},{5,1},{6,2},{7,3},{8,12},{9,13},{10,... | collective-permute-start | bytes 1990664 | tf_op jit(solution)/shard_map/ppermute | solution.py:502
  66.2 35.2 %collective-permute-start.19 = (bf16[72,6656]{1,0:T(8,128)(2,1)S(1)}, bf16[72,6656]{1,0:T(8,128)(2,1)S(1)}, u32[]{:S(2)}, u32[]{:S(2)}) collective-permute-start(bf16[72,6656]{1,0:T(8,128)(2,1)S(1)} %relay.1), channel_id=1, source_target_pairs={{8,0},{0,8},{24,16},{16,24},{9,1},{1,9},{25,17},{17,25},{10,2},{2,... | collective-permute-start | bytes 2875400 | tf_op jit(solution)/shard_map/ppermute | solution.py:508
  68.0 33.4 %copy-start = (bf16[1,896,1024]{2,1,0:T(8,128)(2,1)S(1)}, bf16[1,896,1024]{2,1,0:T(8,128)(2,1)}, u32[]{:S(2)}) copy-start(bf16[1,896,1024]{2,1,0:T(8,128)(2,1)} %momentum_hbm.1) | copy-start | bytes 5505028
  87.1 6.6 %collective-permute-start.15 = (bf16[8,10368]{1,0:T(8,128)(2,1)S(1)}, bf16[8,10368]{1,0:T(8,128)(2,1)S(1)}, u32[]{:S(2)}, u32[]{:S(2)}) collective-permute-start(bf16[8,10368]{1,0:T(8,128)(2,1)S(1)} %get-tuple-element.67), channel_id=1, source_target_pairs={{1,0},{0,1},{3,2},{2,3},{5,4},{4,5},{7,6},{6,7},{9,8},{8,9},{11,10... | collective-permute-start | bytes 497672 | tf_op jit(solution)/shard_map/ppermute | solution.py:498
  88.5 5.1 %collective-permute-start.21 = (bf16[72,1024]{1,0:T(8,128)(2,1)S(1)}, bf16[72,1024]{1,0:T(8,128)(2,1)S(1)}, u32[]{:S(2)}, u32[]{:S(2)}) collective-permute-start(bf16[72,1024]{1,0:T(8,128)(2,1)S(1)} %get-tuple-element.75.refs_0_), channel_id=1, source_target_pairs={{16,0},{24,8},{0,16},{8,24},{17,1},{25,9},{1,17},{9,25},{18,2},{26... | collective-permute-start | bytes 442376 | tf_op jit(solution)/shard_map/ppermute | solution.py:508
  90.0 6.5 %collective-permute-start.16 = (bf16[8,10368]{1,0:T(8,128)(2,1)S(1)}, bf16[8,10368]{1,0:T(8,128)(2,1)S(1)}, u32[]{:S(2)}, u32[]{:S(2)}) collective-permute-start(bf16[8,10368]{1,0:T(8,128)(2,1)S(1)} %get-tuple-element.68), channel_id=1, source_target_pairs={{2,0},{3,1},{0,2},{1,3},{6,4},{7,5},{4,6},{5,7},{10,8},{11,9},{8,1... | collective-permute-start | bytes 497672 | tf_op jit(solution)/shard_map/ppermute | solution.py:498
  90.8 8.0 %collective-permute-start.17 = (bf16[8,10368]{1,0:T(8,128)(2,1)S(1)}, bf16[8,10368]{1,0:T(8,128)(2,1)S(1)}, u32[]{:S(2)}, u32[]{:S(2)}) collective-permute-start(bf16[8,10368]{1,0:T(8,128)(2,1)S(1)} %get-tuple-element.69), channel_id=1, source_target_pairs={{3,0},{2,1},{1,2},{0,3},{7,4},{6,5},{5,6},{4,7},{11,8},{10,9},{9,1... | collective-permute-start | bytes 497672 | tf_op jit(solution)/shard_map/ppermute | solution.py:498
  93.7 10.3 %collective-permute-start.20 = (bf16[72,1024]{1,0:T(8,128)(2,1)S(1)}, bf16[72,1024]{1,0:T(8,128)(2,1)S(1)}, u32[]{:S(2)}, u32[]{:S(2)}) collective-permute-start(bf16[72,1024]{1,0:T(8,128)(2,1)S(1)} %get-tuple-element.75.refs_0_), channel_id=1, source_target_pairs={{8,0},{0,8},{24,16},{16,24},{9,1},{1,9},{25,17},{17,25},{10,2},{2,... | collective-permute-start | bytes 442376 | tf_op jit(solution)/shard_map/ppermute | solution.py:508
  93.7 10.3 %collective-permute-start.22 = (bf16[72,1024]{1,0:T(8,128)(2,1)S(1)}, bf16[72,1024]{1,0:T(8,128)(2,1)S(1)}, u32[]{:S(2)}, u32[]{:S(2)}) collective-permute-start(bf16[72,1024]{1,0:T(8,128)(2,1)S(1)} %collective-permute-done.21.refs_2_), channel_id=1, source_target_pairs={{8,0},{0,8},{24,16},{16,24},{9,1},{1,9},{25,17},{17,25},{10,2},{2,... | collective-permute-start | bytes 442376 | tf_op jit(solution)/shard_map/ppermute | solution.py:508

commit v11 on v9

--- a/solution.py
+++ b/solution.py
@@ -27,6 +27,7 @@
         self.full, self.rest = divmod(self.cap, SUB)
         self.cuts = SUB // self.rest if self.rest else 1
         self.rows = self.half * self.cap
+        self.far_order = [*range(0, self.half, 2), *range(1, self.half, 2)]
         self.share = features // groups
         self.DX = features * self.cap // SUB
         self.FG = hidden * self.cap // SUB
@@ -287,7 +288,7 @@
     plan, placement_ref, weight_ref, folded_grad, near_grads, far_rows, *refs
 ):
     half, groups = plan.half, plan.groups
-    far, refs = refs[:half], refs[half:]
+    far, refs = [refs[plan.far_order.index(m)] for m in range(half)], refs[half:]
     columns, refs = refs[:groups], refs[groups:]
     payload, refs = refs[0], refs[1:]
     shared, rows = refs[:groups], refs[groups]
@@ -409,40 +410,30 @@
         total[span, :] = before + dot_tn(x_all[:, span], g_all)
 
 
-def update_kernel(plan, placement_ref, payload_hbm, *refs):
+def update_kernel(plan, placement_ref, total, old_weight, payload_hbm, *refs):
     groups, share = plan.groups, plan.share
     other_hbm, refs = refs[:groups], refs[groups:]
-    total_hbm, weight_hbm, new_weight, new_momentum, payload, other_g = refs[:6]
-    total, weight, momentum, sems, tile_sems, out_sems = refs[6:]
-    first = [pltpu.make_async_copy(payload_hbm, payload, sems.at[groups])]
+    new_weight, new_momentum, payload, other_g, weight, momentum, sems, out_sems = refs
+    copies = [pltpu.make_async_copy(payload_hbm, payload, sems.at[groups])]
     for m in range(groups):
-        first.append(pltpu.make_async_copy(other_hbm[m], other_g.at[m], sems.at[m]))
-    spans = [pl.ds(i * LANES, LANES) for i in range(share // LANES)]
-    tiles = [
-        [
-            pltpu.make_async_copy(source.at[span, :], target.at[span, :], tile_sems.at[i, j])
-            for j, (source, target) in enumerate(((total_hbm, total), (weight_hbm, weight)))
-        ]
-        for i, span in enumerate(spans)
-    ]
-    for copy in first + [copy for pair in tiles for copy in pair]:
+        copies.append(pltpu.make_async_copy(other_hbm[m], other_g.at[m], sems.at[m]))
+    for copy in copies:
         copy.start()
     hot = is_hot(plan, placement_ref)
-    for copy in first:
+    for copy in copies:
         copy.wait()
     pieces = [payload[:, i * share : (i + 1) * share] for i in range(plan.pieces)]
     x = jnp.concatenate(pieces, axis=0)
     x = jnp.where(hot, x.astype(F32), 0.0).astype(BF16)
     g = rows_of([other_g[m] for m in range(groups)])
     done = []
-    for i, span in enumerate(spans):
-        for copy in tiles[i]:
-            copy.wait()
+    for i in range(share // LANES):
+        span = pl.ds(i * LANES, LANES)
         value = total[span, :] + dot_tn(x[:, i * LANES : (i + 1) * LANES], g)
         value = value.astype(BF16)
         momentum[span, :] = value
         weight[span, :] = (
-            weight[span, :].astype(F32) - learning_rate * value.astype(F32)
+            old_weight[span, :].astype(F32) - learning_rate * value.astype(F32)
         ).astype(BF16)
         for j, (source, target) in enumerate(((momentum, new_momentum), (weight, new_weight))):
             copy = pltpu.make_async_copy(
@@ -582,7 +573,9 @@
     outs = call(
         payload_kernel,
         plan,
-        [placement, held, folded_grad, grads, far_rows] + far + columns_here,
+        [placement, held, folded_grad, grads, far_rows]
+        + [far[m] for m in plan.far_order]
+        + columns_here,
         [SMEM_SPEC] + [VMEM_SPEC] * (4 + half + groups),
         [(half * SUB, C)] + [(rows, 2 * share + 3 * F)] * groups,
         [pltpu.VMEM((rows, D), BF16)],
@@ -649,16 +642,14 @@
     new_weight, new_momentum = pl.pallas_call(
         functools.partial(update_kernel, plan),
         out_shape=[jax.ShapeDtypeStruct((1, share, F), BF16)] * 2,
-        in_specs=[SMEM_SPEC] + [ANY_SPEC] * (groups + 3),
+        in_specs=[SMEM_SPEC] + [VMEM_SPEC] * 2 + [ANY_SPEC] * (groups + 1),
         out_specs=[ANY_SPEC] * 2,
         scratch_shapes=[
             pltpu.VMEM((half * SUB, C), BF16),
             pltpu.VMEM((groups, rows, F), BF16),
-            pltpu.VMEM((share, F), F32),
             pltpu.VMEM((share, F), BF16),
             pltpu.VMEM((share, F), BF16),
             pltpu.SemaphoreType.DMA((groups + 1,)),
-            pltpu.SemaphoreType.DMA((share // LANES, 2)),
             pltpu.SemaphoreType.DMA((share // LANES, 2)),
         ],
         compiler_params=pltpu.CompilerParams(vmem_limit_bytes=20 * MIB),
@@ -666,7 +657,7 @@
             flops=2 * groups * rows * share * F, bytes_accessed=12 * share * F, transcendentals=0
         ),
         name="update",
-    )(placement, payload, *other_g, total, old_weight)
+    )(placement, total, old_weight, payload, *other_g)
 
     expert_out, token_grad = place(1, late, placed, "far_results")
     return expert_out, token_grad, new_weight, new_momentum

time: 102 us -> 98.2 us (0.963); the launches traced: 100 us -> 98 us
  starting transfers between devices: 43.5 us -> 32.9 us
  waiting for transfers between devices: 28.1 us -> 38 us
  Pallas kernels: 27.8 us -> 26.1 us
    ppermute x6, starting transfers between devices: 17.4 us -> 9.02 us  [to_source(): return lax.ppermute(data, 'expert', pairs)]
    ppermute x1, waiting for transfers between devices: 18.8 us -> 23.3 us  [to_partner(): return lax.ppermute(data, 'expert', pairs)]
    ppermute x6, waiting for transfers between devices: 0.02 us -> 2.15 us  [to_source(): return lax.ppermute(data, 'expert', pairs)]
    pallas_call x1, Pallas kernels: 5.58 us -> 3.89 us  [routed(): pl.pallas_call(functools.partial(update_kernel, plan), out_shape=[jax.Sha...]
    ppermute x7, waiting for transfers between devices: 9.26 us -> 10.9 us  [to_slot(): return lax.ppermute(data, 'expert', pairs)]
    ppermute x9, waiting for transfers between devices: 0.02 us -> 1.66 us  [from_group(): return lax.ppermute(data, 'dp', pairs)]
    ppermute x1, starting transfers between devices: 3.98 us -> 2.72 us  [to_partner(): return lax.ppermute(data, 'expert', pairs)]
  transfers between devices with their start and end apart: 23 -> 23, of which waited for: 5 -> 7; matrix products, arithmetic and copies ran while one was open for 0% -> 0% of each run, Pallas kernels for 16% -> 17%
where the time goes in v11:
time: 98.2 us; the launch traced here: 98 us
  waiting for transfers between devices  38 us (39%)
  starting transfers between devices  32.9 us (34%)
  Pallas kernels  26.1 us (27%)
    ppermute x1, waiting for transfers between devices, to_partner(): return lax.ppermute(data, 'expert', pairs)  23.3 us
    pallas_call x10, Pallas kernels, call(): pl.pallas_call(functools.partial(kernel, plan), out_shape=[jax.ShapeDtype...  22.2 us
    ppermute x7, starting transfers between devices, to_slot(): return lax.ppermute(data, 'expert', pairs)  15.3 us
    ppermute x7, waiting for transfers between devices, to_slot(): return lax.ppermute(data, 'expert', pairs)  10.9 us
    ppermute x6, starting transfers between devices, to_source(): return lax.ppermute(data, 'expert', pairs)  9.02 us
    ppermute x9, starting transfers between devices, from_group(): return lax.ppermute(data, 'dp', pairs)  5.88 us
    pallas_call x1, Pallas kernels, routed(): pl.pallas_call(functools.partial(update_kernel, plan), out_shape=[jax.Sha...  3.89 us
    ppermute x1, starting transfers between devices, to_partner(): return lax.ppermute(data, 'expert', pairs)  2.72 us
  transfers between devices with their start and end apart: 23, of which 7 were waited for; matrix products, arithmetic and copies ran while one was open for 0% of the time, Pallas kernels for 17%

profile of v11, /device:TPU:0, one launch (start us, length us, event | category | flops | bytes accessed | tf_op | source)
XLA Modules:
  0.0 98.0 jit_solution(14843302350567742394)
XLA Ops:
  0.6 3.4 %pack.1 = (bf16[16,10368]{1,0:T(8,128)(2,1)}, bf16[16,10368]{1,0:T(8,128)(2,1)}, bf16[16,10368]{1,0:T(8,128)(2,1)}, bf16[16,10368]{1,0:T(8,128)(2,1)}, bf16[8,10...) custom-call(s32[1,128]{1,0:T(1,128)} %bitcast.2, ...), custom_call_target="tpu_custom_call" | custom-call | flops 150994944 | bytes 3171328 | tf_op jit(solution)/shard_map/pack/pallas_call | solution.py:456
  4.0 3.0 %collective-permute-start = (bf16[16,10368]{1,0:T(8,128)(2,1)}, bf16[16,10368]{1,0:T(8,128)(2,1)S(1)}, u32[]{:S(2)}, u32[]{:S(2)}) collective-permute-start(bf16[16,10368]{1,0:T(8,128)(2,1)} %get-tuple-element.45), channel_id=1, source_target_pairs={{0,1},{1,0},{2,3},{3,2},{4,5},{5,4},{6,7},{7,6},{8,9},{9,8},{10,11... | collective-permute-start | bytes 995336 | tf_op jit(solution)/shard_map/ppermute | solution.py:483
  7.1 1.6 %collective-permute-start.1 = (bf16[16,10368]{1,0:T(8,128)(2,1)}, bf16[16,10368]{1,0:T(8,128)(2,1)S(1)}, u32[]{:S(2)}, u32[]{:S(2)}) collective-permute-start(bf16[16,10368]{1,0:T(8,128)(2,1)} %get-tuple-element.46), channel_id=1, source_target_pairs={{0,2},{1,3},{2,0},{3,1},{4,6},{5,7},{6,4},{7,5},{8,10},{9,11},{10,... | collective-permute-start | bytes 995336 | tf_op jit(solution)/shard_map/ppermute | solution.py:483
  8.6 0.0 collective-permute-start.2
  8.6 3.0 %collective-permute-start.3 = (bf16[8,10368]{1,0:T(8,128)(2,1)}, bf16[8,10368]{1,0:T(8,128)(2,1)S(1)}, u32[]{:S(2)}, u32[]{:S(2)}) collective-permute-start(bf16[8,10368]{1,0:T(8,128)(2,1)} %get-tuple-element.52), channel_id=1, source_target_pairs={{0,4},{1,5},{2,6},{3,7},{4,0},{5,1},{6,2},{7,3},{8,12},{9,13},{10,... | collective-permute-start | bytes 497672 | tf_op jit(solution)/shard_map/ppermute | solution.py:483
  11.6 1.4 %collective-permute-start.4 = (bf16[8,10368]{1,0:T(8,128)(2,1)}, bf16[8,10368]{1,0:T(8,128)(2,1)S(1)}, u32[]{:S(2)}, u32[]{:S(2)}) collective-permute-start(bf16[8,10368]{1,0:T(8,128)(2,1)} %get-tuple-element.53), channel_id=1, source_target_pairs={{0,6},{1,7},{2,4},{3,5},{4,2},{5,3},{6,0},{7,1},{8,14},{9,15},{10,... | collective-permute-start | bytes 497672 | tf_op jit(solution)/shard_map/ppermute | solution.py:483
  13.1 3.6 %hold.1 = (bf16[3584,1024]{1,0:T(8,128)(2,1)S(1)}, bf16[896,1024]{1,0:T(8,128)(2,1)S(1)}) custom-call(bf16[1,3584,1024]{2,1,0:T(8,128)(2,1)} %weight_hbm.1), custom_call_target="tpu_custom_call" | custom-call | tf_op jit(solution)/shard_map/hold/pallas_call | solution.py:456
  16.7 0.0 collective-permute-done.refs_1_
  16.7 2.7 %collective-permute-start.5 = (bf16[8,10368]{1,0:T(8,128)(2,1)S(1)}, bf16[8,10368]{1,0:T(8,128)(2,1)S(1)}, u32[]{:S(2)}, u32[]{:S(2)}) collective-permute-start(bf16[8,10368]{1,0:T(8,128)(2,1)S(1)} %copy-done.6), channel_id=1, source_target_pairs={{0,5},{1,4},{2,7},{3,6},{4,1},{5,0},{6,3},{7,2},{8,13},{9,12},{10,... | collective-permute-start | bytes 497672 | tf_op jit(solution)/shard_map/ppermute | solution.py:483
  19.4 4.9 %collective-permute-done.1.refs_2_ = bf16[16,10368]{1,0:T(8,128)(2,1)S(1)} collective-permute-done((bf16[16,10368]{1,0:T(8,128)(2,1)}, bf16[16,10368]{1,0:T(8,128)(2,1)S(1)}, u32[]{:S(2)}, u32[]{:S(2)}) %collective-permute-start.1) | collective-permute-done | bytes 331808 | tf_op jit(solution)/shard_map/ppermute | solution.py:483
  24.3 3.6 %collective-permute-start.6 = (bf16[8,10368]{1,0:T(8,128)(2,1)S(1)}, bf16[8,10368]{1,0:T(8,128)(2,1)S(1)}, u32[]{:S(2)}, u32[]{:S(2)}) collective-permute-start(bf16[8,10368]{1,0:T(8,128)(2,1)S(1)} %copy-done.5), channel_id=1, source_target_pairs={{0,7},{1,6},{2,5},{3,4},{4,3},{5,2},{6,1},{7,0},{8,15},{9,14},{10,... | collective-permute-start | bytes 497672 | tf_op jit(solution)/shard_map/ppermute | solution.py:483
  27.9 6.0 %collective-permute-done.2.refs_3_ = bf16[16,10368]{1,0:T(8,128)(2,1)S(1)} collective-permute-done((bf16[16,10368]{1,0:T(8,128)(2,1)}, bf16[16,10368]{1,0:T(8,128)(2,1)S(1)}, u32[]{:S(2)}, u32[]{:S(2)}) %collective-permute-start.2) | collective-permute-done | bytes 331808 | tf_op jit(solution)/shard_map/ppermute | solution.py:483
  33.9 0.2 near_columns.1
  34.1 0.1 collective-permute-start.7
  34.2 0.0 collective-permute-done.3.refs_0_
  34.2 1.9 %collective-permute-start.8 = (bf16[72,896]{1,0:T(8,128)(2,1)S(1)}, bf16[72,896]{1,0:T(8,128)(2,1)S(1)}, u32[]{:S(2)}, u32[]{:S(2)}) collective-permute-start(bf16[72,896]{1,0:T(8,128)(2,1)S(1)} %get-tuple-element.57), channel_id=1, source_target_pairs={{16,0},{24,8},{0,16},{8,24},{17,1},{25,9},{1,17},{9,25},{18,2},{26... | collective-permute-start | bytes 387080 | tf_op jit(solution)/shard_map/ppermute | solution.py:500
  36.1 0.0 collective-permute-done.4.refs_1_
  36.1 0.1 collective-permute-start.9
  36.2 4.7 %near_rows.1 = (bf16[32,10368]{1,0:T(8,128)(2,1)S(1)}, bf16[32,10368]{1,0:T(8,128)(2,1)S(1)}, bf16[32,2304]{1,0:T(8,128)(2,1)S(1)}, bf16[72,2048]{1,0:T(8,128)(2,1)S(1)}, bf16[72,3584]{1,0:T(8,128)(2,1)S(1)}) custom-call(s32[8]{0:T(128)S(1)} %copy-done.2, bf16[3584,1024]{1,0:T(8,128)(2,1)S(1)} %get-tuple-element.43.weight_ref, ...), custom_call_target="tpu_custom_call" | custom-call | flops 2113929216 | bytes 11081760 | tf_op jit(solution)/shard_map/near_rows/pallas_call | solution.py:456
  40.9 0.0 collective-permute-done.7.refs_5_.refs_1_
  40.9 0.0 collective-permute-done.8.refs_6_.refs_2_
  40.9 1.6 %collective-permute-done.9.refs_7_.refs_3_ = bf16[72,896]{1,0:T(8,128)(2,1)S(1)} collective-permute-done((bf16[72,896]{1,0:T(8,128)(2,1)S(1)}, bf16[72,896]{1,0:T(8,128)(2,1)S(1)}, u32[]{:S(2)}, u32[]{:S(2)}) %collective-permute-start.9) | collective-permute-done | bytes 129056 | tf_op jit(solution)/shard_map/ppermute | solution.py:500
  42.6 2.5 %payload.1 = (bf16[32,10368]{1,0:T(8,128)(2,1)S(1)}, bf16[72,4864]{1,0:T(8,128)(2,1)S(1)}, bf16[72,4864]{1,0:T(8,128)(2,1)S(1)}, bf16[72,4864]{1,0:T(8,128)(2,1)S(1)}, bf16[72,4864]{1,0:T(8,128)(2,1)S(1)}) custom-call(s32[8]{0:T(128)S(1)} %copy-done.2, bf16[3584,1024]{1,0:T(8,128)(2,1)S(1)} %get-tuple-element.43.weight_ref, ...), custom_call_target="tpu_custom_call" | custom-call | flops 1056964608 | bytes 12943392 | tf_op jit(solution)/shard_map/payload/pallas_call | solution.py:456
  45.1 0.0 copy-start
  45.1 0.2 collective-permute-start.11
  45.3 2.7 %collective-permute-start.10 = (bf16[32,10368]{1,0:T(8,128)(2,1)S(1)}, bf16[32,10368]{1,0:T(8,128)(2,1)S(1)}, u32[]{:S(2)}, u32[]{:S(2)}) collective-permute-start(bf16[32,10368]{1,0:T(8,128)(2,1)S(1)} %get-tuple-element.59), channel_id=1, source_target_pairs={{0,4},{1,5},{2,6},{3,7},{4,0},{5,1},{6,2},{7,3},{8,12},{9,13},{10,... | collective-permute-start | bytes 1990664 | tf_op jit(solution)/shard_map/ppermute | solution.py:494
  48.0 1.5 %collective-permute-start.18 = (bf16[72,4864]{1,0:T(8,128)(2,1)S(1)}, bf16[72,4864]{1,0:T(8,128)(2,1)S(1)}, u32[]{:S(2)}, u32[]{:S(2)}) collective-permute-start(bf16[72,4864]{1,0:T(8,128)(2,1)S(1)} %get-tuple-element.76), channel_id=1, source_target_pairs={{16,0},{24,8},{0,16},{8,24},{17,1},{25,9},{1,17},{9,25},{18,2},{26... | collective-permute-start | bytes 2101256 | tf_op jit(solution)/shard_map/ppermute | solution.py:500
  49.6 0.3 collective-permute-start.12
  49.9 4.5 %collective-permute-start.13 = (bf16[8,10368]{1,0:T(8,128)(2,1)S(1)}, bf16[8,10368]{1,0:T(8,128)(2,1)S(1)}, u32[]{:S(2)}, u32[]{:S(2)}) collective-permute-start(bf16[8,10368]{1,0:T(8,128)(2,1)S(1)} %get-tuple-element.64), channel_id=1, source_target_pairs={{2,0},{3,1},{0,2},{1,3},{6,4},{7,5},{4,6},{5,7},{10,8},{11,9},{8,1... | collective-permute-start | bytes 497672 | tf_op jit(solution)/shard_map/ppermute | solution.py:490
  54.3 23.3 %collective-permute-done.10.payload.payload_hbm = bf16[32,10368]{1,0:T(8,128)(2,1)S(1)} collective-permute-done((bf16[32,10368]{1,0:T(8,128)(2,1)S(1)}, bf16[32,10368]{1,0:T(8,128)(2,1)S(1)}, u32[]{:S(2)}, u32[]{:S(2)}) %collective-permute-start.10) | collective-permute-done | bytes 663584 | tf_op jit(solution)/shard_map/ppermute | solution.py:494
  77.6 0.3 collective-permute-start.17
  77.9 0.0 collective-permute-done.12.refs_0_.refs_1_
  77.9 0.0 collective-permute-done.13.refs_1_.refs_2_
  77.9 0.9 after_swap.1
  78.8 1.5 %collective-permute-start.21 = (bf16[72,1024]{1,0:T(8,128)(2,1)S(1)}, bf16[72,1024]{1,0:T(8,128)(2,1)S(1)}, u32[]{:S(2)}, u32[]{:S(2)}) collective-permute-start(bf16[72,1024]{1,0:T(8,128)(2,1)S(1)} %get-tuple-element.79.refs_0_), channel_id=1, source_target_pairs={{16,0},{24,8},{0,16},{8,24},{17,1},{25,9},{1,17},{9,25},{18,2},{26... | collective-permute-start | bytes 442376 | tf_op jit(solution)/shard_map/ppermute | solution.py:500
  80.4 1.8 %collective-permute-start.14 = (bf16[8,10368]{1,0:T(8,128)(2,1)S(1)}, bf16[8,10368]{1,0:T(8,128)(2,1)S(1)}, u32[]{:S(2)}, u32[]{:S(2)}) collective-permute-start(bf16[8,10368]{1,0:T(8,128)(2,1)S(1)} %get-tuple-element.66), channel_id=1, source_target_pairs={{1,0},{0,1},{3,2},{2,3},{5,4},{4,5},{7,6},{6,7},{9,8},{8,9},{11,10... | collective-permute-start | bytes 497672 | tf_op jit(solution)/shard_map/ppermute | solution.py:490
  82.2 0.0 collective-permute-done.18.refs_6_
  82.2 1.5 %collective-permute-start.15 = (bf16[8,10368]{1,0:T(8,128)(2,1)S(1)}, bf16[8,10368]{1,0:T(8,128)(2,1)S(1)}, u32[]{:S(2)}, u32[]{:S(2)}) collective-permute-start(bf16[8,10368]{1,0:T(8,128)(2,1)S(1)} %get-tuple-element.67), channel_id=1, source_target_pairs={{2,0},{3,1},{0,2},{1,3},{6,4},{7,5},{4,6},{5,7},{10,8},{11,9},{8,1... | collective-permute-start | bytes 497672 | tf_op jit(solution)/shard_map/ppermute | solution.py:490
  83.7 0.7 collective-permute-start.16
  84.4 0.2 collective-permute-done.17.refs_3_
  84.5 0.0 collective-permute-done.21.refs_2_
  84.5 0.5 collective-permute-start.22
  85.1 2.5 %own_terms.1.total = f32[896,1024]{1,0:T(8,128)S(1)} custom-call(bf16[1,896,1024]{2,1,0:T(8,128)(2,1)S(1)} %copy-done, bf16[72,896]{1,0:T(8,128)(2,1)S(1)} %get-tuple-element.48.refs_4_.refs_0_, bf16[72,896]{1,0:T(8,128)(2,1)S(1)} %collective-permute-done.7.refs_5_.refs_1_, bf16[72,896]{1,0:T(8,128)(2,1)S(1)} %collective-permute-done.8.refs_6_.refs_2_, ...), custom_call_target="tpu_custom_call" | custom-call | tf_op jit(solution)/shard_map/own_terms/pallas_call | solution.py:456
  87.6 1.7 %near_results.1 = (bf16[128,1024]{1,0:T(8,128)(2,1)S(1)}, bf16[128,3584]{1,0:T(8,128)(2,1)S(1)}) custom-call(s32[1,128]{1,0:T(1,128)S(1)} %bitcast.3, f32[1,128]{1,0:T(1,128)S(1)} %bitcast.6, bf16[8,10368]{1,0:T(8,128)(2,1)S(1)} %get-tuple-element.69.refs_0_, bf16[8,10368]{1,0:T(8,128)(2,1)S(1)} %collective-permute-done.12.refs_0_.refs_1_, ...), custom_call_target="tpu_custom_call" | custom-call | tf_op jit(solution)/shard_map/near_results/pallas_call | solution.py:456
  89.3 0.2 collective-permute-done.14.refs_1_
  89.5 1.8 %collective-permute-done.16.refs_3_ = bf16[8,10368]{1,0:T(8,128)(2,1)S(1)} collective-permute-done((bf16[8,10368]{1,0:T(8,128)(2,1)S(1)}, bf16[8,10368]{1,0:T(8,128)(2,1)S(1)}, u32[]{:S(2)}, u32[]{:S(2)}) %collective-permute-start.16) | collective-permute-done | bytes 165920 | tf_op jit(solution)/shard_map/ppermute | solution.py:490
  91.3 2.6 %far_results.1 = (bf16[128,1024]{1,0:T(8,128)(2,1)}, bf16[128,3584]{1,0:T(8,128)(2,1)}) custom-call(s32[1,128]{1,0:T(1,128)S(1)} %bitcast.4, f32[1,128]{1,0:T(1,128)S(1)} %bitcast.7, bf16[8,10368]{1,0:T(8,128)(2,1)S(1)} %get-tuple-element.65.refs_0_, bf16[8,10368]{1,0:T(8,128)(2,1)S(1)} %collective-permute-done.14.refs_1_, ...), custom_call_target="tpu_custom_call" | custom-call | tf_op jit(solution)/shard_map/far_results/pallas_call | solution.py:456
  93.9 3.9 %update.1 = (bf16[1,896,1024]{2,1,0:T(8,128)(2,1)}, bf16[1,896,1024]{2,1,0:T(8,128)(2,1)}) custom-call(s32[8]{0:T(128)S(1)} %copy-done.2, f32[896,1024]{1,0:T(8,128)S(1)} %own_terms.1.total, bf16[896,1024]{1,0:T(8,128)(2,1)S(1)} %get-tuple-element.78.old_weight, bf16[32,10368]{1,0:T(8,128)(2,1)S(1)} %collective-permute-done.10.payload.payload_hbm, ...), custom_call_target="tpu_custom_call" | custom-call | flops 528482304 | bytes 11010048 | tf_op jit(solution)/shard_map/update/pallas_call | solution.py:642
  (23 shorter events, 0.1 us)
Async XLA Ops:
  4.0 12.6 %collective-permute-start = (bf16[16,10368]{1,0:T(8,128)(2,1)}, bf16[16,10368]{1,0:T(8,128)(2,1)S(1)}, u32[]{:S(2)}, u32[]{:S(2)}) collective-permute-start(bf16[16,10368]{1,0:T(8,128)(2,1)} %get-tuple-element.45), channel_id=1, source_target_pairs={{0,1},{1,0},{2,3},{3,2},{4,5},{5,4},{6,7},{7,6},{8,9},{9,8},{10,11... | collective-permute-start | bytes 995336 | tf_op jit(solution)/shard_map/ppermute | solution.py:483
  7.1 17.3 %collective-permute-start.1 = (bf16[16,10368]{1,0:T(8,128)(2,1)}, bf16[16,10368]{1,0:T(8,128)(2,1)S(1)}, u32[]{:S(2)}, u32[]{:S(2)}) collective-permute-start(bf16[16,10368]{1,0:T(8,128)(2,1)} %get-tuple-element.46), channel_id=1, source_target_pairs={{0,2},{1,3},{2,0},{3,1},{4,6},{5,7},{6,4},{7,5},{8,10},{9,11},{10,... | collective-permute-start | bytes 995336 | tf_op jit(solution)/shard_map/ppermute | solution.py:483
  8.6 25.3 %collective-permute-start.2 = (bf16[16,10368]{1,0:T(8,128)(2,1)}, bf16[16,10368]{1,0:T(8,128)(2,1)S(1)}, u32[]{:S(2)}, u32[]{:S(2)}) collective-permute-start(bf16[16,10368]{1,0:T(8,128)(2,1)} %get-tuple-element.47), channel_id=1, source_target_pairs={{0,3},{1,2},{2,1},{3,0},{4,7},{5,6},{6,5},{7,4},{8,11},{9,10},{10,... | collective-permute-start | bytes 995336 | tf_op jit(solution)/shard_map/ppermute | solution.py:483
  8.6 25.6 %collective-permute-start.3 = (bf16[8,10368]{1,0:T(8,128)(2,1)}, bf16[8,10368]{1,0:T(8,128)(2,1)S(1)}, u32[]{:S(2)}, u32[]{:S(2)}) collective-permute-start(bf16[8,10368]{1,0:T(8,128)(2,1)} %get-tuple-element.52), channel_id=1, source_target_pairs={{0,4},{1,5},{2,6},{3,7},{4,0},{5,1},{6,2},{7,3},{8,12},{9,13},{10,... | collective-permute-start | bytes 497672 | tf_op jit(solution)/shard_map/ppermute | solution.py:483
  11.6 5.1 %copy-start.6 = (bf16[8,10368]{1,0:T(8,128)(2,1)S(1)}, bf16[8,10368]{1,0:T(8,128)(2,1)}, u32[]{:S(2)}) copy-start(bf16[8,10368]{1,0:T(8,128)(2,1)} %get-tuple-element.54) | copy-start | bytes 497668
  11.6 12.7 %copy-start.5 = (bf16[8,10368]{1,0:T(8,128)(2,1)S(1)}, bf16[8,10368]{1,0:T(8,128)(2,1)}, u32[]{:S(2)}) copy-start(bf16[8,10368]{1,0:T(8,128)(2,1)} %get-tuple-element.55) | copy-start | bytes 497668
  11.6 22.3 %copy-start.1 = (bf16[16,10368]{1,0:T(8,128)(2,1)S(1)}, bf16[16,10368]{1,0:T(8,128)(2,1)}, u32[]{:S(2)}) copy-start(bf16[16,10368]{1,0:T(8,128)(2,1)} %get-tuple-element.44.refs_0_) | copy-start | bytes 995332
  11.6 24.6 %copy-start.2 = (s32[8]{0:T(128)S(1)}, s32[8]{0:T(128)}, u32[]{:S(2)}) copy-start(s32[8]{0:T(128)} %placement_ref.7) | copy-start | bytes 100
  11.6 24.5 %collective-permute-start.4 = (bf16[8,10368]{1,0:T(8,128)(2,1)}, bf16[8,10368]{1,0:T(8,128)(2,1)S(1)}, u32[]{:S(2)}, u32[]{:S(2)}) collective-permute-start(bf16[8,10368]{1,0:T(8,128)(2,1)} %get-tuple-element.53), channel_id=1, source_target_pairs={{0,6},{1,7},{2,4},{3,5},{4,2},{5,3},{6,0},{7,1},{8,14},{9,15},{10,... | collective-permute-start | bytes 497672 | tf_op jit(solution)/shard_map/ppermute | solution.py:483
  16.7 24.2 %collective-permute-start.5 = (bf16[8,10368]{1,0:T(8,128)(2,1)S(1)}, bf16[8,10368]{1,0:T(8,128)(2,1)S(1)}, u32[]{:S(2)}, u32[]{:S(2)}) collective-permute-start(bf16[8,10368]{1,0:T(8,128)(2,1)S(1)} %copy-done.6), channel_id=1, source_target_pairs={{0,5},{1,4},{2,7},{3,6},{4,1},{5,0},{6,3},{7,2},{8,13},{9,12},{10,... | collective-permute-start | bytes 497672 | tf_op jit(solution)/shard_map/ppermute | solution.py:483
  24.3 16.6 %collective-permute-start.6 = (bf16[8,10368]{1,0:T(8,128)(2,1)S(1)}, bf16[8,10368]{1,0:T(8,128)(2,1)S(1)}, u32[]{:S(2)}, u32[]{:S(2)}) collective-permute-start(bf16[8,10368]{1,0:T(8,128)(2,1)S(1)} %copy-done.5), channel_id=1, source_target_pairs={{0,7},{1,6},{2,5},{3,4},{4,3},{5,2},{6,1},{7,0},{8,15},{9,14},{10,... | collective-permute-start | bytes 497672 | tf_op jit(solution)/shard_map/ppermute | solution.py:483
  34.1 6.8 %collective-permute-start.7 = (bf16[72,896]{1,0:T(8,128)(2,1)S(1)}, bf16[72,896]{1,0:T(8,128)(2,1)S(1)}, u32[]{:S(2)}, u32[]{:S(2)}) collective-permute-start(bf16[72,896]{1,0:T(8,128)(2,1)S(1)} %get-tuple-element.56), channel_id=1, source_target_pairs={{8,0},{0,8},{24,16},{16,24},{9,1},{1,9},{25,17},{17,25},{10,2},{2,... | collective-permute-start | bytes 387080 | tf_op jit(solution)/shard_map/ppermute | solution.py:500
  34.2 6.7 %collective-permute-start.8 = (bf16[72,896]{1,0:T(8,128)(2,1)S(1)}, bf16[72,896]{1,0:T(8,128)(2,1)S(1)}, u32[]{:S(2)}, u32[]{:S(2)}) collective-permute-start(bf16[72,896]{1,0:T(8,128)(2,1)S(1)} %get-tuple-element.57), channel_id=1, source_target_pairs={{16,0},{24,8},{0,16},{8,24},{17,1},{25,9},{1,17},{9,25},{18,2},{26... | collective-permute-start | bytes 387080 | tf_op jit(solution)/shard_map/ppermute | solution.py:500
  36.1 6.4 %collective-permute-start.9 = (bf16[72,896]{1,0:T(8,128)(2,1)S(1)}, bf16[72,896]{1,0:T(8,128)(2,1)S(1)}, u32[]{:S(2)}, u32[]{:S(2)}) collective-permute-start(bf16[72,896]{1,0:T(8,128)(2,1)S(1)} %get-tuple-element.58), channel_id=1, source_target_pairs={{24,0},{16,8},{8,16},{0,24},{25,1},{17,9},{9,17},{1,25},{26,2},{18... | collective-permute-start | bytes 387080 | tf_op jit(solution)/shard_map/ppermute | solution.py:500
  45.1 40.0 %copy-start = (bf16[1,896,1024]{2,1,0:T(8,128)(2,1)S(1)}, bf16[1,896,1024]{2,1,0:T(8,128)(2,1)}, u32[]{:S(2)}) copy-start(bf16[1,896,1024]{2,1,0:T(8,128)(2,1)} %momentum_hbm.1) | copy-start | bytes 5505028
  45.1 4.5 %collective-permute-start.11 = (bf16[72,4864]{1,0:T(8,128)(2,1)S(1)}, bf16[72,4864]{1,0:T(8,128)(2,1)S(1)}, u32[]{:S(2)}, u32[]{:S(2)}) collective-permute-start(bf16[72,4864]{1,0:T(8,128)(2,1)S(1)} %get-tuple-element.62), channel_id=1, source_target_pairs={{8,0},{0,8},{24,16},{16,24},{9,1},{1,9},{25,17},{17,25},{10,2},{2,... | collective-permute-start | bytes 2101256 | tf_op jit(solution)/shard_map/ppermute | solution.py:500
  45.3 32.3 %collective-permute-start.10 = (bf16[32,10368]{1,0:T(8,128)(2,1)S(1)}, bf16[32,10368]{1,0:T(8,128)(2,1)S(1)}, u32[]{:S(2)}, u32[]{:S(2)}) collective-permute-start(bf16[32,10368]{1,0:T(8,128)(2,1)S(1)} %get-tuple-element.59), channel_id=1, source_target_pairs={{0,4},{1,5},{2,6},{3,7},{4,0},{5,1},{6,2},{7,3},{8,12},{9,13},{10,... | collective-permute-start | bytes 1990664 | tf_op jit(solution)/shard_map/ppermute | solution.py:494
  48.0 34.2 %collective-permute-start.18 = (bf16[72,4864]{1,0:T(8,128)(2,1)S(1)}, bf16[72,4864]{1,0:T(8,128)(2,1)S(1)}, u32[]{:S(2)}, u32[]{:S(2)}) collective-permute-start(bf16[72,4864]{1,0:T(8,128)(2,1)S(1)} %get-tuple-element.76), channel_id=1, source_target_pairs={{16,0},{24,8},{0,16},{8,24},{17,1},{25,9},{1,17},{9,25},{18,2},{26... | collective-permute-start | bytes 2101256 | tf_op jit(solution)/shard_map/ppermute | solution.py:500
  49.5 34.1 %collective-permute-start.19 = (bf16[72,4864]{1,0:T(8,128)(2,1)S(1)}, bf16[72,4864]{1,0:T(8,128)(2,1)S(1)}, u32[]{:S(2)}, u32[]{:S(2)}) collective-permute-start(bf16[72,4864]{1,0:T(8,128)(2,1)S(1)} %get-tuple-element.77), channel_id=1, source_target_pairs={{24,0},{16,8},{8,16},{0,24},{25,1},{17,9},{9,17},{1,25},{26,2},{18... | collective-permute-start | bytes 2101256 | tf_op jit(solution)/shard_map/ppermute | solution.py:500
  49.6 28.3 %collective-permute-start.12 = (bf16[8,10368]{1,0:T(8,128)(2,1)S(1)}, bf16[8,10368]{1,0:T(8,128)(2,1)S(1)}, u32[]{:S(2)}, u32[]{:S(2)}) collective-permute-start(bf16[8,10368]{1,0:T(8,128)(2,1)S(1)} %get-tuple-element.63), channel_id=1, source_target_pairs={{1,0},{0,1},{3,2},{2,3},{5,4},{4,5},{7,6},{6,7},{9,8},{8,9},{11,10... | collective-permute-start | bytes 497672 | tf_op jit(solution)/shard_map/ppermute | solution.py:490
  49.9 28.0 %collective-permute-start.13 = (bf16[8,10368]{1,0:T(8,128)(2,1)S(1)}, bf16[8,10368]{1,0:T(8,128)(2,1)S(1)}, u32[]{:S(2)}, u32[]{:S(2)}) collective-permute-start(bf16[8,10368]{1,0:T(8,128)(2,1)S(1)} %get-tuple-element.64), channel_id=1, source_target_pairs={{2,0},{3,1},{0,2},{1,3},{6,4},{7,5},{4,6},{5,7},{10,8},{11,9},{8,1... | collective-permute-start | bytes 497672 | tf_op jit(solution)/shard_map/ppermute | solution.py:490
  77.6 7.0 %collective-permute-start.17 = (bf16[8,10368]{1,0:T(8,128)(2,1)S(1)}, bf16[8,10368]{1,0:T(8,128)(2,1)S(1)}, u32[]{:S(2)}, u32[]{:S(2)}) collective-permute-start(bf16[8,10368]{1,0:T(8,128)(2,1)S(1)} %get-tuple-element.70), channel_id=1, source_target_pairs={{3,0},{2,1},{1,2},{0,3},{7,4},{6,5},{5,6},{4,7},{11,8},{10,9},{9,1... | collective-permute-start | bytes 497672 | tf_op jit(solution)/shard_map/ppermute | solution.py:490
  78.8 5.7 %collective-permute-start.21 = (bf16[72,1024]{1,0:T(8,128)(2,1)S(1)}, bf16[72,1024]{1,0:T(8,128)(2,1)S(1)}, u32[]{:S(2)}, u32[]{:S(2)}) collective-permute-start(bf16[72,1024]{1,0:T(8,128)(2,1)S(1)} %get-tuple-element.79.refs_0_), channel_id=1, source_target_pairs={{16,0},{24,8},{0,16},{8,24},{17,1},{25,9},{1,17},{9,25},{18,2},{26... | collective-permute-start | bytes 442376 | tf_op jit(solution)/shard_map/ppermute | solution.py:500
  80.4 9.1 %collective-permute-start.14 = (bf16[8,10368]{1,0:T(8,128)(2,1)S(1)}, bf16[8,10368]{1,0:T(8,128)(2,1)S(1)}, u32[]{:S(2)}, u32[]{:S(2)}) collective-permute-start(bf16[8,10368]{1,0:T(8,128)(2,1)S(1)} %get-tuple-element.66), channel_id=1, source_target_pairs={{1,0},{0,1},{3,2},{2,3},{5,4},{4,5},{7,6},{6,7},{9,8},{8,9},{11,10... | collective-permute-start | bytes 497672 | tf_op jit(solution)/shard_map/ppermute | solution.py:490
  82.2 7.3 %collective-permute-start.15 = (bf16[8,10368]{1,0:T(8,128)(2,1)S(1)}, bf16[8,10368]{1,0:T(8,128)(2,1)S(1)}, u32[]{:S(2)}, u32[]{:S(2)}) collective-permute-start(bf16[8,10368]{1,0:T(8,128)(2,1)S(1)} %get-tuple-element.67), channel_id=1, source_target_pairs={{2,0},{3,1},{0,2},{1,3},{6,4},{7,5},{4,6},{5,7},{10,8},{11,9},{8,1... | collective-permute-start | bytes 497672 | tf_op jit(solution)/shard_map/ppermute | solution.py:490
  83.7 7.6 %collective-permute-start.16 = (bf16[8,10368]{1,0:T(8,128)(2,1)S(1)}, bf16[8,10368]{1,0:T(8,128)(2,1)S(1)}, u32[]{:S(2)}, u32[]{:S(2)}) collective-permute-start(bf16[8,10368]{1,0:T(8,128)(2,1)S(1)} %get-tuple-element.68), channel_id=1, source_target_pairs={{3,0},{2,1},{1,2},{0,3},{7,4},{6,5},{5,6},{4,7},{11,8},{10,9},{9,1... | collective-permute-start | bytes 497672 | tf_op jit(solution)/shard_map/ppermute | solution.py:490
  84.5 9.4 %collective-permute-start.20 = (bf16[72,1024]{1,0:T(8,128)(2,1)S(1)}, bf16[72,1024]{1,0:T(8,128)(2,1)S(1)}, u32[]{:S(2)}, u32[]{:S(2)}) collective-permute-start(bf16[72,1024]{1,0:T(8,128)(2,1)S(1)} %get-tuple-element.79.refs_0_), channel_id=1, source_target_pairs={{8,0},{0,8},{24,16},{16,24},{9,1},{1,9},{25,17},{17,25},{10,2},{2,... | collective-permute-start | bytes 442376 | tf_op jit(solution)/shard_map/ppermute | solution.py:500
  84.5 9.4 %collective-permute-start.22 = (bf16[72,1024]{1,0:T(8,128)(2,1)S(1)}, bf16[72,1024]{1,0:T(8,128)(2,1)S(1)}, u32[]{:S(2)}, u32[]{:S(2)}) collective-permute-start(bf16[72,1024]{1,0:T(8,128)(2,1)S(1)} %collective-permute-done.21.refs_2_), channel_id=1, source_target_pairs={{8,0},{0,8},{24,16},{16,24},{9,1},{1,9},{25,17},{17,25},{10,2},{2,... | collective-permute-start | bytes 442376 | tf_op jit(solution)/shard_map/ppermute | solution.py:500
  85.1 2.5 %copy-start.3 = (s32[128]{0:T(128)S(1)}, s32[128]{0:T(128)}, u32[]{:S(2)}) copy-start(s32[128]{0:T(128)} %param.10) | copy-start | bytes 1540
  85.1 2.5 %copy-start.4 = (f32[128]{0:T(128)S(1)}, f32[128]{0:T(128)}, u32[]{:S(2)}) copy-start(f32[128]{0:T(128)} %param.8) | copy-start | bytes 1540

commit v12 on v11

--- a/solution.py
+++ b/solution.py
@@ -323,6 +323,10 @@
         shared[m][:, 2 * width + 2 * plan.F :] = grad_pre
 
 
+def pass_kernel(plan, source, before, target):
+    target[...] = source[...]
+
+
 def early_kernel(plan, near_back, *refs):
     back = near_back[...].astype(F32)
     for m, out in enumerate(refs[-plan.half :]):
@@ -340,24 +344,30 @@
     outs[plan.half][...] = jnp.where(hot, unfold(plan, blocks, plan.F).astype(F32), 0.0).astype(BF16)
 
 
-def unpack_kernel(far, plan, slot_ref, gate_ref, *refs):
+def picks_kernel(plan, slot_ref, gate_ref, before, near, far, gate):
+    block, rank = token_places(plan, slot_ref[...])
+    width = plan.half * SUB
+    for side, out in enumerate((near, far)):
+        place = jnp.where(lax.rem(block, 2) == side, block // 2, -2)
+        picks = []
+        for target in row_targets(plan, place, rank):
+            column = to_column(target).astype(jnp.int32)
+            picks.append((iota((plan.tokens, width), 1) == column).astype(BF16))
+        for q in range(plan.cuts):
+            out[q] = jnp.concatenate(picks[: plan.full] + picks[plan.full + q :][:1], axis=1)
+    gate[...] = to_column(gate_ref[...])
+
+
+def unpack_kernel(plan, picks_ref, gate_ref, *refs):
     half = plan.half
     got, refs = refs[:half], refs[half:]
-    before, refs = (refs[:2], refs[2:]) if far else ((None, None), refs)
+    before, refs = (refs[:-4], refs[-4:])
     out_ref, grad_ref, held, sems = refs
     copies = [
         pltpu.make_async_copy(source, held.at[i], sems.at[i]) for i, source in enumerate(got)
     ]
     for copy in copies:
         copy.start()
-    block, rank = token_places(plan, slot_ref[...])
-    block = jnp.where(lax.rem(block, 2) == far, block // 2, -2)
-    width = half * SUB
-    picks = []
-    for target in row_targets(plan, block, rank):
-        column = to_column(target).astype(jnp.int32)
-        picks.append((iota((plan.tokens, width), 1) == column).astype(BF16))
-    gate = to_column(gate_ref[...])
     for copy in copies:
         copy.wait()
 
@@ -367,21 +377,20 @@
         piece = size // plan.cuts
         for q in range(plan.cuts):
             span = slice(q * piece, (q + 1) * piece)
-            lhs, rhs = list(picks[: plan.full]), []
+            parts = []
             for i in range(plan.full):
-                rhs.append(rows[:, i * size + q * piece : i * size + (q + 1) * piece])
+                parts.append(rows[:, i * size + q * piece : i * size + (q + 1) * piece])
             if plan.rest:
-                lhs.append(picks[plan.full + q])
-                rhs.append(rows[:, plan.full * size :])
-            value = dot(jnp.concatenate(lhs, axis=1), jnp.concatenate(rhs, axis=0))
+                parts.append(rows[:, plan.full * size :])
+            value = dot(picks_ref[q], jnp.concatenate(parts, axis=0))
             if scale is not None:
                 value = scale * value
-            if placed is not None:
-                value = value + placed[:, span].astype(F32)
+            if placed:
+                value = value + placed[0][:, span].astype(F32)
             out[:, span] = value.astype(BF16)
 
-    gather(0, plan.D, None, before[1], grad_ref)
-    gather(plan.DX, plan.F, gate, before[0], out_ref)
+    gather(0, plan.D, None, before[1:], grad_ref)
+    gather(plan.DX, plan.F, gate_ref[...], before[:1], out_ref)
 
 
 def rows_of(parts):
@@ -584,10 +593,23 @@
     )
     payload = to_partner(outs[0])
     shared = from_groups(outs[1:])
+    depth = half * SUB * (plan.full + (1 if plan.rest else 0))
+    near_picks, far_picks, gates = call(
+        picks_kernel,
+        plan,
+        [slot, gate, shared[1]],
+        [VMEM_SPEC] * 2 + [ANY_SPEC],
+        [(plan.cuts, plan.tokens, depth)] * 2 + [(plan.tokens, 1)],
+        [],
+        0,
+        "picks",
+        limit=4,
+        dtypes=[BF16, BF16, F32],
+    )
     outs = call(
         early_kernel,
         plan,
-        [back_near, shared[1]],
+        [back_near, gates],
         [VMEM_SPEC, ANY_SPEC],
         [(SUB, C)] * half,
         [],
@@ -595,7 +617,19 @@
         "early",
         limit=4,
     )
-    early = [outs[0]] + [to_source(outs[m], m) for m in range(1, half)]
+    early = [outs[0]] + [to_source(outs[m], m) for m in range(1, half - 1)]
+    (last,) = call(
+        pass_kernel,
+        plan,
+        [outs[half - 1], early[1]],
+        [VMEM_SPEC, ANY_SPEC],
+        [(SUB, C)],
+        [],
+        0,
+        "pass_on",
+        limit=4,
+    )
+    early.append(to_source(last, half - 1))
     (total,) = call(
         gather_kernel,
         plan,
@@ -611,12 +645,12 @@
         "own_terms",
         dtypes=[F32],
     )
-    def place(far, got, placed, name):
+    def place(picks, got, placed, name):
         return call(
-            functools.partial(unpack_kernel, far),
+            unpack_kernel,
             plan,
-            [slot, gate] + got + placed,
-            [VMEM_SPEC] * 2 + [ANY_SPEC] * half + [VMEM_SPEC] * len(placed),
+            [picks, gates] + got + placed,
+            [VMEM_SPEC] * (2 + half + len(placed)),
             [(plan.tokens, F), (plan.tokens, D)],
             [pltpu.VMEM((half, SUB, C), BF16), pltpu.SemaphoreType.DMA((half,))],
             0,
@@ -624,12 +658,12 @@
             limit=12,
         )
 
-    placed = list(place(0, early, [], "near_results"))
+    placed = list(place(near_picks, early, [], "near_results"))
     outs = call(
         after_kernel,
         plan,
-        [placement, payload, local] + early[1:3],
-        [SMEM_SPEC] + [VMEM_SPEC] * 2 + [ANY_SPEC] * 2,
+        [placement, payload, local, placed[0]],
+        [SMEM_SPEC] + [VMEM_SPEC] * 2 + [ANY_SPEC],
         [(SUB, C)] * half + [(rows, F)],
         [],
         0,
@@ -659,7 +693,7 @@
         name="update",
     )(placement, total, old_weight, payload, *other_g)
 
-    expert_out, token_grad = place(1, late, placed, "far_results")
+    expert_out, token_grad = place(far_picks, late, placed, "far_results")
     return expert_out, token_grad, new_weight, new_momentum
 
 

time: 98.2 us -> 98.8 us (level)
  starting transfers between devices: 32.9 us -> 35.3 us
  waiting for transfers between devices: 38 us -> 36.5 us
    ppermute x1, waiting for transfers between devices: 23.3 us -> 6.62 us  [to_partner(): return lax.ppermute(data, 'expert', pairs)]
    ppermute x6, waiting for transfers between devices: 2.15 us -> 17.3 us  [to_source(): return lax.ppermute(data, 'expert', pairs)]
    ppermute x6, starting transfers between devices: 9.02 us -> 11.3 us  [to_source(): return lax.ppermute(data, 'expert', pairs)]
    pallas_call x10 -> x12, Pallas kernels: 22.2 us -> 22 us  [call(): pl.pallas_call(functools.partial(kernel, plan), out_shape=[jax.ShapeDtype...]
  transfers between devices with their start and end apart: 23 -> 23, of which waited for: 7 -> 9; matrix products, arithmetic and copies ran while one was open for 0% -> 0% of each run, Pallas kernels for 17% -> 16%
where the time goes in v12:
time: 98.8 us; the launch traced here: 98.7 us
  waiting for transfers between devices  36.5 us (37%)
  starting transfers between devices  35.3 us (36%)
  Pallas kernels  25.9 us (26%)
  between operations  1 us (1%)
    pallas_call x12, Pallas kernels, call(): pl.pallas_call(functools.partial(kernel, plan), out_shape=[jax.ShapeDtype...  22 us
    ppermute x6, waiting for transfers between devices, to_source(): return lax.ppermute(data, 'expert', pairs)  17.3 us
    ppermute x7, starting transfers between devices, to_slot(): return lax.ppermute(data, 'expert', pairs)  15.3 us
    ppermute x6, starting transfers between devices, to_source(): return lax.ppermute(data, 'expert', pairs)  11.3 us
    ppermute x7, waiting for transfers between devices, to_slot(): return lax.ppermute(data, 'expert', pairs)  10.9 us
    ppermute x1, waiting for transfers between devices, to_partner(): return lax.ppermute(data, 'expert', pairs)  6.62 us
    ppermute x9, starting transfers between devices, from_group(): return lax.ppermute(data, 'dp', pairs)  5.99 us
    pallas_call x1, Pallas kernels, routed(): pl.pallas_call(functools.partial(update_kernel, plan), out_shape=[jax.Sha...  3.9 us
  transfers between devices with their start and end apart: 23, of which 9 were waited for; matrix products, arithmetic and copies ran while one was open for 0% of the time, Pallas kernels for 16%

profile of v12, /device:TPU:0, one launch (start us, length us, event | category | flops | bytes accessed | tf_op | source)
XLA Modules:
  0.0 98.7 jit_solution(7285928078928089462)
XLA Ops:
  0.6 3.4 %pack.1 = (bf16[16,10368]{1,0:T(8,128)(2,1)}, bf16[16,10368]{1,0:T(8,128)(2,1)}, bf16[16,10368]{1,0:T(8,128)(2,1)}, bf16[16,10368]{1,0:T(8,128)(2,1)}, bf16[8,10...) custom-call(s32[1,128]{1,0:T(1,128)} %bitcast.2, ...), custom_call_target="tpu_custom_call" | custom-call | flops 150994944 | bytes 3171328 | tf_op jit(solution)/shard_map/pack/pallas_call | solution.py:465
  4.0 3.0 %collective-permute-start = (bf16[16,10368]{1,0:T(8,128)(2,1)}, bf16[16,10368]{1,0:T(8,128)(2,1)S(1)}, u32[]{:S(2)}, u32[]{:S(2)}) collective-permute-start(bf16[16,10368]{1,0:T(8,128)(2,1)} %get-tuple-element.48), channel_id=1, source_target_pairs={{0,1},{1,0},{2,3},{3,2},{4,5},{5,4},{6,7},{7,6},{8,9},{9,8},{10,11... | collective-permute-start | bytes 995336 | tf_op jit(solution)/shard_map/ppermute | solution.py:492
  7.0 1.6 %collective-permute-start.1 = (bf16[16,10368]{1,0:T(8,128)(2,1)}, bf16[16,10368]{1,0:T(8,128)(2,1)S(1)}, u32[]{:S(2)}, u32[]{:S(2)}) collective-permute-start(bf16[16,10368]{1,0:T(8,128)(2,1)} %get-tuple-element.49), channel_id=1, source_target_pairs={{0,2},{1,3},{2,0},{3,1},{4,6},{5,7},{6,4},{7,5},{8,10},{9,11},{10,... | collective-permute-start | bytes 995336 | tf_op jit(solution)/shard_map/ppermute | solution.py:492
  8.6 0.0 collective-permute-start.2
  8.6 3.0 %collective-permute-start.3 = (bf16[8,10368]{1,0:T(8,128)(2,1)}, bf16[8,10368]{1,0:T(8,128)(2,1)S(1)}, u32[]{:S(2)}, u32[]{:S(2)}) collective-permute-start(bf16[8,10368]{1,0:T(8,128)(2,1)} %get-tuple-element.55), channel_id=1, source_target_pairs={{0,4},{1,5},{2,6},{3,7},{4,0},{5,1},{6,2},{7,3},{8,12},{9,13},{10,... | collective-permute-start | bytes 497672 | tf_op jit(solution)/shard_map/ppermute | solution.py:492
  11.6 1.4 %collective-permute-start.4 = (bf16[8,10368]{1,0:T(8,128)(2,1)}, bf16[8,10368]{1,0:T(8,128)(2,1)S(1)}, u32[]{:S(2)}, u32[]{:S(2)}) collective-permute-start(bf16[8,10368]{1,0:T(8,128)(2,1)} %get-tuple-element.56), channel_id=1, source_target_pairs={{0,6},{1,7},{2,4},{3,5},{4,2},{5,3},{6,0},{7,1},{8,14},{9,15},{10,... | collective-permute-start | bytes 497672 | tf_op jit(solution)/shard_map/ppermute | solution.py:492
  13.1 3.6 %hold.1 = (bf16[3584,1024]{1,0:T(8,128)(2,1)S(1)}, bf16[896,1024]{1,0:T(8,128)(2,1)S(1)}) custom-call(bf16[1,3584,1024]{2,1,0:T(8,128)(2,1)} %weight_hbm.1), custom_call_target="tpu_custom_call" | custom-call | tf_op jit(solution)/shard_map/hold/pallas_call | solution.py:465
  16.7 2.7 %collective-permute-start.5 = (bf16[8,10368]{1,0:T(8,128)(2,1)S(1)}, bf16[8,10368]{1,0:T(8,128)(2,1)S(1)}, u32[]{:S(2)}, u32[]{:S(2)}) collective-permute-start(bf16[8,10368]{1,0:T(8,128)(2,1)S(1)} %copy-done.6), channel_id=1, source_target_pairs={{0,5},{1,4},{2,7},{3,6},{4,1},{5,0},{6,3},{7,2},{8,13},{9,12},{10,... | collective-permute-start | bytes 497672 | tf_op jit(solution)/shard_map/ppermute | solution.py:492
  19.4 4.9 %collective-permute-done.1.refs_2_ = bf16[16,10368]{1,0:T(8,128)(2,1)S(1)} collective-permute-done((bf16[16,10368]{1,0:T(8,128)(2,1)}, bf16[16,10368]{1,0:T(8,128)(2,1)S(1)}, u32[]{:S(2)}, u32[]{:S(2)}) %collective-permute-start.1) | collective-permute-done | bytes 331808 | tf_op jit(solution)/shard_map/ppermute | solution.py:492
  24.3 3.6 %collective-permute-start.6 = (bf16[8,10368]{1,0:T(8,128)(2,1)S(1)}, bf16[8,10368]{1,0:T(8,128)(2,1)S(1)}, u32[]{:S(2)}, u32[]{:S(2)}) collective-permute-start(bf16[8,10368]{1,0:T(8,128)(2,1)S(1)} %copy-done.5), channel_id=1, source_target_pairs={{0,7},{1,6},{2,5},{3,4},{4,3},{5,2},{6,1},{7,0},{8,15},{9,14},{10,... | collective-permute-start | bytes 497672 | tf_op jit(solution)/shard_map/ppermute | solution.py:492
  27.9 6.0 %collective-permute-done.2.refs_3_ = bf16[16,10368]{1,0:T(8,128)(2,1)S(1)} collective-permute-done((bf16[16,10368]{1,0:T(8,128)(2,1)}, bf16[16,10368]{1,0:T(8,128)(2,1)S(1)}, u32[]{:S(2)}, u32[]{:S(2)}) %collective-permute-start.2) | collective-permute-done | bytes 331808 | tf_op jit(solution)/shard_map/ppermute | solution.py:492
  33.9 0.2 near_columns.1
  34.1 0.1 collective-permute-start.7
  34.2 1.9 %collective-permute-start.8 = (bf16[72,896]{1,0:T(8,128)(2,1)S(1)}, bf16[72,896]{1,0:T(8,128)(2,1)S(1)}, u32[]{:S(2)}, u32[]{:S(2)}) collective-permute-start(bf16[72,896]{1,0:T(8,128)(2,1)S(1)} %get-tuple-element.60), channel_id=1, source_target_pairs={{16,0},{24,8},{0,16},{8,24},{17,1},{25,9},{1,17},{9,25},{18,2},{26... | collective-permute-start | bytes 387080 | tf_op jit(solution)/shard_map/ppermute | solution.py:509
  36.1 0.1 collective-permute-start.9
  36.2 4.7 %near_rows.1 = (bf16[32,10368]{1,0:T(8,128)(2,1)S(1)}, bf16[32,10368]{1,0:T(8,128)(2,1)S(1)}, bf16[32,2304]{1,0:T(8,128)(2,1)S(1)}, bf16[72,2048]{1,0:T(8,128)(2,1)S(1)}, bf16[72,3584]{1,0:T(8,128)(2,1)S(1)}) custom-call(s32[8]{0:T(128)S(1)} %copy-done.2, bf16[3584,1024]{1,0:T(8,128)(2,1)S(1)} %get-tuple-element.46.weight_ref, ...), custom_call_target="tpu_custom_call" | custom-call | flops 2113929216 | bytes 11081760 | tf_op jit(solution)/shard_map/near_rows/pallas_call | solution.py:465
  40.9 0.0 collective-permute-done.7.refs_5_.refs_1_
  40.9 0.0 collective-permute-done.8.refs_6_.refs_2_
  40.9 1.6 %collective-permute-done.9.refs_7_.refs_3_ = bf16[72,896]{1,0:T(8,128)(2,1)S(1)} collective-permute-done((bf16[72,896]{1,0:T(8,128)(2,1)S(1)}, bf16[72,896]{1,0:T(8,128)(2,1)S(1)}, u32[]{:S(2)}, u32[]{:S(2)}) %collective-permute-start.9) | collective-permute-done | bytes 129056 | tf_op jit(solution)/shard_map/ppermute | solution.py:509
  42.6 2.5 %payload.1 = (bf16[32,10368]{1,0:T(8,128)(2,1)S(1)}, bf16[72,4864]{1,0:T(8,128)(2,1)S(1)}, bf16[72,4864]{1,0:T(8,128)(2,1)S(1)}, bf16[72,4864]{1,0:T(8,128)(2,1)S(1)}, bf16[72,4864]{1,0:T(8,128)(2,1)S(1)}) custom-call(s32[8]{0:T(128)S(1)} %copy-done.2, bf16[3584,1024]{1,0:T(8,128)(2,1)S(1)} %get-tuple-element.46.weight_ref, ...), custom_call_target="tpu_custom_call" | custom-call | flops 1056964608 | bytes 12943392 | tf_op jit(solution)/shard_map/payload/pallas_call | solution.py:465
  45.0 0.2 collective-permute-start.10
  45.3 2.7 %collective-permute-start.11 = (bf16[32,10368]{1,0:T(8,128)(2,1)S(1)}, bf16[32,10368]{1,0:T(8,128)(2,1)S(1)}, u32[]{:S(2)}, u32[]{:S(2)}) collective-permute-start(bf16[32,10368]{1,0:T(8,128)(2,1)S(1)} %get-tuple-element.65), channel_id=1, source_target_pairs={{0,4},{1,5},{2,6},{3,7},{4,0},{5,1},{6,2},{7,3},{8,12},{9,13},{10,... | collective-permute-start | bytes 1990664 | tf_op jit(solution)/shard_map/ppermute | solution.py:503
  48.0 1.5 %collective-permute-start.18 = (bf16[72,4864]{1,0:T(8,128)(2,1)S(1)}, bf16[72,4864]{1,0:T(8,128)(2,1)S(1)}, u32[]{:S(2)}, u32[]{:S(2)}) collective-permute-start(bf16[72,4864]{1,0:T(8,128)(2,1)S(1)} %get-tuple-element.82), channel_id=1, source_target_pairs={{16,0},{24,8},{0,16},{8,24},{17,1},{25,9},{1,17},{9,25},{18,2},{26... | collective-permute-start | bytes 2101256 | tf_op jit(solution)/shard_map/ppermute | solution.py:509
  49.5 0.0 collective-permute-done.10.before.refs_5_
  49.5 0.6 picks.1
  50.1 0.0 copy-start
  50.2 2.7 %collective-permute-start.12 = (bf16[8,10368]{1,0:T(8,128)(2,1)S(1)}, bf16[8,10368]{1,0:T(8,128)(2,1)S(1)}, u32[]{:S(2)}, u32[]{:S(2)}) collective-permute-start(bf16[8,10368]{1,0:T(8,128)(2,1)S(1)} %get-tuple-element.70), channel_id=1, source_target_pairs={{1,0},{0,1},{3,2},{2,3},{5,4},{4,5},{7,6},{6,7},{9,8},{8,9},{11,10... | collective-permute-start | bytes 497672 | tf_op jit(solution)/shard_map/ppermute | solution.py:499
  52.9 1.3 %collective-permute-start.13 = (bf16[8,10368]{1,0:T(8,128)(2,1)S(1)}, bf16[8,10368]{1,0:T(8,128)(2,1)S(1)}, u32[]{:S(2)}, u32[]{:S(2)}) collective-permute-start(bf16[8,10368]{1,0:T(8,128)(2,1)S(1)} %get-tuple-element.71), channel_id=1, source_target_pairs={{2,0},{3,1},{0,2},{1,3},{6,4},{7,5},{4,6},{5,7},{10,8},{11,9},{8,1... | collective-permute-start | bytes 497672 | tf_op jit(solution)/shard_map/ppermute | solution.py:499
  54.2 3.7 %collective-permute-done.12.before.refs_1_ = bf16[8,10368]{1,0:T(8,128)(2,1)S(1)} collective-permute-done((bf16[8,10368]{1,0:T(8,128)(2,1)S(1)}, bf16[8,10368]{1,0:T(8,128)(2,1)S(1)}, u32[]{:S(2)}, u32[]{:S(2)}) %collective-permute-start.12) | collective-permute-done | bytes 165920 | tf_op jit(solution)/shard_map/ppermute | solution.py:499
  57.9 2.6 %collective-permute-start.14 = (bf16[8,10368]{1,0:T(8,128)(2,1)S(1)}, bf16[8,10368]{1,0:T(8,128)(2,1)S(1)}, u32[]{:S(2)}, u32[]{:S(2)}) collective-permute-start(bf16[8,10368]{1,0:T(8,128)(2,1)S(1)} %pass_on.1), channel_id=1, source_target_pairs={{3,0},{2,1},{1,2},{0,3},{7,4},{6,5},{5,6},{4,7},{11,8},{10,9},{9,1... | collective-permute-start | bytes 497672 | tf_op jit(solution)/shard_map/ppermute | solution.py:499
  60.5 6.3 %collective-permute-done.13.refs_2_ = bf16[8,10368]{1,0:T(8,128)(2,1)S(1)} collective-permute-done((bf16[8,10368]{1,0:T(8,128)(2,1)S(1)}, bf16[8,10368]{1,0:T(8,128)(2,1)S(1)}, u32[]{:S(2)}, u32[]{:S(2)}) %collective-permute-start.13) | collective-permute-done | bytes 165920 | tf_op jit(solution)/shard_map/ppermute | solution.py:499
  66.9 2.8 %collective-permute-done.14.refs_3_ = bf16[8,10368]{1,0:T(8,128)(2,1)S(1)} collective-permute-done((bf16[8,10368]{1,0:T(8,128)(2,1)S(1)}, bf16[8,10368]{1,0:T(8,128)(2,1)S(1)}, u32[]{:S(2)}, u32[]{:S(2)}) %collective-permute-start.14) | collective-permute-done | bytes 165920 | tf_op jit(solution)/shard_map/ppermute | solution.py:499
  69.7 1.3 %near_results.1 = (bf16[128,1024]{1,0:T(8,128)(2,1)S(1)}, bf16[128,3584]{1,0:T(8,128)(2,1)S(1)}) custom-call(bf16[4,128,96]{2,1,0:T(8,128)(2,1)S(1)} %get-tuple-element.67.picks_ref, f32[128,1]{1,0:T(8,128)S(1)} %get-tuple-element.64.refs_0_.gate_ref, bf16[8,10368]{1,0:T(8,128)(2,1)S(1)} %get-tuple-element.69.refs_0_, ...), custom_call_target="tpu_custom_call" | custom-call | tf_op jit(solution)/shard_map/near_results/pallas_call | solution.py:465
  71.0 6.6 %collective-permute-done.11.payload.payload_hbm = bf16[32,10368]{1,0:T(8,128)(2,1)S(1)} collective-permute-done((bf16[32,10368]{1,0:T(8,128)(2,1)S(1)}, bf16[32,10368]{1,0:T(8,128)(2,1)S(1)}, u32[]{:S(2)}, u32[]{:S(2)}) %collective-permute-start.11) | collective-permute-done | bytes 663584 | tf_op jit(solution)/shard_map/ppermute | solution.py:503
  77.7 0.9 after_swap.1
  78.6 1.6 %collective-permute-start.21 = (bf16[72,1024]{1,0:T(8,128)(2,1)S(1)}, bf16[72,1024]{1,0:T(8,128)(2,1)S(1)}, u32[]{:S(2)}, u32[]{:S(2)}) collective-permute-start(bf16[72,1024]{1,0:T(8,128)(2,1)S(1)} %get-tuple-element.85.refs_0_), channel_id=1, source_target_pairs={{16,0},{24,8},{0,16},{8,24},{17,1},{25,9},{1,17},{9,25},{18,2},{26... | collective-permute-start | bytes 442376 | tf_op jit(solution)/shard_map/ppermute | solution.py:509
  80.3 3.1 %collective-permute-start.15 = (bf16[8,10368]{1,0:T(8,128)(2,1)S(1)}, bf16[8,10368]{1,0:T(8,128)(2,1)S(1)}, u32[]{:S(2)}, u32[]{:S(2)}) collective-permute-start(bf16[8,10368]{1,0:T(8,128)(2,1)S(1)} %get-tuple-element.75), channel_id=1, source_target_pairs={{1,0},{0,1},{3,2},{2,3},{5,4},{4,5},{7,6},{6,7},{9,8},{8,9},{11,10... | collective-permute-start | bytes 497672 | tf_op jit(solution)/shard_map/ppermute | solution.py:499
  83.4 1.5 %collective-permute-start.17 = (bf16[8,10368]{1,0:T(8,128)(2,1)S(1)}, bf16[8,10368]{1,0:T(8,128)(2,1)S(1)}, u32[]{:S(2)}, u32[]{:S(2)}) collective-permute-start(bf16[8,10368]{1,0:T(8,128)(2,1)S(1)} %get-tuple-element.77), channel_id=1, source_target_pairs={{3,0},{2,1},{1,2},{0,3},{7,4},{6,5},{5,6},{4,7},{11,8},{10,9},{9,1... | collective-permute-start | bytes 497672 | tf_op jit(solution)/shard_map/ppermute | solution.py:499
  84.9 0.0 collective-permute-start.20
  84.9 0.0 collective-permute-done.21.refs_2_
  84.9 0.5 collective-permute-start.22
  85.4 2.5 %own_terms.1.total = f32[896,1024]{1,0:T(8,128)S(1)} custom-call(bf16[1,896,1024]{2,1,0:T(8,128)(2,1)S(1)} %copy-done, bf16[72,896]{1,0:T(8,128)(2,1)S(1)} %get-tuple-element.51.refs_4_.refs_0_, bf16[72,896]{1,0:T(8,128)(2,1)S(1)} %collective-permute-done.7.refs_5_.refs_1_, bf16[72,896]{1,0:T(8,128)(2,1)S(1)} %collective-permute-done.8.refs_6_.refs_2_, ...), custom_call_target="tpu_custom_call" | custom-call | tf_op jit(solution)/shard_map/own_terms/pallas_call | solution.py:465
  87.9 0.0 collective-permute-done.15.refs_1_
  87.9 2.7 %collective-permute-done.16.refs_2_ = bf16[8,10368]{1,0:T(8,128)(2,1)S(1)} collective-permute-done((bf16[8,10368]{1,0:T(8,128)(2,1)S(1)}, bf16[8,10368]{1,0:T(8,128)(2,1)S(1)}, u32[]{:S(2)}, u32[]{:S(2)}) %collective-permute-start.16) | collective-permute-done | bytes 165920 | tf_op jit(solution)/shard_map/ppermute | solution.py:499
  90.6 1.7 %collective-permute-done.17.refs_3_ = bf16[8,10368]{1,0:T(8,128)(2,1)S(1)} collective-permute-done((bf16[8,10368]{1,0:T(8,128)(2,1)S(1)}, bf16[8,10368]{1,0:T(8,128)(2,1)S(1)}, u32[]{:S(2)}, u32[]{:S(2)}) %collective-permute-start.17) | collective-permute-done | bytes 165920 | tf_op jit(solution)/shard_map/ppermute | solution.py:499
  92.3 2.3 %far_results.1 = (bf16[128,1024]{1,0:T(8,128)(2,1)}, bf16[128,3584]{1,0:T(8,128)(2,1)}) custom-call(bf16[4,128,96]{2,1,0:T(8,128)(2,1)S(1)} %get-tuple-element.63.picks_ref, f32[128,1]{1,0:T(8,128)S(1)} %get-tuple-element.64.refs_0_.gate_ref, bf16[8,10368]{1,0:T(8,128)(2,1)S(1)} %get-tuple-element.74.refs_0_, ...), custom_call_target="tpu_custom_call" | custom-call | tf_op jit(solution)/shard_map/far_results/pallas_call | solution.py:465
  94.6 0.0 collective-permute-done.20.refs_1_
  94.6 3.9 %update.1 = (bf16[1,896,1024]{2,1,0:T(8,128)(2,1)}, bf16[1,896,1024]{2,1,0:T(8,128)(2,1)}) custom-call(s32[8]{0:T(128)S(1)} %copy-done.2, f32[896,1024]{1,0:T(8,128)S(1)} %own_terms.1.total, bf16[896,1024]{1,0:T(8,128)(2,1)S(1)} %get-tuple-element.84.old_weight, bf16[32,10368]{1,0:T(8,128)(2,1)S(1)} %collective-permute-done.11.payload.payload_hbm, ...), custom_call_target="tpu_custom_call" | custom-call | flops 528482304 | bytes 11010048 | tf_op jit(solution)/shard_map/update/pallas_call | solution.py:676
  (25 shorter events, 0.1 us)
Async XLA Ops:
  4.0 12.6 %collective-permute-start = (bf16[16,10368]{1,0:T(8,128)(2,1)}, bf16[16,10368]{1,0:T(8,128)(2,1)S(1)}, u32[]{:S(2)}, u32[]{:S(2)}) collective-permute-start(bf16[16,10368]{1,0:T(8,128)(2,1)} %get-tuple-element.48), channel_id=1, source_target_pairs={{0,1},{1,0},{2,3},{3,2},{4,5},{5,4},{6,7},{7,6},{8,9},{9,8},{10,11... | collective-permute-start | bytes 995336 | tf_op jit(solution)/shard_map/ppermute | solution.py:492
  7.0 17.3 %collective-permute-start.1 = (bf16[16,10368]{1,0:T(8,128)(2,1)}, bf16[16,10368]{1,0:T(8,128)(2,1)S(1)}, u32[]{:S(2)}, u32[]{:S(2)}) collective-permute-start(bf16[16,10368]{1,0:T(8,128)(2,1)} %get-tuple-element.49), channel_id=1, source_target_pairs={{0,2},{1,3},{2,0},{3,1},{4,6},{5,7},{6,4},{7,5},{8,10},{9,11},{10,... | collective-permute-start | bytes 995336 | tf_op jit(solution)/shard_map/ppermute | solution.py:492
  8.6 25.3 %collective-permute-start.2 = (bf16[16,10368]{1,0:T(8,128)(2,1)}, bf16[16,10368]{1,0:T(8,128)(2,1)S(1)}, u32[]{:S(2)}, u32[]{:S(2)}) collective-permute-start(bf16[16,10368]{1,0:T(8,128)(2,1)} %get-tuple-element.50), channel_id=1, source_target_pairs={{0,3},{1,2},{2,1},{3,0},{4,7},{5,6},{6,5},{7,4},{8,11},{9,10},{10,... | collective-permute-start | bytes 995336 | tf_op jit(solution)/shard_map/ppermute | solution.py:492
  8.6 25.6 %collective-permute-start.3 = (bf16[8,10368]{1,0:T(8,128)(2,1)}, bf16[8,10368]{1,0:T(8,128)(2,1)S(1)}, u32[]{:S(2)}, u32[]{:S(2)}) collective-permute-start(bf16[8,10368]{1,0:T(8,128)(2,1)} %get-tuple-element.55), channel_id=1, source_target_pairs={{0,4},{1,5},{2,6},{3,7},{4,0},{5,1},{6,2},{7,3},{8,12},{9,13},{10,... | collective-permute-start | bytes 497672 | tf_op jit(solution)/shard_map/ppermute | solution.py:492
  11.6 5.1 %copy-start.6 = (bf16[8,10368]{1,0:T(8,128)(2,1)S(1)}, bf16[8,10368]{1,0:T(8,128)(2,1)}, u32[]{:S(2)}) copy-start(bf16[8,10368]{1,0:T(8,128)(2,1)} %get-tuple-element.57) | copy-start | bytes 497668
  11.6 12.7 %copy-start.5 = (bf16[8,10368]{1,0:T(8,128)(2,1)S(1)}, bf16[8,10368]{1,0:T(8,128)(2,1)}, u32[]{:S(2)}) copy-start(bf16[8,10368]{1,0:T(8,128)(2,1)} %get-tuple-element.58) | copy-start | bytes 497668
  11.6 22.3 %copy-start.1 = (bf16[16,10368]{1,0:T(8,128)(2,1)S(1)}, bf16[16,10368]{1,0:T(8,128)(2,1)}, u32[]{:S(2)}) copy-start(bf16[16,10368]{1,0:T(8,128)(2,1)} %get-tuple-element.47.refs_0_) | copy-start | bytes 995332
  11.6 24.6 %copy-start.2 = (s32[8]{0:T(128)S(1)}, s32[8]{0:T(128)}, u32[]{:S(2)}) copy-start(s32[8]{0:T(128)} %placement_ref.7) | copy-start | bytes 100
  11.6 24.5 %collective-permute-start.4 = (bf16[8,10368]{1,0:T(8,128)(2,1)}, bf16[8,10368]{1,0:T(8,128)(2,1)S(1)}, u32[]{:S(2)}, u32[]{:S(2)}) collective-permute-start(bf16[8,10368]{1,0:T(8,128)(2,1)} %get-tuple-element.56), channel_id=1, source_target_pairs={{0,6},{1,7},{2,4},{3,5},{4,2},{5,3},{6,0},{7,1},{8,14},{9,15},{10,... | collective-permute-start | bytes 497672 | tf_op jit(solution)/shard_map/ppermute | solution.py:492
  16.7 24.2 %collective-permute-start.5 = (bf16[8,10368]{1,0:T(8,128)(2,1)S(1)}, bf16[8,10368]{1,0:T(8,128)(2,1)S(1)}, u32[]{:S(2)}, u32[]{:S(2)}) collective-permute-start(bf16[8,10368]{1,0:T(8,128)(2,1)S(1)} %copy-done.6), channel_id=1, source_target_pairs={{0,5},{1,4},{2,7},{3,6},{4,1},{5,0},{6,3},{7,2},{8,13},{9,12},{10,... | collective-permute-start | bytes 497672 | tf_op jit(solution)/shard_map/ppermute | solution.py:492
  24.3 16.6 %collective-permute-start.6 = (bf16[8,10368]{1,0:T(8,128)(2,1)S(1)}, bf16[8,10368]{1,0:T(8,128)(2,1)S(1)}, u32[]{:S(2)}, u32[]{:S(2)}) collective-permute-start(bf16[8,10368]{1,0:T(8,128)(2,1)S(1)} %copy-done.5), channel_id=1, source_target_pairs={{0,7},{1,6},{2,5},{3,4},{4,3},{5,2},{6,1},{7,0},{8,15},{9,14},{10,... | collective-permute-start | bytes 497672 | tf_op jit(solution)/shard_map/ppermute | solution.py:492
  34.1 6.8 %collective-permute-start.7 = (bf16[72,896]{1,0:T(8,128)(2,1)S(1)}, bf16[72,896]{1,0:T(8,128)(2,1)S(1)}, u32[]{:S(2)}, u32[]{:S(2)}) collective-permute-start(bf16[72,896]{1,0:T(8,128)(2,1)S(1)} %get-tuple-element.59), channel_id=1, source_target_pairs={{8,0},{0,8},{24,16},{16,24},{9,1},{1,9},{25,17},{17,25},{10,2},{2,... | collective-permute-start | bytes 387080 | tf_op jit(solution)/shard_map/ppermute | solution.py:509
  34.2 6.7 %collective-permute-start.8 = (bf16[72,896]{1,0:T(8,128)(2,1)S(1)}, bf16[72,896]{1,0:T(8,128)(2,1)S(1)}, u32[]{:S(2)}, u32[]{:S(2)}) collective-permute-start(bf16[72,896]{1,0:T(8,128)(2,1)S(1)} %get-tuple-element.60), channel_id=1, source_target_pairs={{16,0},{24,8},{0,16},{8,24},{17,1},{25,9},{1,17},{9,25},{18,2},{26... | collective-permute-start | bytes 387080 | tf_op jit(solution)/shard_map/ppermute | solution.py:509
  36.1 6.4 %collective-permute-start.9 = (bf16[72,896]{1,0:T(8,128)(2,1)S(1)}, bf16[72,896]{1,0:T(8,128)(2,1)S(1)}, u32[]{:S(2)}, u32[]{:S(2)}) collective-permute-start(bf16[72,896]{1,0:T(8,128)(2,1)S(1)} %get-tuple-element.61), channel_id=1, source_target_pairs={{24,0},{16,8},{8,16},{0,24},{25,1},{17,9},{9,17},{1,25},{26,2},{18... | collective-permute-start | bytes 387080 | tf_op jit(solution)/shard_map/ppermute | solution.py:509
  42.5 7.0 %copy-start.3 = (s32[128]{0:T(128)S(1)}, s32[128]{0:T(128)}, u32[]{:S(2)}) copy-start(s32[128]{0:T(128)} %param.10) | copy-start | bytes 1540
  42.6 7.0 %copy-start.4 = (f32[128]{0:T(128)S(1)}, f32[128]{0:T(128)}, u32[]{:S(2)}) copy-start(f32[128]{0:T(128)} %param.8) | copy-start | bytes 1540
  45.0 4.5 %collective-permute-start.10 = (bf16[72,4864]{1,0:T(8,128)(2,1)S(1)}, bf16[72,4864]{1,0:T(8,128)(2,1)S(1)}, u32[]{:S(2)}, u32[]{:S(2)}) collective-permute-start(bf16[72,4864]{1,0:T(8,128)(2,1)S(1)} %get-tuple-element.62), channel_id=1, source_target_pairs={{8,0},{0,8},{24,16},{16,24},{9,1},{1,9},{25,17},{17,25},{10,2},{2,... | collective-permute-start | bytes 2101256 | tf_op jit(solution)/shard_map/ppermute | solution.py:509
  45.3 32.4 %collective-permute-start.11 = (bf16[32,10368]{1,0:T(8,128)(2,1)S(1)}, bf16[32,10368]{1,0:T(8,128)(2,1)S(1)}, u32[]{:S(2)}, u32[]{:S(2)}) collective-permute-start(bf16[32,10368]{1,0:T(8,128)(2,1)S(1)} %get-tuple-element.65), channel_id=1, source_target_pairs={{0,4},{1,5},{2,6},{3,7},{4,0},{5,1},{6,2},{7,3},{8,12},{9,13},{10,... | collective-permute-start | bytes 1990664 | tf_op jit(solution)/shard_map/ppermute | solution.py:503
  48.0 35.4 %collective-permute-start.18 = (bf16[72,4864]{1,0:T(8,128)(2,1)S(1)}, bf16[72,4864]{1,0:T(8,128)(2,1)S(1)}, u32[]{:S(2)}, u32[]{:S(2)}) collective-permute-start(bf16[72,4864]{1,0:T(8,128)(2,1)S(1)} %get-tuple-element.82), channel_id=1, source_target_pairs={{16,0},{24,8},{0,16},{8,24},{17,1},{25,9},{1,17},{9,25},{18,2},{26... | collective-permute-start | bytes 2101256 | tf_op jit(solution)/shard_map/ppermute | solution.py:509
  49.5 35.4 %collective-permute-start.19 = (bf16[72,4864]{1,0:T(8,128)(2,1)S(1)}, bf16[72,4864]{1,0:T(8,128)(2,1)S(1)}, u32[]{:S(2)}, u32[]{:S(2)}) collective-permute-start(bf16[72,4864]{1,0:T(8,128)(2,1)S(1)} %get-tuple-element.83), channel_id=1, source_target_pairs={{24,0},{16,8},{8,16},{0,24},{25,1},{17,9},{9,17},{1,25},{26,2},{18... | collective-permute-start | bytes 2101256 | tf_op jit(solution)/shard_map/ppermute | solution.py:509
  50.1 35.3 %copy-start = (bf16[1,896,1024]{2,1,0:T(8,128)(2,1)S(1)}, bf16[1,896,1024]{2,1,0:T(8,128)(2,1)}, u32[]{:S(2)}) copy-start(bf16[1,896,1024]{2,1,0:T(8,128)(2,1)} %momentum_hbm.1) | copy-start | bytes 5505028
  50.2 7.7 %collective-permute-start.12 = (bf16[8,10368]{1,0:T(8,128)(2,1)S(1)}, bf16[8,10368]{1,0:T(8,128)(2,1)S(1)}, u32[]{:S(2)}, u32[]{:S(2)}) collective-permute-start(bf16[8,10368]{1,0:T(8,128)(2,1)S(1)} %get-tuple-element.70), channel_id=1, source_target_pairs={{1,0},{0,1},{3,2},{2,3},{5,4},{4,5},{7,6},{6,7},{9,8},{8,9},{11,10... | collective-permute-start | bytes 497672 | tf_op jit(solution)/shard_map/ppermute | solution.py:499
  52.9 14.0 %collective-permute-start.13 = (bf16[8,10368]{1,0:T(8,128)(2,1)S(1)}, bf16[8,10368]{1,0:T(8,128)(2,1)S(1)}, u32[]{:S(2)}, u32[]{:S(2)}) collective-permute-start(bf16[8,10368]{1,0:T(8,128)(2,1)S(1)} %get-tuple-element.71), channel_id=1, source_target_pairs={{2,0},{3,1},{0,2},{1,3},{6,4},{7,5},{4,6},{5,7},{10,8},{11,9},{8,1... | collective-permute-start | bytes 497672 | tf_op jit(solution)/shard_map/ppermute | solution.py:499
  57.9 11.8 %collective-permute-start.14 = (bf16[8,10368]{1,0:T(8,128)(2,1)S(1)}, bf16[8,10368]{1,0:T(8,128)(2,1)S(1)}, u32[]{:S(2)}, u32[]{:S(2)}) collective-permute-start(bf16[8,10368]{1,0:T(8,128)(2,1)S(1)} %pass_on.1), channel_id=1, source_target_pairs={{3,0},{2,1},{1,2},{0,3},{7,4},{6,5},{5,6},{4,7},{11,8},{10,9},{9,1... | collective-permute-start | bytes 497672 | tf_op jit(solution)/shard_map/ppermute | solution.py:499
  78.6 6.3 %collective-permute-start.21 = (bf16[72,1024]{1,0:T(8,128)(2,1)S(1)}, bf16[72,1024]{1,0:T(8,128)(2,1)S(1)}, u32[]{:S(2)}, u32[]{:S(2)}) collective-permute-start(bf16[72,1024]{1,0:T(8,128)(2,1)S(1)} %get-tuple-element.85.refs_0_), channel_id=1, source_target_pairs={{16,0},{24,8},{0,16},{8,24},{17,1},{25,9},{1,17},{9,25},{18,2},{26... | collective-permute-start | bytes 442376 | tf_op jit(solution)/shard_map/ppermute | solution.py:509
  80.3 7.6 %collective-permute-start.15 = (bf16[8,10368]{1,0:T(8,128)(2,1)S(1)}, bf16[8,10368]{1,0:T(8,128)(2,1)S(1)}, u32[]{:S(2)}, u32[]{:S(2)}) collective-permute-start(bf16[8,10368]{1,0:T(8,128)(2,1)S(1)} %get-tuple-element.75), channel_id=1, source_target_pairs={{1,0},{0,1},{3,2},{2,3},{5,4},{4,5},{7,6},{6,7},{9,8},{8,9},{11,10... | collective-permute-start | bytes 497672 | tf_op jit(solution)/shard_map/ppermute | solution.py:499
  83.4 7.2 %collective-permute-start.16 = (bf16[8,10368]{1,0:T(8,128)(2,1)S(1)}, bf16[8,10368]{1,0:T(8,128)(2,1)S(1)}, u32[]{:S(2)}, u32[]{:S(2)}) collective-permute-start(bf16[8,10368]{1,0:T(8,128)(2,1)S(1)} %get-tuple-element.76), channel_id=1, source_target_pairs={{2,0},{3,1},{0,2},{1,3},{6,4},{7,5},{4,6},{5,7},{10,8},{11,9},{8,1... | collective-permute-start | bytes 497672 | tf_op jit(solution)/shard_map/ppermute | solution.py:499
  83.4 8.9 %collective-permute-start.17 = (bf16[8,10368]{1,0:T(8,128)(2,1)S(1)}, bf16[8,10368]{1,0:T(8,128)(2,1)S(1)}, u32[]{:S(2)}, u32[]{:S(2)}) collective-permute-start(bf16[8,10368]{1,0:T(8,128)(2,1)S(1)} %get-tuple-element.77), channel_id=1, source_target_pairs={{3,0},{2,1},{1,2},{0,3},{7,4},{6,5},{5,6},{4,7},{11,8},{10,9},{9,1... | collective-permute-start | bytes 497672 | tf_op jit(solution)/shard_map/ppermute | solution.py:499
  84.9 9.7 %collective-permute-start.20 = (bf16[72,1024]{1,0:T(8,128)(2,1)S(1)}, bf16[72,1024]{1,0:T(8,128)(2,1)S(1)}, u32[]{:S(2)}, u32[]{:S(2)}) collective-permute-start(bf16[72,1024]{1,0:T(8,128)(2,1)S(1)} %get-tuple-element.85.refs_0_), channel_id=1, source_target_pairs={{8,0},{0,8},{24,16},{16,24},{9,1},{1,9},{25,17},{17,25},{10,2},{2,... | collective-permute-start | bytes 442376 | tf_op jit(solution)/shard_map/ppermute | solution.py:509
  84.9 9.7 %collective-permute-start.22 = (bf16[72,1024]{1,0:T(8,128)(2,1)S(1)}, bf16[72,1024]{1,0:T(8,128)(2,1)S(1)}, u32[]{:S(2)}, u32[]{:S(2)}) collective-permute-start(bf16[72,1024]{1,0:T(8,128)(2,1)S(1)} %collective-permute-done.21.refs_2_), channel_id=1, source_target_pairs={{8,0},{0,8},{24,16},{16,24},{9,1},{1,9},{25,17},{17,25},{10,2},{2,... | collective-permute-start | bytes 442376 | tf_op jit(solution)/shard_map/ppermute | solution.py:509

commit v13 on v12

--- a/solution.py
+++ b/solution.py
@@ -27,6 +27,7 @@
         self.full, self.rest = divmod(self.cap, SUB)
         self.cuts = SUB // self.rest if self.rest else 1
         self.rows = self.half * self.cap
+        self.back_order = [*range(0, self.half, 2), *range(1, self.half, 2)]
         self.far_order = [*range(0, self.half, 2), *range(1, self.half, 2)]
         self.share = features // groups
         self.DX = features * self.cap // SUB
@@ -364,7 +365,8 @@
     before, refs = (refs[:-4], refs[-4:])
     out_ref, grad_ref, held, sems = refs
     copies = [
-        pltpu.make_async_copy(source, held.at[i], sems.at[i]) for i, source in enumerate(got)
+        pltpu.make_async_copy(source, held.at[m], sems.at[m])
+        for m, source in zip(plan.back_order, got)
     ]
     for copy in copies:
         copy.start()
@@ -649,7 +651,7 @@
         return call(
             unpack_kernel,
             plan,
-            [picks, gates] + got + placed,
+            [picks, gates] + [got[m] for m in plan.back_order] + placed,
             [VMEM_SPEC] * (2 + half + len(placed)),
             [(plan.tokens, F), (plan.tokens, D)],
             [pltpu.VMEM((half, SUB, C), BF16), pltpu.SemaphoreType.DMA((half,))],

time: 98.8 us -> 98.8 us (level)
  no operation moved by 1% of the time
where the time goes in v13:
time: 98.8 us; the launch traced here: 98.7 us
  waiting for transfers between devices  36.5 us (37%)
  starting transfers between devices  35.3 us (36%)
  Pallas kernels  25.9 us (26%)
  between operations  1 us (1%)
    pallas_call x12, Pallas kernels, call(): pl.pallas_call(functools.partial(kernel, plan), out_shape=[jax.ShapeDtype...  22 us
    ppermute x6, waiting for transfers between devices, to_source(): return lax.ppermute(data, 'expert', pairs)  17.3 us
    ppermute x7, starting transfers between devices, to_slot(): return lax.ppermute(data, 'expert', pairs)  15.3 us
    ppermute x6, starting transfers between devices, to_source(): return lax.ppermute(data, 'expert', pairs)  11.3 us
    ppermute x7, waiting for transfers between devices, to_slot(): return lax.ppermute(data, 'expert', pairs)  10.9 us
    ppermute x1, waiting for transfers between devices, to_partner(): return lax.ppermute(data, 'expert', pairs)  6.62 us
    ppermute x9, starting transfers between devices, from_group(): return lax.ppermute(data, 'dp', pairs)  5.99 us
    pallas_call x1, Pallas kernels, routed(): pl.pallas_call(functools.partial(update_kernel, plan), out_shape=[jax.Sha...  3.89 us
  transfers between devices with their start and end apart: 23, of which 9 were waited for; matrix products, arithmetic and copies ran while one was open for 0% of the time, Pallas kernels for 16%

profile of v13, /device:TPU:0, one launch (start us, length us, event | category | flops | bytes accessed | tf_op | source)
XLA Modules:
  0.0 98.7 jit_solution(35876295879679370)
XLA Ops:
  0.6 3.4 %pack.1 = (bf16[16,10368]{1,0:T(8,128)(2,1)}, bf16[16,10368]{1,0:T(8,128)(2,1)}, bf16[16,10368]{1,0:T(8,128)(2,1)}, bf16[16,10368]{1,0:T(8,128)(2,1)}, bf16[8,10...) custom-call(s32[1,128]{1,0:T(1,128)} %bitcast.2, ...), custom_call_target="tpu_custom_call" | custom-call | flops 150994944 | bytes 3171328 | tf_op jit(solution)/shard_map/pack/pallas_call | solution.py:467
  4.0 3.0 %collective-permute-start = (bf16[16,10368]{1,0:T(8,128)(2,1)}, bf16[16,10368]{1,0:T(8,128)(2,1)S(1)}, u32[]{:S(2)}, u32[]{:S(2)}) collective-permute-start(bf16[16,10368]{1,0:T(8,128)(2,1)} %get-tuple-element.48), channel_id=1, source_target_pairs={{0,1},{1,0},{2,3},{3,2},{4,5},{5,4},{6,7},{7,6},{8,9},{9,8},{10,11... | collective-permute-start | bytes 995336 | tf_op jit(solution)/shard_map/ppermute | solution.py:494
  7.0 1.6 %collective-permute-start.1 = (bf16[16,10368]{1,0:T(8,128)(2,1)}, bf16[16,10368]{1,0:T(8,128)(2,1)S(1)}, u32[]{:S(2)}, u32[]{:S(2)}) collective-permute-start(bf16[16,10368]{1,0:T(8,128)(2,1)} %get-tuple-element.49), channel_id=1, source_target_pairs={{0,2},{1,3},{2,0},{3,1},{4,6},{5,7},{6,4},{7,5},{8,10},{9,11},{10,... | collective-permute-start | bytes 995336 | tf_op jit(solution)/shard_map/ppermute | solution.py:494
  8.6 0.0 collective-permute-start.2
  8.6 3.0 %collective-permute-start.3 = (bf16[8,10368]{1,0:T(8,128)(2,1)}, bf16[8,10368]{1,0:T(8,128)(2,1)S(1)}, u32[]{:S(2)}, u32[]{:S(2)}) collective-permute-start(bf16[8,10368]{1,0:T(8,128)(2,1)} %get-tuple-element.55), channel_id=1, source_target_pairs={{0,4},{1,5},{2,6},{3,7},{4,0},{5,1},{6,2},{7,3},{8,12},{9,13},{10,... | collective-permute-start | bytes 497672 | tf_op jit(solution)/shard_map/ppermute | solution.py:494
  11.6 1.4 %collective-permute-start.4 = (bf16[8,10368]{1,0:T(8,128)(2,1)}, bf16[8,10368]{1,0:T(8,128)(2,1)S(1)}, u32[]{:S(2)}, u32[]{:S(2)}) collective-permute-start(bf16[8,10368]{1,0:T(8,128)(2,1)} %get-tuple-element.56), channel_id=1, source_target_pairs={{0,6},{1,7},{2,4},{3,5},{4,2},{5,3},{6,0},{7,1},{8,14},{9,15},{10,... | collective-permute-start | bytes 497672 | tf_op jit(solution)/shard_map/ppermute | solution.py:494
  13.1 3.6 %hold.1 = (bf16[3584,1024]{1,0:T(8,128)(2,1)S(1)}, bf16[896,1024]{1,0:T(8,128)(2,1)S(1)}) custom-call(bf16[1,3584,1024]{2,1,0:T(8,128)(2,1)} %weight_hbm.1), custom_call_target="tpu_custom_call" | custom-call | tf_op jit(solution)/shard_map/hold/pallas_call | solution.py:467
  16.7 2.7 %collective-permute-start.5 = (bf16[8,10368]{1,0:T(8,128)(2,1)S(1)}, bf16[8,10368]{1,0:T(8,128)(2,1)S(1)}, u32[]{:S(2)}, u32[]{:S(2)}) collective-permute-start(bf16[8,10368]{1,0:T(8,128)(2,1)S(1)} %copy-done.6), channel_id=1, source_target_pairs={{0,5},{1,4},{2,7},{3,6},{4,1},{5,0},{6,3},{7,2},{8,13},{9,12},{10,... | collective-permute-start | bytes 497672 | tf_op jit(solution)/shard_map/ppermute | solution.py:494
  19.4 4.9 %collective-permute-done.1.refs_2_ = bf16[16,10368]{1,0:T(8,128)(2,1)S(1)} collective-permute-done((bf16[16,10368]{1,0:T(8,128)(2,1)}, bf16[16,10368]{1,0:T(8,128)(2,1)S(1)}, u32[]{:S(2)}, u32[]{:S(2)}) %collective-permute-start.1) | collective-permute-done | bytes 331808 | tf_op jit(solution)/shard_map/ppermute | solution.py:494
  24.3 3.6 %collective-permute-start.6 = (bf16[8,10368]{1,0:T(8,128)(2,1)S(1)}, bf16[8,10368]{1,0:T(8,128)(2,1)S(1)}, u32[]{:S(2)}, u32[]{:S(2)}) collective-permute-start(bf16[8,10368]{1,0:T(8,128)(2,1)S(1)} %copy-done.5), channel_id=1, source_target_pairs={{0,7},{1,6},{2,5},{3,4},{4,3},{5,2},{6,1},{7,0},{8,15},{9,14},{10,... | collective-permute-start | bytes 497672 | tf_op jit(solution)/shard_map/ppermute | solution.py:494
  27.9 6.0 %collective-permute-done.2.refs_3_ = bf16[16,10368]{1,0:T(8,128)(2,1)S(1)} collective-permute-done((bf16[16,10368]{1,0:T(8,128)(2,1)}, bf16[16,10368]{1,0:T(8,128)(2,1)S(1)}, u32[]{:S(2)}, u32[]{:S(2)}) %collective-permute-start.2) | collective-permute-done | bytes 331808 | tf_op jit(solution)/shard_map/ppermute | solution.py:494
  33.9 0.2 near_columns.1
  34.1 0.1 collective-permute-start.7
  34.2 1.9 %collective-permute-start.8 = (bf16[72,896]{1,0:T(8,128)(2,1)S(1)}, bf16[72,896]{1,0:T(8,128)(2,1)S(1)}, u32[]{:S(2)}, u32[]{:S(2)}) collective-permute-start(bf16[72,896]{1,0:T(8,128)(2,1)S(1)} %get-tuple-element.60), channel_id=1, source_target_pairs={{16,0},{24,8},{0,16},{8,24},{17,1},{25,9},{1,17},{9,25},{18,2},{26... | collective-permute-start | bytes 387080 | tf_op jit(solution)/shard_map/ppermute | solution.py:511
  36.1 0.1 collective-permute-start.9
  36.2 4.7 %near_rows.1 = (bf16[32,10368]{1,0:T(8,128)(2,1)S(1)}, bf16[32,10368]{1,0:T(8,128)(2,1)S(1)}, bf16[32,2304]{1,0:T(8,128)(2,1)S(1)}, bf16[72,2048]{1,0:T(8,128)(2,1)S(1)}, bf16[72,3584]{1,0:T(8,128)(2,1)S(1)}) custom-call(s32[8]{0:T(128)S(1)} %copy-done.2, bf16[3584,1024]{1,0:T(8,128)(2,1)S(1)} %get-tuple-element.46.weight_ref, ...), custom_call_target="tpu_custom_call" | custom-call | flops 2113929216 | bytes 11081760 | tf_op jit(solution)/shard_map/near_rows/pallas_call | solution.py:467
  40.9 0.0 collective-permute-done.7.refs_5_.refs_1_
  40.9 0.0 collective-permute-done.8.refs_6_.refs_2_
  40.9 1.6 %collective-permute-done.9.refs_7_.refs_3_ = bf16[72,896]{1,0:T(8,128)(2,1)S(1)} collective-permute-done((bf16[72,896]{1,0:T(8,128)(2,1)S(1)}, bf16[72,896]{1,0:T(8,128)(2,1)S(1)}, u32[]{:S(2)}, u32[]{:S(2)}) %collective-permute-start.9) | collective-permute-done | bytes 129056 | tf_op jit(solution)/shard_map/ppermute | solution.py:511
  42.6 2.5 %payload.1 = (bf16[32,10368]{1,0:T(8,128)(2,1)S(1)}, bf16[72,4864]{1,0:T(8,128)(2,1)S(1)}, bf16[72,4864]{1,0:T(8,128)(2,1)S(1)}, bf16[72,4864]{1,0:T(8,128)(2,1)S(1)}, bf16[72,4864]{1,0:T(8,128)(2,1)S(1)}) custom-call(s32[8]{0:T(128)S(1)} %copy-done.2, bf16[3584,1024]{1,0:T(8,128)(2,1)S(1)} %get-tuple-element.46.weight_ref, ...), custom_call_target="tpu_custom_call" | custom-call | flops 1056964608 | bytes 12943392 | tf_op jit(solution)/shard_map/payload/pallas_call | solution.py:467
  45.0 0.2 collective-permute-start.10
  45.3 2.7 %collective-permute-start.11 = (bf16[32,10368]{1,0:T(8,128)(2,1)S(1)}, bf16[32,10368]{1,0:T(8,128)(2,1)S(1)}, u32[]{:S(2)}, u32[]{:S(2)}) collective-permute-start(bf16[32,10368]{1,0:T(8,128)(2,1)S(1)} %get-tuple-element.65), channel_id=1, source_target_pairs={{0,4},{1,5},{2,6},{3,7},{4,0},{5,1},{6,2},{7,3},{8,12},{9,13},{10,... | collective-permute-start | bytes 1990664 | tf_op jit(solution)/shard_map/ppermute | solution.py:505
  48.0 1.5 %collective-permute-start.18 = (bf16[72,4864]{1,0:T(8,128)(2,1)S(1)}, bf16[72,4864]{1,0:T(8,128)(2,1)S(1)}, u32[]{:S(2)}, u32[]{:S(2)}) collective-permute-start(bf16[72,4864]{1,0:T(8,128)(2,1)S(1)} %get-tuple-element.82), channel_id=1, source_target_pairs={{16,0},{24,8},{0,16},{8,24},{17,1},{25,9},{1,17},{9,25},{18,2},{26... | collective-permute-start | bytes 2101256 | tf_op jit(solution)/shard_map/ppermute | solution.py:511
  49.5 0.0 collective-permute-done.10.before.refs_5_
  49.5 0.6 picks.1
  50.1 0.0 copy-start
  50.2 2.7 %collective-permute-start.13 = (bf16[8,10368]{1,0:T(8,128)(2,1)S(1)}, bf16[8,10368]{1,0:T(8,128)(2,1)S(1)}, u32[]{:S(2)}, u32[]{:S(2)}) collective-permute-start(bf16[8,10368]{1,0:T(8,128)(2,1)S(1)} %get-tuple-element.71), channel_id=1, source_target_pairs={{1,0},{0,1},{3,2},{2,3},{5,4},{4,5},{7,6},{6,7},{9,8},{8,9},{11,10... | collective-permute-start | bytes 497672 | tf_op jit(solution)/shard_map/ppermute | solution.py:501
  52.9 1.3 %collective-permute-start.12 = (bf16[8,10368]{1,0:T(8,128)(2,1)S(1)}, bf16[8,10368]{1,0:T(8,128)(2,1)S(1)}, u32[]{:S(2)}, u32[]{:S(2)}) collective-permute-start(bf16[8,10368]{1,0:T(8,128)(2,1)S(1)} %get-tuple-element.70), channel_id=1, source_target_pairs={{2,0},{3,1},{0,2},{1,3},{6,4},{7,5},{4,6},{5,7},{10,8},{11,9},{8,1... | collective-permute-start | bytes 497672 | tf_op jit(solution)/shard_map/ppermute | solution.py:501
  54.2 3.7 %collective-permute-done.13.before.refs_2_ = bf16[8,10368]{1,0:T(8,128)(2,1)S(1)} collective-permute-done((bf16[8,10368]{1,0:T(8,128)(2,1)S(1)}, bf16[8,10368]{1,0:T(8,128)(2,1)S(1)}, u32[]{:S(2)}, u32[]{:S(2)}) %collective-permute-start.13) | collective-permute-done | bytes 165920 | tf_op jit(solution)/shard_map/ppermute | solution.py:501
  57.9 2.6 %collective-permute-start.14 = (bf16[8,10368]{1,0:T(8,128)(2,1)S(1)}, bf16[8,10368]{1,0:T(8,128)(2,1)S(1)}, u32[]{:S(2)}, u32[]{:S(2)}) collective-permute-start(bf16[8,10368]{1,0:T(8,128)(2,1)S(1)} %pass_on.1), channel_id=1, source_target_pairs={{3,0},{2,1},{1,2},{0,3},{7,4},{6,5},{5,6},{4,7},{11,8},{10,9},{9,1... | collective-permute-start | bytes 497672 | tf_op jit(solution)/shard_map/ppermute | solution.py:501
  60.5 6.3 %collective-permute-done.12.refs_1_ = bf16[8,10368]{1,0:T(8,128)(2,1)S(1)} collective-permute-done((bf16[8,10368]{1,0:T(8,128)(2,1)S(1)}, bf16[8,10368]{1,0:T(8,128)(2,1)S(1)}, u32[]{:S(2)}, u32[]{:S(2)}) %collective-permute-start.12) | collective-permute-done | bytes 165920 | tf_op jit(solution)/shard_map/ppermute | solution.py:501
  66.9 2.8 %collective-permute-done.14.refs_3_ = bf16[8,10368]{1,0:T(8,128)(2,1)S(1)} collective-permute-done((bf16[8,10368]{1,0:T(8,128)(2,1)S(1)}, bf16[8,10368]{1,0:T(8,128)(2,1)S(1)}, u32[]{:S(2)}, u32[]{:S(2)}) %collective-permute-start.14) | collective-permute-done | bytes 165920 | tf_op jit(solution)/shard_map/ppermute | solution.py:501
  69.7 1.3 %near_results.1 = (bf16[128,1024]{1,0:T(8,128)(2,1)S(1)}, bf16[128,3584]{1,0:T(8,128)(2,1)S(1)}) custom-call(bf16[4,128,96]{2,1,0:T(8,128)(2,1)S(1)} %get-tuple-element.67.picks_ref, f32[128,1]{1,0:T(8,128)S(1)} %get-tuple-element.64.refs_0_.gate_ref, bf16[8,10368]{1,0:T(8,128)(2,1)S(1)} %get-tuple-element.69.refs_0_, ...), custom_call_target="tpu_custom_call" | custom-call | tf_op jit(solution)/shard_map/near_results/pallas_call | solution.py:467
  71.0 6.6 %collective-permute-done.11.payload.payload_hbm = bf16[32,10368]{1,0:T(8,128)(2,1)S(1)} collective-permute-done((bf16[32,10368]{1,0:T(8,128)(2,1)S(1)}, bf16[32,10368]{1,0:T(8,128)(2,1)S(1)}, u32[]{:S(2)}, u32[]{:S(2)}) %collective-permute-start.11) | collective-permute-done | bytes 663584 | tf_op jit(solution)/shard_map/ppermute | solution.py:505
  77.7 0.9 after_swap.1
  78.6 1.6 %collective-permute-start.21 = (bf16[72,1024]{1,0:T(8,128)(2,1)S(1)}, bf16[72,1024]{1,0:T(8,128)(2,1)S(1)}, u32[]{:S(2)}, u32[]{:S(2)}) collective-permute-start(bf16[72,1024]{1,0:T(8,128)(2,1)S(1)} %get-tuple-element.85.refs_0_), channel_id=1, source_target_pairs={{16,0},{24,8},{0,16},{8,24},{17,1},{25,9},{1,17},{9,25},{18,2},{26... | collective-permute-start | bytes 442376 | tf_op jit(solution)/shard_map/ppermute | solution.py:511
  80.3 1.1 %collective-permute-start.15 = (bf16[8,10368]{1,0:T(8,128)(2,1)S(1)}, bf16[8,10368]{1,0:T(8,128)(2,1)S(1)}, u32[]{:S(2)}, u32[]{:S(2)}) collective-permute-start(bf16[8,10368]{1,0:T(8,128)(2,1)S(1)} %get-tuple-element.75), channel_id=1, source_target_pairs={{2,0},{3,1},{0,2},{1,3},{6,4},{7,5},{4,6},{5,7},{10,8},{11,9},{8,1... | collective-permute-start | bytes 497672 | tf_op jit(solution)/shard_map/ppermute | solution.py:501
  81.4 2.0 %collective-permute-start.16 = (bf16[8,10368]{1,0:T(8,128)(2,1)S(1)}, bf16[8,10368]{1,0:T(8,128)(2,1)S(1)}, u32[]{:S(2)}, u32[]{:S(2)}) collective-permute-start(bf16[8,10368]{1,0:T(8,128)(2,1)S(1)} %get-tuple-element.76), channel_id=1, source_target_pairs={{1,0},{0,1},{3,2},{2,3},{5,4},{4,5},{7,6},{6,7},{9,8},{8,9},{11,10... | collective-permute-start | bytes 497672 | tf_op jit(solution)/shard_map/ppermute | solution.py:501
  83.4 1.5 %collective-permute-start.17 = (bf16[8,10368]{1,0:T(8,128)(2,1)S(1)}, bf16[8,10368]{1,0:T(8,128)(2,1)S(1)}, u32[]{:S(2)}, u32[]{:S(2)}) collective-permute-start(bf16[8,10368]{1,0:T(8,128)(2,1)S(1)} %get-tuple-element.77), channel_id=1, source_target_pairs={{3,0},{2,1},{1,2},{0,3},{7,4},{6,5},{5,6},{4,7},{11,8},{10,9},{9,1... | collective-permute-start | bytes 497672 | tf_op jit(solution)/shard_map/ppermute | solution.py:501
  84.9 0.5 collective-permute-start.22
  85.4 2.5 %own_terms.1.total = f32[896,1024]{1,0:T(8,128)S(1)} custom-call(bf16[1,896,1024]{2,1,0:T(8,128)(2,1)S(1)} %copy-done, bf16[72,896]{1,0:T(8,128)(2,1)S(1)} %get-tuple-element.51.refs_4_.refs_0_, bf16[72,896]{1,0:T(8,128)(2,1)S(1)} %collective-permute-done.7.refs_5_.refs_1_, bf16[72,896]{1,0:T(8,128)(2,1)S(1)} %collective-permute-done.8.refs_6_.refs_2_, ...), custom_call_target="tpu_custom_call" | custom-call | tf_op jit(solution)/shard_map/own_terms/pallas_call | solution.py:467
  87.9 0.0 collective-permute-done.15.refs_1_
  87.9 2.5 %collective-permute-done.16.refs_2_ = bf16[8,10368]{1,0:T(8,128)(2,1)S(1)} collective-permute-done((bf16[8,10368]{1,0:T(8,128)(2,1)S(1)}, bf16[8,10368]{1,0:T(8,128)(2,1)S(1)}, u32[]{:S(2)}, u32[]{:S(2)}) %collective-permute-start.16) | collective-permute-done | bytes 165920 | tf_op jit(solution)/shard_map/ppermute | solution.py:501
  90.4 1.9 %collective-permute-done.17.refs_3_ = bf16[8,10368]{1,0:T(8,128)(2,1)S(1)} collective-permute-done((bf16[8,10368]{1,0:T(8,128)(2,1)S(1)}, bf16[8,10368]{1,0:T(8,128)(2,1)S(1)}, u32[]{:S(2)}, u32[]{:S(2)}) %collective-permute-start.17) | collective-permute-done | bytes 165920 | tf_op jit(solution)/shard_map/ppermute | solution.py:501
  92.3 2.3 %far_results.1 = (bf16[128,1024]{1,0:T(8,128)(2,1)}, bf16[128,3584]{1,0:T(8,128)(2,1)}) custom-call(bf16[4,128,96]{2,1,0:T(8,128)(2,1)S(1)} %get-tuple-element.63.picks_ref, f32[128,1]{1,0:T(8,128)S(1)} %get-tuple-element.64.refs_0_.gate_ref, bf16[8,10368]{1,0:T(8,128)(2,1)S(1)} %get-tuple-element.74.refs_0_, ...), custom_call_target="tpu_custom_call" | custom-call | tf_op jit(solution)/shard_map/far_results/pallas_call | solution.py:467
  94.6 0.0 collective-permute-done.20.refs_1_
  94.6 0.0 collective-permute-done.22.refs_3_
  94.6 3.9 %update.1 = (bf16[1,896,1024]{2,1,0:T(8,128)(2,1)}, bf16[1,896,1024]{2,1,0:T(8,128)(2,1)}) custom-call(s32[8]{0:T(128)S(1)} %copy-done.2, f32[896,1024]{1,0:T(8,128)S(1)} %own_terms.1.total, bf16[896,1024]{1,0:T(8,128)(2,1)S(1)} %get-tuple-element.84.old_weight, bf16[32,10368]{1,0:T(8,128)(2,1)S(1)} %collective-permute-done.11.payload.payload_hbm, ...), custom_call_target="tpu_custom_call" | custom-call | flops 528482304 | bytes 11010048 | tf_op jit(solution)/shard_map/update/pallas_call | solution.py:678
  (25 shorter events, 0.1 us)
Async XLA Ops:
  4.0 12.6 %collective-permute-start = (bf16[16,10368]{1,0:T(8,128)(2,1)}, bf16[16,10368]{1,0:T(8,128)(2,1)S(1)}, u32[]{:S(2)}, u32[]{:S(2)}) collective-permute-start(bf16[16,10368]{1,0:T(8,128)(2,1)} %get-tuple-element.48), channel_id=1, source_target_pairs={{0,1},{1,0},{2,3},{3,2},{4,5},{5,4},{6,7},{7,6},{8,9},{9,8},{10,11... | collective-permute-start | bytes 995336 | tf_op jit(solution)/shard_map/ppermute | solution.py:494
  7.0 17.3 %collective-permute-start.1 = (bf16[16,10368]{1,0:T(8,128)(2,1)}, bf16[16,10368]{1,0:T(8,128)(2,1)S(1)}, u32[]{:S(2)}, u32[]{:S(2)}) collective-permute-start(bf16[16,10368]{1,0:T(8,128)(2,1)} %get-tuple-element.49), channel_id=1, source_target_pairs={{0,2},{1,3},{2,0},{3,1},{4,6},{5,7},{6,4},{7,5},{8,10},{9,11},{10,... | collective-permute-start | bytes 995336 | tf_op jit(solution)/shard_map/ppermute | solution.py:494
  8.6 25.3 %collective-permute-start.2 = (bf16[16,10368]{1,0:T(8,128)(2,1)}, bf16[16,10368]{1,0:T(8,128)(2,1)S(1)}, u32[]{:S(2)}, u32[]{:S(2)}) collective-permute-start(bf16[16,10368]{1,0:T(8,128)(2,1)} %get-tuple-element.50), channel_id=1, source_target_pairs={{0,3},{1,2},{2,1},{3,0},{4,7},{5,6},{6,5},{7,4},{8,11},{9,10},{10,... | collective-permute-start | bytes 995336 | tf_op jit(solution)/shard_map/ppermute | solution.py:494
  8.6 25.6 %collective-permute-start.3 = (bf16[8,10368]{1,0:T(8,128)(2,1)}, bf16[8,10368]{1,0:T(8,128)(2,1)S(1)}, u32[]{:S(2)}, u32[]{:S(2)}) collective-permute-start(bf16[8,10368]{1,0:T(8,128)(2,1)} %get-tuple-element.55), channel_id=1, source_target_pairs={{0,4},{1,5},{2,6},{3,7},{4,0},{5,1},{6,2},{7,3},{8,12},{9,13},{10,... | collective-permute-start | bytes 497672 | tf_op jit(solution)/shard_map/ppermute | solution.py:494
  11.6 5.1 %copy-start.6 = (bf16[8,10368]{1,0:T(8,128)(2,1)S(1)}, bf16[8,10368]{1,0:T(8,128)(2,1)}, u32[]{:S(2)}) copy-start(bf16[8,10368]{1,0:T(8,128)(2,1)} %get-tuple-element.57) | copy-start | bytes 497668
  11.6 12.7 %copy-start.5 = (bf16[8,10368]{1,0:T(8,128)(2,1)S(1)}, bf16[8,10368]{1,0:T(8,128)(2,1)}, u32[]{:S(2)}) copy-start(bf16[8,10368]{1,0:T(8,128)(2,1)} %get-tuple-element.58) | copy-start | bytes 497668
  11.6 22.3 %copy-start.1 = (bf16[16,10368]{1,0:T(8,128)(2,1)S(1)}, bf16[16,10368]{1,0:T(8,128)(2,1)}, u32[]{:S(2)}) copy-start(bf16[16,10368]{1,0:T(8,128)(2,1)} %get-tuple-element.47.refs_0_) | copy-start | bytes 995332
  11.6 24.6 %copy-start.2 = (s32[8]{0:T(128)S(1)}, s32[8]{0:T(128)}, u32[]{:S(2)}) copy-start(s32[8]{0:T(128)} %placement_ref.7) | copy-start | bytes 100
  11.6 24.5 %collective-permute-start.4 = (bf16[8,10368]{1,0:T(8,128)(2,1)}, bf16[8,10368]{1,0:T(8,128)(2,1)S(1)}, u32[]{:S(2)}, u32[]{:S(2)}) collective-permute-start(bf16[8,10368]{1,0:T(8,128)(2,1)} %get-tuple-element.56), channel_id=1, source_target_pairs={{0,6},{1,7},{2,4},{3,5},{4,2},{5,3},{6,0},{7,1},{8,14},{9,15},{10,... | collective-permute-start | bytes 497672 | tf_op jit(solution)/shard_map/ppermute | solution.py:494
  16.7 24.2 %collective-permute-start.5 = (bf16[8,10368]{1,0:T(8,128)(2,1)S(1)}, bf16[8,10368]{1,0:T(8,128)(2,1)S(1)}, u32[]{:S(2)}, u32[]{:S(2)}) collective-permute-start(bf16[8,10368]{1,0:T(8,128)(2,1)S(1)} %copy-done.6), channel_id=1, source_target_pairs={{0,5},{1,4},{2,7},{3,6},{4,1},{5,0},{6,3},{7,2},{8,13},{9,12},{10,... | collective-permute-start | bytes 497672 | tf_op jit(solution)/shard_map/ppermute | solution.py:494
  24.3 16.6 %collective-permute-start.6 = (bf16[8,10368]{1,0:T(8,128)(2,1)S(1)}, bf16[8,10368]{1,0:T(8,128)(2,1)S(1)}, u32[]{:S(2)}, u32[]{:S(2)}) collective-permute-start(bf16[8,10368]{1,0:T(8,128)(2,1)S(1)} %copy-done.5), channel_id=1, source_target_pairs={{0,7},{1,6},{2,5},{3,4},{4,3},{5,2},{6,1},{7,0},{8,15},{9,14},{10,... | collective-permute-start | bytes 497672 | tf_op jit(solution)/shard_map/ppermute | solution.py:494
  34.1 6.8 %collective-permute-start.7 = (bf16[72,896]{1,0:T(8,128)(2,1)S(1)}, bf16[72,896]{1,0:T(8,128)(2,1)S(1)}, u32[]{:S(2)}, u32[]{:S(2)}) collective-permute-start(bf16[72,896]{1,0:T(8,128)(2,1)S(1)} %get-tuple-element.59), channel_id=1, source_target_pairs={{8,0},{0,8},{24,16},{16,24},{9,1},{1,9},{25,17},{17,25},{10,2},{2,... | collective-permute-start | bytes 387080 | tf_op jit(solution)/shard_map/ppermute | solution.py:511
  34.2 6.7 %collective-permute-start.8 = (bf16[72,896]{1,0:T(8,128)(2,1)S(1)}, bf16[72,896]{1,0:T(8,128)(2,1)S(1)}, u32[]{:S(2)}, u32[]{:S(2)}) collective-permute-start(bf16[72,896]{1,0:T(8,128)(2,1)S(1)} %get-tuple-element.60), channel_id=1, source_target_pairs={{16,0},{24,8},{0,16},{8,24},{17,1},{25,9},{1,17},{9,25},{18,2},{26... | collective-permute-start | bytes 387080 | tf_op jit(solution)/shard_map/ppermute | solution.py:511
  36.1 6.4 %collective-permute-start.9 = (bf16[72,896]{1,0:T(8,128)(2,1)S(1)}, bf16[72,896]{1,0:T(8,128)(2,1)S(1)}, u32[]{:S(2)}, u32[]{:S(2)}) collective-permute-start(bf16[72,896]{1,0:T(8,128)(2,1)S(1)} %get-tuple-element.61), channel_id=1, source_target_pairs={{24,0},{16,8},{8,16},{0,24},{25,1},{17,9},{9,17},{1,25},{26,2},{18... | collective-permute-start | bytes 387080 | tf_op jit(solution)/shard_map/ppermute | solution.py:511
  42.5 7.0 %copy-start.3 = (s32[128]{0:T(128)S(1)}, s32[128]{0:T(128)}, u32[]{:S(2)}) copy-start(s32[128]{0:T(128)} %param.10) | copy-start | bytes 1540
  42.6 7.0 %copy-start.4 = (f32[128]{0:T(128)S(1)}, f32[128]{0:T(128)}, u32[]{:S(2)}) copy-start(f32[128]{0:T(128)} %param.8) | copy-start | bytes 1540
  45.0 4.5 %collective-permute-start.10 = (bf16[72,4864]{1,0:T(8,128)(2,1)S(1)}, bf16[72,4864]{1,0:T(8,128)(2,1)S(1)}, u32[]{:S(2)}, u32[]{:S(2)}) collective-permute-start(bf16[72,4864]{1,0:T(8,128)(2,1)S(1)} %get-tuple-element.62), channel_id=1, source_target_pairs={{8,0},{0,8},{24,16},{16,24},{9,1},{1,9},{25,17},{17,25},{10,2},{2,... | collective-permute-start | bytes 2101256 | tf_op jit(solution)/shard_map/ppermute | solution.py:511
  45.3 32.4 %collective-permute-start.11 = (bf16[32,10368]{1,0:T(8,128)(2,1)S(1)}, bf16[32,10368]{1,0:T(8,128)(2,1)S(1)}, u32[]{:S(2)}, u32[]{:S(2)}) collective-permute-start(bf16[32,10368]{1,0:T(8,128)(2,1)S(1)} %get-tuple-element.65), channel_id=1, source_target_pairs={{0,4},{1,5},{2,6},{3,7},{4,0},{5,1},{6,2},{7,3},{8,12},{9,13},{10,... | collective-permute-start | bytes 1990664 | tf_op jit(solution)/shard_map/ppermute | solution.py:505
  48.0 35.4 %collective-permute-start.18 = (bf16[72,4864]{1,0:T(8,128)(2,1)S(1)}, bf16[72,4864]{1,0:T(8,128)(2,1)S(1)}, u32[]{:S(2)}, u32[]{:S(2)}) collective-permute-start(bf16[72,4864]{1,0:T(8,128)(2,1)S(1)} %get-tuple-element.82), channel_id=1, source_target_pairs={{16,0},{24,8},{0,16},{8,24},{17,1},{25,9},{1,17},{9,25},{18,2},{26... | collective-permute-start | bytes 2101256 | tf_op jit(solution)/shard_map/ppermute | solution.py:511
  49.5 35.4 %collective-permute-start.19 = (bf16[72,4864]{1,0:T(8,128)(2,1)S(1)}, bf16[72,4864]{1,0:T(8,128)(2,1)S(1)}, u32[]{:S(2)}, u32[]{:S(2)}) collective-permute-start(bf16[72,4864]{1,0:T(8,128)(2,1)S(1)} %get-tuple-element.83), channel_id=1, source_target_pairs={{24,0},{16,8},{8,16},{0,24},{25,1},{17,9},{9,17},{1,25},{26,2},{18... | collective-permute-start | bytes 2101256 | tf_op jit(solution)/shard_map/ppermute | solution.py:511
  50.1 35.3 %copy-start = (bf16[1,896,1024]{2,1,0:T(8,128)(2,1)S(1)}, bf16[1,896,1024]{2,1,0:T(8,128)(2,1)}, u32[]{:S(2)}) copy-start(bf16[1,896,1024]{2,1,0:T(8,128)(2,1)} %momentum_hbm.1) | copy-start | bytes 5505028
  50.2 7.7 %collective-permute-start.13 = (bf16[8,10368]{1,0:T(8,128)(2,1)S(1)}, bf16[8,10368]{1,0:T(8,128)(2,1)S(1)}, u32[]{:S(2)}, u32[]{:S(2)}) collective-permute-start(bf16[8,10368]{1,0:T(8,128)(2,1)S(1)} %get-tuple-element.71), channel_id=1, source_target_pairs={{1,0},{0,1},{3,2},{2,3},{5,4},{4,5},{7,6},{6,7},{9,8},{8,9},{11,10... | collective-permute-start | bytes 497672 | tf_op jit(solution)/shard_map/ppermute | solution.py:501
  52.9 14.0 %collective-permute-start.12 = (bf16[8,10368]{1,0:T(8,128)(2,1)S(1)}, bf16[8,10368]{1,0:T(8,128)(2,1)S(1)}, u32[]{:S(2)}, u32[]{:S(2)}) collective-permute-start(bf16[8,10368]{1,0:T(8,128)(2,1)S(1)} %get-tuple-element.70), channel_id=1, source_target_pairs={{2,0},{3,1},{0,2},{1,3},{6,4},{7,5},{4,6},{5,7},{10,8},{11,9},{8,1... | collective-permute-start | bytes 497672 | tf_op jit(solution)/shard_map/ppermute | solution.py:501
  57.9 11.8 %collective-permute-start.14 = (bf16[8,10368]{1,0:T(8,128)(2,1)S(1)}, bf16[8,10368]{1,0:T(8,128)(2,1)S(1)}, u32[]{:S(2)}, u32[]{:S(2)}) collective-permute-start(bf16[8,10368]{1,0:T(8,128)(2,1)S(1)} %pass_on.1), channel_id=1, source_target_pairs={{3,0},{2,1},{1,2},{0,3},{7,4},{6,5},{5,6},{4,7},{11,8},{10,9},{9,1... | collective-permute-start | bytes 497672 | tf_op jit(solution)/shard_map/ppermute | solution.py:501
  78.6 6.3 %collective-permute-start.21 = (bf16[72,1024]{1,0:T(8,128)(2,1)S(1)}, bf16[72,1024]{1,0:T(8,128)(2,1)S(1)}, u32[]{:S(2)}, u32[]{:S(2)}) collective-permute-start(bf16[72,1024]{1,0:T(8,128)(2,1)S(1)} %get-tuple-element.85.refs_0_), channel_id=1, source_target_pairs={{16,0},{24,8},{0,16},{8,24},{17,1},{25,9},{1,17},{9,25},{18,2},{26... | collective-permute-start | bytes 442376 | tf_op jit(solution)/shard_map/ppermute | solution.py:511
  80.3 7.6 %collective-permute-start.15 = (bf16[8,10368]{1,0:T(8,128)(2,1)S(1)}, bf16[8,10368]{1,0:T(8,128)(2,1)S(1)}, u32[]{:S(2)}, u32[]{:S(2)}) collective-permute-start(bf16[8,10368]{1,0:T(8,128)(2,1)S(1)} %get-tuple-element.75), channel_id=1, source_target_pairs={{2,0},{3,1},{0,2},{1,3},{6,4},{7,5},{4,6},{5,7},{10,8},{11,9},{8,1... | collective-permute-start | bytes 497672 | tf_op jit(solution)/shard_map/ppermute | solution.py:501
  81.4 9.0 %collective-permute-start.16 = (bf16[8,10368]{1,0:T(8,128)(2,1)S(1)}, bf16[8,10368]{1,0:T(8,128)(2,1)S(1)}, u32[]{:S(2)}, u32[]{:S(2)}) collective-permute-start(bf16[8,10368]{1,0:T(8,128)(2,1)S(1)} %get-tuple-element.76), channel_id=1, source_target_pairs={{1,0},{0,1},{3,2},{2,3},{5,4},{4,5},{7,6},{6,7},{9,8},{8,9},{11,10... | collective-permute-start | bytes 497672 | tf_op jit(solution)/shard_map/ppermute | solution.py:501
  83.4 8.9 %collective-permute-start.17 = (bf16[8,10368]{1,0:T(8,128)(2,1)S(1)}, bf16[8,10368]{1,0:T(8,128)(2,1)S(1)}, u32[]{:S(2)}, u32[]{:S(2)}) collective-permute-start(bf16[8,10368]{1,0:T(8,128)(2,1)S(1)} %get-tuple-element.77), channel_id=1, source_target_pairs={{3,0},{2,1},{1,2},{0,3},{7,4},{6,5},{5,6},{4,7},{11,8},{10,9},{9,1... | collective-permute-start | bytes 497672 | tf_op jit(solution)/shard_map/ppermute | solution.py:501
  84.9 9.7 %collective-permute-start.20 = (bf16[72,1024]{1,0:T(8,128)(2,1)S(1)}, bf16[72,1024]{1,0:T(8,128)(2,1)S(1)}, u32[]{:S(2)}, u32[]{:S(2)}) collective-permute-start(bf16[72,1024]{1,0:T(8,128)(2,1)S(1)} %get-tuple-element.85.refs_0_), channel_id=1, source_target_pairs={{8,0},{0,8},{24,16},{16,24},{9,1},{1,9},{25,17},{17,25},{10,2},{2,... | collective-permute-start | bytes 442376 | tf_op jit(solution)/shard_map/ppermute | solution.py:511
  84.9 9.7 %collective-permute-start.22 = (bf16[72,1024]{1,0:T(8,128)(2,1)S(1)}, bf16[72,1024]{1,0:T(8,128)(2,1)S(1)}, u32[]{:S(2)}, u32[]{:S(2)}) collective-permute-start(bf16[72,1024]{1,0:T(8,128)(2,1)S(1)} %collective-permute-done.21.refs_2_), channel_id=1, source_target_pairs={{8,0},{0,8},{24,16},{16,24},{9,1},{1,9},{25,17},{17,25},{10,2},{2,... | collective-permute-start | bytes 442376 | tf_op jit(solution)/shard_map/ppermute | solution.py:511

commit v14 on v13

--- a/solution.py
+++ b/solution.py
@@ -362,19 +362,12 @@
 def unpack_kernel(plan, picks_ref, gate_ref, *refs):
     half = plan.half
     got, refs = refs[:half], refs[half:]
-    before, refs = (refs[:-4], refs[-4:])
-    out_ref, grad_ref, held, sems = refs
-    copies = [
-        pltpu.make_async_copy(source, held.at[m], sems.at[m])
-        for m, source in zip(plan.back_order, got)
-    ]
-    for copy in copies:
-        copy.start()
-    for copy in copies:
-        copy.wait()
+    before, refs = refs[:-2], refs[-2:]
+    out_ref, grad_ref = refs
+    blocks = [got[plan.back_order.index(m)] for m in range(half)]
 
     def gather(base, size, scale, placed, out):
-        rows = [held[i, :, base : base + size * plan.cap // SUB].astype(F32) for i in range(half)]
+        rows = blocks_of(blocks, base, base + size * plan.cap // SUB)
         rows = jnp.concatenate(rows, axis=0).astype(BF16)
         piece = size // plan.cuts
         for q in range(plan.cuts):
@@ -423,20 +416,16 @@
 
 def update_kernel(plan, placement_ref, total, old_weight, payload_hbm, *refs):
     groups, share = plan.groups, plan.share
-    other_hbm, refs = refs[:groups], refs[groups:]
-    new_weight, new_momentum, payload, other_g, weight, momentum, sems, out_sems = refs
-    copies = [pltpu.make_async_copy(payload_hbm, payload, sems.at[groups])]
-    for m in range(groups):
-        copies.append(pltpu.make_async_copy(other_hbm[m], other_g.at[m], sems.at[m]))
-    for copy in copies:
-        copy.start()
+    other_g, refs = refs[:groups], refs[groups:]
+    new_weight, new_momentum, payload, weight, momentum, sem, out_sems = refs
+    copy = pltpu.make_async_copy(payload_hbm, payload, sem)
+    copy.start()
     hot = is_hot(plan, placement_ref)
-    for copy in copies:
-        copy.wait()
+    g = rows_of([data[...] for data in other_g])
+    copy.wait()
     pieces = [payload[:, i * share : (i + 1) * share] for i in range(plan.pieces)]
     x = jnp.concatenate(pieces, axis=0)
     x = jnp.where(hot, x.astype(F32), 0.0).astype(BF16)
-    g = rows_of([other_g[m] for m in range(groups)])
     done = []
     for i in range(share // LANES):
         span = pl.ds(i * LANES, LANES)
@@ -654,7 +643,7 @@
             [picks, gates] + [got[m] for m in plan.back_order] + placed,
             [VMEM_SPEC] * (2 + half + len(placed)),
             [(plan.tokens, F), (plan.tokens, D)],
-            [pltpu.VMEM((half, SUB, C), BF16), pltpu.SemaphoreType.DMA((half,))],
+            [],
             0,
             name,
             limit=12,
@@ -678,14 +667,13 @@
     new_weight, new_momentum = pl.pallas_call(
         functools.partial(update_kernel, plan),
         out_shape=[jax.ShapeDtypeStruct((1, share, F), BF16)] * 2,
-        in_specs=[SMEM_SPEC] + [VMEM_SPEC] * 2 + [ANY_SPEC] * (groups + 1),
+        in_specs=[SMEM_SPEC] + [VMEM_SPEC] * 2 + [ANY_SPEC] + [VMEM_SPEC] * groups,
         out_specs=[ANY_SPEC] * 2,
         scratch_shapes=[
             pltpu.VMEM((half * SUB, C), BF16),
-            pltpu.VMEM((groups, rows, F), BF16),
             pltpu.VMEM((share, F), BF16),
             pltpu.VMEM((share, F), BF16),
-            pltpu.SemaphoreType.DMA((groups + 1,)),
+            pltpu.SemaphoreType.DMA,
             pltpu.SemaphoreType.DMA((share // LANES, 2)),
         ],
         compiler_params=pltpu.CompilerParams(vmem_limit_bytes=20 * MIB),

time: 98.8 us -> 96 us (0.972); the launches traced: 98.7 us -> 94.6 us
  waiting for transfers between devices: 36.5 us -> 33.8 us
  Pallas kernels: 25.9 us -> 23.4 us
  starting transfers between devices: 35.3 us -> 36.4 us
    ppermute x6, waiting for transfers between devices: 17.3 us -> 13.7 us  [to_source(): return lax.ppermute(data, 'expert', pairs)]
    pallas_call x12, Pallas kernels: 22 us -> 20.3 us  [call(): pl.pallas_call(functools.partial(kernel, plan), out_shape=[jax.ShapeDtype...]
    ppermute x6, starting transfers between devices: 11.3 us -> 12.6 us  [to_source(): return lax.ppermute(data, 'expert', pairs)]
  transfers between devices with their start and end apart: 23 -> 23, of which waited for: 9 -> 10; matrix products, arithmetic and copies ran while one was open for 0% -> 0% of each run, Pallas kernels for 16% -> 15%
where the time goes in v14:
time: 96 us; the launch traced here: 94.6 us
  starting transfers between devices  36.4 us (38%)
  waiting for transfers between devices  33.8 us (35%)
  Pallas kernels  23.4 us (24%)
  between operations  0.97 us (1%)
    pallas_call x12, Pallas kernels, call(): pl.pallas_call(functools.partial(kernel, plan), out_shape=[jax.ShapeDtype...  20.3 us
    ppermute x7, starting transfers between devices, to_slot(): return lax.ppermute(data, 'expert', pairs)  15.3 us
    ppermute x6, waiting for transfers between devices, to_source(): return lax.ppermute(data, 'expert', pairs)  13.7 us
    ppermute x6, starting transfers between devices, to_source(): return lax.ppermute(data, 'expert', pairs)  12.6 us
    ppermute x7, waiting for transfers between devices, to_slot(): return lax.ppermute(data, 'expert', pairs)  10.9 us
    ppermute x1, waiting for transfers between devices, to_partner(): return lax.ppermute(data, 'expert', pairs)  7.36 us
    ppermute x9, starting transfers between devices, from_group(): return lax.ppermute(data, 'dp', pairs)  5.87 us
    pallas_call x1, Pallas kernels, routed(): pl.pallas_call(functools.partial(update_kernel, plan), out_shape=[jax.Sha...  3.13 us
  transfers between devices with their start and end apart: 23, of which 10 were waited for; matrix products, arithmetic and copies ran while one was open for 0% of the time, Pallas kernels for 15%

profile of v14, /device:TPU:0, one launch (start us, length us, event | category | flops | bytes accessed | tf_op | source)
XLA Modules:
  0.0 94.6 jit_solution(736225252532363692)
XLA Ops:
  0.6 3.4 %pack.1 = (bf16[16,10368]{1,0:T(8,128)(2,1)}, bf16[16,10368]{1,0:T(8,128)(2,1)}, bf16[16,10368]{1,0:T(8,128)(2,1)}, bf16[16,10368]{1,0:T(8,128)(2,1)}, bf16[8,10...) custom-call(s32[1,128]{1,0:T(1,128)} %bitcast.2, ...), custom_call_target="tpu_custom_call" | custom-call | flops 150994944 | bytes 3171328 | tf_op jit(solution)/shard_map/pack/pallas_call | solution.py:456
  4.0 3.0 %collective-permute-start = (bf16[16,10368]{1,0:T(8,128)(2,1)}, bf16[16,10368]{1,0:T(8,128)(2,1)S(1)}, u32[]{:S(2)}, u32[]{:S(2)}) collective-permute-start(bf16[16,10368]{1,0:T(8,128)(2,1)} %get-tuple-element.48), channel_id=1, source_target_pairs={{0,1},{1,0},{2,3},{3,2},{4,5},{5,4},{6,7},{7,6},{8,9},{9,8},{10,11... | collective-permute-start | bytes 995336 | tf_op jit(solution)/shard_map/ppermute | solution.py:483
  7.0 1.6 %collective-permute-start.1 = (bf16[16,10368]{1,0:T(8,128)(2,1)}, bf16[16,10368]{1,0:T(8,128)(2,1)S(1)}, u32[]{:S(2)}, u32[]{:S(2)}) collective-permute-start(bf16[16,10368]{1,0:T(8,128)(2,1)} %get-tuple-element.49), channel_id=1, source_target_pairs={{0,2},{1,3},{2,0},{3,1},{4,6},{5,7},{6,4},{7,5},{8,10},{9,11},{10,... | collective-permute-start | bytes 995336 | tf_op jit(solution)/shard_map/ppermute | solution.py:483
  8.6 0.0 collective-permute-start.2
  8.6 3.0 %collective-permute-start.3 = (bf16[8,10368]{1,0:T(8,128)(2,1)}, bf16[8,10368]{1,0:T(8,128)(2,1)S(1)}, u32[]{:S(2)}, u32[]{:S(2)}) collective-permute-start(bf16[8,10368]{1,0:T(8,128)(2,1)} %get-tuple-element.55), channel_id=1, source_target_pairs={{0,4},{1,5},{2,6},{3,7},{4,0},{5,1},{6,2},{7,3},{8,12},{9,13},{10,... | collective-permute-start | bytes 497672 | tf_op jit(solution)/shard_map/ppermute | solution.py:483
  11.6 1.4 %collective-permute-start.4 = (bf16[8,10368]{1,0:T(8,128)(2,1)}, bf16[8,10368]{1,0:T(8,128)(2,1)S(1)}, u32[]{:S(2)}, u32[]{:S(2)}) collective-permute-start(bf16[8,10368]{1,0:T(8,128)(2,1)} %get-tuple-element.56), channel_id=1, source_target_pairs={{0,6},{1,7},{2,4},{3,5},{4,2},{5,3},{6,0},{7,1},{8,14},{9,15},{10,... | collective-permute-start | bytes 497672 | tf_op jit(solution)/shard_map/ppermute | solution.py:483
  13.1 3.6 %hold.1 = (bf16[3584,1024]{1,0:T(8,128)(2,1)S(1)}, bf16[896,1024]{1,0:T(8,128)(2,1)S(1)}) custom-call(bf16[1,3584,1024]{2,1,0:T(8,128)(2,1)} %weight_hbm.1), custom_call_target="tpu_custom_call" | custom-call | tf_op jit(solution)/shard_map/hold/pallas_call | solution.py:456
  16.7 0.0 collective-permute-done.refs_1_
  16.7 2.7 %collective-permute-start.5 = (bf16[8,10368]{1,0:T(8,128)(2,1)S(1)}, bf16[8,10368]{1,0:T(8,128)(2,1)S(1)}, u32[]{:S(2)}, u32[]{:S(2)}) collective-permute-start(bf16[8,10368]{1,0:T(8,128)(2,1)S(1)} %copy-done.6), channel_id=1, source_target_pairs={{0,5},{1,4},{2,7},{3,6},{4,1},{5,0},{6,3},{7,2},{8,13},{9,12},{10,... | collective-permute-start | bytes 497672 | tf_op jit(solution)/shard_map/ppermute | solution.py:483
  19.4 4.9 %collective-permute-done.1.refs_2_ = bf16[16,10368]{1,0:T(8,128)(2,1)S(1)} collective-permute-done((bf16[16,10368]{1,0:T(8,128)(2,1)}, bf16[16,10368]{1,0:T(8,128)(2,1)S(1)}, u32[]{:S(2)}, u32[]{:S(2)}) %collective-permute-start.1) | collective-permute-done | bytes 331808 | tf_op jit(solution)/shard_map/ppermute | solution.py:483
  24.3 3.6 %collective-permute-start.6 = (bf16[8,10368]{1,0:T(8,128)(2,1)S(1)}, bf16[8,10368]{1,0:T(8,128)(2,1)S(1)}, u32[]{:S(2)}, u32[]{:S(2)}) collective-permute-start(bf16[8,10368]{1,0:T(8,128)(2,1)S(1)} %copy-done.5), channel_id=1, source_target_pairs={{0,7},{1,6},{2,5},{3,4},{4,3},{5,2},{6,1},{7,0},{8,15},{9,14},{10,... | collective-permute-start | bytes 497672 | tf_op jit(solution)/shard_map/ppermute | solution.py:483
  27.9 6.0 %collective-permute-done.2.refs_3_ = bf16[16,10368]{1,0:T(8,128)(2,1)S(1)} collective-permute-done((bf16[16,10368]{1,0:T(8,128)(2,1)}, bf16[16,10368]{1,0:T(8,128)(2,1)S(1)}, u32[]{:S(2)}, u32[]{:S(2)}) %collective-permute-start.2) | collective-permute-done | bytes 331808 | tf_op jit(solution)/shard_map/ppermute | solution.py:483
  33.9 0.2 near_columns.1
  34.1 0.1 collective-permute-start.7
  34.2 0.0 collective-permute-done.3.refs_0_
  34.2 1.9 %collective-permute-start.8 = (bf16[72,896]{1,0:T(8,128)(2,1)S(1)}, bf16[72,896]{1,0:T(8,128)(2,1)S(1)}, u32[]{:S(2)}, u32[]{:S(2)}) collective-permute-start(bf16[72,896]{1,0:T(8,128)(2,1)S(1)} %get-tuple-element.60), channel_id=1, source_target_pairs={{16,0},{24,8},{0,16},{8,24},{17,1},{25,9},{1,17},{9,25},{18,2},{26... | collective-permute-start | bytes 387080 | tf_op jit(solution)/shard_map/ppermute | solution.py:500
  36.1 0.1 collective-permute-start.9
  36.2 4.7 %near_rows.1 = (bf16[32,10368]{1,0:T(8,128)(2,1)S(1)}, bf16[32,10368]{1,0:T(8,128)(2,1)S(1)}, bf16[32,2304]{1,0:T(8,128)(2,1)S(1)}, bf16[72,2048]{1,0:T(8,128)(2,1)S(1)}, bf16[72,3584]{1,0:T(8,128)(2,1)S(1)}) custom-call(s32[8]{0:T(128)S(1)} %copy-done.2, bf16[3584,1024]{1,0:T(8,128)(2,1)S(1)} %get-tuple-element.46.weight_ref, ...), custom_call_target="tpu_custom_call" | custom-call | flops 2113929216 | bytes 11081760 | tf_op jit(solution)/shard_map/near_rows/pallas_call | solution.py:456
  40.9 0.0 collective-permute-done.5.refs_2_
  40.9 0.0 collective-permute-done.6.refs_3_
  40.9 0.0 collective-permute-done.7.refs_5_.refs_1_
  40.9 1.6 %collective-permute-done.9.refs_7_.refs_3_ = bf16[72,896]{1,0:T(8,128)(2,1)S(1)} collective-permute-done((bf16[72,896]{1,0:T(8,128)(2,1)S(1)}, bf16[72,896]{1,0:T(8,128)(2,1)S(1)}, u32[]{:S(2)}, u32[]{:S(2)}) %collective-permute-start.9) | collective-permute-done | bytes 129056 | tf_op jit(solution)/shard_map/ppermute | solution.py:500
  42.6 2.5 %payload.1 = (bf16[32,10368]{1,0:T(8,128)(2,1)S(1)}, bf16[72,4864]{1,0:T(8,128)(2,1)S(1)}, bf16[72,4864]{1,0:T(8,128)(2,1)S(1)}, bf16[72,4864]{1,0:T(8,128)(2,1)S(1)}, bf16[72,4864]{1,0:T(8,128)(2,1)S(1)}) custom-call(s32[8]{0:T(128)S(1)} %copy-done.2, bf16[3584,1024]{1,0:T(8,128)(2,1)S(1)} %get-tuple-element.46.weight_ref, ...), custom_call_target="tpu_custom_call" | custom-call | flops 1056964608 | bytes 12943392 | tf_op jit(solution)/shard_map/payload/pallas_call | solution.py:456
  45.0 0.2 collective-permute-start.10
  45.3 2.7 %collective-permute-start.11 = (bf16[32,10368]{1,0:T(8,128)(2,1)S(1)}, bf16[32,10368]{1,0:T(8,128)(2,1)S(1)}, u32[]{:S(2)}, u32[]{:S(2)}) collective-permute-start(bf16[32,10368]{1,0:T(8,128)(2,1)S(1)} %get-tuple-element.65), channel_id=1, source_target_pairs={{0,4},{1,5},{2,6},{3,7},{4,0},{5,1},{6,2},{7,3},{8,12},{9,13},{10,... | collective-permute-start | bytes 1990664 | tf_op jit(solution)/shard_map/ppermute | solution.py:494
  48.0 1.5 %collective-permute-start.18 = (bf16[72,4864]{1,0:T(8,128)(2,1)S(1)}, bf16[72,4864]{1,0:T(8,128)(2,1)S(1)}, u32[]{:S(2)}, u32[]{:S(2)}) collective-permute-start(bf16[72,4864]{1,0:T(8,128)(2,1)S(1)} %get-tuple-element.82), channel_id=1, source_target_pairs={{16,0},{24,8},{0,16},{8,24},{17,1},{25,9},{1,17},{9,25},{18,2},{26... | collective-permute-start | bytes 2101256 | tf_op jit(solution)/shard_map/ppermute | solution.py:500
  49.5 0.6 picks.1
  50.1 0.0 copy-start
  50.2 0.3 collective-permute-start.13
  50.5 4.5 %collective-permute-start.12 = (bf16[8,10368]{1,0:T(8,128)(2,1)S(1)}, bf16[8,10368]{1,0:T(8,128)(2,1)S(1)}, u32[]{:S(2)}, u32[]{:S(2)}) collective-permute-start(bf16[8,10368]{1,0:T(8,128)(2,1)S(1)} %get-tuple-element.70), channel_id=1, source_target_pairs={{2,0},{3,1},{0,2},{1,3},{6,4},{7,5},{4,6},{5,7},{10,8},{11,9},{8,1... | collective-permute-start | bytes 497672 | tf_op jit(solution)/shard_map/ppermute | solution.py:490
  54.9 2.1 %collective-permute-done.13.before.refs_2_ = bf16[8,10368]{1,0:T(8,128)(2,1)S(1)} collective-permute-done((bf16[8,10368]{1,0:T(8,128)(2,1)S(1)}, bf16[8,10368]{1,0:T(8,128)(2,1)S(1)}, u32[]{:S(2)}, u32[]{:S(2)}) %collective-permute-start.13) | collective-permute-done | bytes 165920 | tf_op jit(solution)/shard_map/ppermute | solution.py:490
  57.1 4.3 %collective-permute-start.14 = (bf16[8,10368]{1,0:T(8,128)(2,1)S(1)}, bf16[8,10368]{1,0:T(8,128)(2,1)S(1)}, u32[]{:S(2)}, u32[]{:S(2)}) collective-permute-start(bf16[8,10368]{1,0:T(8,128)(2,1)S(1)} %pass_on.1), channel_id=1, source_target_pairs={{3,0},{2,1},{1,2},{0,3},{7,4},{6,5},{5,6},{4,7},{11,8},{10,9},{9,1... | collective-permute-start | bytes 497672 | tf_op jit(solution)/shard_map/ppermute | solution.py:490
  61.4 5.5 %collective-permute-done.12.refs_1_ = bf16[8,10368]{1,0:T(8,128)(2,1)S(1)} collective-permute-done((bf16[8,10368]{1,0:T(8,128)(2,1)S(1)}, bf16[8,10368]{1,0:T(8,128)(2,1)S(1)}, u32[]{:S(2)}, u32[]{:S(2)}) %collective-permute-start.12) | collective-permute-done | bytes 165920 | tf_op jit(solution)/shard_map/ppermute | solution.py:490
  66.9 2.8 %collective-permute-done.14.refs_3_ = bf16[8,10368]{1,0:T(8,128)(2,1)S(1)} collective-permute-done((bf16[8,10368]{1,0:T(8,128)(2,1)S(1)}, bf16[8,10368]{1,0:T(8,128)(2,1)S(1)}, u32[]{:S(2)}, u32[]{:S(2)}) %collective-permute-start.14) | collective-permute-done | bytes 165920 | tf_op jit(solution)/shard_map/ppermute | solution.py:490
  69.7 0.5 near_results.1
  70.2 7.4 %collective-permute-done.11.payload.payload_hbm = bf16[32,10368]{1,0:T(8,128)(2,1)S(1)} collective-permute-done((bf16[32,10368]{1,0:T(8,128)(2,1)S(1)}, bf16[32,10368]{1,0:T(8,128)(2,1)S(1)}, u32[]{:S(2)}, u32[]{:S(2)}) %collective-permute-start.11) | collective-permute-done | bytes 663584 | tf_op jit(solution)/shard_map/ppermute | solution.py:494
  77.6 0.9 %after_swap.1 = (bf16[8,10368]{1,0:T(8,128)(2,1)S(1)}, bf16[8,10368]{1,0:T(8,128)(2,1)S(1)}, bf16[8,10368]{1,0:T(8,128)(2,1)S(1)}, bf16[8,10368]{1,0:T(8,128)(2,1)S(1)}, bf16[72,1024]{1,0:T(8,128)(2,1)S(1)}) custom-call(s32[8]{0:T(128)S(1)} %copy-done.2, bf16[32,10368]{1,0:T(8,128)(2,1)S(1)} %collective-permute-done.11.payload.payload_hbm, ...), custom_call_target="tpu_custom_call" | custom-call | tf_op jit(solution)/shard_map/after_swap/pallas_call | solution.py:456
  78.5 1.6 %collective-permute-start.21 = (bf16[72,1024]{1,0:T(8,128)(2,1)S(1)}, bf16[72,1024]{1,0:T(8,128)(2,1)S(1)}, u32[]{:S(2)}, u32[]{:S(2)}) collective-permute-start(bf16[72,1024]{1,0:T(8,128)(2,1)S(1)} %get-tuple-element.85.refs_0_), channel_id=1, source_target_pairs={{16,0},{24,8},{0,16},{8,24},{17,1},{25,9},{1,17},{9,25},{18,2},{26... | collective-permute-start | bytes 442376 | tf_op jit(solution)/shard_map/ppermute | solution.py:500
  80.2 0.6 collective-permute-start.15
  80.7 0.6 collective-permute-start.16
  81.3 2.3 %collective-permute-start.17 = (bf16[8,10368]{1,0:T(8,128)(2,1)S(1)}, bf16[8,10368]{1,0:T(8,128)(2,1)S(1)}, u32[]{:S(2)}, u32[]{:S(2)}) collective-permute-start(bf16[8,10368]{1,0:T(8,128)(2,1)S(1)} %get-tuple-element.77), channel_id=1, source_target_pairs={{3,0},{2,1},{1,2},{0,3},{7,4},{6,5},{5,6},{4,7},{11,8},{10,9},{9,1... | collective-permute-start | bytes 497672 | tf_op jit(solution)/shard_map/ppermute | solution.py:490
  83.7 0.1 collective-permute-done.21.refs_2_
  83.8 0.4 collective-permute-start.22
  84.2 2.5 %own_terms.1.total = f32[896,1024]{1,0:T(8,128)S(1)} custom-call(bf16[1,896,1024]{2,1,0:T(8,128)(2,1)S(1)} %copy-done, bf16[72,896]{1,0:T(8,128)(2,1)S(1)} %get-tuple-element.51.refs_4_.refs_0_, bf16[72,896]{1,0:T(8,128)(2,1)S(1)} %collective-permute-done.7.refs_5_.refs_1_, bf16[72,896]{1,0:T(8,128)(2,1)S(1)} %collective-permute-done.8.refs_6_.refs_2_, ...), custom_call_target="tpu_custom_call" | custom-call | tf_op jit(solution)/shard_map/own_terms/pallas_call | solution.py:456
  86.6 0.4 collective-permute-done.15.refs_1_
  87.0 2.9 %collective-permute-done.16.refs_2_ = bf16[8,10368]{1,0:T(8,128)(2,1)S(1)} collective-permute-done((bf16[8,10368]{1,0:T(8,128)(2,1)S(1)}, bf16[8,10368]{1,0:T(8,128)(2,1)S(1)}, u32[]{:S(2)}, u32[]{:S(2)}) %collective-permute-start.16) | collective-permute-done | bytes 165920 | tf_op jit(solution)/shard_map/ppermute | solution.py:490
  89.9 1.4 %far_results.1 = (bf16[128,1024]{1,0:T(8,128)(2,1)}, bf16[128,3584]{1,0:T(8,128)(2,1)}) custom-call(bf16[4,128,96]{2,1,0:T(8,128)(2,1)S(1)} %get-tuple-element.63.picks_ref, f32[128,1]{1,0:T(8,128)S(1)} %get-tuple-element.64.refs_0_.gate_ref, bf16[8,10368]{1,0:T(8,128)(2,1)S(1)} %get-tuple-element.74.refs_0_, ...), custom_call_target="tpu_custom_call" | custom-call | tf_op jit(solution)/shard_map/far_results/pallas_call | solution.py:456
  91.3 3.1 %update.1 = (bf16[1,896,1024]{2,1,0:T(8,128)(2,1)}, bf16[1,896,1024]{2,1,0:T(8,128)(2,1)}) custom-call(s32[8]{0:T(128)S(1)} %copy-done.2, f32[896,1024]{1,0:T(8,128)S(1)} %own_terms.1.total, bf16[896,1024]{1,0:T(8,128)(2,1)S(1)} %get-tuple-element.84.old_weight, bf16[32,10368]{1,0:T(8,128)(2,1)S(1)} %collective-permute-done.11.payload.payload_hbm, ...), custom_call_target="tpu_custom_call" | custom-call | flops 528482304 | bytes 11010048 | tf_op jit(solution)/shard_map/update/pallas_call | solution.py:667
  (25 shorter events, 0.1 us)
Async XLA Ops:
  4.0 12.6 %collective-permute-start = (bf16[16,10368]{1,0:T(8,128)(2,1)}, bf16[16,10368]{1,0:T(8,128)(2,1)S(1)}, u32[]{:S(2)}, u32[]{:S(2)}) collective-permute-start(bf16[16,10368]{1,0:T(8,128)(2,1)} %get-tuple-element.48), channel_id=1, source_target_pairs={{0,1},{1,0},{2,3},{3,2},{4,5},{5,4},{6,7},{7,6},{8,9},{9,8},{10,11... | collective-permute-start | bytes 995336 | tf_op jit(solution)/shard_map/ppermute | solution.py:483
  7.0 17.3 %collective-permute-start.1 = (bf16[16,10368]{1,0:T(8,128)(2,1)}, bf16[16,10368]{1,0:T(8,128)(2,1)S(1)}, u32[]{:S(2)}, u32[]{:S(2)}) collective-permute-start(bf16[16,10368]{1,0:T(8,128)(2,1)} %get-tuple-element.49), channel_id=1, source_target_pairs={{0,2},{1,3},{2,0},{3,1},{4,6},{5,7},{6,4},{7,5},{8,10},{9,11},{10,... | collective-permute-start | bytes 995336 | tf_op jit(solution)/shard_map/ppermute | solution.py:483
  8.6 25.3 %collective-permute-start.2 = (bf16[16,10368]{1,0:T(8,128)(2,1)}, bf16[16,10368]{1,0:T(8,128)(2,1)S(1)}, u32[]{:S(2)}, u32[]{:S(2)}) collective-permute-start(bf16[16,10368]{1,0:T(8,128)(2,1)} %get-tuple-element.50), channel_id=1, source_target_pairs={{0,3},{1,2},{2,1},{3,0},{4,7},{5,6},{6,5},{7,4},{8,11},{9,10},{10,... | collective-permute-start | bytes 995336 | tf_op jit(solution)/shard_map/ppermute | solution.py:483
  8.6 25.6 %collective-permute-start.3 = (bf16[8,10368]{1,0:T(8,128)(2,1)}, bf16[8,10368]{1,0:T(8,128)(2,1)S(1)}, u32[]{:S(2)}, u32[]{:S(2)}) collective-permute-start(bf16[8,10368]{1,0:T(8,128)(2,1)} %get-tuple-element.55), channel_id=1, source_target_pairs={{0,4},{1,5},{2,6},{3,7},{4,0},{5,1},{6,2},{7,3},{8,12},{9,13},{10,... | collective-permute-start | bytes 497672 | tf_op jit(solution)/shard_map/ppermute | solution.py:483
  11.6 5.1 %copy-start.6 = (bf16[8,10368]{1,0:T(8,128)(2,1)S(1)}, bf16[8,10368]{1,0:T(8,128)(2,1)}, u32[]{:S(2)}) copy-start(bf16[8,10368]{1,0:T(8,128)(2,1)} %get-tuple-element.57) | copy-start | bytes 497668
  11.6 12.7 %copy-start.5 = (bf16[8,10368]{1,0:T(8,128)(2,1)S(1)}, bf16[8,10368]{1,0:T(8,128)(2,1)}, u32[]{:S(2)}) copy-start(bf16[8,10368]{1,0:T(8,128)(2,1)} %get-tuple-element.58) | copy-start | bytes 497668
  11.6 22.3 %copy-start.1 = (bf16[16,10368]{1,0:T(8,128)(2,1)S(1)}, bf16[16,10368]{1,0:T(8,128)(2,1)}, u32[]{:S(2)}) copy-start(bf16[16,10368]{1,0:T(8,128)(2,1)} %get-tuple-element.47.refs_0_) | copy-start | bytes 995332
  11.6 24.6 %copy-start.2 = (s32[8]{0:T(128)S(1)}, s32[8]{0:T(128)}, u32[]{:S(2)}) copy-start(s32[8]{0:T(128)} %placement_ref.7) | copy-start | bytes 100
  11.6 24.5 %collective-permute-start.4 = (bf16[8,10368]{1,0:T(8,128)(2,1)}, bf16[8,10368]{1,0:T(8,128)(2,1)S(1)}, u32[]{:S(2)}, u32[]{:S(2)}) collective-permute-start(bf16[8,10368]{1,0:T(8,128)(2,1)} %get-tuple-element.56), channel_id=1, source_target_pairs={{0,6},{1,7},{2,4},{3,5},{4,2},{5,3},{6,0},{7,1},{8,14},{9,15},{10,... | collective-permute-start | bytes 497672 | tf_op jit(solution)/shard_map/ppermute | solution.py:483
  16.7 24.2 %collective-permute-start.5 = (bf16[8,10368]{1,0:T(8,128)(2,1)S(1)}, bf16[8,10368]{1,0:T(8,128)(2,1)S(1)}, u32[]{:S(2)}, u32[]{:S(2)}) collective-permute-start(bf16[8,10368]{1,0:T(8,128)(2,1)S(1)} %copy-done.6), channel_id=1, source_target_pairs={{0,5},{1,4},{2,7},{3,6},{4,1},{5,0},{6,3},{7,2},{8,13},{9,12},{10,... | collective-permute-start | bytes 497672 | tf_op jit(solution)/shard_map/ppermute | solution.py:483
  24.3 16.6 %collective-permute-start.6 = (bf16[8,10368]{1,0:T(8,128)(2,1)S(1)}, bf16[8,10368]{1,0:T(8,128)(2,1)S(1)}, u32[]{:S(2)}, u32[]{:S(2)}) collective-permute-start(bf16[8,10368]{1,0:T(8,128)(2,1)S(1)} %copy-done.5), channel_id=1, source_target_pairs={{0,7},{1,6},{2,5},{3,4},{4,3},{5,2},{6,1},{7,0},{8,15},{9,14},{10,... | collective-permute-start | bytes 497672 | tf_op jit(solution)/shard_map/ppermute | solution.py:483
  34.1 6.8 %collective-permute-start.7 = (bf16[72,896]{1,0:T(8,128)(2,1)S(1)}, bf16[72,896]{1,0:T(8,128)(2,1)S(1)}, u32[]{:S(2)}, u32[]{:S(2)}) collective-permute-start(bf16[72,896]{1,0:T(8,128)(2,1)S(1)} %get-tuple-element.59), channel_id=1, source_target_pairs={{8,0},{0,8},{24,16},{16,24},{9,1},{1,9},{25,17},{17,25},{10,2},{2,... | collective-permute-start | bytes 387080 | tf_op jit(solution)/shard_map/ppermute | solution.py:500
  34.2 6.7 %collective-permute-start.8 = (bf16[72,896]{1,0:T(8,128)(2,1)S(1)}, bf16[72,896]{1,0:T(8,128)(2,1)S(1)}, u32[]{:S(2)}, u32[]{:S(2)}) collective-permute-start(bf16[72,896]{1,0:T(8,128)(2,1)S(1)} %get-tuple-element.60), channel_id=1, source_target_pairs={{16,0},{24,8},{0,16},{8,24},{17,1},{25,9},{1,17},{9,25},{18,2},{26... | collective-permute-start | bytes 387080 | tf_op jit(solution)/shard_map/ppermute | solution.py:500
  36.1 6.4 %collective-permute-start.9 = (bf16[72,896]{1,0:T(8,128)(2,1)S(1)}, bf16[72,896]{1,0:T(8,128)(2,1)S(1)}, u32[]{:S(2)}, u32[]{:S(2)}) collective-permute-start(bf16[72,896]{1,0:T(8,128)(2,1)S(1)} %get-tuple-element.61), channel_id=1, source_target_pairs={{24,0},{16,8},{8,16},{0,24},{25,1},{17,9},{9,17},{1,25},{26,2},{18... | collective-permute-start | bytes 387080 | tf_op jit(solution)/shard_map/ppermute | solution.py:500
  42.5 7.0 %copy-start.3 = (s32[128]{0:T(128)S(1)}, s32[128]{0:T(128)}, u32[]{:S(2)}) copy-start(s32[128]{0:T(128)} %param.10) | copy-start | bytes 1540
  42.6 7.0 %copy-start.4 = (f32[128]{0:T(128)S(1)}, f32[128]{0:T(128)}, u32[]{:S(2)}) copy-start(f32[128]{0:T(128)} %param.8) | copy-start | bytes 1540
  45.0 4.5 %collective-permute-start.10 = (bf16[72,4864]{1,0:T(8,128)(2,1)S(1)}, bf16[72,4864]{1,0:T(8,128)(2,1)S(1)}, u32[]{:S(2)}, u32[]{:S(2)}) collective-permute-start(bf16[72,4864]{1,0:T(8,128)(2,1)S(1)} %get-tuple-element.62), channel_id=1, source_target_pairs={{8,0},{0,8},{24,16},{16,24},{9,1},{1,9},{25,17},{17,25},{10,2},{2,... | collective-permute-start | bytes 2101256 | tf_op jit(solution)/shard_map/ppermute | solution.py:500
  45.3 32.3 %collective-permute-start.11 = (bf16[32,10368]{1,0:T(8,128)(2,1)S(1)}, bf16[32,10368]{1,0:T(8,128)(2,1)S(1)}, u32[]{:S(2)}, u32[]{:S(2)}) collective-permute-start(bf16[32,10368]{1,0:T(8,128)(2,1)S(1)} %get-tuple-element.65), channel_id=1, source_target_pairs={{0,4},{1,5},{2,6},{3,7},{4,0},{5,1},{6,2},{7,3},{8,12},{9,13},{10,... | collective-permute-start | bytes 1990664 | tf_op jit(solution)/shard_map/ppermute | solution.py:494
  48.0 33.3 %collective-permute-start.18 = (bf16[72,4864]{1,0:T(8,128)(2,1)S(1)}, bf16[72,4864]{1,0:T(8,128)(2,1)S(1)}, u32[]{:S(2)}, u32[]{:S(2)}) collective-permute-start(bf16[72,4864]{1,0:T(8,128)(2,1)S(1)} %get-tuple-element.82), channel_id=1, source_target_pairs={{16,0},{24,8},{0,16},{8,24},{17,1},{25,9},{1,17},{9,25},{18,2},{26... | collective-permute-start | bytes 2101256 | tf_op jit(solution)/shard_map/ppermute | solution.py:500
  49.5 34.1 %collective-permute-start.19 = (bf16[72,4864]{1,0:T(8,128)(2,1)S(1)}, bf16[72,4864]{1,0:T(8,128)(2,1)S(1)}, u32[]{:S(2)}, u32[]{:S(2)}) collective-permute-start(bf16[72,4864]{1,0:T(8,128)(2,1)S(1)} %get-tuple-element.83), channel_id=1, source_target_pairs={{24,0},{16,8},{8,16},{0,24},{25,1},{17,9},{9,17},{1,25},{26,2},{18... | collective-permute-start | bytes 2101256 | tf_op jit(solution)/shard_map/ppermute | solution.py:500
  50.1 34.0 %copy-start = (bf16[1,896,1024]{2,1,0:T(8,128)(2,1)S(1)}, bf16[1,896,1024]{2,1,0:T(8,128)(2,1)}, u32[]{:S(2)}) copy-start(bf16[1,896,1024]{2,1,0:T(8,128)(2,1)} %momentum_hbm.1) | copy-start | bytes 5505028
  50.2 6.8 %collective-permute-start.13 = (bf16[8,10368]{1,0:T(8,128)(2,1)S(1)}, bf16[8,10368]{1,0:T(8,128)(2,1)S(1)}, u32[]{:S(2)}, u32[]{:S(2)}) collective-permute-start(bf16[8,10368]{1,0:T(8,128)(2,1)S(1)} %get-tuple-element.71), channel_id=1, source_target_pairs={{1,0},{0,1},{3,2},{2,3},{5,4},{4,5},{7,6},{6,7},{9,8},{8,9},{11,10... | collective-permute-start | bytes 497672 | tf_op jit(solution)/shard_map/ppermute | solution.py:490
  50.5 16.4 %collective-permute-start.12 = (bf16[8,10368]{1,0:T(8,128)(2,1)S(1)}, bf16[8,10368]{1,0:T(8,128)(2,1)S(1)}, u32[]{:S(2)}, u32[]{:S(2)}) collective-permute-start(bf16[8,10368]{1,0:T(8,128)(2,1)S(1)} %get-tuple-element.70), channel_id=1, source_target_pairs={{2,0},{3,1},{0,2},{1,3},{6,4},{7,5},{4,6},{5,7},{10,8},{11,9},{8,1... | collective-permute-start | bytes 497672 | tf_op jit(solution)/shard_map/ppermute | solution.py:490
  57.1 12.7 %collective-permute-start.14 = (bf16[8,10368]{1,0:T(8,128)(2,1)S(1)}, bf16[8,10368]{1,0:T(8,128)(2,1)S(1)}, u32[]{:S(2)}, u32[]{:S(2)}) collective-permute-start(bf16[8,10368]{1,0:T(8,128)(2,1)S(1)} %pass_on.1), channel_id=1, source_target_pairs={{3,0},{2,1},{1,2},{0,3},{7,4},{6,5},{5,6},{4,7},{11,8},{10,9},{9,1... | collective-permute-start | bytes 497672 | tf_op jit(solution)/shard_map/ppermute | solution.py:490
  78.5 5.3 %collective-permute-start.21 = (bf16[72,1024]{1,0:T(8,128)(2,1)S(1)}, bf16[72,1024]{1,0:T(8,128)(2,1)S(1)}, u32[]{:S(2)}, u32[]{:S(2)}) collective-permute-start(bf16[72,1024]{1,0:T(8,128)(2,1)S(1)} %get-tuple-element.85.refs_0_), channel_id=1, source_target_pairs={{16,0},{24,8},{0,16},{8,24},{17,1},{25,9},{1,17},{9,25},{18,2},{26... | collective-permute-start | bytes 442376 | tf_op jit(solution)/shard_map/ppermute | solution.py:500
  80.2 6.9 %collective-permute-start.15 = (bf16[8,10368]{1,0:T(8,128)(2,1)S(1)}, bf16[8,10368]{1,0:T(8,128)(2,1)S(1)}, u32[]{:S(2)}, u32[]{:S(2)}) collective-permute-start(bf16[8,10368]{1,0:T(8,128)(2,1)S(1)} %get-tuple-element.75), channel_id=1, source_target_pairs={{2,0},{3,1},{0,2},{1,3},{6,4},{7,5},{4,6},{5,7},{10,8},{11,9},{8,1... | collective-permute-start | bytes 497672 | tf_op jit(solution)/shard_map/ppermute | solution.py:490
  80.7 9.2 %collective-permute-start.16 = (bf16[8,10368]{1,0:T(8,128)(2,1)S(1)}, bf16[8,10368]{1,0:T(8,128)(2,1)S(1)}, u32[]{:S(2)}, u32[]{:S(2)}) collective-permute-start(bf16[8,10368]{1,0:T(8,128)(2,1)S(1)} %get-tuple-element.76), channel_id=1, source_target_pairs={{1,0},{0,1},{3,2},{2,3},{5,4},{4,5},{7,6},{6,7},{9,8},{8,9},{11,10... | collective-permute-start | bytes 497672 | tf_op jit(solution)/shard_map/ppermute | solution.py:490
  81.3 8.6 %collective-permute-start.17 = (bf16[8,10368]{1,0:T(8,128)(2,1)S(1)}, bf16[8,10368]{1,0:T(8,128)(2,1)S(1)}, u32[]{:S(2)}, u32[]{:S(2)}) collective-permute-start(bf16[8,10368]{1,0:T(8,128)(2,1)S(1)} %get-tuple-element.77), channel_id=1, source_target_pairs={{3,0},{2,1},{1,2},{0,3},{7,4},{6,5},{5,6},{4,7},{11,8},{10,9},{9,1... | collective-permute-start | bytes 497672 | tf_op jit(solution)/shard_map/ppermute | solution.py:490
  83.7 7.7 %collective-permute-start.20 = (bf16[72,1024]{1,0:T(8,128)(2,1)S(1)}, bf16[72,1024]{1,0:T(8,128)(2,1)S(1)}, u32[]{:S(2)}, u32[]{:S(2)}) collective-permute-start(bf16[72,1024]{1,0:T(8,128)(2,1)S(1)} %get-tuple-element.85.refs_0_), channel_id=1, source_target_pairs={{8,0},{0,8},{24,16},{16,24},{9,1},{1,9},{25,17},{17,25},{10,2},{2,... | collective-permute-start | bytes 442376 | tf_op jit(solution)/shard_map/ppermute | solution.py:500
  83.8 7.5 %collective-permute-start.22 = (bf16[72,1024]{1,0:T(8,128)(2,1)S(1)}, bf16[72,1024]{1,0:T(8,128)(2,1)S(1)}, u32[]{:S(2)}, u32[]{:S(2)}) collective-permute-start(bf16[72,1024]{1,0:T(8,128)(2,1)S(1)} %collective-permute-done.21.refs_2_), channel_id=1, source_target_pairs={{8,0},{0,8},{24,16},{16,24},{9,1},{1,9},{25,17},{17,25},{10,2},{2,... | collective-permute-start | bytes 442376 | tf_op jit(solution)/shard_map/ppermute | solution.py:500
